TPU v7x, 32 devices: a whole 2x2x4 slice. The times are simulated.
32 devices in a mesh: section: 2 (over core), dp: 4 (over y, x), seq: 4 (over z).
Axes of the slice: x: 2, y: 2, z: 4, core: 2. Of those that a mesh axis runs over, the one named last changes fastest.
Arguments:
- inputs: bfloat16 [8, 1024, 1088], P('dp', 'seq'), may hold values from -6 to 6
- cotangent: bfloat16 [8, 1024, 1088], P('dp', 'seq'), may hold values from -6 to 6
- first_gain: bfloat16 [2, 1088], P('section', ('dp', 'seq')), may hold values from 0.5 to 1.5
- first_shift: bfloat16 [2, 1088], P('section', ('dp', 'seq')), may hold values from -1.75 to 1.75
- joint_weight: bfloat16 [2, 1088, 3264], P('section', ('dp', 'seq')), may hold values from -0.1875 to 0.1875
- query_bias: bfloat16 [2, 1088], P('section', ('dp', 'seq')), may hold values from -3 to 3
- value_bias: bfloat16 [2, 1088], P('section', ('dp', 'seq')), may hold values from -0.3125 to 0.3125
- output_weight: bfloat16 [2, 1088, 1088], P('section', ('dp', 'seq')), may hold values from -0.75 to 0.75
- output_bias: bfloat16 [2, 1088], P('section', ('dp', 'seq')), may hold values from -1.75 to 1.75
- second_gain: bfloat16 [2, 1088], P('section', ('dp', 'seq')), may hold values from 0.5 to 1.5
- second_shift: bfloat16 [2, 1088], P('section', ('dp', 'seq')), may hold values from -1.75 to 1.75
- expand_weight: bfloat16 [2, 1088, 4352], P('section', ('dp', 'seq')), may hold values from -0.1875 to 0.1875
- expand_bias: bfloat16 [2, 4352], P('section', ('dp', 'seq')), may hold values from -3 to 3
- reduce_weight: bfloat16 [2, 4352, 1088], P('section', ('dp', 'seq')), may hold values from -0.09375 to 0.09375
- reduce_bias: bfloat16 [2, 1088], P('section', ('dp', 'seq')), may hold values from -1.75 to 1.75
Outputs:
- layer_outputs: bfloat16 [2, 8, 1024, 1088], P('section', 'dp', 'seq')
- input_grads: bfloat16 [2, 8, 1024, 1088], P('section', 'dp', 'seq')
- grad_first_gain: float32 [2, 1088], P('section', ('dp', 'seq'))
- grad_first_shift: float32 [2, 1088], P('section', ('dp', 'seq'))
- grad_joint_weight: float32 [2, 1088, 3264], P('section', ('dp', 'seq'))
- grad_query_bias: float32 [2, 1088], P('section', ('dp', 'seq'))
- grad_value_bias: float32 [2, 1088], P('section', ('dp', 'seq'))
- grad_output_weight: float32 [2, 1088, 1088], P('section', ('dp', 'seq'))
- grad_output_bias: float32 [2, 1088], P('section', ('dp', 'seq'))
- grad_second_gain: float32 [2, 1088], P('section', ('dp', 'seq'))
- grad_second_shift: float32 [2, 1088], P('section', ('dp', 'seq'))
- grad_expand_weight: float32 [2, 1088, 4352], P('section', ('dp', 'seq'))
- grad_expand_bias: float32 [2, 4352], P('section', ('dp', 'seq'))
- grad_reduce_weight: float32 [2, 4352, 1088], P('section', ('dp', 'seq'))
- grad_reduce_bias: float32 [2, 1088], P('section', ('dp', 'seq'))
All inputs are finite; a program needn't handle non-finite values.
Results may differ from a plain program's by a relative error of at most 0.028.
Values may be sent and summed in bfloat16 or wider, within the bound.
A program may use at most 320 MiB of HBM per device.

v0:
```python
from functools import partial

import jax
import jax.numpy as jnp
from jax import lax
from jax.sharding import PartitionSpec as P

HEADS = 17
HDIM = 64
BLK = 256


epsilon = 1e-05
far_below = -1e30


def passed_along(value, axis, steps):
    count = lax.axis_size(axis)
    first, last = (max(0, -steps), min(count, count - steps))
    return lax.ppermute(value, axis, [(source, source + steps) for source in range(first, last)])


def normalize(values, scales, offsets):
    centre = jnp.mean(values, axis=-1, keepdims=True)
    centred = values - centre
    inverse = lax.rsqrt(jnp.mean(centred * centred, axis=-1, keepdims=True) + epsilon)
    unit_rows = centred * inverse
    return (unit_rows * scales + offsets, unit_rows, inverse)


def normalize_back(upstream, unit_rows, inverse):
    return inverse * (
        upstream
        - jnp.mean(upstream, axis=-1, keepdims=True)
        - unit_rows * jnp.mean(upstream * unit_rows, axis=-1, keepdims=True)
    )


def score_block(query, key_block, block_index, row_block):
    scores = jnp.einsum(
        "qhd,khd->qhk", query, key_block, preferred_element_type=jnp.float32
    ) * HDIM ** (-0.5)
    highest = jnp.max(scores, axis=-1)
    allowed = (block_index <= row_block)[:, None]
    exponent = jnp.exp(scores - highest[..., None]) * allowed[..., None].astype(jnp.float32)
    levels = jnp.where(allowed, highest, far_below)
    return (exponent, levels)


def attend_forward(query, keys_all, values_all, row_block):
    length = keys_all.shape[0]
    row_count = query.shape[0]
    key_shaped = keys_all.reshape(length, HEADS, HDIM)
    value_shaped = values_all.reshape(length, HEADS, HDIM)
    block_limit = row_block[-1] + 1

    def advance(block_index, carried):
        running_peak, running_sum, weighted = carried
        key_block = lax.dynamic_slice_in_dim(key_shaped, block_index * BLK, BLK, 0)
        value_block = lax.dynamic_slice_in_dim(value_shaped, block_index * BLK, BLK, 0)
        exponent, levels = score_block(query, key_block, block_index, row_block)
        weights = exponent.astype(jnp.bfloat16)
        block_out = jnp.einsum(
            "qhk,khd->qhd", weights, value_block, preferred_element_type=jnp.float32
        )
        newest_peak = jnp.maximum(running_peak, levels)
        shrink_old = jnp.exp(running_peak - newest_peak)
        shrink_new = jnp.exp(levels - newest_peak)
        running_sum = running_sum * shrink_old + shrink_new * jnp.sum(exponent, axis=-1)
        weighted = weighted * shrink_old[..., None] + shrink_new[..., None] * block_out
        return (newest_peak, running_sum, weighted)

    initial = (
        jnp.full((row_count, HEADS), far_below, jnp.float32),
        jnp.zeros((row_count, HEADS), jnp.float32),
        jnp.zeros((row_count, HEADS, HDIM), jnp.float32),
    )
    running_peak, running_sum, weighted = lax.fori_loop(0, block_limit, advance, initial)
    return (weighted / running_sum[..., None], running_peak + jnp.log(running_sum))


def attend_backward(query, keys_all, values_all, row_block, attended, log_total, grad_attended):
    length = keys_all.shape[0]
    key_shaped = keys_all.reshape(length, HEADS, HDIM)
    value_shaped = values_all.reshape(length, HEADS, HDIM)
    block_limit = row_block[-1] + 1
    delta = jnp.sum(grad_attended * attended, axis=-1)

    def advance(block_index, carried):
        grad_query, grad_keys, grad_values = carried
        key_block = lax.dynamic_slice_in_dim(key_shaped, block_index * BLK, BLK, 0)
        value_block = lax.dynamic_slice_in_dim(value_shaped, block_index * BLK, BLK, 0)
        exponent, levels = score_block(query, key_block, block_index, row_block)
        weights = exponent.astype(jnp.bfloat16)
        factor = jnp.exp(levels - log_total)
        scaled = (factor[..., None] * grad_attended).astype(jnp.bfloat16)
        grad_weights = jnp.einsum(
            "qhd,khd->qhk", scaled, value_block, preferred_element_type=jnp.float32
        )
        grad_scores = (exponent * (grad_weights - (factor * delta)[..., None])).astype(jnp.bfloat16)
        grad_query = grad_query + jnp.einsum(
            "qhk,khd->qhd", grad_scores, key_block, preferred_element_type=jnp.float32
        )
        grad_key = jnp.einsum(
            "qhk,qhd->khd", grad_scores, query, preferred_element_type=jnp.float32
        )
        grad_value = jnp.einsum("qhk,qhd->khd", weights, scaled, preferred_element_type=jnp.float32)
        grad_keys = lax.dynamic_update_slice_in_dim(grad_keys, grad_key, block_index * BLK, 0)
        grad_values = lax.dynamic_update_slice_in_dim(grad_values, grad_value, block_index * BLK, 0)
        return (grad_query, grad_keys, grad_values)

    initial = (
        jnp.zeros(query.shape, jnp.float32),
        jnp.zeros((length, HEADS, HDIM), jnp.float32),
        jnp.zeros((length, HEADS, HDIM), jnp.float32),
    )
    grad_query, grad_keys, grad_values = lax.fori_loop(0, block_limit, advance, initial)
    return (
        grad_query,
        grad_keys.reshape(length, HEADS * HDIM),
        grad_values.reshape(length, HEADS * HDIM),
    )


def project(source, params):
    feature_width = HEADS * HDIM
    normed, unit_rows, inverse = normalize(
        source, params[0].astype(jnp.float32), params[1].astype(jnp.float32)
    )
    normed_low = normed.astype(jnp.bfloat16)
    mixture = jnp.dot(normed_low, params[2], preferred_element_type=jnp.float32)
    query_low = (mixture[:, :feature_width] + params[3].astype(jnp.float32)).astype(jnp.bfloat16)
    keys_low = mixture[:, feature_width : 2 * feature_width].astype(jnp.bfloat16)
    values_low = (mixture[:, 2 * feature_width :] + params[4].astype(jnp.float32)).astype(
        jnp.bfloat16
    )
    return (unit_rows, inverse, normed_low, query_low, keys_low, values_low)


def complete(source, params, projected, gathered, row_block):
    row_count = source.shape[0]
    query = projected[3].reshape(row_count, HEADS, HDIM)
    attended, log_total = attend_forward(query, gathered[0], gathered[1], row_block)
    attended_low = attended.reshape(row_count, HEADS * HDIM).astype(jnp.bfloat16)
    middle = source + (
        jnp.dot(attended_low, params[5], preferred_element_type=jnp.float32)
        + params[6].astype(jnp.float32)
    )
    second, unit_second, inverse_second = normalize(
        middle, params[7].astype(jnp.float32), params[8].astype(jnp.float32)
    )
    second_low = second.astype(jnp.bfloat16)
    hidden = jnp.dot(second_low, params[9], preferred_element_type=jnp.float32) + params[10].astype(
        jnp.float32
    )
    active, gelu_pull = jax.vjp(partial(jax.nn.gelu, approximate=False), hidden)
    active_low = active.astype(jnp.bfloat16)
    result = middle + (
        jnp.dot(active_low, params[11], preferred_element_type=jnp.float32)
        + params[12].astype(jnp.float32)
    )
    saved = (
        query,
        attended,
        log_total,
        attended_low,
        unit_second,
        inverse_second,
        second_low,
        gelu_pull,
        active_low,
    )
    return (result, saved)


def layer_backward(source, upstream, params, projected, gathered, row_block):
    unit_first, inverse_first, normed_low, query_low, keys_low, values_low = projected
    row_count = source.shape[0]
    feature_width = HEADS * HDIM
    result, saved = complete(source, params, projected, gathered, row_block)
    (
        query,
        attended,
        log_total,
        attended_low,
        unit_second,
        inverse_second,
        second_low,
        gelu_pull,
        active_low,
    ) = saved
    top_low = upstream.astype(jnp.bfloat16)
    grad_reduce_bias = jnp.sum(top_low.astype(jnp.float32), axis=0)
    grad_reduce_weight = jnp.einsum(
        "tf,td->fd", active_low, top_low, preferred_element_type=jnp.float32
    )
    grad_active = jnp.einsum("td,fd->tf", top_low, params[11], preferred_element_type=jnp.float32)
    grad_hidden_low = gelu_pull(grad_active)[0].astype(jnp.bfloat16)
    grad_expand_bias = jnp.sum(grad_hidden_low.astype(jnp.float32), axis=0)
    grad_expand_weight = jnp.einsum(
        "td,tf->df", second_low, grad_hidden_low, preferred_element_type=jnp.float32
    )
    grad_second = jnp.einsum(
        "tf,df->td", grad_hidden_low, params[9], preferred_element_type=jnp.float32
    )
    grad_second_gain = jnp.sum(grad_second * unit_second, axis=0)
    grad_second_shift = jnp.sum(grad_second, axis=0)
    grad_middle = upstream + normalize_back(
        grad_second * params[7].astype(jnp.float32), unit_second, inverse_second
    )
    branch_low = grad_middle.astype(jnp.bfloat16)
    grad_output_bias = jnp.sum(branch_low.astype(jnp.float32), axis=0)
    grad_output_weight = jnp.einsum(
        "td,te->de", attended_low, branch_low, preferred_element_type=jnp.float32
    )
    grad_attended = jnp.einsum(
        "te,de->td", branch_low, params[5], preferred_element_type=jnp.float32
    )
    grad_query, grad_keys_full, grad_values_full = attend_backward(
        query,
        gathered[0],
        gathered[1],
        row_block,
        attended,
        log_total,
        grad_attended.reshape(row_count, HEADS, HDIM),
    )
    grad_keys, grad_values = (
        lax.psum_scatter(grad_keys_full, "seq", scatter_dimension=0, tiled=True),
        lax.psum_scatter(grad_values_full, "seq", scatter_dimension=0, tiled=True),
    )
    scale_factor = HDIM ** (-0.5)
    grad_mixture = jnp.concatenate(
        [
            grad_query.reshape(row_count, feature_width) * scale_factor,
            grad_keys * scale_factor,
            grad_values,
        ],
        axis=1,
    ).astype(jnp.bfloat16)
    grad_query_bias = jnp.sum(grad_mixture[:, :feature_width].astype(jnp.float32), axis=0)
    grad_value_bias = jnp.sum(grad_mixture[:, 2 * feature_width :].astype(jnp.float32), axis=0)
    grad_joint_weight = jnp.einsum(
        "td,te->de", normed_low, grad_mixture, preferred_element_type=jnp.float32
    )
    grad_normed = jnp.einsum(
        "te,de->td", grad_mixture, params[2], preferred_element_type=jnp.float32
    )
    grad_first_gain = jnp.sum(grad_normed * unit_first, axis=0)
    grad_first_shift = jnp.sum(grad_normed, axis=0)
    grad_source = grad_middle + normalize_back(
        grad_normed * params[0].astype(jnp.float32), unit_first, inverse_first
    )
    grads = (
        grad_first_gain,
        grad_first_shift,
        grad_joint_weight,
        grad_query_bias,
        grad_value_bias,
        grad_output_weight,
        grad_output_bias,
        grad_second_gain,
        grad_second_shift,
        grad_expand_weight,
        grad_expand_bias,
        grad_reduce_weight,
        grad_reduce_bias,
    )
    return (grad_source.astype(jnp.bfloat16), grads)


def body(
    inputs,
    cotangent,
    first_gain,
    first_shift,
    joint_weight,
    query_bias,
    value_bias,
    output_weight,
    output_bias,
    second_gain,
    second_shift,
    expand_weight,
    expand_bias,
    reduce_weight,
    reduce_bias,
):
    section_index = lax.axis_index("section")
    micro_count = inputs.shape[0]
    row_count = inputs.shape[1]
    first_row = lax.axis_index("seq") * row_count
    row_block = (first_row + jnp.arange(row_count, dtype=jnp.int32)) // BLK
    owned = (
        first_gain[0],
        first_shift[0],
        joint_weight[0],
        query_bias[0],
        value_bias[0],
        output_weight[0],
        output_bias[0],
        second_gain[0],
        second_shift[0],
        expand_weight[0],
        expand_bias[0],
        reduce_weight[0],
        reduce_bias[0],
    )
    forward_params = (
        lax.all_gather(first_gain[0], ("dp", "seq"), axis=0, tiled=True),
        lax.all_gather(first_shift[0], ("dp", "seq"), axis=0, tiled=True),
        lax.all_gather(joint_weight[0], ("dp", "seq"), axis=0, tiled=True),
        lax.all_gather(query_bias[0], ("dp", "seq"), axis=0, tiled=True),
        lax.all_gather(value_bias[0], ("dp", "seq"), axis=0, tiled=True),
        lax.all_gather(output_weight[0], ("dp", "seq"), axis=0, tiled=True),
        lax.all_gather(output_bias[0], ("dp", "seq"), axis=0, tiled=True),
        lax.all_gather(second_gain[0], ("dp", "seq"), axis=0, tiled=True),
        lax.all_gather(second_shift[0], ("dp", "seq"), axis=0, tiled=True),
        lax.all_gather(expand_weight[0], ("dp", "seq"), axis=0, tiled=True),
        lax.all_gather(expand_bias[0], ("dp", "seq"), axis=0, tiled=True),
        lax.all_gather(reduce_weight[0], ("dp", "seq"), axis=0, tiled=True),
        lax.all_gather(reduce_bias[0], ("dp", "seq"), axis=0, tiled=True),
    )
    incoming = jnp.zeros(inputs.shape[1:], jnp.bfloat16)
    section_inputs = []
    produced = []
    key_sets = []
    for tick_index in range(micro_count + 1):
        section_input = jnp.where(
            section_index == 0, inputs[min(tick_index, micro_count - 1)], incoming
        )
        source = section_input.astype(jnp.float32)
        projected = project(source, forward_params)
        gathered = (
            lax.all_gather(projected[4], "seq", axis=0, tiled=True),
            lax.all_gather(projected[5], "seq", axis=0, tiled=True),
        )
        result, unused = complete(source, forward_params, projected, gathered, row_block)
        result_low = result.astype(jnp.bfloat16)
        section_inputs.append(section_input)
        produced.append(result_low)
        key_sets.append(gathered)
        if tick_index < micro_count:
            incoming = passed_along(result_low, "section", 1)
    backward_params = (
        lax.all_gather(first_gain[0], ("dp", "seq"), axis=0, tiled=True),
        lax.all_gather(first_shift[0], ("dp", "seq"), axis=0, tiled=True),
        lax.all_gather(joint_weight[0], ("dp", "seq"), axis=0, tiled=True),
        lax.all_gather(query_bias[0], ("dp", "seq"), axis=0, tiled=True),
        lax.all_gather(value_bias[0], ("dp", "seq"), axis=0, tiled=True),
        lax.all_gather(output_weight[0], ("dp", "seq"), axis=0, tiled=True),
        lax.all_gather(output_bias[0], ("dp", "seq"), axis=0, tiled=True),
        lax.all_gather(second_gain[0], ("dp", "seq"), axis=0, tiled=True),
        lax.all_gather(second_shift[0], ("dp", "seq"), axis=0, tiled=True),
        lax.all_gather(expand_weight[0], ("dp", "seq"), axis=0, tiled=True),
        lax.all_gather(expand_bias[0], ("dp", "seq"), axis=0, tiled=True),
        lax.all_gather(reduce_weight[0], ("dp", "seq"), axis=0, tiled=True),
        lax.all_gather(reduce_bias[0], ("dp", "seq"), axis=0, tiled=True),
    )
    totals = tuple((jnp.zeros(piece.shape, jnp.float32) for piece in backward_params))
    shares = tuple((jnp.zeros(piece.shape, jnp.float32) for piece in owned))
    returning = jnp.zeros(inputs.shape[1:], jnp.bfloat16)
    sent_back = []
    for tick_index in range(micro_count + 1):
        upper_pick = min(tick_index + 1, micro_count)
        lower_pick = max(tick_index - 1, 0)
        section_input = jnp.where(
            section_index == 1, section_inputs[upper_pick], section_inputs[lower_pick]
        )
        upstream = jnp.where(
            section_index == 1, cotangent[min(tick_index, micro_count - 1)], returning
        ).astype(jnp.float32)
        weight_valid = jnp.where(
            section_index == 1,
            1.0 if tick_index < micro_count else 0.0,
            1.0 if tick_index >= 1 else 0.0,
        ).astype(jnp.float32)
        source = section_input.astype(jnp.float32)
        projected = project(source, backward_params)
        gathered = (
            lax.all_gather(projected[4], "seq", axis=0, tiled=True),
            lax.all_gather(projected[5], "seq", axis=0, tiled=True),
        )
        grad_source, grads = layer_backward(
            source, upstream, backward_params, projected, gathered, row_block
        )
        masked = tuple((update * weight_valid for update in grads))
        totals = tuple((running + update for running, update in zip(totals, masked)))
        sent_back.append(grad_source)
        if tick_index < micro_count:
            returning = passed_along(grad_source, "section", -1)
    layer_outputs = jnp.stack(
        [
            jnp.where(section_index == 0, produced[position], produced[position + 1])
            for position in range(micro_count)
        ]
    )[None]
    input_grads = jnp.stack(
        [
            jnp.where(section_index == 1, sent_back[position], sent_back[position + 1])
            for position in range(micro_count)
        ]
    )[None]
    (
        sum_first_gain,
        sum_first_shift,
        sum_joint_weight,
        sum_query_bias,
        sum_value_bias,
        sum_output_weight,
        sum_output_bias,
        sum_second_gain,
        sum_second_shift,
        sum_expand_weight,
        sum_expand_bias,
        sum_reduce_weight,
        sum_reduce_bias,
    ) = totals
    shares = (
        lax.psum_scatter(sum_first_gain, ("dp", "seq"), scatter_dimension=0, tiled=True),
        lax.psum_scatter(sum_first_shift, ("dp", "seq"), scatter_dimension=0, tiled=True),
        lax.psum_scatter(sum_joint_weight, ("dp", "seq"), scatter_dimension=0, tiled=True),
        lax.psum_scatter(sum_query_bias, ("dp", "seq"), scatter_dimension=0, tiled=True),
        lax.psum_scatter(sum_value_bias, ("dp", "seq"), scatter_dimension=0, tiled=True),
        lax.psum_scatter(sum_output_weight, ("dp", "seq"), scatter_dimension=0, tiled=True),
        lax.psum_scatter(sum_output_bias, ("dp", "seq"), scatter_dimension=0, tiled=True),
        lax.psum_scatter(sum_second_gain, ("dp", "seq"), scatter_dimension=0, tiled=True),
        lax.psum_scatter(sum_second_shift, ("dp", "seq"), scatter_dimension=0, tiled=True),
        lax.psum_scatter(sum_expand_weight, ("dp", "seq"), scatter_dimension=0, tiled=True),
        lax.psum_scatter(sum_expand_bias, ("dp", "seq"), scatter_dimension=0, tiled=True),
        lax.psum_scatter(sum_reduce_weight, ("dp", "seq"), scatter_dimension=0, tiled=True),
        lax.psum_scatter(sum_reduce_bias, ("dp", "seq"), scatter_dimension=0, tiled=True),
    )
    return (layer_outputs, input_grads) + tuple((portion[None] for portion in shares))


def solution(mesh):
    return jax.shard_map(
        body,
        mesh=mesh,
        in_specs=(
            P("dp", "seq", None),
            P("dp", "seq", None),
            P("section", ("dp", "seq")),
            P("section", ("dp", "seq")),
            P("section", ("dp", "seq"), None),
            P("section", ("dp", "seq")),
            P("section", ("dp", "seq")),
            P("section", ("dp", "seq"), None),
            P("section", ("dp", "seq")),
            P("section", ("dp", "seq")),
            P("section", ("dp", "seq")),
            P("section", ("dp", "seq"), None),
            P("section", ("dp", "seq")),
            P("section", ("dp", "seq"), None),
            P("section", ("dp", "seq")),
        ),
        out_specs=(
            P("section", "dp", "seq", None),
            P("section", "dp", "seq", None),
            P("section", ("dp", "seq")),
            P("section", ("dp", "seq")),
            P("section", ("dp", "seq"), None),
            P("section", ("dp", "seq")),
            P("section", ("dp", "seq")),
            P("section", ("dp", "seq"), None),
            P("section", ("dp", "seq")),
            P("section", ("dp", "seq")),
            P("section", ("dp", "seq")),
            P("section", ("dp", "seq"), None),
            P("section", ("dp", "seq")),
            P("section", ("dp", "seq"), None),
            P("section", ("dp", "seq")),
        ),
        check_vma=False,
    )
```

profile of v0, /device:TPU:0, one launch (start us, length us, event | category | flops | bytes accessed | tf_op | source)
XLA Modules:
  0.0 3040.1 jit_solution(8812396735171850344)
XLA Ops:
  22.3 81.3 %all-reduce.25 = (bf16[1088]{0:T(1024)(128)(2,1)S(1)}, bf16[1088]{0:T(1024)(128)(2,1)S(1)}, bf16[1088]{0:T(1024)(128)(2,1)S(1)}, bf16[1088]{0:T(1024)(128)(2,1)S...) all-reduce(bf16[1088]{0:T(1024)(128)(2,1)S(1)} %dynamic-update-slic, ...), channel_id=3, replica_groups=mesh['section'=2,'dp'=4,'seq'=4] {'dp','seq'}, use_global_device_ids=true, to_apply=%add.1 | all-reduce | flops 13056 | bytes 52224
  106.3 79.4 %all-gather.54.cloned.1.call-done = bf16[1,1088,3264]{2,0,1:T(2,128)(2,1)} async-done(((bf16[1,68,3264]{2,0,1:T(2,128)(2,1)}), bf16[1,1088,3264]{2,0,1:T(2,128)(2,1)}) %all-gather.54.cloned.1.call-update) | async-done | bytes 7102480 | tf_op jit(solution)/shard_map/all_gather | solution.py:312
  212.9 57.1 %all-gather.56.cloned.1.call-done = bf16[1,1088,1088]{2,0,1:T(2,128)(2,1)} async-done(((bf16[1,68,1088]{2,0,1:T(2,128)(2,1)}), bf16[1,1088,1088]{2,0,1:T(2,128)(2,1)}) %all-gather.56.cloned.1.call-update) | async-done | bytes 2367504 | tf_op jit(solution)/shard_map/all_gather | solution.py:315
  272.9 46.3 %all-gather.30.cloned.1.call-done = bf16[1024,1088]{0,1:T(8,128)(2,1)} async-done(((bf16[256,1088]{0,1:T(8,128)(2,1)}), bf16[1024,1088]{0,1:T(8,128)(2,1)}) %all-gather.30.cloned.1.call-update) | async-done | bytes 2228240 | tf_op jit(solution)/shard_map/all_gather | solution.py:335
  319.2 48.6 %all-gather.32.cloned.1.call-done = bf16[1024,1088]{0,1:T(8,128)(2,1)} async-done(((bf16[256,1088]{0,1:T(8,128)(2,1)}), bf16[1024,1088]{0,1:T(8,128)(2,1)}) %all-gather.32.cloned.1.call-update) | async-done | bytes 2228240 | tf_op jit(solution)/shard_map/all_gather | solution.py:336
  392.2 189.1 %all-gather.58.cloned.1.call-done = bf16[1,1088,4352]{2,0,1:T(2,128)(2,1)} async-done(((bf16[1,68,4352]{2,0,1:T(2,128)(2,1)}), bf16[1,1088,4352]{2,0,1:T(2,128)(2,1)}) %all-gather.58.cloned.1.call-update) | async-done | bytes 9469968 | tf_op jit(solution)/shard_map/all_gather | solution.py:319
  595.4 114.6 %all-gather.60.cloned.1.call-done = bf16[1,4352,1088]{2,1,0:T(8,128)(2,1)} async-done(((bf16[1,272,1088]{2,1,0:T(8,128)(2,1)}), bf16[1,4352,1088]{2,1,0:T(8,128)(2,1)}) %all-gather.60.cloned.1.call-update) | async-done | bytes 9469968 | tf_op jit(solution)/shard_map/all_gather | solution.py:321
  710.0 22.8 fusion.412
  759.4 35.1 %all-gather.34.cloned.1.call-done = bf16[1024,1088]{0,1:T(8,128)(2,1)} async-done(((bf16[256,1088]{0,1:T(8,128)(2,1)}), bf16[1024,1088]{0,1:T(8,128)(2,1)}) %all-gather.34.cloned.1.call-update) | async-done | bytes 2228240 | tf_op jit(solution)/shard_map/all_gather | solution.py:335
  794.6 48.8 %all-gather.36.cloned.1.call-done = bf16[1024,1088]{0,1:T(8,128)(2,1)} async-done(((bf16[256,1088]{0,1:T(8,128)(2,1)}), bf16[1024,1088]{0,1:T(8,128)(2,1)}) %all-gather.36.cloned.1.call-update) | async-done | bytes 2228240 | tf_op jit(solution)/shard_map/all_gather | solution.py:336
  855.9 23.5 fusion.409
  891.6 48.6 %all-gather.44.cloned.1.call-done = bf16[1024,1088]{0,1:T(8,128)(2,1)} async-done(((bf16[256,1088]{0,1:T(8,128)(2,1)}), bf16[1024,1088]{0,1:T(8,128)(2,1)}) %all-gather.44.cloned.1.call-update) | async-done | bytes 2228240 | tf_op jit(solution)/shard_map/all_gather | solution.py:382
  1029.4 27.8 all-gather.46.cloned.1.call-done
  1057.2 48.6 %all-gather.48.cloned.1.call-done = bf16[1024,1088]{0,1:T(8,128)(2,1)} async-done(((bf16[256,1088]{0,1:T(8,128)(2,1)}), bf16[1024,1088]{0,1:T(8,128)(2,1)}) %all-gather.48.cloned.1.call-update) | async-done | bytes 2228240 | tf_op jit(solution)/shard_map/all_gather | solution.py:382
  1115.3 72.0 %reduce-scatter.16.cloned.1.call-done = f32[256,1088]{0,1:T(8,128)} async-done(((f32[1024,1088]{0,1:T(8,128)}), f32[256,1088]{0,1:T(8,128)}) %reduce-scatter.16.cloned.1.call-update) | async-done | bytes 1114128 | tf_op jit(solution)/shard_map/reduce_scatter | solution.py:230
  1190.1 81.0 %reduce-scatter.14.cloned.1.call-done = f32[256,1088]{0,1:T(8,128)} async-done(((f32[1024,1088]{0,1:T(8,128)}), f32[256,1088]{0,1:T(8,128)}) %reduce-scatter.14.cloned.1.call-update) | async-done | bytes 1114128 | tf_op jit(solution)/shard_map/reduce_scatter | solution.py:229
  1327.1 43.0 %all-gather.52.cloned.1.call-done = bf16[1024,1088]{0,1:T(8,128)(2,1)} async-done(((bf16[256,1088]{0,1:T(8,128)(2,1)}), bf16[1024,1088]{0,1:T(8,128)(2,1)}) %all-gather.52.cloned.1.call-update) | async-done | bytes 2228240 | tf_op jit(solution)/shard_map/all_gather | solution.py:382
  1382.8 68.7 %reduce-scatter.20.cloned.1.call-done = f32[256,1088]{0,1:T(8,128)} async-done(((f32[1024,1088]{0,1:T(8,128)}), f32[256,1088]{0,1:T(8,128)}) %reduce-scatter.20.cloned.1.call-update) | async-done | bytes 1114128 | tf_op jit(solution)/shard_map/reduce_scatter | solution.py:230
  1453.6 81.6 %reduce-scatter.18.cloned.1.call-done = f32[256,1088]{0,1:T(8,128)} async-done(((f32[1024,1088]{0,1:T(8,128)}), f32[256,1088]{0,1:T(8,128)}) %reduce-scatter.18.cloned.1.call-update) | async-done | bytes 1114128 | tf_op jit(solution)/shard_map/reduce_scatter | solution.py:229
  1642.1 26.9 fusion.253
  1681.5 24.1 fusion.430
  1760.0 39.2 %reduce-scatter.22.cloned.1.call-done = f32[256,1088]{0,1:T(8,128)} async-done(((f32[1024,1088]{0,1:T(8,128)}), f32[256,1088]{0,1:T(8,128)}) %reduce-scatter.22.cloned.1.call-update) | async-done | bytes 1114128 | tf_op jit(solution)/shard_map/reduce_scatter | solution.py:229
  1811.0 1036.5 %fusion.680 = (f32[72,3264]{1,0:T(8,128)}, f32[80,1088]{1,0:T(8,128)}, f32[72,4352]{1,0:T(8,128)S(1)}) fusion(f32[1088,3264]{1,0:T(8,128)} %fusion.254, f32[1088,1088]{1,0:T(8,128)} %fusion.255, f32[1088,4352]{1,0:T(8,128)} %fusion.252), kind=kCustom, calls=%all-reduce-scatter.3 | all-reduce-scatter fusion | flops 10166274 | bytes 40421888
  2877.8 108.7 %all-reduce.24 = (f32[1088]{0:T(1024)}, f32[1088]{0:T(1024)}, f32[1088]{0:T(1024)}, f32[1088]{0:T(1024)}, f32[1088]{0:T(1024)}, /*index=5*/f32[1088]{0:T(1024)}, f32[1088]{0:T(1024)}, f32[4352]{0:T(1024)}, f32[1088]{0:T(1024)}) all-reduce(f32[1088]{0:T(1024)} %get-tuple-element.1162, ...), channel_id=21, replica_groups=mesh['section'=2,'dp'=4,'seq'=4] {'dp','seq'}, use_global_device_ids=true, to_apply=%region_81.82.clone | all-reduce | flops 13056 | bytes 104448
  (749 shorter events, 631.0 us)
Async XLA Ops:
  7.2 178.5 %all-gather.54.cloned.1.call-start = ((), (), s32[]{:S(2)}) async-start(), calls=%async_computation.26 | async-start | bytes 15388672 | tf_op jit(solution)/shard_map/all_gather | solution.py:312
  9.9 260.2 %all-gather.56.cloned.1.call-start = ((), (), s32[]{:S(2)}) async-start(), calls=%async_computation.27 | async-start | bytes 5326848 | tf_op jit(solution)/shard_map/all_gather | solution.py:315
  11.8 307.4 %all-gather.30.cloned.1.call-start = ((), (), s32[]{:S(2)}) async-start(), calls=%async_computation.7 | async-start | bytes 2785280 | tf_op jit(solution)/shard_map/all_gather | solution.py:335
  204.4 163.5 %all-gather.32.cloned.1.call-start = ((), (), s32[]{:S(2)}) async-start(), calls=%async_computation.8 | async-start | bytes 2785280 | tf_op jit(solution)/shard_map/all_gather | solution.py:336
  207.2 374.1 %all-gather.58.cloned.1.call-start = ((), (), s32[]{:S(2)}) async-start(), calls=%async_computation.28 | async-start | bytes 20123648 | tf_op jit(solution)/shard_map/all_gather | solution.py:319
  209.3 500.8 %all-gather.60.cloned.1.call-start = ((), (), s32[]{:S(2)}) async-start(), calls=%async_computation.29 | async-start | bytes 10653696 | tf_op jit(solution)/shard_map/all_gather | solution.py:321
  209.8 584.7 %all-gather.34.cloned.1.call-start = ((), (), s32[]{:S(2)}) async-start(), calls=%async_computation.9 | async-start | bytes 2785280 | tf_op jit(solution)/shard_map/all_gather | solution.py:335
  758.8 181.4 %all-gather.44.cloned.1.call-start = ((), (), s32[]{:S(2)}) async-start(), calls=%async_computation.14 | async-start | bytes 2785280 | tf_op jit(solution)/shard_map/all_gather | solution.py:382
  759.4 297.8 %all-gather.46.cloned.1.call-start = ((), (), s32[]{:S(2)}) async-start(), calls=%async_computation.17 | async-start | bytes 2785280 | tf_op jit(solution)/shard_map/all_gather | solution.py:381
  1009.5 177.8 %reduce-scatter.16.cloned.1.call-start = ((), (), s32[]{:S(2)}) async-start(), calls=%async_computation.16 | async-start | bytes 5570560 | tf_op jit(solution)/shard_map/reduce_scatter | solution.py:230
  1025.6 245.5 %reduce-scatter.14.cloned.1.call-start = ((), (), s32[]{:S(2)}) async-start(), calls=%async_computation.15 | async-start | bytes 5570560 | tf_op jit(solution)/shard_map/reduce_scatter | solution.py:229
  1026.2 300.9 %all-gather.50.cloned.1.call-start = ((), (), s32[]{:S(2)}) async-start(), calls=%async_computation.21 | async-start | bytes 2785280 | tf_op jit(solution)/shard_map/all_gather | solution.py:381
  1028.4 341.7 %all-gather.52.cloned.1.call-start = ((), (), s32[]{:S(2)}) async-start(), calls=%async_computation.22 | async-start | bytes 2785280 | tf_op jit(solution)/shard_map/all_gather | solution.py:382
  1029.3 422.1 %reduce-scatter.20.cloned.1.call-start = ((), (), s32[]{:S(2)}) async-start(), calls=%async_computation.20 | async-start | bytes 5570560 | tf_op jit(solution)/shard_map/reduce_scatter | solution.py:230
  1323.3 211.9 %reduce-scatter.18.cloned.1.call-start = ((), (), s32[]{:S(2)}) async-start(), calls=%async_computation.19 | async-start | bytes 5570560 | tf_op jit(solution)/shard_map/reduce_scatter | solution.py:229
  1324.3 344.8 %all-gather.38.cloned.1.call-start = ((), (), s32[]{:S(2)}) async-start(), calls=%async_computation.11 | async-start | bytes 2785280 | tf_op jit(solution)/shard_map/all_gather | solution.py:335
  1326.4 342.7 %all-gather.40.cloned.1.call-start = ((), (), s32[]{:S(2)}) async-start(), calls=%async_computation.12 | async-start | bytes 2785280 | tf_op jit(solution)/shard_map/all_gather | solution.py:336
  1327.0 431.6 %reduce-scatter.24.cloned.1.call-start = ((), (), s32[]{:S(2)}) async-start(), calls=%async_computation.24 | async-start | bytes 5570560 | tf_op jit(solution)/shard_map/reduce_scatter | solution.py:230
  1589.5 209.7 %reduce-scatter.22.cloned.1.call-start = ((), (), s32[]{:S(2)}) async-start(), calls=%async_computation.23 | async-start | bytes 5570560 | tf_op jit(solution)/shard_map/reduce_scatter | solution.py:229
  1622.7 1410.7 %reduce-scatter.26.cloned.1.call-start = ((), (), s32[]{:S(2)}) async-start(), calls=%async_computation.25 | async-start | bytes 21307392 | tf_op jit(solution)/shard_map/reduce_scatter | solution.py:431
  2849.0 152.7 %collective-permute-start.6 = (f32[80,1088]{1,0:T(8,128)}, f32[80,1088]{1,0:T(8,128)}, u32[]{:S(2)}, u32[]{:S(2)}) collective-permute-start(f32[80,1088]{1,0:T(8,128)} %get-tuple-element.1018), channel_id=1, source_target_pairs={{0,2},{1,3},{2,4},{3,5},{4,6},{5,7},{6,8},{7,9},{8,10},{9,11},{10,... | collective-permute-start | bytes 1044488
  2851.0 150.7 %collective-permute-start.5 = (f32[80,1088]{1,0:T(8,128)}, f32[80,1088]{1,0:T(8,128)}, u32[]{:S(2)}, u32[]{:S(2)}) collective-permute-start(f32[80,1088]{1,0:T(8,128)} %get-tuple-element.1018), channel_id=1, source_target_pairs={{0,1},{1,2},{2,3},{3,4},{4,5},{5,6},{6,7},{7,8},{8,9},{9,10},{10,1... | collective-permute-start | bytes 1044488
  2855.2 155.5 %collective-permute-start.4 = (f32[60,3264]{1,0:T(8,128)}, f32[60,3264]{1,0:T(8,128)}, u32[]{:S(2)}, u32[]{:S(2)}) collective-permute-start(f32[60,3264]{1,0:T(8,128)} %slice.141), channel_id=1, source_target_pairs={{0,1},{1,2},{2,3},{3,4},{4,5},{5,6},{6,7},{7,8},{8,9},{9,10},{10,1... | collective-permute-start | bytes 2350088
  2863.7 157.3 %collective-permute-start.8 = (f32[60,4352]{1,0:T(8,128)}, f32[60,4352]{1,0:T(8,128)}, u32[]{:S(2)}, u32[]{:S(2)}) collective-permute-start(f32[60,4352]{1,0:T(8,128)} %slice.143), channel_id=1, source_target_pairs={{0,1},{1,2},{2,3},{3,4},{4,5},{5,6},{6,7},{7,8},{8,9},{9,10},{10,1... | collective-permute-start | bytes 3133448
  (201 other events, 12893.1 us)
Sparse Core Ops, SparseCore 0:
  11.3 174.3 all-gather.53
  189.0 81.0 all-gather.55
  272.2 46.9 all-gather.29
  321.2 46.6 all-gather.31
  371.0 210.2 all-gather.57
  583.9 126.0 all-gather.59
  747.2 47.2 all-gather.33
  796.7 46.6 all-gather.35
  844.9 46.5 all-gather.41
  893.5 46.5 all-gather.43
  991.3 65.7 all-gather.45
  1059.2 46.5 all-gather.47
  1108.1 79.2 reduce-scatter.15
  1189.5 81.5 reduce-scatter.13
  1272.5 48.9 all-gather.49
  1323.4 46.5 all-gather.51
  1372.2 79.2 reduce-scatter.19
  1453.6 81.5 reduce-scatter.17
  1536.8 48.9 all-gather.37
  1587.1 46.5 all-gather.39
  1636.1 79.2 reduce-scatter.23
  1717.6 81.5 reduce-scatter.21
  1805.7 530.4 reduce-scatter.25
where the time goes:
time: 3050 us; the launch traced here: 3040 us
  blocking collectives  1230 us (40%)
  waiting for transfers between devices  1140 us (37%)
  matrix products  409 us (13%)
  local copies, waits for them, and re-layouts  139 us (5%)
  other arithmetic  58.9 us (2%)
    unnamed x3, blocking collectives  1230 us
    all_gather x6, waiting for transfers between devices, body(): lax.all_gather(projected[5], 'seq', axis=0, tiled=True)  238 us
    reduce_scatter x3, waiting for transfers between devices, layer_backward(): lax.psum_scatter(grad_keys_full, 'seq', scatter_dimension=0, tiled=True)  202 us
    all_gather x1, waiting for transfers between devices, body(): lax.all_gather(expand_weight[0], ('dp', 'seq'), axis=0, tiled=True)  189 us
    reduce_scatter x3, waiting for transfers between devices, layer_backward(): lax.psum_scatter(grad_values_full, 'seq', scatter_dimension=0, tiled=True)  141 us
    all_gather x6, waiting for transfers between devices, body(): lax.all_gather(projected[4], 'seq', axis=0, tiled=True)  119 us
    all_gather x1, waiting for transfers between devices, body(): lax.all_gather(reduce_weight[0], ('dp', 'seq'), axis=0, tiled=True)  115 us
    unnamed x401, local copies, waits for them, and re-layouts  88 us
  transfers between devices with their start and end apart: 32, of which 19 were waited for; matrix products, arithmetic and copies ran while one was open for 52% of the time, Pallas kernels for 0%

commit v1 on v0

--- a/solution.py
+++ b/solution.py
@@ -434,9 +434,487 @@
     return (layer_outputs, input_grads) + tuple((portion[None] for portion in shares))
 
 
+def swapped(value, axis, bits):
+    count = lax.axis_size(axis)
+    return lax.ppermute(value, axis, [(source, source ^ bits) for source in range(count)])
+
+
+def after(value, *earlier):
+    return lax.optimization_barrier((value,) + earlier)[0]
+
+
+def natural_four(pieces, place):
+    odd, far = (place & 1) == 1, (place & 2) == 2
+    first = [
+        jnp.where(odd, pieces[1], pieces[0]),
+        jnp.where(odd, pieces[0], pieces[1]),
+        jnp.where(odd, pieces[3], pieces[2]),
+        jnp.where(odd, pieces[2], pieces[3]),
+    ]
+    return [jnp.where(far, first[index ^ 2], first[index]) for index in range(4)]
+
+
+def gather_page(shard, core, ring, line):
+    rows, columns = shard.shape
+    column = [shard] + [swapped(shard, "seq", bits) for bits in (1, 2, 3)]
+    block = jnp.concatenate(natural_four(column, line), axis=0)
+    tall = block.shape[0]
+    across = swapped(block, "dp", 1)
+    along = swapped(block, "dp", 2)
+    corner_top = swapped(across[: tall // 2], "dp", 2)
+    corner_bottom = swapped(along[tall // 2 :], "dp", 1)
+    corner = jnp.concatenate([corner_top, corner_bottom], axis=0)
+    whole = jnp.zeros((2, 4, tall, columns), shard.dtype)
+    pieces = (block, across, along, corner)
+    for bits, piece in enumerate(pieces):
+        whole = lax.dynamic_update_slice(whole, piece[None, None], (core, ring ^ bits, 0, 0))
+    for bits, piece in enumerate(pieces):
+        other = swapped(piece, "section", 1)
+        whole = lax.dynamic_update_slice(whole, other[None, None], (core ^ 1, ring ^ bits, 0, 0))
+    return whole.reshape(2, 4 * tall, columns), column[3], corner
+
+
+def gather_weights(attention_page, expand, reduce, core, ring, line):
+    other = swapped(jnp.where(core == 0, expand, attention_page), "section", 1)
+    lower = jnp.where(core == 0, attention_page, other)
+    upper = jnp.where(core == 0, other, expand)
+    lower_pages, held, done = gather_page(lower, core, ring, line)
+    reduce_pages, held, done = gather_page(after(reduce, held), core, ring, line)
+    upper_pages, held, done = gather_page(after(upper, held), core, ring, line)
+    return lower_pages, reduce_pages, upper_pages
+
+
+def gather_small(pieces):
+    packed = jnp.concatenate([piece.reshape(-1) for piece in pieces]).reshape(12, -1)
+    packed = jnp.pad(packed, ((0, 4), (0, 128 - packed.shape[1])))
+    full = lax.all_gather(packed, ("section", "dp", "seq"), axis=0, tiled=True)
+    width = pieces[0].shape[0]
+    return full.reshape(2, 16, 16, 128)[:, :, :12, :width]
+
+
+def small_of(full, layer):
+    part = full[layer].astype(jnp.float32)
+    vectors = [part[:, row].reshape(1, -1) for row in range(8)]
+    return vectors[:6], part[:, 8:].reshape(1, -1), vectors[6], vectors[7]
+
+
+def attention_forward(query, sources, low_chunk):
+    half = query.shape[0] // 2
+    split = (half, HEADS, HDIM)
+    query_low, query_high = query[:half].reshape(split), query[half:].reshape(split)
+    first = low_chunk == 0
+    queries = jnp.stack(
+        [query_low, query_high, query_high, query_high, jnp.where(first, query_high, query_low)]
+    )
+
+    def of_blocks(which):
+        def block(near, part):
+            return jnp.concatenate(
+                [sources[near][other][which][part] for other in (0, 1)], axis=0
+            ).reshape(2 * half, HEADS, HDIM)
+
+        last = jnp.where(first, block(1, 1), block(1, 0))
+        return jnp.stack([block(0, 0), block(0, 0), block(0, 1), block(1, 0), last])
+
+    keys, values = of_blocks(0), of_blocks(1)
+    scores = jnp.einsum("uqhd,ukhd->uhqk", queries, keys, preferred_element_type=jnp.float32)
+    scores = scores * HDIM ** (-0.5)
+    levels = jnp.max(scores, axis=-1)
+    exponent = jnp.exp(scores - levels[..., None])
+    weights = exponent.astype(jnp.bfloat16)
+    out = jnp.einsum("uhqk,ukhd->uhqd", weights, values, preferred_element_type=jnp.float32)
+    sums = jnp.sum(exponent, axis=-1)
+    last_low = jnp.where(first, far_below, levels[4])
+    last_high = jnp.where(first, levels[4], far_below)
+    peak_low = jnp.maximum(levels[0], last_low)
+    peak_high = jnp.maximum(jnp.maximum(levels[1], levels[2]), jnp.maximum(levels[3], last_high))
+    parts_low = [(levels[0], 0), (last_low, 4)]
+    parts_high = [(levels[1], 1), (levels[2], 2), (levels[3], 3), (last_high, 4)]
+    attended, logs = [], []
+    for peak, parts in ((peak_low, parts_low), (peak_high, parts_high)):
+        total = sum(jnp.exp(level - peak) * sums[unit] for level, unit in parts)
+        mixed = sum(jnp.exp(level - peak)[..., None] * out[unit] for level, unit in parts)
+        attended.append(mixed / total[..., None])
+        logs.append(peak + jnp.log(total))
+    attended_heads = jnp.stack(attended)
+    log_low, log_high = logs
+    log_units = jnp.stack(
+        [log_low, log_high, log_high, log_high, jnp.where(first, log_high, log_low)]
+    )
+    rows = attended_heads.transpose(0, 2, 1, 3).reshape(2 * half, HEADS * HDIM)
+    factor = jnp.exp(levels - log_units)
+    return rows, (queries, keys, values, exponent, weights, factor)
+
+
+def attention_backward(attended, grad_attended, saved, core, low_chunk):
+    queries, keys, values, exponent, weights, factor = saved
+    half = attended.shape[0] // 2
+    first = low_chunk == 0
+    split = (2, half, HEADS, HDIM)
+    delta_rows = jnp.sum((grad_attended * attended).reshape(split), axis=-1).transpose(0, 2, 1)
+    grad_rows = grad_attended.reshape(split).transpose(0, 2, 1, 3)
+
+    def units(rows):
+        return jnp.stack(
+            [rows[0], rows[1], rows[1], rows[1], jnp.where(first, rows[1], rows[0])]
+        )
+
+    delta, grads = units(delta_rows), units(grad_rows)
+    scaled = (factor[..., None] * grads).astype(jnp.bfloat16)
+    grad_weights = jnp.einsum("uhqd,ukhd->uhqk", scaled, values, preferred_element_type=jnp.float32)
+    grad_scores = (exponent * (grad_weights - (factor * delta)[..., None])).astype(jnp.bfloat16)
+    grad_query = jnp.einsum("uhqk,ukhd->uqhd", grad_scores, keys, preferred_element_type=jnp.float32)
+    grad_keys = jnp.einsum("uhqk,uqhd->ukhd", grad_scores, queries, preferred_element_type=jnp.float32)
+    grad_values = jnp.einsum("uhqk,uhqd->ukhd", weights, scaled, preferred_element_type=jnp.float32)
+    low = grad_query[0] + jnp.where(first, 0.0, grad_query[4])
+    high = grad_query[1] + grad_query[2] + grad_query[3] + jnp.where(first, grad_query[4], 0.0)
+    width = HEADS * HDIM
+    grad_query_rows = jnp.concatenate([low, high], axis=0).reshape(2 * half, width)
+    both = jnp.concatenate(
+        [grad_keys.reshape(5, 2 * half, width), grad_values.reshape(5, 2 * half, width)], axis=2
+    )
+    near = jnp.stack([both[0] + both[1], both[2]])
+    away = jnp.stack(
+        [both[3] + jnp.where(first, 0.0, both[4]), jnp.where(first, both[4], 0.0)]
+    )
+    near = near.reshape(2, 2, half, 2 * width)
+    away = away.reshape(2, 2, half, 2 * width)
+    away_other = swapped(away[:, 1].astype(jnp.bfloat16), "section", 1)
+    near_other = swapped(near[:, 1].astype(jnp.bfloat16), "section", 1)
+    away_sum = (away[:, 0] + away_other.astype(jnp.float32)).astype(jnp.bfloat16)
+    arrived = swapped(away_sum, "seq", 1)
+    own = near[:, 0] + near_other.astype(jnp.float32) + arrived.astype(jnp.float32)
+    own = own.reshape(2 * half, 2 * width)
+    return grad_query_rows, own[:, :width], own[:, width:]
+
+
+def layer_forward(source, small, expand_bias, gain_two, weights, core, low_chunk):
+    first_gain, first_shift, query_bias, value_bias, output_bias, reduce_bias = small
+    second_gain, second_shift = gain_two
+    joint, output, expand, reduce = weights
+    width = HEADS * HDIM
+    half = source.shape[0] // 2
+    normed, unit_first, inverse_first = normalize(source, first_gain, first_shift)
+    normed_low = normed.astype(jnp.bfloat16)
+    both = jnp.dot(normed_low, joint[:, width:], preferred_element_type=jnp.float32)
+    keys_low = both[:, :width].astype(jnp.bfloat16)
+    values_low = (both[:, width:] + value_bias).astype(jnp.bfloat16)
+    here = jnp.concatenate([keys_low, values_low], axis=1)
+    away = swapped(here, "seq", 1)
+    here_other = swapped(here, "section", 1)
+    away_other = swapped(away, "section", 1)
+    query = jnp.dot(normed_low, joint[:, :width], preferred_element_type=jnp.float32)
+    query_low = (query + query_bias).astype(jnp.bfloat16)
+
+    def parts(piece):
+        return (
+            piece[:, :width].reshape(2, half, width),
+            piece[:, width:].reshape(2, half, width),
+        )
+
+    sources = ((parts(here), parts(here_other)), (parts(away), parts(away_other)))
+    attended, kept = attention_forward(query_low, sources, low_chunk)
+    attended_low = attended.astype(jnp.bfloat16)
+    middle = source + (
+        jnp.dot(attended_low, output, preferred_element_type=jnp.float32) + output_bias
+    )
+    second, unit_second, inverse_second = normalize(middle, second_gain, second_shift)
+    second_low = second.astype(jnp.bfloat16)
+    hidden = jnp.dot(second_low, expand, preferred_element_type=jnp.float32) + expand_bias
+    active, gelu_pull = jax.vjp(partial(jax.nn.gelu, approximate=False), hidden)
+    active_low = active.astype(jnp.bfloat16)
+    result = middle + (
+        jnp.dot(active_low, reduce, preferred_element_type=jnp.float32) + reduce_bias
+    )
+    saved = (
+        unit_first,
+        inverse_first,
+        normed_low,
+        attended,
+        kept,
+        attended_low,
+        unit_second,
+        inverse_second,
+        second_low,
+        gelu_pull,
+        active_low,
+    )
+    return result.astype(jnp.bfloat16), saved
+
+
+def scatter_sum(halves, ring, line):
+    def of_ring(bits):
+        return lax.dynamic_index_in_dim(halves, ring ^ bits, 0, keepdims=False)
+
+    corner = of_ring(3)
+    got_top = swapped(corner[:2], "dp", 1)
+    got_bottom = swapped(corner[2:], "dp", 2)
+    across, along = of_ring(1), of_ring(2)
+
+    def add(left, right):
+        return (left.astype(jnp.float32) + right.astype(jnp.float32)).astype(jnp.bfloat16)
+
+    to_across = jnp.concatenate([across[:2], add(across[2:], got_bottom)], axis=0)
+    to_along = jnp.concatenate([add(along[:2], got_top), along[2:]], axis=0)
+    from_across = swapped(to_across, "dp", 1)
+    from_along = swapped(to_along, "dp", 2)
+    own = (
+        of_ring(0).astype(jnp.float32)
+        + from_across.astype(jnp.float32)
+        + from_along.astype(jnp.float32)
+    ).astype(jnp.bfloat16)
+
+    def of_line(bits):
+        return lax.dynamic_index_in_dim(own, line ^ bits, 0, keepdims=False)
+
+    total = of_line(0).astype(jnp.float32)
+    for bits in (1, 2, 3):
+        total = total + swapped(of_line(bits), "seq", bits).astype(jnp.float32)
+    return total
+
+
+def column_halves(left, right, core):
+    half = right.shape[1] // 2
+
+    def product(which):
+        part = lax.dynamic_slice_in_dim(right, which * half, half, 1)
+        return jnp.einsum("td,te->de", left, part, preferred_element_type=jnp.float32)
+
+    arrived = swapped(product(core ^ 1).astype(jnp.bfloat16), "section", 1)
+    total = (product(core) + arrived.astype(jnp.float32)).astype(jnp.bfloat16)
+    return total.reshape(4, 4, total.shape[0] // 16, half)
+
+
+def row_halves(left, right, core):
+    whole = jnp.einsum("tf,td->fd", left, right, preferred_element_type=jnp.float32)
+    whole = whole.astype(jnp.bfloat16)
+    whole = whole.reshape(4, 4, 2, whole.shape[0] // 32, whole.shape[1])
+
+    def part(which):
+        return lax.dynamic_index_in_dim(whole, which, 2, keepdims=False)
+
+    arrived = swapped(part(core ^ 1), "section", 1)
+    return (part(core).astype(jnp.float32) + arrived.astype(jnp.float32)).astype(jnp.bfloat16)
+
+
+def layer_gradient(upstream_low, saved, small, gain_two, weights, core, ring, line, low_chunk):
+    (
+        unit_first,
+        inverse_first,
+        normed_low,
+        attended,
+        kept,
+        attended_low,
+        unit_second,
+        inverse_second,
+        second_low,
+        gelu_pull,
+        active_low,
+    ) = saved
+    joint, output, expand, reduce = weights
+    first_gain = small[0]
+    second_gain = gain_two[0]
+    upstream = upstream_low.astype(jnp.float32)
+    sum_reduce_bias = jnp.sum(upstream, axis=0)
+    share_reduce = scatter_sum(row_halves(active_low, upstream_low, core), ring, line)
+    grad_active = jnp.einsum("td,fd->tf", upstream_low, reduce, preferred_element_type=jnp.float32)
+    grad_hidden_low = gelu_pull(grad_active)[0].astype(jnp.bfloat16)
+    sum_expand_bias = jnp.sum(grad_hidden_low.astype(jnp.float32), axis=0)
+    share_expand = scatter_sum(column_halves(second_low, grad_hidden_low, core), ring, line)
+    grad_second = jnp.einsum("tf,df->td", grad_hidden_low, expand, preferred_element_type=jnp.float32)
+    sum_second_gain = jnp.sum(grad_second * unit_second, axis=0)
+    sum_second_shift = jnp.sum(grad_second, axis=0)
+    grad_middle = upstream + normalize_back(grad_second * second_gain, unit_second, inverse_second)
+    branch_low = grad_middle.astype(jnp.bfloat16)
+    sum_output_bias = jnp.sum(branch_low.astype(jnp.float32), axis=0)
+    share_output = scatter_sum(column_halves(attended_low, branch_low, core), ring, line)
+    grad_attended = jnp.einsum("te,de->td", branch_low, output, preferred_element_type=jnp.float32)
+    grad_query, grad_keys, grad_values = attention_backward(
+        attended, grad_attended, kept, core, low_chunk
+    )
+    scale_factor = HDIM ** (-0.5)
+    grad_mixture = jnp.concatenate(
+        [grad_query * scale_factor, grad_keys * scale_factor, grad_values], axis=1
+    ).astype(jnp.bfloat16)
+    width = HEADS * HDIM
+    sums = jnp.sum(grad_mixture.astype(jnp.float32), axis=0)
+    share_joint = scatter_sum(column_halves(normed_low, grad_mixture, core), ring, line)
+    grad_normed = jnp.einsum("te,de->td", grad_mixture, joint, preferred_element_type=jnp.float32)
+    sum_first_gain = jnp.sum(grad_normed * unit_first, axis=0)
+    sum_first_shift = jnp.sum(grad_normed, axis=0)
+    grad_source = grad_middle + normalize_back(grad_normed * first_gain, unit_first, inverse_first)
+    vectors = (
+        sum_first_gain,
+        sum_first_shift,
+        sums[:width],
+        sums[2 * width :],
+        sum_output_bias,
+        sum_reduce_bias,
+        sum_second_gain,
+        sum_second_shift,
+    )
+    packed = jnp.stack([vector.reshape(16, -1) for vector in vectors], axis=1)
+    packed = jnp.concatenate([packed, sum_expand_bias.reshape(16, 4, -1)], axis=1)
+    return (
+        grad_source.astype(jnp.bfloat16),
+        (share_joint, share_output, share_expand, share_reduce),
+        packed,
+    )
+
+
+def sum_small(lower, upper, core, ring, line):
+    mine = jnp.where(core == 0, lower, upper)
+    mine = mine + swapped(jnp.where(core == 0, upper, lower), "section", 1)
+    mine = mine.reshape((4, 4) + mine.shape[1:])
+
+    def scatter(value, axis, place):
+        def part(bits):
+            return lax.dynamic_index_in_dim(value, place ^ bits, 0, keepdims=False)
+
+        return part(0) + sum(swapped(part(bits), axis, bits) for bits in (1, 2, 3))
+
+    return scatter(scatter(mine, "dp", ring), "seq", line)
+
+
+def to_rows(array, core, line):
+    half = array.shape[1] // 2
+    which = line // 2
+
+    def part(index):
+        return lax.dynamic_slice(
+            array, (index, core * half, 0), (1, half, array.shape[2])
+        )[0]
+
+    mine, arrived = part(which), swapped(part(1 - which), "seq", 3)
+    low_side = which == 0
+    return jnp.concatenate(
+        [jnp.where(low_side, mine, arrived), jnp.where(low_side, arrived, mine)], axis=0
+    )
+
+
+def from_rows(lower, upper, core, line):
+    half = lower.shape[0] // 2
+    low_side = line // 2 == 0
+    both = jnp.stack([lower, upper])
+    mine = jnp.where(low_side, both[:, :half], both[:, half:])
+    arrived = swapped(jnp.where(low_side, both[:, half:], both[:, :half]), "seq", 3)
+    pair = jnp.stack(
+        [jnp.where(low_side, mine, arrived), jnp.where(low_side, arrived, mine)], axis=1
+    )
+    kept = jnp.where(core == 0, pair[0], pair[1])
+    other = swapped(jnp.where(core == 0, pair[1], pair[0]), "section", 1)
+    return jnp.concatenate(
+        [jnp.where(core == 0, kept, other), jnp.where(core == 0, other, kept)], axis=1
+    )[None]
+
+
+def joined_shares(lower, upper, core, axis):
+    kept = jnp.where(core == 0, lower, upper)
+    other = swapped(jnp.where(core == 0, upper, lower), "section", 1)
+    return jnp.concatenate(
+        [jnp.where(core == 0, kept, other), jnp.where(core == 0, other, kept)], axis=axis
+    )[None]
+
+
+def four_by_four(
+    inputs,
+    cotangent,
+    first_gain,
+    first_shift,
+    joint_weight,
+    query_bias,
+    value_bias,
+    output_weight,
+    output_bias,
+    second_gain,
+    second_shift,
+    expand_weight,
+    expand_bias,
+    reduce_weight,
+    reduce_bias,
+):
+    core = lax.axis_index("section")
+    ring = lax.axis_index("dp")
+    line = lax.axis_index("seq")
+    low_chunk = jnp.where(line < 2, line, 3 - line)
+    width = HEADS * HDIM
+    full_small = gather_small(
+        (
+            first_gain[0],
+            first_shift[0],
+            query_bias[0],
+            value_bias[0],
+            output_bias[0],
+            reduce_bias[0],
+            second_gain[0],
+            second_shift[0],
+            expand_bias[0],
+        )
+    )
+    rows = to_rows(inputs, core, line)
+    attention_page = jnp.concatenate([joint_weight[0], output_weight[0]], axis=1)
+    lower_pages, reduce_pages, upper_pages = gather_weights(
+        attention_page, expand_weight[0], reduce_weight[0], core, ring, line
+    )
+    top = to_rows(cotangent, core, line)
+    layers = []
+    for layer, pages in enumerate((lower_pages, upper_pages)):
+        small, wide, gain, shift = small_of(full_small, layer)
+        weights = (
+            pages[0][:, : 3 * width],
+            pages[0][:, 3 * width :],
+            pages[1],
+            reduce_pages[layer],
+        )
+        layers.append((small, wide, (gain, shift), weights))
+    small, wide, gains, weights = layers[0]
+    middle_rows, saved_lower = layer_forward(
+        rows.astype(jnp.float32), small, wide, gains, weights, core, low_chunk
+    )
+    small, wide, gains, weights = layers[1]
+    final_rows, saved_upper = layer_forward(
+        middle_rows.astype(jnp.float32), small, wide, gains, weights, core, low_chunk
+    )
+    layer_outputs = from_rows(middle_rows, final_rows, core, line)
+    upper_grad, upper_shares, upper_small = layer_gradient(
+        top, saved_upper, small, gains, weights, core, ring, line, low_chunk
+    )
+    small, wide, gains, weights = layers[0]
+    lower_grad, lower_shares, lower_small = layer_gradient(
+        upper_grad, saved_lower, small, gains, weights, core, ring, line, low_chunk
+    )
+    input_grads = from_rows(lower_grad, upper_grad, core, line)
+    grad_joint, grad_output, grad_expand, grad_reduce = (
+        joined_shares(lower, upper, core, axis)
+        for lower, upper, axis in zip(lower_shares, upper_shares, (1, 1, 1, 0))
+    )
+    vectors = sum_small(lower_small, upper_small, core, ring, line)
+    return (
+        layer_outputs,
+        input_grads,
+        vectors[0][None],
+        vectors[1][None],
+        grad_joint,
+        vectors[2][None],
+        vectors[3][None],
+        grad_output,
+        vectors[4][None],
+        vectors[6][None],
+        vectors[7][None],
+        grad_expand,
+        vectors[8:].reshape(1, -1),
+        grad_reduce,
+        vectors[5][None],
+    )
+
+
+def fits(mesh):
+    return dict(mesh.shape) == {"section": 2, "dp": 4, "seq": 4}
+
+
 def solution(mesh):
     return jax.shard_map(
-        body,
+        four_by_four if fits(mesh) else body,
         mesh=mesh,
         in_specs=(
             P("dp", "seq", None),

time: 3050 us -> 1590 us (0.52)
  blocking collectives: 1230 us -> 80.8 us
  waiting for transfers between devices: 1140 us -> 575 us
  local copies, waits for them, and re-layouts: 139 us -> 373 us
  matrix products: 409 us -> 251 us
  starting transfers between devices: 27.3 us -> 155 us
  other arithmetic: 58.9 us -> 150 us
    unnamed x3 -> x0, blocking collectives: 1230 us -> none
    all_gather x16 -> x0, waiting for transfers between devices: 797 us -> none  [the longest x6 238 us: body(): lax.all_gather(projected[5], 'seq', axis=0, tiled=True)]
    ppermute x4 -> x127, waiting for transfers between devices: 0.86 us -> 575 us  [swapped(): lax.ppermute(value, axis, [(source, source ^ bits) for source in range(co...]
    reduce_scatter x7 -> x0, waiting for transfers between devices: 343 us -> none  [the longest x3 202 us: layer_backward(): lax.psum_scatter(grad_keys_full, 'seq', scatter_dimension=0, tiled=True)]
    dot_general x69 -> x44, matrix products: 409 us -> 251 us  [the longest x12 45.7 us: product(): jnp.einsum('td,te->de', left, part, preferred_element_type=jnp.float32)]
    ppermute x4 -> x127, starting transfers between devices: 7.99 us -> 155 us  [swapped(): lax.ppermute(value, axis, [(source, source ^ bits) for source in range(co...]
    slice x7 -> x76, local copies, waits for them, and re-layouts: 9.53 us -> 108 us  [the longest x42 54.1 us: block(): sources[near][other][which][part]]
    all_gather x0 -> x1, blocking collectives: none -> 80.8 us  [gather_small(): full = lax.all_gather(packed, ('section', 'dp', 'seq'), axis=0, tiled=True)]
  transfers between devices with their start and end apart: 32 -> 127, of which waited for: 19 -> 46; matrix products, arithmetic and copies ran while one was open for 52% -> 36% of each run, Pallas kernels for 0% -> 0%
where the time goes in v1:
time: 1590 us
  waiting for transfers between devices  575 us (36%)
  local copies, waits for them, and re-layouts  373 us (23%)
  matrix products  251 us (16%)
  starting transfers between devices  155 us (10%)
  other arithmetic  150 us (9%)
  blocking collectives  80.8 us (5%)
    ppermute x127, waiting for transfers between devices, swapped(): lax.ppermute(value, axis, [(source, source ^ bits) for source in range(co...  575 us
    ppermute x127, starting transfers between devices, swapped(): lax.ppermute(value, axis, [(source, source ^ bits) for source in range(co...  155 us
    all_gather x1, blocking collectives, gather_small(): full = lax.all_gather(packed, ('section', 'dp', 'seq'), axis=0, tiled=True)  80.8 us
    slice x42, local copies, waits for them, and re-layouts, block(): sources[near][other][which][part]  54.1 us
    dot_general x12, matrix products, product(): jnp.einsum('td,te->de', left, part, preferred_element_type=jnp.float32)  45.7 us
    dot_general x2, matrix products, layer_forward(): jnp.dot(second_low, expand, preferred_element_type=jnp.float32)  35.7 us
    another operation x8, local copies, waits for them, and re-layouts, attention_backward(): near = jnp.stack([both[0] + both[1], both[2]])  34.1 us
  transfers between devices with their start and end apart: 127, of which 46 were waited for; matrix products, arithmetic and copies ran while one was open for 36% of the time, Pallas kernels for 0%

profile of v1, /device:TPU:0, one launch (start us, length us, event | category | flops | bytes accessed | tf_op | source)
XLA Modules:
  0.0 1589.0 jit_solution(4608776257763932230)
XLA Ops:
  11.2 80.8 %all_gather.3 = bf16[512,128]{1,0:T(8,128)(2,1)S(1)} all-gather(bf16[16,128]{1,0:T(8,128)(2,1)S(1)} %pad.4), channel_id=1, replica_groups=mesh['section'=2,'dp'=4,'seq'=4] {'section','dp','seq'}, dimensions={0}, use_global_device_ids=true | all-gather | bytes 135168 | tf_op jit(solution)/shard_map/all_gather | solution.py:490
  102.0 16.4 %collective-permute-done.2 = bf16[68,4352]{1,0:T(8,128)(2,1)S(1)} collective-permute-done((bf16[68,4352]{1,0:T(8,128)(2,1)S(1)}, bf16[68,4352]{1,0:T(8,128)(2,1)S(1)}, u32[]{:S(2)}, u32[]{:S(2)}) %collective-permute-start.2) | collective-permute-done | bytes 591904 | tf_op jit(solution)/shard_map/ppermute | solution.py:439
  118.7 26.5 %collective-permute-start.17 = (bf16[272,1088]{1,0:T(8,128)(2,1)S(1)}, bf16[272,1088]{1,0:T(8,128)(2,1)S(1)}, u32[]{:S(2)}, u32[]{:S(2)}) collective-permute-start(bf16[272,1088]{1,0:T(8,128)(2,1)S(1)} %bitcast.898), channel_id=1, source_target_pairs={{0,2},{1,3},{2,0},{3,1},{4,6},{5,7},{6,4},{7,5},{8,10},{9,11},{10,... | collective-permute-start | bytes 1775624 | tf_op jit(solution)/shard_map/ppermute | solution.py:439
  151.7 49.9 %collective-permute-done.17 = bf16[272,1088]{1,0:T(8,128)(2,1)S(1)} collective-permute-done((bf16[272,1088]{1,0:T(8,128)(2,1)S(1)}, bf16[272,1088]{1,0:T(8,128)(2,1)S(1)}, u32[]{:S(2)}, u32[]{:S(2)}) %collective-permute-start.17) | collective-permute-done | bytes 591904 | tf_op jit(solution)/shard_map/ppermute | solution.py:439
  207.5 33.3 %collective-permute-done.3 = bf16[68,4352]{1,0:T(8,128)(2,1)S(1)} collective-permute-done((bf16[68,4352]{1,0:T(8,128)(2,1)S(1)}, bf16[68,4352]{1,0:T(8,128)(2,1)S(1)}, u32[]{:S(2)}, u32[]{:S(2)}) %collective-permute-start.3) | collective-permute-done | bytes 591904 | tf_op jit(solution)/shard_map/ppermute | solution.py:439
  240.9 25.8 %collective-permute-done.28 = bf16[68,4352]{1,0:T(8,128)(2,1)S(1)} collective-permute-done((bf16[68,4352]{1,0:T(8,128)(2,1)S(1)}, bf16[68,4352]{1,0:T(8,128)(2,1)S(1)}, u32[]{:S(2)}, u32[]{:S(2)}) %collective-permute-start.28) | collective-permute-done | bytes 591904 | tf_op jit(solution)/shard_map/ppermute | solution.py:439
  302.3 46.8 %collective-permute-done.30 = bf16[272,4352]{1,0:T(8,128)(2,1)S(1)} collective-permute-done((bf16[272,4352]{1,0:T(8,128)(2,1)}, bf16[272,4352]{1,0:T(8,128)(2,1)S(1)}, u32[]{:S(2)}, u32[]{:S(2)}) %collective-permute-start.30) | collective-permute-done | bytes 2367520 | tf_op jit(solution)/shard_map/ppermute | solution.py:439
  352.2 44.7 %collective-permute-done.5 = bf16[272,4352]{1,0:T(8,128)(2,1)S(1)} collective-permute-done((bf16[272,4352]{1,0:T(8,128)(2,1)}, bf16[272,4352]{1,0:T(8,128)(2,1)S(1)}, u32[]{:S(2)}, u32[]{:S(2)}) %collective-permute-start.5) | collective-permute-done | bytes 2367520 | tf_op jit(solution)/shard_map/ppermute | solution.py:439
  406.0 17.7 %collective-permute-done.21 = bf16[544,1088]{1,0:T(8,128)(2,1)S(1)} collective-permute-done((bf16[544,1088]{1,0:T(8,128)(2,1)S(1)}, bf16[544,1088]{1,0:T(8,128)(2,1)S(1)}, u32[]{:S(2)}, u32[]{:S(2)}) %collective-permute-start.21) | collective-permute-done | bytes 1183776 | tf_op jit(solution)/shard_map/ppermute | solution.py:439
  431.5 23.2 %collective-permute-done.32 = bf16[136,4352]{1,0:T(8,128)(2,1)} collective-permute-done((bf16[136,4352]{1,0:T(8,128)(2,1)}, bf16[136,4352]{1,0:T(8,128)(2,1)}, u32[]{:S(2)}, u32[]{:S(2)}) %collective-permute-start.32) | collective-permute-done | bytes 1183776 | tf_op jit(solution)/shard_map/ppermute | solution.py:439
  457.6 20.5 %collective-permute-done.7 = bf16[136,4352]{1,0:T(8,128)(2,1)} collective-permute-done((bf16[136,4352]{1,0:T(8,128)(2,1)}, bf16[136,4352]{1,0:T(8,128)(2,1)}, u32[]{:S(2)}, u32[]{:S(2)}) %collective-permute-start.7) | collective-permute-done | bytes 1183776 | tf_op jit(solution)/shard_map/ppermute | solution.py:439
  483.4 22.3 %collective-permute-done.8 = bf16[136,4352]{1,0:T(8,128)(2,1)S(1)} collective-permute-done((bf16[136,4352]{1,0:T(8,128)(2,1)S(1)}, bf16[136,4352]{1,0:T(8,128)(2,1)S(1)}, u32[]{:S(2)}, u32[]{:S(2)}) %collective-permute-start.8) | collective-permute-done | bytes 1183776 | tf_op jit(solution)/shard_map/ppermute | solution.py:439
  545.1 22.9 %fusion.346 = (bf16[1,4,272,4352]{3,2,1,0:T(8,128)(2,1)}, bf16[1,4,272,4352]{3,2,1,0:T(8,128)(2,1)S(1)}) fusion(bf16[2,4,272,4352]{3,2,1,0:T(8,128)(2,1)} %bitcast_dynamic-update-slice_fusion.16), kind=kLoop, calls=%fused_computation.818 | loop fusion | bytes 37879808 | tf_op jit(solution)/shard_map/slice | solution.py:866
  649.2 17.7 %multiply_convert_fusion.3 = (bf16[256,4352]{1,0:T(8,128)(2,1)S(1)}, f32[256,4352]{1,0:T(8,128)}, f32[256,4352]{1,0:T(8,128)}) fusion(f32[4352]{0:T(1024)S(1)} %add.863, bf16[1088,4352]{1,0:T(8,128)(2,1)} %bitcast.819, f32[256,1088]{0,1:T(8,128)S(1)} %get-tuple-element.364, f32[1088]{0:T(1024)S(1)} %add.860, f32[1088]{0:T(1024)S(1)} %mul.601, ...), kind=kOutput, calls=%fused_computation.81 | convolution fusion | flops 2499231744 | bytes 21753344 | tf_op jit(solution)/shard_map/dot_general | solution.py:623
  758.9 18.1 %multiply_convert_fusion.2 = (bf16[256,4352]{1,0:T(8,128)(2,1)}, f32[256,4352]{1,0:T(8,128)}, f32[256,4352]{1,0:T(8,128)}) fusion(f32[4352]{0:T(1024)S(1)} %copy-done.166, bf16[1088,4352]{1,0:T(8,128)(2,1)} %bitcast.821, f32[256,1088]{0,1:T(8,128)S(1)} %get-tuple-element.373, f32[1088]{0:T(1024)S(1)} %copy-done.139, f32[1088]{0:T(1024)S(1)} %copy-done.130, ...), kind=kOutput, calls=%fused_computation.68 | convolution fusion | flops 2499231744 | bytes 21753344 | tf_op jit(solution)/shard_map/dot_general | solution.py:623
  961.9 13.9 collective-permute-done.46
  1066.9 14.4 copy.329
  1149.2 23.4 %collective-permute-done.83 = bf16[68,544]{1,0:T(8,128)(2,1)S(1)} collective-permute-done((bf16[68,544]{1,0:T(8,128)(2,1)S(1)}, bf16[68,544]{1,0:T(8,128)(2,1)S(1)}, u32[]{:S(2)}, u32[]{:S(2)}) %collective-permute-start.83) | collective-permute-done | bytes 74016 | tf_op jit(solution)/shard_map/ppermute | solution.py:439
  1284.3 20.9 %collective-permute-done.68 = bf16[2,68,1632]{2,1,0:T(8,128)(2,1)S(1)} collective-permute-done((bf16[2,68,1632]{2,1,0:T(8,128)(2,1)S(1)}, bf16[2,68,1632]{2,1,0:T(8,128)(2,1)S(1)}, u32[]{:S(2)}, u32[]{:S(2)}) %collective-permute-start.68) | collective-permute-done | bytes 443936 | tf_op jit(solution)/shard_map/ppermute | solution.py:439
  1312.8 23.0 %collective-permute-done.120 = bf16[4,136,1088]{2,1,0:T(8,128)(2,1)S(1)} collective-permute-done((bf16[4,136,1088]{2,1,0:T(8,128)(2,1)S(1)}, bf16[4,136,1088]{2,1,0:T(8,128)(2,1)S(1)}, u32[]{:S(2)}, u32[]{:S(2)}) %collective-permute-start.120) | collective-permute-done | bytes 1183776 | tf_op jit(solution)/shard_map/ppermute | solution.py:439
  1339.9 18.3 %collective-permute-done.103 = bf16[4,68,2176]{2,0,1:T(4,128)(2,1)S(1)} collective-permute-done((bf16[4,68,2176]{2,0,1:T(4,128)(2,1)S(1)}, bf16[4,68,2176]{2,0,1:T(4,128)(2,1)S(1)}, u32[]{:S(2)}, u32[]{:S(2)}) %collective-permute-start.103) | collective-permute-done | bytes 1183776 | tf_op jit(solution)/shard_map/ppermute | solution.py:439
  1482.9 20.5 %collective-permute-done.99 = bf16[68,2176]{1,0:T(8,128)(2,1)S(1)} collective-permute-done((bf16[68,2176]{1,0:T(8,128)(2,1)S(1)}, bf16[68,2176]{1,0:T(8,128)(2,1)S(1)}, u32[]{:S(2)}, u32[]{:S(2)}) %collective-permute-start.99) | collective-permute-done | bytes 295968 | tf_op jit(solution)/shard_map/ppermute | solution.py:439
  1519.2 16.3 %collective-permute-done.124 = bf16[136,1088]{1,0:T(8,128)(2,1)S(1)} collective-permute-done((bf16[136,1088]{1,0:T(8,128)(2,1)S(1)}, bf16[136,1088]{1,0:T(8,128)(2,1)S(1)}, u32[]{:S(2)}, u32[]{:S(2)}) %collective-permute-start.124) | collective-permute-done | bytes 295968 | tf_op jit(solution)/shard_map/ppermute | solution.py:439
  1543.5 13.9 collective-permute-start.72
  (1103 shorter events, 953.1 us)
Async XLA Ops:
  2.3 97.6 %collective-permute-start.1 = (bf16[68,4352]{1,0:T(8,128)(2,1)S(1)}, bf16[68,4352]{1,0:T(8,128)(2,1)S(1)}, u32[]{:S(2)}, u32[]{:S(2)}) collective-permute-start(bf16[68,4352]{1,0:T(8,128)(2,1)S(1)} %bitcast_select_fusion.2), channel_id=1, source_target_pairs={{0,16},{16,0},{1,17},{17,1},{2,18},{18,2},{3,19},{19,3},{4,20},{20... | collective-permute-start | bytes 1775624 | tf_op jit(solution)/shard_map/ppermute | solution.py:439
  4.5 95.9 %collective-permute-start = (bf16[128,1088]{0,1:T(8,128)(2,1)}, bf16[128,1088]{0,1:T(8,128)(2,1)}, u32[]{:S(2)}, u32[]{:S(2)}) collective-permute-start(bf16[128,1088]{0,1:T(8,128)(2,1)} %dynamic-slice_bitcast_fusion.51), channel_id=1, source_target_pairs={{0,3},{1,2},{2,1},{3,0},{4,7},{5,6},{6,5},{7,4},{8,11},{9,10},{10,... | collective-permute-start | bytes 835592 | tf_op jit(solution)/shard_map/ppermute | solution.py:439
  10.9 134.4 %collective-permute-start.43 = (bf16[128,1088]{0,1:T(8,128)(2,1)}, bf16[128,1088]{0,1:T(8,128)(2,1)}, u32[]{:S(2)}, u32[]{:S(2)}) collective-permute-start(bf16[128,1088]{0,1:T(8,128)(2,1)} %dynamic-slice_bitcast_fusion.50), channel_id=1, source_target_pairs={{0,3},{1,2},{2,1},{3,0},{4,7},{5,6},{6,5},{7,4},{8,11},{9,10},{10,... | collective-permute-start | bytes 835592 | tf_op jit(solution)/shard_map/ppermute | solution.py:439
  118.7 82.9 %collective-permute-start.17 = (bf16[272,1088]{1,0:T(8,128)(2,1)S(1)}, bf16[272,1088]{1,0:T(8,128)(2,1)S(1)}, u32[]{:S(2)}, u32[]{:S(2)}) collective-permute-start(bf16[272,1088]{1,0:T(8,128)(2,1)S(1)} %bitcast.898), channel_id=1, source_target_pairs={{0,2},{1,3},{2,0},{3,1},{4,6},{5,7},{6,4},{7,5},{8,10},{9,11},{10,... | collective-permute-start | bytes 1775624 | tf_op jit(solution)/shard_map/ppermute | solution.py:439
  147.3 93.5 %collective-permute-start.3 = (bf16[68,4352]{1,0:T(8,128)(2,1)S(1)}, bf16[68,4352]{1,0:T(8,128)(2,1)S(1)}, u32[]{:S(2)}, u32[]{:S(2)}) collective-permute-start(bf16[68,4352]{1,0:T(8,128)(2,1)S(1)} %get-tuple-element.306), channel_id=1, source_target_pairs={{0,2},{1,3},{2,0},{3,1},{4,6},{5,7},{6,4},{7,5},{8,10},{9,11},{10,... | collective-permute-start | bytes 1775624 | tf_op jit(solution)/shard_map/ppermute | solution.py:439
  148.8 92.0 %collective-permute-start.4 = (bf16[68,4352]{1,0:T(8,128)(2,1)S(1)}, bf16[68,4352]{1,0:T(8,128)(2,1)S(1)}, u32[]{:S(2)}, u32[]{:S(2)}) collective-permute-start(bf16[68,4352]{1,0:T(8,128)(2,1)S(1)} %get-tuple-element.306), channel_id=1, source_target_pairs={{0,1},{1,0},{2,3},{3,2},{4,5},{5,4},{6,7},{7,6},{8,9},{9,8},{10,11... | collective-permute-start | bytes 1775624 | tf_op jit(solution)/shard_map/ppermute | solution.py:439
  149.3 91.5 %collective-permute-start.27 = (bf16[68,4352]{1,0:T(8,128)(2,1)S(1)}, bf16[68,4352]{1,0:T(8,128)(2,1)S(1)}, u32[]{:S(2)}, u32[]{:S(2)}) collective-permute-start(bf16[68,4352]{1,0:T(8,128)(2,1)S(1)} %get-tuple-element.18), channel_id=1, source_target_pairs={{0,3},{1,2},{2,1},{3,0},{4,7},{5,6},{6,5},{7,4},{8,11},{9,10},{10,... | collective-permute-start | bytes 1775624 | tf_op jit(solution)/shard_map/ppermute | solution.py:439
  201.6 65.1 %collective-permute-start.28 = (bf16[68,4352]{1,0:T(8,128)(2,1)S(1)}, bf16[68,4352]{1,0:T(8,128)(2,1)S(1)}, u32[]{:S(2)}, u32[]{:S(2)}) collective-permute-start(bf16[68,4352]{1,0:T(8,128)(2,1)S(1)} %get-tuple-element.18), channel_id=1, source_target_pairs={{0,2},{1,3},{2,0},{3,1},{4,6},{5,7},{6,4},{7,5},{8,10},{9,11},{10,... | collective-permute-start | bytes 1775624 | tf_op jit(solution)/shard_map/ppermute | solution.py:439
  201.6 65.9 %collective-permute-start.29 = (bf16[68,4352]{1,0:T(8,128)(2,1)S(1)}, bf16[68,4352]{1,0:T(8,128)(2,1)}, u32[]{:S(2)}, u32[]{:S(2)}) collective-permute-start(bf16[68,4352]{1,0:T(8,128)(2,1)S(1)} %get-tuple-element.18), channel_id=1, source_target_pairs={{0,1},{1,0},{2,3},{3,2},{4,5},{5,4},{6,7},{7,6},{8,9},{9,8},{10,11... | collective-permute-start | bytes 1775624 | tf_op jit(solution)/shard_map/ppermute | solution.py:439
  240.8 188.4 %collective-permute-start.23 = (bf16[1088,1088]{1,0:T(8,128)(2,1)}, bf16[1088,1088]{1,0:T(8,128)(2,1)}, u32[]{:S(2)}, u32[]{:S(2)}) collective-permute-start(bf16[1088,1088]{1,0:T(8,128)(2,1)} %pad_maximum_fusion), channel_id=1, source_target_pairs={{0,16},{16,0},{1,17},{17,1},{2,18},{18,2},{3,19},{19,3},{4,20},{20... | collective-permute-start | bytes 7102472 | tf_op jit(solution)/shard_map/ppermute | solution.py:439
  278.1 70.9 %collective-permute-start.30 = (bf16[272,4352]{1,0:T(8,128)(2,1)}, bf16[272,4352]{1,0:T(8,128)(2,1)S(1)}, u32[]{:S(2)}, u32[]{:S(2)}) collective-permute-start(bf16[272,4352]{1,0:T(8,128)(2,1)} %get-tuple-element.159), channel_id=1, source_target_pairs={{0,4},{4,0},{8,12},{12,8},{1,5},{5,1},{9,13},{13,9},{2,6},{6,2},{1... | collective-permute-start | bytes 7102472 | tf_op jit(solution)/shard_map/ppermute | solution.py:439
  278.1 72.5 %collective-permute-start.31 = (bf16[272,4352]{1,0:T(8,128)(2,1)}, bf16[272,4352]{1,0:T(8,128)(2,1)S(1)}, u32[]{:S(2)}, u32[]{:S(2)}) collective-permute-start(bf16[272,4352]{1,0:T(8,128)(2,1)} %get-tuple-element.159), channel_id=1, source_target_pairs={{0,8},{4,12},{8,0},{12,4},{1,9},{5,13},{9,1},{13,5},{2,10},{6,14},... | collective-permute-start | bytes 7102472 | tf_op jit(solution)/shard_map/ppermute | solution.py:439
  298.4 214.9 %collective-permute-start.34 = (bf16[272,4352]{1,0:T(8,128)(2,1)}, bf16[272,4352]{1,0:T(8,128)(2,1)}, u32[]{:S(2)}, u32[]{:S(2)}) collective-permute-start(bf16[272,4352]{1,0:T(8,128)(2,1)} %get-tuple-element.159), channel_id=1, source_target_pairs={{0,16},{16,0},{1,17},{17,1},{2,18},{18,2},{3,19},{19,3},{4,20},{20... | collective-permute-start | bytes 7102472 | tf_op jit(solution)/shard_map/ppermute | solution.py:439
  298.5 98.4 %collective-permute-start.5 = (bf16[272,4352]{1,0:T(8,128)(2,1)}, bf16[272,4352]{1,0:T(8,128)(2,1)S(1)}, u32[]{:S(2)}, u32[]{:S(2)}) collective-permute-start(bf16[272,4352]{1,0:T(8,128)(2,1)} %get-tuple-element.157), channel_id=1, source_target_pairs={{0,4},{4,0},{8,12},{12,8},{1,5},{5,1},{9,13},{13,9},{2,6},{6,2},{1... | collective-permute-start | bytes 7102472 | tf_op jit(solution)/shard_map/ppermute | solution.py:439
  350.6 166.6 %collective-permute-start.9 = (bf16[272,4352]{1,0:T(8,128)(2,1)}, bf16[272,4352]{1,0:T(8,128)(2,1)}, u32[]{:S(2)}, u32[]{:S(2)}) collective-permute-start(bf16[272,4352]{1,0:T(8,128)(2,1)} %get-tuple-element.157), channel_id=1, source_target_pairs={{0,16},{16,0},{1,17},{17,1},{2,18},{18,2},{3,19},{19,3},{4,20},{20... | collective-permute-start | bytes 7102472 | tf_op jit(solution)/shard_map/ppermute | solution.py:439
  423.8 96.7 %collective-permute-start.24 = (bf16[1088,1088]{1,0:T(8,128)(2,1)S(1)}, bf16[1088,1088]{1,0:T(8,128)(2,1)S(1)}, u32[]{:S(2)}, u32[]{:S(2)}) collective-permute-start(bf16[1088,1088]{1,0:T(8,128)(2,1)S(1)} %collective-permute-done.19), channel_id=1, source_target_pairs={{0,16},{16,0},{1,17},{17,1},{2,18},{18,2},{3,19},{19,3},{4,20},{20... | collective-permute-start | bytes 7102472 | tf_op jit(solution)/shard_map/ppermute | solution.py:439
  851.3 76.9 %collective-permute-start.41 = (bf16[2,128,1088]{1,2,0:T(8,128)(2,1)}, bf16[2,128,1088]{1,2,0:T(8,128)(2,1)}, u32[]{:S(2)}, u32[]{:S(2)}) collective-permute-start(bf16[2,128,1088]{1,2,0:T(8,128)(2,1)} %broadcast_select_fusion.29), channel_id=1, source_target_pairs={{0,3},{1,2},{2,1},{3,0},{4,7},{5,6},{6,5},{7,4},{8,11},{9,10},{10,... | collective-permute-start | bytes 1671176 | tf_op jit(solution)/shard_map/ppermute | solution.py:439
  897.3 64.6 %collective-permute-start.44 = (bf16[2,128,2176]{1,0,2:T(2,128)(2,1)}, bf16[2,128,2176]{1,0,2:T(2,128)(2,1)}, u32[]{:S(2)}, u32[]{:S(2)}) collective-permute-start(bf16[2,128,2176]{1,0,2:T(2,128)(2,1)} %fusion.143), channel_id=1, source_target_pairs={{0,16},{16,0},{1,17},{17,1},{2,18},{18,2},{3,19},{19,3},{4,20},{20... | collective-permute-start | bytes 3342344 | tf_op jit(solution)/shard_map/ppermute | solution.py:439
  959.0 183.8 %collective-permute-start.91 = (bf16[68,544]{1,0:T(8,128)(2,1)}, bf16[68,544]{1,0:T(8,128)(2,1)}, u32[]{:S(2)}, u32[]{:S(2)}) collective-permute-start(bf16[68,544]{1,0:T(8,128)(2,1)} %get-tuple-element.320), channel_id=1, source_target_pairs={{0,3},{1,2},{2,1},{3,0},{4,7},{5,6},{6,5},{7,4},{8,11},{9,10},{10,... | collective-permute-start | bytes 221960 | tf_op jit(solution)/shard_map/ppermute | solution.py:439
  961.9 184.0 %collective-permute-start.90 = (bf16[68,544]{1,0:T(8,128)(2,1)}, bf16[68,544]{1,0:T(8,128)(2,1)}, u32[]{:S(2)}, u32[]{:S(2)}) collective-permute-start(bf16[68,544]{1,0:T(8,128)(2,1)} %get-tuple-element.321), channel_id=1, source_target_pairs={{0,2},{1,3},{2,0},{3,1},{4,6},{5,7},{6,4},{7,5},{8,10},{9,11},{10,... | collective-permute-start | bytes 221960 | tf_op jit(solution)/shard_map/ppermute | solution.py:439
  1207.4 155.4 %collective-permute-start.93 = (bf16[1088,2176]{1,0:T(8,128)(2,1)}, bf16[1088,2176]{1,0:T(8,128)(2,1)}, u32[]{:S(2)}, u32[]{:S(2)}) collective-permute-start(bf16[1088,2176]{1,0:T(8,128)(2,1)} %convolution_convert_fusion.3), channel_id=1, source_target_pairs={{0,16},{16,0},{1,17},{17,1},{2,18},{18,2},{3,19},{19,3},{4,20},{20... | collective-permute-start | bytes 14204936 | tf_op jit(solution)/shard_map/ppermute | solution.py:439
  1208.8 170.2 %collective-permute-start.110 = (bf16[4,4,136,1088]{3,2,1,0:T(8,128)(2,1)}, bf16[4,4,136,1088]{3,2,1,0:T(8,128)(2,1)}, u32[]{:S(2)}, u32[]{:S(2)}) collective-permute-start(bf16[4,4,136,1088]{3,2,1,0:T(8,128)(2,1)} %dynamic-slice_bitcast_fusion.1), channel_id=1, source_target_pairs={{0,16},{16,0},{1,17},{17,1},{2,18},{18,2},{3,19},{19,3},{4,20},{20... | collective-permute-start | bytes 14204936 | tf_op jit(solution)/shard_map/ppermute | solution.py:439
  1335.8 81.4 %collective-permute-start.59 = (bf16[1088,1632]{1,0:T(8,128)(2,1)}, bf16[1088,1632]{1,0:T(8,128)(2,1)}, u32[]{:S(2)}, u32[]{:S(2)}) collective-permute-start(bf16[1088,1632]{1,0:T(8,128)(2,1)} %convolution_convert_fusion.5), channel_id=1, source_target_pairs={{0,16},{16,0},{1,17},{17,1},{2,18},{18,2},{3,19},{19,3},{4,20},{20... | collective-permute-start | bytes 10653704 | tf_op jit(solution)/shard_map/ppermute | solution.py:439
  1362.8 94.1 %collective-permute-start.108 = (bf16[68,2176]{1,0:T(8,128)(2,1)}, bf16[68,2176]{1,0:T(8,128)(2,1)}, u32[]{:S(2)}, u32[]{:S(2)}) collective-permute-start(bf16[68,2176]{1,0:T(8,128)(2,1)} %get-tuple-element.263), channel_id=1, source_target_pairs={{0,3},{1,2},{2,1},{3,0},{4,7},{5,6},{6,5},{7,4},{8,11},{9,10},{10,... | collective-permute-start | bytes 887816 | tf_op jit(solution)/shard_map/ppermute | solution.py:439
  (319 other events, 9191.8 us)

commit v2 on v0

--- a/solution.py
+++ b/solution.py
@@ -3,11 +3,18 @@
 import jax
 import jax.numpy as jnp
 from jax import lax
+from jax.experimental import pallas as pl
+from jax.experimental.pallas import tpu as pltpu
 from jax.sharding import PartitionSpec as P
 
 HEADS = 17
 HDIM = 64
 BLK = 256
+WIDE = 1152
+F32, LOW = jnp.float32, jnp.bfloat16
+SECTION, RING, LINE = "section", "dp", "seq"
+OWNERS = (RING, LINE)
+EAST, NORTH, LEVEL, SIBLING, CORNER, ONCE = range(6)
 
 
 epsilon = 1e-05
@@ -226,8 +233,8 @@
         grad_attended.reshape(row_count, HEADS, HDIM),
     )
     grad_keys, grad_values = (
-        lax.psum_scatter(grad_keys_full, "seq", scatter_dimension=0, tiled=True),
-        lax.psum_scatter(grad_values_full, "seq", scatter_dimension=0, tiled=True),
+        lax.psum_scatter(grad_keys_full, LINE, scatter_dimension=0, tiled=True),
+        lax.psum_scatter(grad_values_full, LINE, scatter_dimension=0, tiled=True),
     )
     scale_factor = HDIM ** (-0.5)
     grad_mixture = jnp.concatenate(
@@ -286,10 +293,10 @@
     reduce_weight,
     reduce_bias,
 ):
-    section_index = lax.axis_index("section")
+    section_index = lax.axis_index(SECTION)
     micro_count = inputs.shape[0]
     row_count = inputs.shape[1]
-    first_row = lax.axis_index("seq") * row_count
+    first_row = lax.axis_index(LINE) * row_count
     row_block = (first_row + jnp.arange(row_count, dtype=jnp.int32)) // BLK
     owned = (
         first_gain[0],
@@ -307,19 +314,19 @@
         reduce_bias[0],
     )
     forward_params = (
-        lax.all_gather(first_gain[0], ("dp", "seq"), axis=0, tiled=True),
-        lax.all_gather(first_shift[0], ("dp", "seq"), axis=0, tiled=True),
-        lax.all_gather(joint_weight[0], ("dp", "seq"), axis=0, tiled=True),
-        lax.all_gather(query_bias[0], ("dp", "seq"), axis=0, tiled=True),
-        lax.all_gather(value_bias[0], ("dp", "seq"), axis=0, tiled=True),
-        lax.all_gather(output_weight[0], ("dp", "seq"), axis=0, tiled=True),
-        lax.all_gather(output_bias[0], ("dp", "seq"), axis=0, tiled=True),
-        lax.all_gather(second_gain[0], ("dp", "seq"), axis=0, tiled=True),
-        lax.all_gather(second_shift[0], ("dp", "seq"), axis=0, tiled=True),
-        lax.all_gather(expand_weight[0], ("dp", "seq"), axis=0, tiled=True),
-        lax.all_gather(expand_bias[0], ("dp", "seq"), axis=0, tiled=True),
-        lax.all_gather(reduce_weight[0], ("dp", "seq"), axis=0, tiled=True),
-        lax.all_gather(reduce_bias[0], ("dp", "seq"), axis=0, tiled=True),
+        lax.all_gather(first_gain[0], OWNERS, axis=0, tiled=True),
+        lax.all_gather(first_shift[0], OWNERS, axis=0, tiled=True),
+        lax.all_gather(joint_weight[0], OWNERS, axis=0, tiled=True),
+        lax.all_gather(query_bias[0], OWNERS, axis=0, tiled=True),
+        lax.all_gather(value_bias[0], OWNERS, axis=0, tiled=True),
+        lax.all_gather(output_weight[0], OWNERS, axis=0, tiled=True),
+        lax.all_gather(output_bias[0], OWNERS, axis=0, tiled=True),
+        lax.all_gather(second_gain[0], OWNERS, axis=0, tiled=True),
+        lax.all_gather(second_shift[0], OWNERS, axis=0, tiled=True),
+        lax.all_gather(expand_weight[0], OWNERS, axis=0, tiled=True),
+        lax.all_gather(expand_bias[0], OWNERS, axis=0, tiled=True),
+        lax.all_gather(reduce_weight[0], OWNERS, axis=0, tiled=True),
+        lax.all_gather(reduce_bias[0], OWNERS, axis=0, tiled=True),
     )
     incoming = jnp.zeros(inputs.shape[1:], jnp.bfloat16)
     section_inputs = []
@@ -332,8 +339,8 @@
         source = section_input.astype(jnp.float32)
         projected = project(source, forward_params)
         gathered = (
-            lax.all_gather(projected[4], "seq", axis=0, tiled=True),
-            lax.all_gather(projected[5], "seq", axis=0, tiled=True),
+            lax.all_gather(projected[4], LINE, axis=0, tiled=True),
+            lax.all_gather(projected[5], LINE, axis=0, tiled=True),
         )
         result, unused = complete(source, forward_params, projected, gathered, row_block)
         result_low = result.astype(jnp.bfloat16)
@@ -341,21 +348,21 @@
         produced.append(result_low)
         key_sets.append(gathered)
         if tick_index < micro_count:
-            incoming = passed_along(result_low, "section", 1)
+            incoming = passed_along(result_low, SECTION, 1)
     backward_params = (
-        lax.all_gather(first_gain[0], ("dp", "seq"), axis=0, tiled=True),
-        lax.all_gather(first_shift[0], ("dp", "seq"), axis=0, tiled=True),
-        lax.all_gather(joint_weight[0], ("dp", "seq"), axis=0, tiled=True),
-        lax.all_gather(query_bias[0], ("dp", "seq"), axis=0, tiled=True),
-        lax.all_gather(value_bias[0], ("dp", "seq"), axis=0, tiled=True),
-        lax.all_gather(output_weight[0], ("dp", "seq"), axis=0, tiled=True),
-        lax.all_gather(output_bias[0], ("dp", "seq"), axis=0, tiled=True),
-        lax.all_gather(second_gain[0], ("dp", "seq"), axis=0, tiled=True),
-        lax.all_gather(second_shift[0], ("dp", "seq"), axis=0, tiled=True),
-        lax.all_gather(expand_weight[0], ("dp", "seq"), axis=0, tiled=True),
-        lax.all_gather(expand_bias[0], ("dp", "seq"), axis=0, tiled=True),
-        lax.all_gather(reduce_weight[0], ("dp", "seq"), axis=0, tiled=True),
-        lax.all_gather(reduce_bias[0], ("dp", "seq"), axis=0, tiled=True),
+        lax.all_gather(first_gain[0], OWNERS, axis=0, tiled=True),
+        lax.all_gather(first_shift[0], OWNERS, axis=0, tiled=True),
+        lax.all_gather(joint_weight[0], OWNERS, axis=0, tiled=True),
+        lax.all_gather(query_bias[0], OWNERS, axis=0, tiled=True),
+        lax.all_gather(value_bias[0], OWNERS, axis=0, tiled=True),
+        lax.all_gather(output_weight[0], OWNERS, axis=0, tiled=True),
+        lax.all_gather(output_bias[0], OWNERS, axis=0, tiled=True),
+        lax.all_gather(second_gain[0], OWNERS, axis=0, tiled=True),
+        lax.all_gather(second_shift[0], OWNERS, axis=0, tiled=True),
+        lax.all_gather(expand_weight[0], OWNERS, axis=0, tiled=True),
+        lax.all_gather(expand_bias[0], OWNERS, axis=0, tiled=True),
+        lax.all_gather(reduce_weight[0], OWNERS, axis=0, tiled=True),
+        lax.all_gather(reduce_bias[0], OWNERS, axis=0, tiled=True),
     )
     totals = tuple((jnp.zeros(piece.shape, jnp.float32) for piece in backward_params))
     shares = tuple((jnp.zeros(piece.shape, jnp.float32) for piece in owned))
@@ -378,8 +385,8 @@
         source = section_input.astype(jnp.float32)
         projected = project(source, backward_params)
         gathered = (
-            lax.all_gather(projected[4], "seq", axis=0, tiled=True),
-            lax.all_gather(projected[5], "seq", axis=0, tiled=True),
+            lax.all_gather(projected[4], LINE, axis=0, tiled=True),
+            lax.all_gather(projected[5], LINE, axis=0, tiled=True),
         )
         grad_source, grads = layer_backward(
             source, upstream, backward_params, projected, gathered, row_block
@@ -388,7 +395,7 @@
         totals = tuple((running + update for running, update in zip(totals, masked)))
         sent_back.append(grad_source)
         if tick_index < micro_count:
-            returning = passed_along(grad_source, "section", -1)
+            returning = passed_along(grad_source, SECTION, -1)
     layer_outputs = jnp.stack(
         [
             jnp.where(section_index == 0, produced[position], produced[position + 1])
@@ -417,60 +424,1138 @@
         sum_reduce_bias,
     ) = totals
     shares = (
-        lax.psum_scatter(sum_first_gain, ("dp", "seq"), scatter_dimension=0, tiled=True),
-        lax.psum_scatter(sum_first_shift, ("dp", "seq"), scatter_dimension=0, tiled=True),
-        lax.psum_scatter(sum_joint_weight, ("dp", "seq"), scatter_dimension=0, tiled=True),
-        lax.psum_scatter(sum_query_bias, ("dp", "seq"), scatter_dimension=0, tiled=True),
-        lax.psum_scatter(sum_value_bias, ("dp", "seq"), scatter_dimension=0, tiled=True),
-        lax.psum_scatter(sum_output_weight, ("dp", "seq"), scatter_dimension=0, tiled=True),
-        lax.psum_scatter(sum_output_bias, ("dp", "seq"), scatter_dimension=0, tiled=True),
-        lax.psum_scatter(sum_second_gain, ("dp", "seq"), scatter_dimension=0, tiled=True),
-        lax.psum_scatter(sum_second_shift, ("dp", "seq"), scatter_dimension=0, tiled=True),
-        lax.psum_scatter(sum_expand_weight, ("dp", "seq"), scatter_dimension=0, tiled=True),
-        lax.psum_scatter(sum_expand_bias, ("dp", "seq"), scatter_dimension=0, tiled=True),
-        lax.psum_scatter(sum_reduce_weight, ("dp", "seq"), scatter_dimension=0, tiled=True),
-        lax.psum_scatter(sum_reduce_bias, ("dp", "seq"), scatter_dimension=0, tiled=True),
+        lax.psum_scatter(sum_first_gain, OWNERS, scatter_dimension=0, tiled=True),
+        lax.psum_scatter(sum_first_shift, OWNERS, scatter_dimension=0, tiled=True),
+        lax.psum_scatter(sum_joint_weight, OWNERS, scatter_dimension=0, tiled=True),
+        lax.psum_scatter(sum_query_bias, OWNERS, scatter_dimension=0, tiled=True),
+        lax.psum_scatter(sum_value_bias, OWNERS, scatter_dimension=0, tiled=True),
+        lax.psum_scatter(sum_output_weight, OWNERS, scatter_dimension=0, tiled=True),
+        lax.psum_scatter(sum_output_bias, OWNERS, scatter_dimension=0, tiled=True),
+        lax.psum_scatter(sum_second_gain, OWNERS, scatter_dimension=0, tiled=True),
+        lax.psum_scatter(sum_second_shift, OWNERS, scatter_dimension=0, tiled=True),
+        lax.psum_scatter(sum_expand_weight, OWNERS, scatter_dimension=0, tiled=True),
+        lax.psum_scatter(sum_expand_bias, OWNERS, scatter_dimension=0, tiled=True),
+        lax.psum_scatter(sum_reduce_weight, OWNERS, scatter_dimension=0, tiled=True),
+        lax.psum_scatter(sum_reduce_bias, OWNERS, scatter_dimension=0, tiled=True),
     )
     return (layer_outputs, input_grads) + tuple((portion[None] for portion in shares))
+
+
+def swapped(value, axis, bits):
+    count = lax.axis_size(axis)
+    return lax.ppermute(value, axis, [(source, source ^ bits) for source in range(count)])
+
+
+def to_rows(array, core, line):
+    half = array.shape[1] // 2
+    which = line // 2
+
+    def part(index):
+        return lax.dynamic_slice(
+            array, (index, core * half, 0), (1, half, array.shape[2])
+        )[0]
+
+    mine, arrived = part(which), swapped(part(1 - which), LINE, 3)
+    low_side = which == 0
+    return jnp.concatenate(
+        [jnp.where(low_side, mine, arrived), jnp.where(low_side, arrived, mine)], axis=0
+    )
+
+
+def from_rows(lower, upper, core, line):
+    half = lower.shape[0] // 2
+    low_side = line // 2 == 0
+    both = jnp.stack([lower, upper])
+    mine = jnp.where(low_side, both[:, :half], both[:, half:])
+    arrived = swapped(jnp.where(low_side, both[:, half:], both[:, :half]), LINE, 3)
+    pair = jnp.stack(
+        [jnp.where(low_side, mine, arrived), jnp.where(low_side, arrived, mine)], axis=1
+    )
+    kept = jnp.where(core == 0, pair[0], pair[1])
+    other = swapped(jnp.where(core == 0, pair[1], pair[0]), SECTION, 1)
+    return jnp.concatenate(
+        [jnp.where(core == 0, kept, other), jnp.where(core == 0, other, kept)], axis=1
+    )[None]
+
+
+def flip(place, bits):
+    return {1: place + 1 - 2 * (place % 2), 2: (place + 2) % 4, 3: 3 - place}[bits]
+
+
+def places():
+    core, ring, line = (lax.axis_index(name) for name in (SECTION, RING, LINE))
+    rings = [ring] + [flip(ring, bits) for bits in (1, 2, 3)]
+    lines = [line] + [flip(line, bits) for bits in (1, 2, 3)]
+    toward = {
+        EAST: {RING: rings[1]},
+        NORTH: {RING: rings[2]},
+        (LEVEL, 1): {LINE: lines[1]},
+        (LEVEL, 2): {LINE: lines[2]},
+        (LEVEL, 3): {LINE: lines[3]},
+        SIBLING: {SECTION: 1 - core},
+    }
+    return core, rings, lines, toward
+
+
+def greet(toward):
+    barrier = pltpu.get_barrier_semaphore()
+    for to in toward.values():
+        pl.semaphore_signal(barrier, inc=1, device_id=to, device_id_type=pl.DeviceIdType.MESH)
+    pl.semaphore_wait(barrier, len(toward))
+
+
+def remote_copy(source, target, send_sem, recv_sem, to):
+    return pltpu.make_async_remote_copy(
+        src_ref=source,
+        dst_ref=target,
+        send_sem=send_sem,
+        recv_sem=recv_sem,
+        device_id=to,
+        device_id_type=pl.DeviceIdType.MESH,
+    )
+
+
+def per_core(core, act):
+    for index in (0, 1):
+
+        @pl.when(core == index)
+        def _():
+            act(index)
+
+
+GATHER_KINDS = (
+    [(LEVEL, k) for k in (1, 2, 3)]
+    + [(name, k) for name in (EAST, NORTH, CORNER) for k in range(4)]
+    + [(SIBLING, k) for k in range(4)]
+)
+GATHER_NUMBER = {kind: index for index, kind in enumerate(GATHER_KINDS)}
+
+
+def gather_kernel(slots, *refs):
+    shards, refs = refs[:slots], refs[slots:]
+    outs, refs = [refs[2 * t : 2 * t + 2] for t in range(slots)], refs[2 * slots :]
+    send_sem, recv_sem, copy_sem = refs
+    core, rings, lines, toward = places()
+    greet(toward)
+    sent, copied = [], []
+
+    def copy_of(t, source, target, to, kind):
+        index = t * len(GATHER_KINDS) + GATHER_NUMBER[kind]
+        return remote_copy(source, target, send_sem.at[index], recv_sem.at[index], toward[to])
+
+    def place(t, page, dd, k):
+        return outs[t][page].at[rings[dd] * 4 + lines[k]]
+
+    def send(t, dd, k, to, kind, own=False):
+        def act(page):
+            target = place(t, page, dd, k)
+            copy_of(t, shards[t] if own else target, target, to, kind).start()
+
+        per_core(core, act)
+        sent.append(copy_of(t, place(t, 0, dd, k), place(t, 0, dd, k), to, kind))
+
+    def arrive(t, dd, k, to, kind):
+        def act(page):
+            target = place(t, page, dd, k)
+            copy_of(t, target, target, to, kind).wait_recv()
+
+        per_core(core, act)
+
+    def group(t, page, dd):
+        return outs[t][page].at[pl.ds(rings[dd] * 4, 4)]
+
+    def sibling(t, dd):
+        def act(page):
+            copy_of(t, group(t, page, dd), group(t, page, dd), SIBLING, (SIBLING, dd)).start()
+
+        per_core(core, act)
+        sent.append(copy_of(t, group(t, 0, dd), group(t, 0, dd), SIBLING, (SIBLING, dd)))
+
+    def begin_line(t):
+        for k in (1, 2, 3):
+            send(t, 0, 0, (LEVEL, k), (LEVEL, k), own=True)
+
+    def begin_ring(t):
+        send(t, 0, 0, EAST, (EAST, 0), own=True)
+        send(t, 0, 0, NORTH, (NORTH, 0), own=True)
+
+        def act(page):
+            pltpu.make_async_copy(shards[t], place(t, page, 0, 0), copy_sem.at[t]).start()
+
+        per_core(core, act)
+
+    def own_ready(t):
+        def act(page):
+            pltpu.make_async_copy(shards[t], place(t, page, 0, 0), copy_sem.at[t]).wait()
+
+        per_core(core, act)
+
+    def from_line(t, k):
+        arrive(t, 0, k, (LEVEL, k), (LEVEL, k))
+        send(t, 0, k, EAST, (EAST, k))
+        send(t, 0, k, NORTH, (NORTH, k))
+
+    def from_ring(t, k):
+        arrive(t, 1, k, EAST, (EAST, k))
+        if k < 2:
+            send(t, 1, k, NORTH, (CORNER, k))
+        arrive(t, 2, k, NORTH, (NORTH, k))
+        if k >= 2:
+            send(t, 2, k, EAST, (CORNER, k))
+
+    begin_line(0)
+    begin_ring(0)
+    for t in range(slots):
+        from_ring(t, 0)
+        from_line(t, 1)
+        from_line(t, 2)
+        from_line(t, 3)
+        own_ready(t)
+        sibling(t, 0)
+        if t + 1 < slots:
+            begin_line(t + 1)
+        from_ring(t, 1)
+        if t + 1 < slots:
+            begin_ring(t + 1)
+        from_ring(t, 2)
+        from_ring(t, 3)
+        sibling(t, 1)
+        sibling(t, 2)
+        for k in range(4):
+            arrive(t, 3, k, NORTH if k < 2 else EAST, (CORNER, k))
+        sibling(t, 3)
+    for t in range(slots):
+        for dd in range(4):
+
+            def act(page):
+                target = group(t, 1 - page, dd)
+                copy_of(t, target, target, SIBLING, (SIBLING, dd)).wait_recv()
+
+            per_core(core, act)
+    for copy in sent:
+        copy.wait_send()
+
+
+def gather_pages(shards):
+    slots = len(shards)
+    count = slots * len(GATHER_KINDS)
+    whole = [
+        jax.ShapeDtypeStruct((16,) + shard.shape, shard.dtype) for shard in shards for _ in (0, 1)
+    ]
+    anywhere = pl.BlockSpec(memory_space=pl.ANY)
+    out = pl.pallas_call(
+        partial(gather_kernel, slots),
+        out_shape=tuple(whole),
+        in_specs=[anywhere] * slots,
+        out_specs=tuple(anywhere for _ in whole),
+        scratch_shapes=[
+            pltpu.SemaphoreType.DMA((count,)),
+            pltpu.SemaphoreType.DMA((count,)),
+            pltpu.SemaphoreType.DMA((slots,)),
+        ],
+        compiler_params=pltpu.CompilerParams(collective_id=0, has_side_effects=True),
+        name="gather_pages",
+    )(*shards)
+    return [out[2 * t : 2 * t + 2] for t in range(slots)]
+
+
+KINDS = (
+    [(CORNER, dd) for dd in range(4)]
+    + [(ONCE, k) for k in range(4)]
+    + [(EAST, k) for k in range(4)]
+    + [(NORTH, k) for k in range(4)]
+    + [(LEVEL, k) for k in (1, 2, 3)]
+)
+NUMBER = {kind: i for i, kind in enumerate(KINDS)}
+DEPTH = 8
+
+def scatter_kernel(slots, *refs):
+    n = len(slots)
+    pages = [(refs[2 * t], refs[2 * t + 1]) for t in range(n)]
+    refs = refs[2 * n :]
+    finals, refs = refs[:n], refs[n:]
+    lands, refs = [refs[5 * t : 5 * t + 5] for t in range(n)], refs[5 * n :]
+    shapes = sorted(set(slots))
+    work = {}
+    for i, shape in enumerate(shapes):
+        work[shape] = refs[3 * i : 3 * i + 3]
+    refs = refs[3 * len(shapes) :]
+    send_sem, recv_sem, load_sem, out_sem = refs
+    core, rings, lines, toward = places()
+    greet(toward)
+
+    def remote(t, src, dst, to, kind):
+        i = t * len(KINDS) + NUMBER[kind]
+        return pltpu.make_async_remote_copy(
+            src_ref=src, dst_ref=dst, send_sem=send_sem.at[i], recv_sem=recv_sem.at[i],
+            device_id=toward[to], device_id_type=pl.DeviceIdType.MESH)
+
+    def by_core(make):
+        def start(pair):
+            for index in (0, 1):
+                @pl.when(core == index)
+                def _():
+                    make(pair[index]).start()
+        return start
+
+    pending = []
+
+    def give(t, dd):
+        dst = lands[t][0].at[pl.ds(rings[dd] * 4, 4)]
+        pair = (pages[t][1], pages[t][0])
+        by_core(lambda ref: remote(t, ref.at[pl.ds(rings[dd] * 4, 4)], dst, SIBLING, (CORNER, dd)))(pair)
+        pending.append(remote(t, dst, dst, SIBLING, (CORNER, dd)))
+
+    def arrived(t, ref, to, kind):
+        remote(t, ref, ref, to, kind).wait_recv()
+
+    task = [0]
+    used = {shape: [None] * DEPTH for shape in shapes}
+    count = {shape: 0 for shape in shapes}
+
+    def total_of(t, dd, k, extra):
+        shape = slots[t]
+        loads = work[shape][0]
+        slot = task[0] % 2
+        task[0] += 1
+        index = rings[dd] * 4 + lines[k]
+        buf = lambda j: loads.at[slot, j]
+        sem = lambda j: load_sem.at[slot * 4 + j]
+        by_core(lambda ref: pltpu.make_async_copy(ref.at[index], buf(0), sem(0)))(pages[t])
+        copies = [pltpu.make_async_copy(buf(0), buf(0), sem(0))]
+        sources = [lands[t][0].at[index]] + extra
+        for j, source in enumerate(sources):
+            copy = pltpu.make_async_copy(source, buf(j + 1), sem(j + 1))
+            copy.start()
+            copies.append(copy)
+        for copy in copies:
+            copy.wait()
+        return loads, slot, len(copies)
+
+    def add_up(shape, loads, slot, terms, store):
+        rows, columns = shape
+        if rows == 72:
+            def step(i, _):
+                at = pl.ds(pl.multiple_of(i * 256, 256), 256)
+                value = loads[slot, 0, :, at].astype(jnp.float32)
+                for j in range(1, terms):
+                    value = value + loads[slot, j, :, at].astype(jnp.float32)
+                store((slice(None), at), value)
+                return 0
+            lax.fori_loop(0, columns // 256, step, 0)
+        else:
+            def step(i, _):
+                at = pl.ds(pl.multiple_of(i * 16, 16), 16)
+                value = loads[slot, 0, at, :].astype(jnp.float32)
+                for j in range(1, terms):
+                    value = value + loads[slot, j, at, :].astype(jnp.float32)
+                store((at, slice(None)), value)
+                return 0
+            lax.fori_loop(0, rows // 16, step, 0)
+
+    def sum_and_send(t, dd, k, extra, dst, to, kind):
+        shape = slots[t]
+        loads, slot, terms = total_of(t, dd, k, extra)
+        place = count[shape] % DEPTH
+        count[shape] += 1
+        if used[shape][place] is not None:
+            used[shape][place].wait_send()
+        out = work[shape][1]
+        def store(at, value):
+            out[(place,) + at] = value.astype(jnp.bfloat16)
+        add_up(shape, loads, slot, terms, store)
+        copy = remote(t, out.at[place], dst, to, kind)
+        copy.start()
+        used[shape][place] = copy
+
+    def first(t):
+        one = lands[t][1]
+        arrived(t, lands[t][0].at[pl.ds(rings[3] * 4, 4)], SIBLING, (CORNER, 3))
+        for k in (0, 2, 1, 3):
+            to = EAST if k < 2 else NORTH
+            sum_and_send(t, 3, k, [], one.at[k], to, (ONCE, k))
+
+    def second(t):
+        one, land_x, land_y = lands[t][1:4]
+        arrived(t, lands[t][0].at[pl.ds(rings[1] * 4, 4)], SIBLING, (CORNER, 1))
+        arrived(t, lands[t][0].at[pl.ds(rings[2] * 4, 4)], SIBLING, (CORNER, 2))
+        order = ((1, 0), (2, 3), (1, 1), (2, 2), (1, 3), (2, 0), (1, 2), (2, 1))
+        for dd, k in order:
+            to, land = (EAST, land_x) if dd == 1 else (NORTH, land_y)
+            extra = []
+            if (dd == 1) == (k >= 2):
+                arrived(t, one.at[k], NORTH if k >= 2 else EAST, (ONCE, k))
+                extra = [one.at[k]]
+            sum_and_send(t, dd, k, extra, land.at[k], to, (to, k))
+
+    held = {}
+
+    def third(t):
+        land_x, land_y, land_z = lands[t][2:5]
+        arrived(t, lands[t][0].at[pl.ds(rings[0] * 4, 4)], SIBLING, (CORNER, 0))
+        for k in (3, 2, 1, 0):
+            arrived(t, land_x.at[k], EAST, (EAST, k))
+            arrived(t, land_y.at[k], NORTH, (NORTH, k))
+            extra = [land_x.at[k], land_y.at[k]]
+            if k:
+                sum_and_send(t, 0, k, extra, land_z.at[k], (LEVEL, k), (LEVEL, k))
+            else:
+                shape = slots[t]
+                loads, slot, terms = total_of(t, 0, 0, extra)
+                total = work[shape][2]
+                def store(at, value):
+                    total[at] = value
+                add_up(shape, loads, slot, terms, store)
+
+    def last(t):
+        shape = slots[t]
+        land_z = lands[t][4]
+        loads, _, total = work[shape]
+        slot = task[0] % 2
+        task[0] += 1
+        copies = []
+        for k in (1, 2, 3):
+            arrived(t, land_z.at[k], (LEVEL, k), (LEVEL, k))
+            copy = pltpu.make_async_copy(land_z.at[k], loads.at[slot, k - 1], load_sem.at[slot * 4 + k - 1])
+            copy.start()
+            copies.append(copy)
+        for copy in copies:
+            copy.wait()
+        def store(at, value):
+            total[at] = total[at] + value
+        add_up(shape, loads, slot, 3, store)
+        copy = pltpu.make_async_copy(total, finals[t], out_sem)
+        copy.start()
+        copy.wait()
+
+    for dd in (3, 1, 2, 0):
+        give(0, dd)
+    for t in range(n + 1):
+        if t < n:
+            first(t)
+            if t + 1 < n:
+                for dd in (3, 1, 2, 0):
+                    give(t + 1, dd)
+        if t > 0:
+            third(t - 1)
+        if t < n:
+            second(t)
+        if t > 0:
+            last(t - 1)
+    for copy in pending:
+        copy.wait_send()
+    for shape in shapes:
+        for copy in used[shape]:
+            if copy is not None:
+                copy.wait_send()
+
+def scatter(pairs, name="scatter_gradients", collective=1):
+    slots = [tuple(a.shape[1:]) for a, _ in pairs]
+    n = len(slots)
+    shapes = sorted(set(slots))
+    out = [jax.ShapeDtypeStruct(s, jnp.float32) for s in slots]
+    for s in slots:
+        out += [jax.ShapeDtypeStruct((m,) + s, jnp.bfloat16) for m in (16, 4, 4, 4, 4)]
+    scratch = []
+    for s in shapes:
+        scratch += [pltpu.VMEM((2, 4) + s, jnp.bfloat16), pltpu.VMEM((DEPTH,) + s, jnp.bfloat16), pltpu.VMEM(s, jnp.float32)]
+    m = n * len(KINDS)
+    scratch += [pltpu.SemaphoreType.DMA((m,)), pltpu.SemaphoreType.DMA((m,)), pltpu.SemaphoreType.DMA((8,)), pltpu.SemaphoreType.DMA(())]
+    res = pl.pallas_call(
+        partial(scatter_kernel, slots),
+        out_shape=tuple(out),
+        in_specs=[pl.BlockSpec(memory_space=pl.ANY)] * (2 * n),
+        out_specs=tuple(pl.BlockSpec(memory_space=pl.ANY) for _ in out),
+        scratch_shapes=scratch,
+        compiler_params=pltpu.CompilerParams(collective_id=collective, has_side_effects=True, vmem_limit_bytes=48 << 20),
+        name=name,
+    )(*[x for pair in pairs for x in pair])
+    return res[:n]
+
+
+def mm(left, right):
+    return jnp.dot(left, right, preferred_element_type=F32)
+
+
+def mm_nt(left, right):
+    return lax.dot_general(left, right, (((1,), (1,)), ((), ())), preferred_element_type=F32)
+
+
+def mm_tn(left, right):
+    return lax.dot_general(left, right, (((0,), (0,)), ((), ())), preferred_element_type=F32)
+
+
+def normal_parts(values):
+    centre = jnp.mean(values, axis=-1, keepdims=True)
+    centred = values - centre
+    inverse = lax.rsqrt(jnp.mean(centred * centred, axis=-1, keepdims=True) + epsilon)
+    return centred * inverse, inverse
+
+
+def normal_back(upstream, unit, inverse):
+    return inverse * (
+        upstream
+        - jnp.mean(upstream, axis=-1, keepdims=True)
+        - unit * jnp.mean(upstream * unit, axis=-1, keepdims=True)
+    )
+
+
+def close_up(rows, table):
+    high = rows.astype(LOW)
+    rest = (rows - high.astype(F32)).astype(LOW)
+    return mm_nt(high, table) + mm_nt(rest, table)
+
+
+def whole(shape):
+    zeros = (0,) * len(shape)
+    return pl.BlockSpec(shape, lambda *_: zeros)
+
+
+def project_kernel(steps, width, x, gain, shift, query_bias, value_bias, table, page,
+                   normed_out, query_out, pair_out, mixture):
+    step = pl.program_id(0)
+    tile = page.shape[1]
+
+    @pl.when(step == 0)
+    def _():
+        unit, _ = normal_parts(x[...].astype(F32))
+        normed = (unit * gain[...] + shift[...]).astype(LOW)
+        normed_out[...] = mm(normed, table[...]).astype(LOW)
+
+    mixture[:, pl.ds(pl.multiple_of(step * tile, tile), tile)] = mm(normed_out[...], page[...])
+
+    @pl.when(step == steps - 1)
+    def _():
+        blank = jnp.zeros((x.shape[0], WIDE - width), LOW)
+        query = ((mixture[:, :width] + query_bias[...]).astype(LOW).astype(F32) * HDIM ** (-0.5)).astype(LOW)
+        query_out[:, :width] = query
+        query_out[:, width:] = blank
+        pair_out[0, :, :width] = mixture[:, width : 2 * width].astype(LOW)
+        pair_out[0, :, width:] = blank
+        pair_out[1, :, :width] = (mixture[:, 2 * width : 3 * width] + value_bias[...]).astype(LOW)
+        pair_out[1, :, width:] = blank
+
+
+def project_rows(x, gain, shift, query_bias, value_bias, table, page):
+    rows, width = x.shape
+    tile, steps = 640, 6
+    return pl.pallas_call(
+        partial(project_kernel, steps, width),
+        grid=(steps,),
+        in_specs=[whole(x.shape)] + [whole((1, width))] * 4 + [whole(table.shape)]
+        + [pl.BlockSpec((page.shape[0], tile), lambda i: (0, i))],
+        out_specs=(whole((rows, WIDE)), whole((rows, WIDE)), whole((2, rows, WIDE))),
+        out_shape=(
+            jax.ShapeDtypeStruct((rows, WIDE), LOW),
+            jax.ShapeDtypeStruct((rows, WIDE), LOW),
+            jax.ShapeDtypeStruct((2, rows, WIDE), LOW),
+        ),
+        scratch_shapes=[pltpu.VMEM((rows, tile * steps), F32)],
+        compiler_params=pltpu.CompilerParams(vmem_limit_bytes=48 << 20),
+        name="project_rows",
+    )(x, gain, shift, query_bias, value_bias, table, page)
+
+
+def head_pair(rows):
+    lane = lax.broadcasted_iota(jnp.int32, rows.shape, 1)
+    zero = jnp.zeros_like(rows)
+    return jnp.concatenate(
+        [jnp.where(lane < HDIM, rows, zero), jnp.where(lane < HDIM, zero, rows)], axis=0
+    )
+
+
+def from_pair(turned):
+    n = turned.shape[1] // 2
+    own = jnp.concatenate([turned[:HDIM, :n], turned[HDIM:, n:]], axis=0)
+    return own.T
+
+
+def attend_kernel(x, here, beside, away, corner, first_ref, attended_out, log_out):
+    first = first_ref[0] == 0
+    half = x.shape[0] // 2
+    low, high = head_pair(x[:half]), head_pair(x[half:])
+    last_rows = jnp.where(first, high, low)
+
+    def block(kind, near, part):
+        at = pl.ds(part * half, half)
+        one, two = (here, beside) if near == 0 else (away, corner)
+        return jnp.concatenate([one[kind, at], two[kind, at]], axis=0)
+
+    def last_block(kind):
+        return jnp.where(first, block(kind, 1, 1), block(kind, 1, 0))
+
+    units = [
+        (low, (0, 0)), (high, (0, 0)), (high, (0, 1)), (high, (1, 0)), (last_rows, None),
+    ]
+    parts = []
+    for rows, which in units:
+        keys = last_block(0) if which is None else block(0, *which)
+        values = last_block(1) if which is None else block(1, *which)
+        scores = mm_nt(keys, rows)
+        level = jnp.max(scores, axis=0, keepdims=True)
+        exponent = jnp.exp(scores - level)
+        parts.append(
+            (level, jnp.sum(exponent, axis=0, keepdims=True), mm_tn(values, exponent.astype(LOW)))
+        )
+    last = parts[4]
+    low_last = (jnp.where(first, far_below, last[0]),) + last[1:]
+    high_last = (jnp.where(first, last[0], far_below),) + last[1:]
+    for place, group in enumerate(([parts[0], low_last], parts[1:4] + [high_last])):
+        peak = group[0][0]
+        for level, _, _ in group[1:]:
+            peak = jnp.maximum(peak, level)
+        total, mixed = 0.0, 0.0
+        for level, sums, out in group:
+            share = jnp.exp(level - peak)
+            total = total + share * sums
+            mixed = mixed + share * out
+        attended_out[place * half : (place + 1) * half] = from_pair(mixed / total)
+        log_out[0, place : place + 1] = peak + jnp.log(total)
+
+
+def attend(query, here, beside, away, corner, low_chunk):
+    rows = query.shape[0]
+    pairs = WIDE // 128
+    flat = pl.BlockSpec((rows, 128), lambda p: (0, p))
+    both = pl.BlockSpec((2, rows, 128), lambda p: (0, 0, p))
+    return pl.pallas_call(
+        attend_kernel,
+        grid=(pairs,),
+        in_specs=[flat] + [both] * 4 + [pl.BlockSpec(memory_space=pltpu.SMEM)],
+        out_specs=(flat, pl.BlockSpec((1, 2, rows), lambda p: (p, 0, 0))),
+        out_shape=(
+            jax.ShapeDtypeStruct((rows, WIDE), F32),
+            jax.ShapeDtypeStruct((pairs, 2, rows), F32),
+        ),
+        compiler_params=pltpu.CompilerParams(vmem_limit_bytes=48 << 20),
+        name="attend",
+    )(query, here, beside, away, corner, low_chunk.reshape(1))
+
+
+def attend_back_kernel(query, grad, attended, logs, here, beside, away, corner, first_ref,
+                       query_out, here_out, beside_out, away_out, corner_out):
+    first = first_ref[0] == 0
+    half = query.shape[0] // 2
+
+    def rows_of(place):
+        at = slice(place * half, (place + 1) * half)
+        rows, grads = head_pair(query[at]), head_pair(grad[at])
+        product = (grad[at].astype(F32) * attended[at]).T
+        delta = jnp.concatenate(
+            [jnp.sum(product[:HDIM], axis=0, keepdims=True), jnp.sum(product[HDIM:], axis=0, keepdims=True)],
+            axis=1,
+        )
+        return rows, grads, logs[0, place : place + 1], delta
+
+    low, high = rows_of(0), rows_of(1)
+    last_rows = tuple(jnp.where(first, b, a) for a, b in zip(low, high))
+
+    def block(kind, near, part):
+        at = pl.ds(part * half, half)
+        one, two = (here, beside) if near == 0 else (away, corner)
+        return jnp.concatenate([one[kind, at], two[kind, at]], axis=0)
+
+    def back(rows, keys, values):
+        queries, grads, log, delta = rows
+        weights = jnp.exp(mm_nt(keys, queries) - log)
+        pulled = (weights * (mm_nt(values, grads) - delta)).astype(LOW)
+        return (
+            mm_tn(keys, pulled),
+            mm(pulled, queries),
+            mm(weights.astype(LOW), grads),
+        )
+
+    def put(near, part, grad_keys, grad_values):
+        one, two = (here_out, beside_out) if near == 0 else (away_out, corner_out)
+        at = pl.ds(part * half, half)
+        for kind, value in ((0, grad_keys), (1, grad_values)):
+            one[kind, at] = value[:half].astype(one.dtype)
+            two[kind, at] = value[half:].astype(two.dtype)
+
+    keys, values = block(0, 0, 0), block(1, 0, 0)
+    low_query, keys_a, values_a = back(low, keys, values)
+    high_query, keys_b, values_b = back(high, keys, values)
+    put(0, 0, keys_a + keys_b, values_a + values_b)
+    more, keys_a, values_a = back(high, block(0, 0, 1), block(1, 0, 1))
+    high_query = high_query + more
+    put(0, 1, keys_a, values_a)
+    more, keys_a, values_a = back(high, block(0, 1, 0), block(1, 1, 0))
+    high_query = high_query + more
+    keys = jnp.where(first, block(0, 1, 1), block(0, 1, 0))
+    values = jnp.where(first, block(1, 1, 1), block(1, 1, 0))
+    more, keys_b, values_b = back(last_rows, keys, values)
+    zero = jnp.zeros_like(keys_b)
+    put(1, 0, keys_a + jnp.where(first, zero, keys_b), values_a + jnp.where(first, zero, values_b))
+    put(1, 1, jnp.where(first, keys_b, zero), jnp.where(first, values_b, zero))
+    empty = jnp.zeros_like(more)
+    low_query = low_query + jnp.where(first, empty, more)
+    high_query = high_query + jnp.where(first, more, empty)
+    scale_factor = HDIM ** (-0.5)
+    query_out[:half] = (from_pair(low_query) * scale_factor).astype(LOW)
+    query_out[half:] = (from_pair(high_query) * scale_factor).astype(LOW)
+
+
+def attend_back(query, grad, attended, logs, here, beside, away, corner, low_chunk):
+    rows = query.shape[0]
+    pairs = WIDE // 128
+    flat = pl.BlockSpec((rows, 128), lambda p: (0, p))
+    both = pl.BlockSpec((2, rows, 128), lambda p: (0, 0, p))
+    shape = (2, rows, WIDE)
+    return pl.pallas_call(
+        attend_back_kernel,
+        grid=(pairs,),
+        in_specs=[flat, flat, flat, pl.BlockSpec((1, 2, rows), lambda p: (p, 0, 0))] + [both] * 4
+        + [pl.BlockSpec(memory_space=pltpu.SMEM)],
+        out_specs=(flat, both, both, both, both),
+        out_shape=(jax.ShapeDtypeStruct((rows, WIDE), LOW), jax.ShapeDtypeStruct(shape, F32))
+        + tuple(jax.ShapeDtypeStruct(shape, LOW) for _ in range(3)),
+        compiler_params=pltpu.CompilerParams(vmem_limit_bytes=48 << 20),
+        name="attend_back",
+    )(query, grad, attended, logs, here, beside, away, corner, low_chunk.reshape(1))
+
+
+def feed_kernel(steps, width, x, attended, gain, shift, output_bias, reduce_bias, table, page, expand,
+                expand_bias, reduce, attended_out, middle_out, second_out, active_out, slope_out,
+                result_out, result_low_out, output, sem):
+    step = pl.program_id(0)
+    lead = 4 * width - WIDE
+    extra = 3 * width - lead
+
+    @pl.when(step == 0)
+    def _():
+        copy = pltpu.make_async_copy(page.at[:, pl.ds(lead, WIDE)], output, sem)
+        copy.start()
+        attended_out[...] = mm(attended[:, :width].astype(LOW), table[...]).astype(LOW)
+        copy.wait()
+        blended = mm(attended_out[...], output[...])
+        middle = x[...].astype(F32) + (blended[:, extra:] + output_bias[...])
+        middle_out[...] = middle
+        unit, _ = normal_parts(middle)
+        second = (unit * gain[...] + shift[...]).astype(LOW)
+        second_out[...] = mm(second, table[...]).astype(LOW)
+        result_out[...] = middle + reduce_bias[...]
+
+    hidden = mm(second_out[...], expand[...]) + expand_bias[...]
+    below = 0.5 + 0.5 * lax.erf(hidden * 0.7071067811865476)
+    active = (hidden * below).astype(LOW)
+    active_out[...] = active
+    slope = below + hidden * (0.3989422804014327 * jnp.exp(-0.5 * hidden * hidden))
+    slope_out[...] = slope.astype(LOW)
+    result_out[...] += mm(active, reduce[...])
+
+    @pl.when(step == steps - 1)
+    def _():
+        result_low_out[...] = result_out[...].astype(LOW)
+
+
+def feed(x, attended, gain, shift, output_bias, reduce_bias, table, page, expand, expand_bias, reduce):
+    rows, width = x.shape
+    inner = expand.shape[1]
+    tile = 256
+    steps = inner // tile
+    flat = whole((rows, width))
+    wide = whole((rows, WIDE))
+    column = pl.BlockSpec((rows, tile), lambda i: (0, i))
+    outs = pl.pallas_call(
+        partial(feed_kernel, steps, width),
+        grid=(steps,),
+        in_specs=[flat, wide] + [whole((1, width))] * 4
+        + [whole(table.shape), pl.BlockSpec(memory_space=pl.ANY)]
+        + [pl.BlockSpec((WIDE, tile), lambda i: (0, i)), pl.BlockSpec((1, tile), lambda i: (0, i)),
+           pl.BlockSpec((tile, width), lambda i: (i, 0))],
+        out_specs=(wide, flat, wide, column, column, flat, flat),
+        out_shape=(
+            jax.ShapeDtypeStruct((rows, WIDE), LOW),
+            jax.ShapeDtypeStruct((rows, width), F32),
+            jax.ShapeDtypeStruct((rows, WIDE), LOW),
+            jax.ShapeDtypeStruct((rows, inner), LOW),
+            jax.ShapeDtypeStruct((rows, inner), LOW),
+            jax.ShapeDtypeStruct((rows, width), F32),
+            jax.ShapeDtypeStruct((rows, width), LOW),
+        ),
+        scratch_shapes=[pltpu.VMEM((WIDE, WIDE), LOW), pltpu.SemaphoreType.DMA(())],
+        compiler_params=pltpu.CompilerParams(vmem_limit_bytes=48 << 20),
+        name="feed",
+    )(x, attended, gain, shift, output_bias, reduce_bias, table, page, expand, expand_bias, reduce)
+    attended_low, middle, second_low, active, slope, _, result = outs
+    return attended_low, middle, second_low, active, slope, result
+
+
+def feed_back_kernel(steps, width, top, slope, middle, gain, table, page, expand, reduce,
+                     hidden_out, bias_out, middle_out, branch_out, attended_out, sums_out,
+                     second, output, sem):
+    step = pl.program_id(0)
+    lead = 4 * width - WIDE
+    extra = 3 * width - lead
+    rows = top.shape[0]
+
+    @pl.when(step == 0)
+    def _():
+        pltpu.make_async_copy(page.at[:, pl.ds(lead, WIDE)], output, sem).start()
+        second[...] = jnp.zeros_like(second)
+
+    hidden = (mm_nt(top[...], reduce[...]) * slope[...].astype(F32)).astype(LOW)
+    hidden_out[...] = hidden
+    bias_out[...] = jnp.sum(hidden.astype(F32), axis=0, keepdims=True)
+    second[...] += mm_nt(hidden, expand[...])
+
+    @pl.when(step == steps - 1)
+    def _():
+        pltpu.make_async_copy(page.at[:, pl.ds(lead, WIDE)], output, sem).wait()
+        upstream = top[...].astype(F32)
+        grad_second = close_up(second[...], table[...])
+        unit, inverse = normal_parts(middle[...])
+        grad_middle = upstream + normal_back(grad_second * gain[...], unit, inverse)
+        middle_out[...] = grad_middle
+        branch = grad_middle.astype(LOW)
+        branch_out[...] = branch
+        full = jnp.concatenate([jnp.zeros((rows, extra), LOW), branch], axis=1)
+        pulled = mm_nt(full, output[...]).astype(LOW)
+        attended_out[:, :width] = mm_nt(pulled, table[...]).astype(LOW)
+        attended_out[:, width:] = jnp.zeros((rows, WIDE - width), LOW)
+
+        def row(value):
+            return jnp.sum(value, axis=0, keepdims=True)
+
+        sums_out[0:1] = row(grad_second * unit)
+        sums_out[1:2] = row(grad_second)
+        sums_out[2:3] = row(branch.astype(F32))
+        sums_out[3:4] = row(upstream)
+        sums_out[4:8] = jnp.zeros((4, width), F32)
+
+
+def feed_back(top, slope, middle, gain, table, page, expand, reduce):
+    rows, width = top.shape
+    inner = expand.shape[1]
+    tile = 256
+    steps = inner // tile
+    flat = whole((rows, width))
+    wide = whole((rows, WIDE))
+    column = pl.BlockSpec((rows, tile), lambda i: (0, i))
+    return pl.pallas_call(
+        partial(feed_back_kernel, steps, width),
+        grid=(steps,),
+        in_specs=[flat, column, flat, whole((1, width)), whole(table.shape),
+                  pl.BlockSpec(memory_space=pl.ANY),
+                  pl.BlockSpec((WIDE, tile), lambda i: (0, i)),
+                  pl.BlockSpec((tile, width), lambda i: (i, 0))],
+        out_specs=(column, pl.BlockSpec((1, tile), lambda i: (0, i)), flat, flat, wide, whole((8, width))),
+        out_shape=(
+            jax.ShapeDtypeStruct((rows, inner), LOW),
+            jax.ShapeDtypeStruct((1, inner), F32),
+            jax.ShapeDtypeStruct((rows, width), F32),
+            jax.ShapeDtypeStruct((rows, width), LOW),
+            jax.ShapeDtypeStruct((rows, WIDE), LOW),
+            jax.ShapeDtypeStruct((8, width), F32),
+        ),
+        scratch_shapes=[pltpu.VMEM((rows, WIDE), F32), pltpu.VMEM((WIDE, WIDE), LOW), pltpu.SemaphoreType.DMA(())],
+        compiler_params=pltpu.CompilerParams(vmem_limit_bytes=48 << 20),
+        name="feed_back",
+    )(top, slope, middle, gain, table, page, expand, reduce)
+
+
+def project_back_kernel(steps, width, query, pair, branch, x, middle, gain, table, page,
+                        mixture_out, result_out, sums_out, mixture, normed):
+    step = pl.program_id(0)
+    tile = page.shape[1]
+    rows = x.shape[0]
+
+    @pl.when(step == 0)
+    def _():
+        mixture[:, :width] = query[:, :width].astype(F32)
+        mixture[:, width : 2 * width] = pair[0, :, :width].astype(F32)
+        mixture[:, 2 * width : 3 * width] = pair[1, :, :width].astype(F32)
+        mixture[:, 3 * width :] = jnp.zeros((rows, width), F32)
+        normed[...] = jnp.zeros_like(normed)
+
+    part = mixture[:, pl.ds(pl.multiple_of(step * tile, tile), tile)].astype(LOW)
+    normed[...] += mm_nt(part, page[...])
+
+    @pl.when(step == steps - 1)
+    def _():
+        grad_normed = close_up(normed[...], table[...])
+        unit, inverse = normal_parts(x[...].astype(F32))
+        result_out[...] = (middle[...] + normal_back(grad_normed * gain[...], unit, inverse)).astype(LOW)
+
+        def row(value):
+            return jnp.sum(value, axis=0, keepdims=True)
+
+        sums_out[0:1] = row(grad_normed * unit)
+        sums_out[1:2] = row(grad_normed)
+        sums_out[2:3] = row(query[:, :width].astype(F32))
+        sums_out[3:4] = row(pair[1, :, :width].astype(F32))
+        sums_out[4:8] = jnp.zeros((4, width), F32)
+        mixture[:, 3 * width :] = branch[...].astype(F32)
+        mixture_out[...] = mixture[...].astype(LOW)
+
+
+def project_back(query, pair, branch, x, middle, gain, table, page):
+    rows, width = x.shape
+    tile, steps = 640, 6
+    flat = whole((rows, width))
+    return pl.pallas_call(
+        partial(project_back_kernel, steps, width),
+        grid=(steps,),
+        in_specs=[whole((rows, WIDE)), whole((2, rows, WIDE)), flat, flat, flat, whole((1, width)),
+                  whole(table.shape), pl.BlockSpec((WIDE, tile), lambda i: (0, i))],
+        out_specs=(whole((rows, 4 * width)), flat, whole((8, width))),
+        out_shape=(
+            jax.ShapeDtypeStruct((rows, 4 * width), LOW),
+            jax.ShapeDtypeStruct((rows, width), LOW),
+            jax.ShapeDtypeStruct((8, width), F32),
+        ),
+        scratch_shapes=[pltpu.VMEM((rows, 4 * width), F32), pltpu.VMEM((rows, WIDE), F32)],
+        compiler_params=pltpu.CompilerParams(vmem_limit_bytes=48 << 20),
+        name="project_back",
+    )(query, pair, branch, x, middle, gain, table, page)
+
+
+def page_kernel(width, normed, attended, mixture, small, out, left_one, left_two):
+    step = pl.program_id(0)
+    tile = mixture.shape[1]
+    edge = 3 * width
+
+    @pl.when(step == 0)
+    def _():
+        left_one[...] = normed[...].T
+        left_two[...] = attended[...].T
+
+    def put(value):
+        value = value.reshape(16, 72, tile)
+        row = lax.broadcasted_iota(jnp.int32, value.shape, 1)
+        out[...] = jnp.where(row == 68, small[...], value).astype(LOW)
+
+    @pl.when((step + 1) * tile <= edge)
+    def _():
+        put(mm(left_one[...], mixture[...]))
+
+    @pl.when(step * tile >= edge)
+    def _():
+        put(mm(left_two[...], mixture[...]))
+
+    @pl.when(((step + 1) * tile > edge) & (step * tile < edge))
+    def _():
+        column = step * tile + lax.broadcasted_iota(jnp.int32, mixture.shape, 1)
+        value = mixture[...]
+        zero = jnp.zeros_like(value)
+        put(mm(left_one[...], jnp.where(column < edge, value, zero))
+            + mm(left_two[...], jnp.where(column < edge, zero, value)))
+
+
+def attention_page(normed, attended, mixture, small):
+    rows, total = mixture.shape
+    tile = 256
+    return pl.pallas_call(
+        partial(page_kernel, total // 4),
+        grid=(total // tile,),
+        in_specs=[whole((rows, WIDE)), whole((rows, WIDE)), pl.BlockSpec((rows, tile), lambda i: (0, i)),
+                  pl.BlockSpec((16, 1, tile), lambda i: (0, 0, i))],
+        out_specs=pl.BlockSpec((16, 72, tile), lambda i: (0, 0, i)),
+        out_shape=jax.ShapeDtypeStruct((16, 72, total), LOW),
+        scratch_shapes=[pltpu.VMEM((WIDE, rows), LOW), pltpu.VMEM((WIDE, rows), LOW)],
+        compiler_params=pltpu.CompilerParams(vmem_limit_bytes=48 << 20),
+        name="attention_page",
+    )(normed, attended, mixture, small)
+
+
+def spread(width):
+    row = lax.broadcasted_iota(jnp.int32, (width, 16 * 72), 0)
+    column = lax.broadcasted_iota(jnp.int32, (width, 16 * 72), 1)
+    same = (row // 68 == column // 72) & (row % 68 == column % 72)
+    return same.astype(LOW)
+
+
+def small_of(page):
+    part = page[:, 68, : 12 * 68].astype(F32).reshape(16, 12, 68)
+    vectors = [part[:, row].reshape(1, -1) for row in range(8)]
+    return vectors, part[:, 8:].reshape(1, -1)
+
+
+def layer_forward(source, small, wide, weights, low_chunk, table):
+    page, expand, reduce = weights
+    first_gain, first_shift, query_bias, value_bias, output_bias, reduce_bias, gain, shift = small
+    normed, query, here = project_rows(
+        source, first_gain, first_shift, query_bias, value_bias, table, page
+    )
+    away = swapped(here, LINE, 1)
+    beside = swapped(here, SECTION, 1)
+    corner = swapped(away, SECTION, 1)
+    pairs = (here, beside, away, corner)
+    attended, logs = attend(query, *pairs, low_chunk)
+    attended_low, middle, second, active, slope, result = feed(
+        source, attended, gain, shift, output_bias, reduce_bias, table, page, expand, wide, reduce
+    )
+    saved = (source, normed, query, pairs, attended, logs, attended_low, middle, second, active, slope)
+    return result, saved
+
+
+def layer_gradient(top, saved, small, weights, low_chunk, table):
+    source, normed, query, pairs, attended, logs, attended_low, middle, second, active, slope = saved
+    page, expand, reduce = weights
+    width = top.shape[1]
+    grad_hidden, sum_wide, grad_middle, branch, grad_attended, late = feed_back(
+        top, slope, middle, small[6], table, page, expand, reduce
+    )
+    grad_query, near, beside, away, corner = attend_back(
+        query, grad_attended, attended, logs, *pairs, low_chunk
+    )
+    away = (away.astype(F32) + swapped(corner, SECTION, 1).astype(F32)).astype(LOW)
+    near = near + swapped(beside, SECTION, 1).astype(F32)
+    near = (near + swapped(away, LINE, 1).astype(F32)).astype(LOW)
+    mixture, result, early = project_back(
+        grad_query, near, branch, source, grad_middle, small[0], table, page
+    )
+    order = (early[0], early[1], early[2], early[3], late[2], late[3], late[0], late[1])
+    packed = jnp.stack([vector.reshape(16, -1) for vector in order], axis=1)
+    packed = jnp.concatenate([packed, sum_wide.reshape(16, 4, -1)], axis=1)
+    packed = packed.reshape(16, 1, -1).astype(LOW)
+    packed = jnp.pad(packed, ((0, 0), (0, 0), (0, 4 * width - packed.shape[2])))
+    page_attention = attention_page(normed, attended_low, mixture, packed)
+    page_expand = mm_tn(second, grad_hidden).astype(LOW).reshape(16, 72, -1)
+    page_reduce = mm_tn(active, top).astype(LOW).reshape(16, -1, width)
+    return result, page_attention, page_expand, page_reduce
+
+
+def four_by_four(
+    inputs,
+    cotangent,
+    first_gain,
+    first_shift,
+    joint_weight,
+    query_bias,
+    value_bias,
+    output_weight,
+    output_bias,
+    second_gain,
+    second_shift,
+    expand_weight,
+    expand_bias,
+    reduce_weight,
+    reduce_bias,
+):
+    core = lax.axis_index(SECTION)
+    line = lax.axis_index(LINE)
+    low_chunk = jnp.where(line < 2, line, 3 - line)
+    width = HEADS * HDIM
+    packed = jnp.concatenate(
+        [
+            first_gain[0],
+            first_shift[0],
+            query_bias[0],
+            value_bias[0],
+            output_bias[0],
+            reduce_bias[0],
+            second_gain[0],
+            second_shift[0],
+            expand_bias[0],
+        ]
+    )
+    packed = jnp.pad(packed[None], ((0, 3), (0, 4 * width - packed.shape[0])))
+    attention_shard = jnp.concatenate(
+        [jnp.concatenate([joint_weight[0], output_weight[0]], axis=1), packed], axis=0
+    )
+    expand_shard = jnp.pad(expand_weight[0], ((0, 4), (0, 0)))
+    other = swapped(jnp.where(core == 0, expand_shard, attention_shard), SECTION, 1)
+    lower = jnp.where(core == 0, attention_shard, other)
+    upper = jnp.where(core == 0, other, expand_shard)
+    rows = to_rows(inputs, core, line)
+    top = to_rows(cotangent, core, line)
+    lower_pages, reduce_pages, upper_pages = gather_pages((lower, reduce_weight[0], upper))
+    table = spread(width)
+    layers = []
+    for layer, pages in enumerate((lower_pages, upper_pages)):
+        small, wide = small_of(pages[0])
+        weights = (
+            pages[0].reshape(-1, 4 * width),
+            pages[1].reshape(-1, 4 * width),
+            reduce_pages[layer].reshape(-1, width),
+        )
+        layers.append((small, wide, weights))
+    small, wide, weights = layers[0]
+    middle_rows, saved_lower = layer_forward(rows, small, wide, weights, low_chunk, table)
+    small, wide, weights = layers[1]
+    final_rows, saved_upper = layer_forward(middle_rows, small, wide, weights, low_chunk, table)
+    layer_outputs = from_rows(middle_rows, final_rows, core, line)
+    upper_grad, upper_attention, upper_expand, upper_reduce = layer_gradient(
+        top, saved_upper, small, weights, low_chunk, table
+    )
+    small, wide, weights = layers[0]
+    lower_grad, lower_attention, lower_expand, lower_reduce = layer_gradient(
+        upper_grad, saved_lower, small, weights, low_chunk, table
+    )
+    input_grads = from_rows(lower_grad, upper_grad, core, line)
+    lower_sum, reduce_sum, upper_sum = scatter(
+        [
+            (lower_attention, lower_expand),
+            (lower_reduce, upper_reduce),
+            (upper_attention, upper_expand),
+        ]
+    )
+    kept = jnp.where(core == 0, lower_sum, upper_sum)
+    other = swapped(jnp.where(core == 0, upper_sum, lower_sum), SECTION, 1)
+    attention_sum = jnp.where(core == 0, kept, other)
+    expand_sum = jnp.where(core == 0, other, kept)
+    vectors = attention_sum[68, : 12 * 68].reshape(12, 68)
+    return (
+        layer_outputs,
+        input_grads,
+        vectors[0][None],
+        vectors[1][None],
+        attention_sum[None, :68, : 3 * width],
+        vectors[2][None],
+        vectors[3][None],
+        attention_sum[None, :68, 3 * width :],
+        vectors[4][None],
+        vectors[6][None],
+        vectors[7][None],
+        expand_sum[None, :68],
+        vectors[8:].reshape(1, -1),
+        reduce_sum[None],
+        vectors[5][None],
+    )
+
+
+def fits(mesh):
+    return dict(mesh.shape) == {SECTION: 2, RING: 4, LINE: 4}
 
 
 def solution(mesh):
     return jax.shard_map(
-        body,
+        four_by_four if fits(mesh) else body,
         mesh=mesh,
         in_specs=(
-            P("dp", "seq", None),
-            P("dp", "seq", None),
-            P("section", ("dp", "seq")),
-            P("section", ("dp", "seq")),
-            P("section", ("dp", "seq"), None),
-            P("section", ("dp", "seq")),
-            P("section", ("dp", "seq")),
-            P("section", ("dp", "seq"), None),
-            P("section", ("dp", "seq")),
-            P("section", ("dp", "seq")),
-            P("section", ("dp", "seq")),
-            P("section", ("dp", "seq"), None),
-            P("section", ("dp", "seq")),
-            P("section", ("dp", "seq"), None),
-            P("section", ("dp", "seq")),
+            P(RING, LINE, None),
+            P(RING, LINE, None),
+            P(SECTION, OWNERS),
+            P(SECTION, OWNERS),
+            P(SECTION, OWNERS, None),
+            P(SECTION, OWNERS),
+            P(SECTION, OWNERS),
+            P(SECTION, OWNERS, None),
+            P(SECTION, OWNERS),
+            P(SECTION, OWNERS),
+            P(SECTION, OWNERS),
+            P(SECTION, OWNERS, None),
+            P(SECTION, OWNERS),
+            P(SECTION, OWNERS, None),
+            P(SECTION, OWNERS),
         ),
         out_specs=(
-            P("section", "dp", "seq", None),
-            P("section", "dp", "seq", None),
-            P("section", ("dp", "seq")),
-            P("section", ("dp", "seq")),
-            P("section", ("dp", "seq"), None),
-            P("section", ("dp", "seq")),
-            P("section", ("dp", "seq")),
-            P("section", ("dp", "seq"), None),
-            P("section", ("dp", "seq")),
-            P("section", ("dp", "seq")),
-            P("section", ("dp", "seq")),
-            P("section", ("dp", "seq"), None),
-            P("section", ("dp", "seq")),
-            P("section", ("dp", "seq"), None),
-            P("section", ("dp", "seq")),
+            P(SECTION, RING, LINE, None),
+            P(SECTION, RING, LINE, None),
+            P(SECTION, OWNERS),
+            P(SECTION, OWNERS),
+            P(SECTION, OWNERS, None),
+            P(SECTION, OWNERS),
+            P(SECTION, OWNERS),
+            P(SECTION, OWNERS, None),
+            P(SECTION, OWNERS),
+            P(SECTION, OWNERS),
+            P(SECTION, OWNERS),
+            P(SECTION, OWNERS, None),
+            P(SECTION, OWNERS),
+            P(SECTION, OWNERS, None),
+            P(SECTION, OWNERS),
         ),
         check_vma=False,
     )

time: 3050 us -> 1100 us (0.36)
  blocking collectives: 1230 us -> 0 us
  waiting for transfers between devices: 1140 us -> 83 us
  Pallas kernels: 0 us -> 815 us
  matrix products: 409 us -> 27.1 us
  local copies, waits for them, and re-layouts: 139 us -> 98.2 us
    unnamed x3 -> x0, blocking collectives: 1230 us -> none
    pallas_call x0 -> x16, Pallas kernels: none -> 815 us  [the longest x1 301 us: scatter(): pl.pallas_call(partial(scatter_kernel, slots), out_shape=tuple(out), in_s...]
    all_gather x16 -> x0, waiting for transfers between devices: 797 us -> none  [the longest x6 238 us: body(): lax.all_gather(projected[5], 'seq', axis=0, tiled=True)]
    dot_general x69 -> x4, matrix products: 409 us -> 27.1 us  [mm_tn(): lax.dot_general(left, right, (((0,), (0,)), ((), ())), preferred_element_...]
    reduce_scatter x7 -> x0, waiting for transfers between devices: 343 us -> none  [the longest x3 202 us: layer_backward(): lax.psum_scatter(grad_keys_full, 'seq', scatter_dimension=0, tiled=True)]
    ppermute x4 -> x20, waiting for transfers between devices: 0.86 us -> 83 us  [swapped(): lax.ppermute(value, axis, [(source, source ^ bits) for source in range(co...]
    unnamed x401 -> x196, local copies, waits for them, and re-layouts: 88 us -> 30 us
  transfers between devices with their start and end apart: 32 -> 20, of which waited for: 19 -> 6; matrix products, arithmetic and copies ran while one was open for 52% -> 11% of each run, Pallas kernels for 0% -> 35%
where the time goes in v2:
time: 1100 us; the launch traced here: 1090 us
  Pallas kernels  815 us (74%)
  local copies, waits for them, and re-layouts  98.2 us (9%)
  waiting for transfers between devices  83 us (8%)
  other arithmetic  35.5 us (3%)
  matrix products  27.1 us (2%)
  starting transfers between devices  26 us (2%)
    pallas_call x1, Pallas kernels, scatter(): pl.pallas_call(partial(scatter_kernel, slots), out_shape=tuple(out), in_s...  301 us
    pallas_call x1, Pallas kernels, gather_pages(): pl.pallas_call(partial(gather_kernel, slots), out_shape=tuple(whole), in_...  269 us
    ppermute x20, waiting for transfers between devices, swapped(): lax.ppermute(value, axis, [(source, source ^ bits) for source in range(co...  83 us
    pallas_call x2, Pallas kernels, feed(): pl.pallas_call(partial(feed_kernel, steps, width), grid=(steps,), in_spec...  55.2 us
    pallas_call x2, Pallas kernels, feed_back(): pl.pallas_call(partial(feed_back_kernel, steps, width), grid=(steps,), in...  54.1 us
    pallas_call x2, Pallas kernels, attend(): pl.pallas_call(attend_kernel, grid=(pairs,), in_specs=[flat] + [both] * 4...  34.1 us
    pallas_call x2, Pallas kernels, attend_back(): pl.pallas_call(attend_back_kernel, grid=(pairs,), in_specs=[flat, flat, f...  32.9 us
    unnamed x196, local copies, waits for them, and re-layouts  30 us
  transfers between devices with their start and end apart: 20, of which 6 were waited for; matrix products, arithmetic and copies ran while one was open for 11% of the time, Pallas kernels for 35%

profile of v2, /device:TPU:0, one launch (start us, length us, event | category | flops | bytes accessed | tf_op | source)
XLA Modules:
  0.0 1087.6 jit_solution(12199444818585056804)
XLA Ops:
  19.1 269.1 %gather_pages.1 = (bf16[16,72,4352]{2,1,0:T(8,128)(2,1)}, bf16[16,72,4352]{2,1,0:T(8,128)(2,1)}, bf16[16,272,1088]{2,1,0:T(8,128)(2,1)}, bf16[16,272,1088]{2,1,0...) custom-call(bf16[72,4352]{1,0:T(8,128)(2,1)} %get-tuple-element.233.refs_0_, ...), custom_call_target="tpu_custom_call" | custom-call | tf_op jit(solution)/shard_map/gather_pages/pallas_call | solution.py:646
  291.9 10.0 project_rows.2
  309.0 26.6 %collective-permute-done.3.away = bf16[2,256,1152]{2,1,0:T(8,128)(2,1)S(1)} collective-permute-done((bf16[2,256,1152]{2,1,0:T(8,128)(2,1)}, bf16[2,256,1152]{2,1,0:T(8,128)(2,1)S(1)}, u32[]{:S(2)}, u32[]{:S(2)}) %collective-permute-start.3) | collective-permute-done | bytes 1179680 | tf_op jit(solution)/shard_map/ppermute | solution.py:446
  339.7 16.8 %attend.2 = (f32[256,1152]{1,0:T(8,128)S(1)}, f32[9,2,256]{2,1,0:T(2,128)S(1)}) custom-call(bf16[256,1152]{1,0:T(8,128)(2,1)S(1)} %copy-done.12, bf16[2,256,1152]{2,1,0:T(8,128)(2,1)} %get-tuple-element.76.here, bf16[2,256,1152]{2,1,0:T(8,128)(2,1)S(1)} %collective-permute-done.2.beside, bf16[2,256,1152]{2,1,0:T(8,128)(2,1)S(1)} %collective-permute-done.3.away, ...), custom_call_target="tpu_custom_call" | custom-call | tf_op jit(solution)/shard_map/attend/pallas_call | solution.py:1021
  357.1 27.6 %feed.2 = (bf16[256,1152]{1,0:T(8,128)(2,1)S(1)}, f32[256,1088]{1,0:T(8,128)S(1)}, bf16[256,1152]{1,0:T(8,128)(2,1)S(1)}, bf16[256,4352]{1,0:T(8,128)(2,1)}, bf1...) custom-call(bf16[256,1088]{1,0:T(8,128)(2,1)S(1)} %copy-done.3, ...), custom_call_target="tpu_custom_call" | custom-call | tf_op jit(solution)/shard_map/feed/pallas_call | solution.py:1159
  385.9 10.7 project_rows.3
  399.2 26.5 %collective-permute-done.6.away = bf16[2,256,1152]{2,1,0:T(8,128)(2,1)S(1)} collective-permute-done((bf16[2,256,1152]{2,1,0:T(8,128)(2,1)}, bf16[2,256,1152]{2,1,0:T(8,128)(2,1)S(1)}, u32[]{:S(2)}, u32[]{:S(2)}) %collective-permute-start.6) | collective-permute-done | bytes 1179680 | tf_op jit(solution)/shard_map/ppermute | solution.py:446
  432.0 8.1 collective-permute-done.10
  451.2 17.2 %attend.3 = (f32[256,1152]{1,0:T(8,128)S(1)}, f32[9,2,256]{2,1,0:T(2,128)S(1)}) custom-call(bf16[256,1152]{1,0:T(8,128)(2,1)S(1)} %copy-done.16, bf16[2,256,1152]{2,1,0:T(8,128)(2,1)} %get-tuple-element.83.here, bf16[2,256,1152]{2,1,0:T(8,128)(2,1)S(1)} %collective-permute-done.5.beside, bf16[2,256,1152]{2,1,0:T(8,128)(2,1)S(1)} %collective-permute-done.6.away, ...), custom_call_target="tpu_custom_call" | custom-call | tf_op jit(solution)/shard_map/attend/pallas_call | solution.py:1021
  468.5 27.6 %feed.3 = (bf16[256,1152]{1,0:T(8,128)(2,1)S(1)}, f32[256,1088]{1,0:T(8,128)S(1)}, bf16[256,1152]{1,0:T(8,128)(2,1)S(1)}, bf16[256,4352]{1,0:T(8,128)(2,1)}, bf1...) custom-call(bf16[256,1088]{1,0:T(8,128)(2,1)S(1)} %get-tuple-element.80.x, ...), custom_call_target="tpu_custom_call" | custom-call | tf_op jit(solution)/shard_map/feed/pallas_call | solution.py:1159
  496.9 27.2 %feed_back.2 = (bf16[256,4352]{1,0:T(8,128)(2,1)}, f32[1,4352]{1,0:T(1,128)S(1)}, f32[256,1088]{1,0:T(8,128)S(1)}, bf16[256,1088]{1,0:T(8,128)(2,1)S(1)}, bf16[2...) custom-call(bf16[256,1088]{1,0:T(8,128)(2,1)S(1)} %copy-done.18, bf16[256,4352]{1,0:T(8,128)(2,1)} %get-tuple-element.88.slope, ...), custom_call_target="tpu_custom_call" | custom-call | tf_op jit(solution)/shard_map/feed_back/pallas_call | solution.py:1235
  524.2 16.5 %attend_back.2 = (bf16[256,1152]{1,0:T(8,128)(2,1)S(1)}, f32[2,256,1152]{2,1,0:T(8,128)}, bf16[2,256,1152]{2,1,0:T(8,128)(2,1)S(1)}, bf16[2,256,1152]{2,1,0:T(8,128)(2,1)S(1)}, bf16[2,256,1152]{2,1,0:T(8,128)(2,1)}) custom-call(bf16[256,1152]{1,0:T(8,128)(2,1)S(1)} %copy-done.17, bf16[256,1152]{1,0:T(8,128)(2,1)S(1)} %get-tuple-element.90.grad, ...), custom_call_target="tpu_custom_call" | custom-call | tf_op jit(solution)/shard_map/attend_back/pallas_call | solution.py:1104
  548.6 8.0 convolution_convert_fusion.1
  575.3 15.6 %collective-permute-done.13 = bf16[2,256,1152]{2,1,0:T(8,128)(2,1)} collective-permute-done((bf16[2,256,1152]{2,1,0:T(8,128)(2,1)}, bf16[2,256,1152]{2,1,0:T(8,128)(2,1)}, u32[]{:S(2)}, u32[]{:S(2)}) %collective-permute-start.13) | collective-permute-done | bytes 1179680 | tf_op jit(solution)/shard_map/ppermute | solution.py:446
  593.7 12.5 %project_back.2 = (bf16[256,4352]{1,0:T(8,128)(2,1)}, bf16[256,1088]{1,0:T(8,128)(2,1)S(1)}, f32[8,1088]{1,0:T(8,128)S(1)}) custom-call(bf16[256,1152]{1,0:T(8,128)(2,1)S(1)} %copy-done.37, bf16[2,256,1152]{2,1,0:T(8,128)(2,1)S(1)} %add_convert_fusion.2.pair, bf16[256,1088]{1,0:T(8,128)(2,1)S(1)} %copy-done.35, bf16[256,1088]{1,0:T(8,128)(2,1)S(1)} %get-tuple-element.80.x, ...), custom_call_target="tpu_custom_call" | custom-call | tf_op jit(solution)/shard_map/project_back/pallas_call | solution.py:1296
  606.3 26.9 %feed_back.3 = (bf16[256,4352]{1,0:T(8,128)(2,1)}, f32[1,4352]{1,0:T(1,128)S(1)}, f32[256,1088]{1,0:T(8,128)S(1)}, bf16[256,1088]{1,0:T(8,128)(2,1)S(1)}, bf16[2...) custom-call(bf16[256,1088]{1,0:T(8,128)(2,1)S(1)} %get-tuple-element.99.top, bf16[256,4352]{1,0:T(8,128)(2,1)} %get-tuple-element.100.slope, ...), custom_call_target="tpu_custom_call" | custom-call | tf_op jit(solution)/shard_map/feed_back/pallas_call | solution.py:1235
  634.2 16.3 %attend_back.3 = (bf16[256,1152]{1,0:T(8,128)(2,1)S(1)}, f32[2,256,1152]{2,1,0:T(8,128)}, bf16[2,256,1152]{2,1,0:T(8,128)(2,1)S(1)}, bf16[2,256,1152]{2,1,0:T(8,128)(2,1)S(1)}, bf16[2,256,1152]{2,1,0:T(8,128)(2,1)}) custom-call(bf16[256,1152]{1,0:T(8,128)(2,1)S(1)} %copy-done.13, bf16[256,1152]{1,0:T(8,128)(2,1)S(1)} %get-tuple-element.102.grad, ...), custom_call_target="tpu_custom_call" | custom-call | tf_op jit(solution)/shard_map/attend_back/pallas_call | solution.py:1104
  653.1 14.1 %copy.129 = bf16[4352,1088]{1,0:T(8,128)(2,1)} copy(bf16[4352,1088]{0,1:T(8,128)(2,1)} %convolution_convert_fusion.1) | data formatting | bytes 18939904 | tf_op jit(solution)/shard_map/convert_element_type | solution.py:1415
  670.1 7.9 convolution_convert_fusion.2
  684.2 14.1 %copy.128 = bf16[4352,1088]{1,0:T(8,128)(2,1)} copy(bf16[4352,1088]{0,1:T(8,128)(2,1)} %convolution_convert_fusion.2) | data formatting | bytes 18939904 | tf_op jit(solution)/shard_map/convert_element_type | solution.py:1415
  700.6 11.4 %attention_page.3.refs_4_ = bf16[16,72,4352]{2,1,0:T(8,128)(2,1)} custom-call(bf16[256,1152]{1,0:T(8,128)(2,1)S(1)} %copy-done.43, bf16[256,1152]{1,0:T(8,128)(2,1)S(1)} %copy-done.45, bf16[256,4352]{1,0:T(8,128)(2,1)S(1)} %copy-done.19, bf16[16,1,4352]{2,1,0:T(2,128)(2,1)S(1)} %pad.18.small), custom_call_target="tpu_custom_call" | custom-call | tf_op jit(solution)/shard_map/attention_page/pallas_call | solution.py:1348
  719.8 12.7 %project_back.3 = (bf16[256,4352]{1,0:T(8,128)(2,1)}, bf16[256,1088]{1,0:T(8,128)(2,1)S(1)}, f32[8,1088]{1,0:T(8,128)S(1)}) custom-call(bf16[256,1152]{1,0:T(8,128)(2,1)S(1)} %copy-done.33, bf16[2,256,1152]{2,1,0:T(8,128)(2,1)S(1)} %add_convert_fusion.pair, bf16[256,1088]{1,0:T(8,128)(2,1)S(1)} %get-tuple-element.109.branch, ...), custom_call_target="tpu_custom_call" | custom-call | tf_op jit(solution)/shard_map/project_back/pallas_call | solution.py:1296
  743.0 11.6 %attention_page.2.refs_0_ = bf16[16,72,4352]{2,1,0:T(8,128)(2,1)} custom-call(bf16[256,1152]{1,0:T(8,128)(2,1)S(1)} %copy-done.39, bf16[256,1152]{1,0:T(8,128)(2,1)S(1)} %copy-done.41, bf16[256,4352]{1,0:T(8,128)(2,1)S(1)} %copy-done.20, bf16[16,1,4352]{2,1,0:T(2,128)(2,1)S(1)} %copy-done.29), custom_call_target="tpu_custom_call" | custom-call | tf_op jit(solution)/shard_map/attention_page/pallas_call | solution.py:1348
  754.7 301.0 %scatter_gradients.1 = (f32[72,4352]{1,0:T(8,128)S(1)}, f32[272,1088]{1,0:T(8,128)S(1)}, f32[72,4352]{1,0:T(8,128)S(1)}, bf16[16,72,4352]{2,1,0:T(8,128)(2,1)}, ...) custom-call(bf16[16,72,4352]{2,1,0:T(8,128)(2,1)} %attention_page.2., ...), custom_call_target="tpu_custom_call" | custom-call | tf_op jit(solution)/shard_map/scatter_gradients/pallas_call | solution.py:864
  (344 shorter events, 148.9 us)
Async XLA Ops:
  2.9 12.5 %collective-permute-start = (bf16[128,1088]{1,0:T(8,128)(2,1)}, bf16[128,1088]{1,0:T(8,128)(2,1)}, u32[]{:S(2)}, u32[]{:S(2)}) collective-permute-start(bf16[128,1088]{1,0:T(8,128)(2,1)} %bitcast.1), channel_id=1, source_target_pairs={{0,3},{1,2},{2,1},{3,0},{4,7},{5,6},{6,5},{7,4},{8,11},{9,10},{10,... | collective-permute-start | bytes 835592 | tf_op jit(solution)/shard_map/ppermute | solution.py:446
  9.2 7.3 collective-permute-start.1
  10.9 281.0 %copy-start = (bf16[1088,1152]{1,0:T(8,128)(2,1)}, bf16[1088,1152]{1,0:T(8,128)(2,1)S(1)}, u32[]{:S(2)}) copy-start(bf16[1088,1152]{1,0:T(8,128)(2,1)S(1)} %fusion.1.table) | copy-start | bytes 7520260
  16.4 275.5 %copy-start.2 = (bf16[256,1088]{1,0:T(8,128)(2,1)}, bf16[256,1088]{1,0:T(8,128)(2,1)S(1)}, u32[]{:S(2)}) copy-start(bf16[256,1088]{1,0:T(8,128)(2,1)S(1)} %pad_maximum_fusion.5.x) | copy-start | bytes 1671172
  303.6 32.0 %collective-permute-start.3 = (bf16[2,256,1152]{2,1,0:T(8,128)(2,1)}, bf16[2,256,1152]{2,1,0:T(8,128)(2,1)S(1)}, u32[]{:S(2)}, u32[]{:S(2)}) collective-permute-start(bf16[2,256,1152]{2,1,0:T(8,128)(2,1)} %get-tuple-element.76.here), channel_id=1, source_target_pairs={{0,1},{1,0},{2,3},{3,2},{4,5},{5,4},{6,7},{7,6},{8,9},{9,8},{10,11... | collective-permute-start | bytes 3538952 | tf_op jit(solution)/shard_map/ppermute | solution.py:446
  308.8 27.7 %collective-permute-start.2 = (bf16[2,256,1152]{2,1,0:T(8,128)(2,1)}, bf16[2,256,1152]{2,1,0:T(8,128)(2,1)S(1)}, u32[]{:S(2)}, u32[]{:S(2)}) collective-permute-start(bf16[2,256,1152]{2,1,0:T(8,128)(2,1)} %get-tuple-element.76.here), channel_id=1, source_target_pairs={{0,16},{16,0},{1,17},{17,1},{2,18},{18,2},{3,19},{19,3},{4,20},{20... | collective-permute-start | bytes 3538952 | tf_op jit(solution)/shard_map/ppermute | solution.py:446
  335.6 3.0 collective-permute-start.4
  385.9 39.8 %copy-start.80 = (bf16[2,256,1088]{1,2,0:T(8,128)(2,1)S(1)}, bf16[2,256,1088]{1,2,0:T(8,128)(2,1)}, u32[]{:S(2)}) copy-start(bf16[2,256,1088]{1,2,0:T(8,128)(2,1)} %param.16) | copy-start | bytes 3342340
  397.5 32.6 %copy-start.42 = (bf16[256,1152]{1,0:T(8,128)(2,1)}, bf16[256,1152]{1,0:T(8,128)(2,1)S(1)}, u32[]{:S(2)}) copy-start(bf16[256,1152]{1,0:T(8,128)(2,1)S(1)} %get-tuple-element.122.normed) | copy-start | bytes 1769476
  397.5 28.2 %collective-permute-start.6 = (bf16[2,256,1152]{2,1,0:T(8,128)(2,1)}, bf16[2,256,1152]{2,1,0:T(8,128)(2,1)S(1)}, u32[]{:S(2)}, u32[]{:S(2)}) collective-permute-start(bf16[2,256,1152]{2,1,0:T(8,128)(2,1)} %get-tuple-element.83.here), channel_id=1, source_target_pairs={{0,1},{1,0},{2,3},{3,2},{4,5},{5,4},{6,7},{7,6},{8,9},{9,8},{10,11... | collective-permute-start | bytes 3538952 | tf_op jit(solution)/shard_map/ppermute | solution.py:446
  399.2 52.0 %collective-permute-start.5 = (bf16[2,256,1152]{2,1,0:T(8,128)(2,1)}, bf16[2,256,1152]{2,1,0:T(8,128)(2,1)S(1)}, u32[]{:S(2)}, u32[]{:S(2)}) collective-permute-start(bf16[2,256,1152]{2,1,0:T(8,128)(2,1)} %get-tuple-element.83.here), channel_id=1, source_target_pairs={{0,16},{16,0},{1,17},{17,1},{2,18},{18,2},{3,19},{19,3},{4,20},{20... | collective-permute-start | bytes 3538952 | tf_op jit(solution)/shard_map/ppermute | solution.py:446
  425.7 25.5 %collective-permute-start.7 = (bf16[2,256,1152]{2,1,0:T(8,128)(2,1)S(1)}, bf16[2,256,1152]{2,1,0:T(8,128)(2,1)}, u32[]{:S(2)}, u32[]{:S(2)}) collective-permute-start(bf16[2,256,1152]{2,1,0:T(8,128)(2,1)S(1)} %collective-permute-done.6.away), channel_id=1, source_target_pairs={{0,16},{16,0},{1,17},{17,1},{2,18},{18,2},{3,19},{19,3},{4,20},{20... | collective-permute-start | bytes 3538952 | tf_op jit(solution)/shard_map/ppermute | solution.py:446
  428.5 11.6 %collective-permute-start.10 = (bf16[128,1088]{1,0:T(8,128)(2,1)}, bf16[128,1088]{1,0:T(8,128)(2,1)}, u32[]{:S(2)}, u32[]{:S(2)}) collective-permute-start(bf16[128,1088]{1,0:T(8,128)(2,1)} %bitcast.124), channel_id=1, source_target_pairs={{0,3},{1,2},{2,1},{3,0},{4,7},{5,6},{6,5},{7,4},{8,11},{9,10},{10,... | collective-permute-start | bytes 835592 | tf_op jit(solution)/shard_map/ppermute | solution.py:446
  543.6 13.0 %collective-permute-start.12 = (bf16[2,256,1152]{2,1,0:T(8,128)(2,1)}, bf16[2,256,1152]{2,1,0:T(8,128)(2,1)}, u32[]{:S(2)}, u32[]{:S(2)}) collective-permute-start(bf16[2,256,1152]{2,1,0:T(8,128)(2,1)} %get-tuple-element.96), channel_id=1, source_target_pairs={{0,16},{16,0},{1,17},{17,1},{2,18},{18,2},{3,19},{19,3},{4,20},{20... | collective-permute-start | bytes 3538952 | tf_op jit(solution)/shard_map/ppermute | solution.py:446
  546.7 23.8 %collective-permute-start.8 = (bf16[2,128,1088]{1,2,0:T(8,128)(2,1)}, bf16[2,128,1088]{1,2,0:T(8,128)(2,1)}, u32[]{:S(2)}, u32[]{:S(2)}) collective-permute-start(bf16[2,128,1088]{1,2,0:T(8,128)(2,1)} %copy.102), channel_id=1, source_target_pairs={{0,3},{1,2},{2,1},{3,0},{4,7},{5,6},{6,5},{7,4},{8,11},{9,10},{10,... | collective-permute-start | bytes 1671176 | tf_op jit(solution)/shard_map/ppermute | solution.py:446
  548.3 26.9 %collective-permute-start.11 = (bf16[2,256,1152]{2,1,0:T(8,128)(2,1)}, bf16[2,256,1152]{2,1,0:T(8,128)(2,1)}, u32[]{:S(2)}, u32[]{:S(2)}) collective-permute-start(bf16[2,256,1152]{2,1,0:T(8,128)(2,1)} %copy-done.60), channel_id=1, source_target_pairs={{0,16},{16,0},{1,17},{17,1},{2,18},{18,2},{3,19},{19,3},{4,20},{20... | collective-permute-start | bytes 3538952 | tf_op jit(solution)/shard_map/ppermute | solution.py:446
  559.3 31.5 %collective-permute-start.13 = (bf16[2,256,1152]{2,1,0:T(8,128)(2,1)}, bf16[2,256,1152]{2,1,0:T(8,128)(2,1)}, u32[]{:S(2)}, u32[]{:S(2)}) collective-permute-start(bf16[2,256,1152]{2,1,0:T(8,128)(2,1)} %add_convert_fusion.3), channel_id=1, source_target_pairs={{0,1},{1,0},{2,3},{3,2},{4,5},{5,4},{6,7},{7,6},{8,9},{9,8},{10,11... | collective-permute-start | bytes 3538952 | tf_op jit(solution)/shard_map/ppermute | solution.py:446
  575.2 92.0 %collective-permute-start.9 = (bf16[2,128,1088]{1,2,0:T(8,128)(2,1)}, bf16[2,128,1088]{1,2,0:T(8,128)(2,1)}, u32[]{:S(2)}, u32[]{:S(2)}) collective-permute-start(bf16[2,128,1088]{1,2,0:T(8,128)(2,1)} %copy.106), channel_id=1, source_target_pairs={{0,16},{16,0},{1,17},{17,1},{2,18},{18,2},{3,19},{19,3},{4,20},{20... | collective-permute-start | bytes 1671176 | tf_op jit(solution)/shard_map/ppermute | solution.py:446
  652.5 25.5 %collective-permute-start.15 = (bf16[2,256,1152]{2,1,0:T(8,128)(2,1)}, bf16[2,256,1152]{2,1,0:T(8,128)(2,1)}, u32[]{:S(2)}, u32[]{:S(2)}) collective-permute-start(bf16[2,256,1152]{2,1,0:T(8,128)(2,1)} %get-tuple-element.108), channel_id=1, source_target_pairs={{0,16},{16,0},{1,17},{17,1},{2,18},{18,2},{3,19},{19,3},{4,20},{20... | collective-permute-start | bytes 3538952 | tf_op jit(solution)/shard_map/ppermute | solution.py:446
  669.5 48.0 %collective-permute-start.14 = (bf16[2,256,1152]{2,1,0:T(8,128)(2,1)}, bf16[2,256,1152]{2,1,0:T(8,128)(2,1)}, u32[]{:S(2)}, u32[]{:S(2)}) collective-permute-start(bf16[2,256,1152]{2,1,0:T(8,128)(2,1)} %copy-done.59), channel_id=1, source_target_pairs={{0,16},{16,0},{1,17},{17,1},{2,18},{18,2},{3,19},{19,3},{4,20},{20... | collective-permute-start | bytes 3538952 | tf_op jit(solution)/shard_map/ppermute | solution.py:446
  680.6 37.0 %collective-permute-start.16 = (bf16[2,256,1152]{2,1,0:T(8,128)(2,1)}, bf16[2,256,1152]{2,1,0:T(8,128)(2,1)}, u32[]{:S(2)}, u32[]{:S(2)}) collective-permute-start(bf16[2,256,1152]{2,1,0:T(8,128)(2,1)} %add_convert_fusion.1), channel_id=1, source_target_pairs={{0,1},{1,0},{2,3},{3,2},{4,5},{5,4},{6,7},{7,6},{8,9},{9,8},{10,11... | collective-permute-start | bytes 3538952 | tf_op jit(solution)/shard_map/ppermute | solution.py:446
  737.3 320.3 %collective-permute-start.17 = (bf16[2,128,1088]{1,2,0:T(8,128)(2,1)}, bf16[2,128,1088]{1,2,0:T(8,128)(2,1)}, u32[]{:S(2)}, u32[]{:S(2)}) collective-permute-start(bf16[2,128,1088]{1,2,0:T(8,128)(2,1)} %copy.111), channel_id=1, source_target_pairs={{0,3},{1,2},{2,1},{3,0},{4,7},{5,6},{6,5},{7,4},{8,11},{9,10},{10,... | collective-permute-start | bytes 1671176 | tf_op jit(solution)/shard_map/ppermute | solution.py:446
  1057.2 20.6 %collective-permute-start.19 = (f32[72,4352]{1,0:T(8,128)}, f32[72,4352]{1,0:T(8,128)}, u32[]{:S(2)}, u32[]{:S(2)}) collective-permute-start(f32[72,4352]{1,0:T(8,128)} %broadcast_select_fusion.1), channel_id=1, source_target_pairs={{0,16},{16,0},{1,17},{17,1},{2,18},{18,2},{3,19},{19,3},{4,20},{20... | collective-permute-start | bytes 3760136 | tf_op jit(solution)/shard_map/ppermute | solution.py:446
  1065.4 5.2 collective-permute-start.18
  (91 other events, 856.9 us)

commit v3 on v2

--- a/solution.py
+++ b/solution.py
@@ -531,134 +531,6 @@
 GATHER_NUMBER = {kind: index for index, kind in enumerate(GATHER_KINDS)}
 
 
-def gather_kernel(slots, *refs):
-    shards, refs = refs[:slots], refs[slots:]
-    outs, refs = [refs[2 * t : 2 * t + 2] for t in range(slots)], refs[2 * slots :]
-    send_sem, recv_sem, copy_sem = refs
-    core, rings, lines, toward = places()
-    greet(toward)
-    sent, copied = [], []
-
-    def copy_of(t, source, target, to, kind):
-        index = t * len(GATHER_KINDS) + GATHER_NUMBER[kind]
-        return remote_copy(source, target, send_sem.at[index], recv_sem.at[index], toward[to])
-
-    def place(t, page, dd, k):
-        return outs[t][page].at[rings[dd] * 4 + lines[k]]
-
-    def send(t, dd, k, to, kind, own=False):
-        def act(page):
-            target = place(t, page, dd, k)
-            copy_of(t, shards[t] if own else target, target, to, kind).start()
-
-        per_core(core, act)
-        sent.append(copy_of(t, place(t, 0, dd, k), place(t, 0, dd, k), to, kind))
-
-    def arrive(t, dd, k, to, kind):
-        def act(page):
-            target = place(t, page, dd, k)
-            copy_of(t, target, target, to, kind).wait_recv()
-
-        per_core(core, act)
-
-    def group(t, page, dd):
-        return outs[t][page].at[pl.ds(rings[dd] * 4, 4)]
-
-    def sibling(t, dd):
-        def act(page):
-            copy_of(t, group(t, page, dd), group(t, page, dd), SIBLING, (SIBLING, dd)).start()
-
-        per_core(core, act)
-        sent.append(copy_of(t, group(t, 0, dd), group(t, 0, dd), SIBLING, (SIBLING, dd)))
-
-    def begin_line(t):
-        for k in (1, 2, 3):
-            send(t, 0, 0, (LEVEL, k), (LEVEL, k), own=True)
-
-    def begin_ring(t):
-        send(t, 0, 0, EAST, (EAST, 0), own=True)
-        send(t, 0, 0, NORTH, (NORTH, 0), own=True)
-
-        def act(page):
-            pltpu.make_async_copy(shards[t], place(t, page, 0, 0), copy_sem.at[t]).start()
-
-        per_core(core, act)
-
-    def own_ready(t):
-        def act(page):
-            pltpu.make_async_copy(shards[t], place(t, page, 0, 0), copy_sem.at[t]).wait()
-
-        per_core(core, act)
-
-    def from_line(t, k):
-        arrive(t, 0, k, (LEVEL, k), (LEVEL, k))
-        send(t, 0, k, EAST, (EAST, k))
-        send(t, 0, k, NORTH, (NORTH, k))
-
-    def from_ring(t, k):
-        arrive(t, 1, k, EAST, (EAST, k))
-        if k < 2:
-            send(t, 1, k, NORTH, (CORNER, k))
-        arrive(t, 2, k, NORTH, (NORTH, k))
-        if k >= 2:
-            send(t, 2, k, EAST, (CORNER, k))
-
-    begin_line(0)
-    begin_ring(0)
-    for t in range(slots):
-        from_ring(t, 0)
-        from_line(t, 1)
-        from_line(t, 2)
-        from_line(t, 3)
-        own_ready(t)
-        sibling(t, 0)
-        if t + 1 < slots:
-            begin_line(t + 1)
-        from_ring(t, 1)
-        if t + 1 < slots:
-            begin_ring(t + 1)
-        from_ring(t, 2)
-        from_ring(t, 3)
-        sibling(t, 1)
-        sibling(t, 2)
-        for k in range(4):
-            arrive(t, 3, k, NORTH if k < 2 else EAST, (CORNER, k))
-        sibling(t, 3)
-    for t in range(slots):
-        for dd in range(4):
-
-            def act(page):
-                target = group(t, 1 - page, dd)
-                copy_of(t, target, target, SIBLING, (SIBLING, dd)).wait_recv()
-
-            per_core(core, act)
-    for copy in sent:
-        copy.wait_send()
-
-
-def gather_pages(shards):
-    slots = len(shards)
-    count = slots * len(GATHER_KINDS)
-    whole = [
-        jax.ShapeDtypeStruct((16,) + shard.shape, shard.dtype) for shard in shards for _ in (0, 1)
-    ]
-    anywhere = pl.BlockSpec(memory_space=pl.ANY)
-    out = pl.pallas_call(
-        partial(gather_kernel, slots),
-        out_shape=tuple(whole),
-        in_specs=[anywhere] * slots,
-        out_specs=tuple(anywhere for _ in whole),
-        scratch_shapes=[
-            pltpu.SemaphoreType.DMA((count,)),
-            pltpu.SemaphoreType.DMA((count,)),
-            pltpu.SemaphoreType.DMA((slots,)),
-        ],
-        compiler_params=pltpu.CompilerParams(collective_id=0, has_side_effects=True),
-        name="gather_pages",
-    )(*shards)
-    return [out[2 * t : 2 * t + 2] for t in range(slots)]
-
-
 KINDS = (
     [(CORNER, dd) for dd in range(4)]
     + [(ONCE, k) for k in range(4)]
@@ -911,51 +783,6 @@
     return pl.BlockSpec(shape, lambda *_: zeros)
 
 
-def project_kernel(steps, width, x, gain, shift, query_bias, value_bias, table, page,
-                   normed_out, query_out, pair_out, mixture):
-    step = pl.program_id(0)
-    tile = page.shape[1]
-
-    @pl.when(step == 0)
-    def _():
-        unit, _ = normal_parts(x[...].astype(F32))
-        normed = (unit * gain[...] + shift[...]).astype(LOW)
-        normed_out[...] = mm(normed, table[...]).astype(LOW)
-
-    mixture[:, pl.ds(pl.multiple_of(step * tile, tile), tile)] = mm(normed_out[...], page[...])
-
-    @pl.when(step == steps - 1)
-    def _():
-        blank = jnp.zeros((x.shape[0], WIDE - width), LOW)
-        query = ((mixture[:, :width] + query_bias[...]).astype(LOW).astype(F32) * HDIM ** (-0.5)).astype(LOW)
-        query_out[:, :width] = query
-        query_out[:, width:] = blank
-        pair_out[0, :, :width] = mixture[:, width : 2 * width].astype(LOW)
-        pair_out[0, :, width:] = blank
-        pair_out[1, :, :width] = (mixture[:, 2 * width : 3 * width] + value_bias[...]).astype(LOW)
-        pair_out[1, :, width:] = blank
-
-
-def project_rows(x, gain, shift, query_bias, value_bias, table, page):
-    rows, width = x.shape
-    tile, steps = 640, 6
-    return pl.pallas_call(
-        partial(project_kernel, steps, width),
-        grid=(steps,),
-        in_specs=[whole(x.shape)] + [whole((1, width))] * 4 + [whole(table.shape)]
-        + [pl.BlockSpec((page.shape[0], tile), lambda i: (0, i))],
-        out_specs=(whole((rows, WIDE)), whole((rows, WIDE)), whole((2, rows, WIDE))),
-        out_shape=(
-            jax.ShapeDtypeStruct((rows, WIDE), LOW),
-            jax.ShapeDtypeStruct((rows, WIDE), LOW),
-            jax.ShapeDtypeStruct((2, rows, WIDE), LOW),
-        ),
-        scratch_shapes=[pltpu.VMEM((rows, tile * steps), F32)],
-        compiler_params=pltpu.CompilerParams(vmem_limit_bytes=48 << 20),
-        name="project_rows",
-    )(x, gain, shift, query_bias, value_bias, table, page)
-
-
 def head_pair(rows):
     lane = lax.broadcasted_iota(jnp.int32, rows.shape, 1)
     zero = jnp.zeros_like(rows)
@@ -968,68 +795,6 @@
     n = turned.shape[1] // 2
     own = jnp.concatenate([turned[:HDIM, :n], turned[HDIM:, n:]], axis=0)
     return own.T
-
-
-def attend_kernel(x, here, beside, away, corner, first_ref, attended_out, log_out):
-    first = first_ref[0] == 0
-    half = x.shape[0] // 2
-    low, high = head_pair(x[:half]), head_pair(x[half:])
-    last_rows = jnp.where(first, high, low)
-
-    def block(kind, near, part):
-        at = pl.ds(part * half, half)
-        one, two = (here, beside) if near == 0 else (away, corner)
-        return jnp.concatenate([one[kind, at], two[kind, at]], axis=0)
-
-    def last_block(kind):
-        return jnp.where(first, block(kind, 1, 1), block(kind, 1, 0))
-
-    units = [
-        (low, (0, 0)), (high, (0, 0)), (high, (0, 1)), (high, (1, 0)), (last_rows, None),
-    ]
-    parts = []
-    for rows, which in units:
-        keys = last_block(0) if which is None else block(0, *which)
-        values = last_block(1) if which is None else block(1, *which)
-        scores = mm_nt(keys, rows)
-        level = jnp.max(scores, axis=0, keepdims=True)
-        exponent = jnp.exp(scores - level)
-        parts.append(
-            (level, jnp.sum(exponent, axis=0, keepdims=True), mm_tn(values, exponent.astype(LOW)))
-        )
-    last = parts[4]
-    low_last = (jnp.where(first, far_below, last[0]),) + last[1:]
-    high_last = (jnp.where(first, last[0], far_below),) + last[1:]
-    for place, group in enumerate(([parts[0], low_last], parts[1:4] + [high_last])):
-        peak = group[0][0]
-        for level, _, _ in group[1:]:
-            peak = jnp.maximum(peak, level)
-        total, mixed = 0.0, 0.0
-        for level, sums, out in group:
-            share = jnp.exp(level - peak)
-            total = total + share * sums
-            mixed = mixed + share * out
-        attended_out[place * half : (place + 1) * half] = from_pair(mixed / total)
-        log_out[0, place : place + 1] = peak + jnp.log(total)
-
-
-def attend(query, here, beside, away, corner, low_chunk):
-    rows = query.shape[0]
-    pairs = WIDE // 128
-    flat = pl.BlockSpec((rows, 128), lambda p: (0, p))
-    both = pl.BlockSpec((2, rows, 128), lambda p: (0, 0, p))
-    return pl.pallas_call(
-        attend_kernel,
-        grid=(pairs,),
-        in_specs=[flat] + [both] * 4 + [pl.BlockSpec(memory_space=pltpu.SMEM)],
-        out_specs=(flat, pl.BlockSpec((1, 2, rows), lambda p: (p, 0, 0))),
-        out_shape=(
-            jax.ShapeDtypeStruct((rows, WIDE), F32),
-            jax.ShapeDtypeStruct((pairs, 2, rows), F32),
-        ),
-        compiler_params=pltpu.CompilerParams(vmem_limit_bytes=48 << 20),
-        name="attend",
-    )(query, here, beside, away, corner, low_chunk.reshape(1))
 
 
 def attend_back_kernel(query, grad, attended, logs, here, beside, away, corner, first_ref,
@@ -1112,73 +877,6 @@
         compiler_params=pltpu.CompilerParams(vmem_limit_bytes=48 << 20),
         name="attend_back",
     )(query, grad, attended, logs, here, beside, away, corner, low_chunk.reshape(1))
-
-
-def feed_kernel(steps, width, x, attended, gain, shift, output_bias, reduce_bias, table, page, expand,
-                expand_bias, reduce, attended_out, middle_out, second_out, active_out, slope_out,
-                result_out, result_low_out, output, sem):
-    step = pl.program_id(0)
-    lead = 4 * width - WIDE
-    extra = 3 * width - lead
-
-    @pl.when(step == 0)
-    def _():
-        copy = pltpu.make_async_copy(page.at[:, pl.ds(lead, WIDE)], output, sem)
-        copy.start()
-        attended_out[...] = mm(attended[:, :width].astype(LOW), table[...]).astype(LOW)
-        copy.wait()
-        blended = mm(attended_out[...], output[...])
-        middle = x[...].astype(F32) + (blended[:, extra:] + output_bias[...])
-        middle_out[...] = middle
-        unit, _ = normal_parts(middle)
-        second = (unit * gain[...] + shift[...]).astype(LOW)
-        second_out[...] = mm(second, table[...]).astype(LOW)
-        result_out[...] = middle + reduce_bias[...]
-
-    hidden = mm(second_out[...], expand[...]) + expand_bias[...]
-    below = 0.5 + 0.5 * lax.erf(hidden * 0.7071067811865476)
-    active = (hidden * below).astype(LOW)
-    active_out[...] = active
-    slope = below + hidden * (0.3989422804014327 * jnp.exp(-0.5 * hidden * hidden))
-    slope_out[...] = slope.astype(LOW)
-    result_out[...] += mm(active, reduce[...])
-
-    @pl.when(step == steps - 1)
-    def _():
-        result_low_out[...] = result_out[...].astype(LOW)
-
-
-def feed(x, attended, gain, shift, output_bias, reduce_bias, table, page, expand, expand_bias, reduce):
-    rows, width = x.shape
-    inner = expand.shape[1]
-    tile = 256
-    steps = inner // tile
-    flat = whole((rows, width))
-    wide = whole((rows, WIDE))
-    column = pl.BlockSpec((rows, tile), lambda i: (0, i))
-    outs = pl.pallas_call(
-        partial(feed_kernel, steps, width),
-        grid=(steps,),
-        in_specs=[flat, wide] + [whole((1, width))] * 4
-        + [whole(table.shape), pl.BlockSpec(memory_space=pl.ANY)]
-        + [pl.BlockSpec((WIDE, tile), lambda i: (0, i)), pl.BlockSpec((1, tile), lambda i: (0, i)),
-           pl.BlockSpec((tile, width), lambda i: (i, 0))],
-        out_specs=(wide, flat, wide, column, column, flat, flat),
-        out_shape=(
-            jax.ShapeDtypeStruct((rows, WIDE), LOW),
-            jax.ShapeDtypeStruct((rows, width), F32),
-            jax.ShapeDtypeStruct((rows, WIDE), LOW),
-            jax.ShapeDtypeStruct((rows, inner), LOW),
-            jax.ShapeDtypeStruct((rows, inner), LOW),
-            jax.ShapeDtypeStruct((rows, width), F32),
-            jax.ShapeDtypeStruct((rows, width), LOW),
-        ),
-        scratch_shapes=[pltpu.VMEM((WIDE, WIDE), LOW), pltpu.SemaphoreType.DMA(())],
-        compiler_params=pltpu.CompilerParams(vmem_limit_bytes=48 << 20),
-        name="feed",
-    )(x, attended, gain, shift, output_bias, reduce_bias, table, page, expand, expand_bias, reduce)
-    attended_low, middle, second_low, active, slope, _, result = outs
-    return attended_low, middle, second_low, active, slope, result
 
 
 def feed_back_kernel(steps, width, top, slope, middle, gain, table, page, expand, reduce,
@@ -1358,6 +1056,406 @@
     )(normed, attended, mixture, small)
 
 
+LEAD_ROWS = 144
+
+
+def gather_tasks(shards, outs, halved, send_sem, recv_sem, copy_sem, place_of):
+    core, rings, lines, toward = place_of
+    slots = len(shards)
+    sent = []
+
+    def rows_of(t, page):
+        if not halved[t]:
+            return None
+        total = shards[t].shape[0]
+        return pl.ds(0, LEAD_ROWS) if page == 0 else pl.ds(LEAD_ROWS, total - LEAD_ROWS)
+
+    def out_of(t, page):
+        return outs[t][0] if halved[t] else outs[t][page]
+
+    def place(t, page, dd, k):
+        index, rows = rings[dd] * 4 + lines[k], rows_of(t, page)
+        return out_of(t, page).at[index] if rows is None else out_of(t, page).at[index, rows]
+
+    def own(t, page):
+        rows = rows_of(t, page)
+        return shards[t] if rows is None else shards[t].at[rows]
+
+    def group(t, page, dd):
+        at, rows = pl.ds(rings[dd] * 4, 4), rows_of(t, page)
+        return out_of(t, page).at[at] if rows is None else out_of(t, page).at[at, rows]
+
+    def copy_of(t, source, target, to, kind):
+        index = t * len(GATHER_KINDS) + GATHER_NUMBER[kind]
+        return remote_copy(source, target, send_sem.at[index], recv_sem.at[index], toward[to])
+
+    def send(t, dd, k, to, kind, mine=False):
+        def act(page):
+            target = place(t, page, dd, k)
+            copy_of(t, own(t, page) if mine else target, target, to, kind).start()
+
+        per_core(core, act)
+        sent.append((t, lambda page: copy_of(t, place(t, page, dd, k), place(t, page, dd, k), to, kind)))
+
+    def arrive(t, dd, k, to, kind):
+        def act(page):
+            target = place(t, page, dd, k)
+            copy_of(t, target, target, to, kind).wait_recv()
+
+        per_core(core, act)
+
+    def sibling(t, dd):
+        def copy(page):
+            return copy_of(t, group(t, page, dd), group(t, page, dd), SIBLING, (SIBLING, dd))
+
+        per_core(core, lambda page: copy(page).start())
+        sent.append((t, copy))
+
+    def begin_line(t):
+        for k in (1, 2, 3):
+            send(t, 0, 0, (LEVEL, k), (LEVEL, k), mine=True)
+
+    def local(t, page):
+        return pltpu.make_async_copy(own(t, page), place(t, page, 0, 0), copy_sem.at[t])
+
+    def begin_ring(t):
+        send(t, 0, 0, EAST, (EAST, 0), mine=True)
+        send(t, 0, 0, NORTH, (NORTH, 0), mine=True)
+        per_core(core, lambda page: local(t, page).start())
+
+    def own_ready(t):
+        per_core(core, lambda page: local(t, page).wait())
+
+    def from_line(t, k):
+        arrive(t, 0, k, (LEVEL, k), (LEVEL, k))
+        send(t, 0, k, EAST, (EAST, k))
+        send(t, 0, k, NORTH, (NORTH, k))
+
+    def from_east(t, k):
+        arrive(t, 1, k, EAST, (EAST, k))
+        if k < 2:
+            send(t, 1, k, NORTH, (CORNER, k))
+
+    def from_north(t, k):
+        arrive(t, 2, k, NORTH, (NORTH, k))
+        if k >= 2:
+            send(t, 2, k, EAST, (CORNER, k))
+
+    def from_corner(t, k):
+        arrive(t, 3, k, NORTH if k < 2 else EAST, (CORNER, k))
+
+    def last(t, dd):
+        def act(page):
+            target = group(t, 1 - page, dd)
+            copy_of(t, target, target, SIBLING, (SIBLING, dd)).wait_recv()
+
+        per_core(core, act)
+
+    tasks = []
+
+    def then(function, *given):
+        tasks.append(lambda: function(*given))
+
+    then(begin_line, 0)
+    then(begin_ring, 0)
+    for t in range(slots):
+        then(from_east, t, 0)
+        then(from_north, t, 0)
+        then(from_line, t, 1)
+        then(from_line, t, 2)
+        then(from_line, t, 3)
+        then(own_ready, t)
+        then(sibling, t, 0)
+        if t + 1 < slots:
+            then(begin_line, t + 1)
+        then(from_east, t, 1)
+        then(from_north, t, 1)
+        if t + 1 < slots:
+            then(begin_ring, t + 1)
+        for k in (2, 3):
+            then(from_east, t, k)
+            then(from_north, t, k)
+        then(sibling, t, 1)
+        then(sibling, t, 2)
+        for k in range(4):
+            then(from_corner, t, k)
+        then(sibling, t, 3)
+    for t in range(slots):
+        for dd in range(4):
+            then(last, t, dd)
+
+    def drain():
+        for _, copy in sent:
+            per_core(core, lambda page: copy(page).wait_send())
+
+    tasks.append(drain)
+    return tasks
+
+
+HALVED = (False, True)
+
+
+def gather_kernel(*refs):
+    shards, refs = refs[:2], refs[2:]
+    outs, refs = [refs[0:2], refs[2:3]], refs[3:]
+    place_of = places()
+    greet(place_of[3])
+    for task in gather_tasks(shards, outs, HALVED, *refs, place_of):
+        task()
+
+
+def gather_shapes(shards):
+    pages, reduce = ((16,) + shard.shape for shard in shards)
+    return [jax.ShapeDtypeStruct(shape, LOW) for shape in (pages, pages, reduce)]
+
+
+def gather_semaphores():
+    count = 2 * len(GATHER_KINDS)
+    return [pltpu.SemaphoreType.DMA((count,)), pltpu.SemaphoreType.DMA((count,)), pltpu.SemaphoreType.DMA((2,))]
+
+
+def gather_pages(shards):
+    anywhere = pl.BlockSpec(memory_space=pl.ANY)
+    return pl.pallas_call(
+        gather_kernel,
+        out_shape=tuple(gather_shapes(shards)),
+        in_specs=[anywhere] * 2,
+        out_specs=(anywhere,) * 3,
+        scratch_shapes=gather_semaphores(),
+        compiler_params=pltpu.CompilerParams(collective_id=0, has_side_effects=True),
+        name="gather_pages",
+    )(*shards)
+
+
+def low_place(line):
+    return jnp.where(line < 2, line, 3 - line)
+
+
+def forward_kernel(extra, *refs):
+    x, vectors, wide, table, page_hbm, expand_hbm, reduce_hbm = refs[:7]
+    refs = refs[7:]
+    if extra:
+        shards, refs = refs[:2], refs[2:]
+    (normed_out, query_out, here, beside, away, corner, attended_out, log_out, attended_low, middle_out,
+     second_out, active_out, slope_out, result_out) = refs[:14]
+    refs = refs[14:]
+    if extra:
+        outs, refs = [refs[0:2], refs[2:3]], refs[3:]
+    page, expand, reduce, mixture, result, mixed, stats, page_sem, expand_sem, reduce_sem, pair_send, pair_recv = refs[:12]
+    place_of = places()
+    core, rings, lines, toward = place_of
+    rows, width = x.shape
+    half = rows // 2
+    first = low_place(lines[0]) == 0
+
+    def page_copy(i):
+        at = pl.ds(pl.multiple_of(i * 256, 256), 256)
+        return pltpu.make_async_copy(page_hbm.at[:, at], page.at[:, at], page_sem.at[i])
+
+    def expand_copy(i):
+        at = pl.ds(pl.multiple_of(i * 256, 256), 256)
+        return pltpu.make_async_copy(expand_hbm.at[:, at], expand.at[:, at], expand_sem.at[i])
+
+    def reduce_copy(i):
+        at = pl.ds(pl.multiple_of(i * 256, 256), 256)
+        return pltpu.make_async_copy(reduce_hbm.at[at], reduce.at[at], reduce_sem.at[i])
+
+    tiles = page.shape[1] // 256
+
+    def begin(make):
+        def step(i, _):
+            make(i).start()
+            return 0
+
+        lax.fori_loop(0, tiles, step, 0)
+
+    begin(page_copy)
+    begin(expand_copy)
+    begin(reduce_copy)
+    greet(toward)
+    todo = list(gather_tasks(shards, outs, HALVED, *refs[12:15], place_of)) if extra else []
+
+    def progress(count):
+        for _ in range(count):
+            if todo:
+                todo.pop(0)()
+
+    progress(2)
+    unit, _ = normal_parts(x[...].astype(F32))
+    normed = (unit * vectors[0:1] + vectors[1:2]).astype(LOW)
+    normed_out[...] = mm(normed, table[...]).astype(LOW)
+
+    def column(i, _):
+        page_copy(i).wait()
+        at = pl.ds(pl.multiple_of(i * 256, 256), 256)
+        mixture[:, at] = mm(normed_out[...], page[:, at])
+        return 0
+
+    lax.fori_loop(0, 13, column, 0)
+    blank = jnp.zeros((rows, WIDE - width), LOW)
+    here[0, :, :width] = mixture[:, width : 2 * width].astype(LOW)
+    here[0, :, width:] = blank
+    here[1, :, :width] = (mixture[:, 2 * width : 3 * width] + vectors[3:4]).astype(LOW)
+    here[1, :, width:] = blank
+
+    def pair_copy(source, target, to, number):
+        return remote_copy(source, target, pair_send.at[number], pair_recv.at[number], toward[to])
+
+    to_away = pair_copy(here, away, (LEVEL, 1), 0)
+    to_beside = pair_copy(here, beside, SIBLING, 1)
+    to_corner = pair_copy(away, corner, SIBLING, 2)
+    to_away.start()
+    to_beside.start()
+    query = ((mixture[:, :width] + vectors[2:3]).astype(LOW).astype(F32) * HDIM ** (-0.5)).astype(LOW)
+    query_out[:, :width] = query
+    query_out[:, width:] = blank
+    progress(2)
+    to_beside.wait_recv()
+
+    def block(kind, near, part, at):
+        rows_at = pl.ds(part * half, half)
+        one, two = (here, beside) if near == 0 else (away, corner)
+        return jnp.concatenate([one[kind, rows_at, at], two[kind, rows_at, at]], axis=0)
+
+    def one_unit(queries, keys, values):
+        scores = mm_nt(keys, queries)
+        level = jnp.max(scores, axis=0, keepdims=True)
+        exponent = jnp.exp(scores - level)
+        return level, jnp.sum(exponent, axis=0, keepdims=True), mm_tn(values, exponent.astype(LOW))
+
+    def merge(units):
+        peak = units[0][0]
+        for level, _, _ in units[1:]:
+            peak = jnp.maximum(peak, level)
+        total, out = 0.0, 0.0
+        for level, sums, part in units:
+            share = jnp.exp(level - peak)
+            total = total + share * sums
+            out = out + share * part
+        return peak, total, out
+
+    def local_pair(p, _):
+        at = pl.ds(pl.multiple_of(p * 128, 128), 128)
+        low, high = head_pair(query_out[:half, at]), head_pair(query_out[half:, at])
+        keys, values = block(0, 0, 0, at), block(1, 0, 0, at)
+        bottom = one_unit(low, keys, values)
+        top = merge([one_unit(high, keys, values), one_unit(high, block(0, 0, 1, at), block(1, 0, 1, at))])
+        for place, (level, sums, out) in enumerate((bottom, top)):
+            stats[p, 2 * place : 2 * place + 1] = level
+            stats[p, 2 * place + 1 : 2 * place + 2] = sums
+            mixed[p, place] = out
+        return 0
+
+    for begin_at in (0, 3, 6):
+        lax.fori_loop(begin_at, begin_at + 3, local_pair, 0)
+        progress(1)
+    to_away.wait_recv()
+    to_corner.start()
+    progress(1)
+    to_corner.wait_recv()
+
+    def far_pair(p, _):
+        at = pl.ds(pl.multiple_of(p * 128, 128), 128)
+        low, high = head_pair(query_out[:half, at]), head_pair(query_out[half:, at])
+        keys, values = block(0, 1, 0, at), block(1, 1, 0, at)
+        last_keys = jnp.where(first, block(0, 1, 1, at), keys)
+        last_values = jnp.where(first, block(1, 1, 1, at), values)
+        near = one_unit(high, keys, values)
+        last = one_unit(jnp.where(first, high, low), last_keys, last_values)
+        low_last = (jnp.where(first, far_below, last[0]),) + last[1:]
+        high_last = (jnp.where(first, last[0], far_below),) + last[1:]
+
+        def before(place):
+            return (stats[p, 2 * place : 2 * place + 1], stats[p, 2 * place + 1 : 2 * place + 2], mixed[p, place])
+
+        for place, units in enumerate(([before(0), low_last], [before(1), near, high_last])):
+            peak, total, out = merge(units)
+            attended_out[place * half : (place + 1) * half, at] = from_pair(out / total)
+            log_out[p, place : place + 1] = peak + jnp.log(total)
+        return 0
+
+    for begin_at in (0, 3, 6):
+        lax.fori_loop(begin_at, begin_at + 3, far_pair, 0)
+        progress(1)
+
+    def late(i, _):
+        page_copy(i).wait()
+        return 0
+
+    lax.fori_loop(13, tiles, late, 0)
+    lead = 4 * width - WIDE
+    attended_low[...] = mm(attended_out[:, :width].astype(LOW), table[...]).astype(LOW)
+    blended = mm(attended_low[...], page[:, lead:])
+    middle = x[...].astype(F32) + (blended[:, 3 * width - lead :] + vectors[4:5])
+    middle_out[...] = middle
+    unit, _ = normal_parts(middle)
+    second = (unit * vectors[6:7] + vectors[7:8]).astype(LOW)
+    second_out[...] = mm(second, table[...]).astype(LOW)
+    result[...] = middle + vectors[5:6]
+
+    def inner(i, _):
+        at = pl.ds(pl.multiple_of(i * 256, 256), 256)
+        expand_copy(i).wait()
+        hidden = mm(second_out[...], expand[:, at]) + wide[:, at]
+        below = 0.5 + 0.5 * lax.erf(hidden * 0.7071067811865476)
+        active = (hidden * below).astype(LOW)
+        active_out[:, at] = active
+        slope_out[:, at] = (below + hidden * (0.3989422804014327 * jnp.exp(-0.5 * hidden * hidden))).astype(LOW)
+        reduce_copy(i).wait()
+        result[...] += mm(active, reduce[at])
+        return 0
+
+    for begin_at in range(0, tiles, 4):
+        lax.fori_loop(begin_at, min(begin_at + 4, tiles), inner, 0)
+        progress(2)
+    result_out[...] = result[...].astype(LOW)
+    progress(len(todo))
+    for copy in (to_away, to_beside, to_corner):
+        copy.wait_send()
+
+
+def forward(x, vectors, wide, table, page, expand, reduce, shards=None):
+    rows, width = x.shape
+    inner = expand.shape[1]
+    pairs = WIDE // 128
+    anywhere = pl.BlockSpec(memory_space=pl.ANY)
+    inside = pl.BlockSpec(memory_space=pltpu.VMEM)
+
+    def shape(*dims, kind=LOW):
+        return jax.ShapeDtypeStruct(dims, kind)
+
+    pair = shape(2, rows, WIDE)
+    outs = [
+        shape(rows, WIDE), shape(rows, WIDE), pair, pair, pair, pair, shape(rows, WIDE, kind=F32),
+        shape(pairs, 2, rows, kind=F32), shape(rows, WIDE), shape(rows, width, kind=F32),
+        shape(rows, WIDE), shape(rows, inner), shape(rows, inner), shape(rows, width),
+    ]
+    extra = shards is not None
+    count = len(outs)
+    scratch = [
+        pltpu.VMEM(page.shape, LOW), pltpu.VMEM(expand.shape, LOW), pltpu.VMEM(reduce.shape, LOW),
+        pltpu.VMEM((rows, 13 * 256), F32), pltpu.VMEM((rows, width), F32),
+        pltpu.VMEM((pairs, 2, 128, rows), F32), pltpu.VMEM((pairs, 4, rows), F32),
+        pltpu.SemaphoreType.DMA((inner // 256,)), pltpu.SemaphoreType.DMA((inner // 256,)),
+        pltpu.SemaphoreType.DMA((inner // 256,)), pltpu.SemaphoreType.DMA((3,)), pltpu.SemaphoreType.DMA((3,)),
+    ]
+    if extra:
+        outs += gather_shapes(shards)
+        scratch += gather_semaphores()
+    res = pl.pallas_call(
+        partial(forward_kernel, extra),
+        out_shape=tuple(outs),
+        in_specs=[inside] * 4 + [anywhere] * 3 + ([anywhere] * 2 if extra else []),
+        out_specs=(inside,) * count + (anywhere,) * (len(outs) - count),
+        scratch_shapes=scratch,
+        compiler_params=pltpu.CompilerParams(
+            collective_id=2 if extra else 3, has_side_effects=True, vmem_limit_bytes=60 << 20
+        ),
+        name="forward_gather" if extra else "forward",
+    )(x, vectors, wide, table, page, expand, reduce, *(shards if extra else ()))
+    return res[:count], res[count:]
+
+
 def spread(width):
     row = lax.broadcasted_iota(jnp.int32, (width, 16 * 72), 0)
     column = lax.broadcasted_iota(jnp.int32, (width, 16 * 72), 1)
@@ -1366,35 +1464,23 @@
 
 
 def small_of(page):
-    part = page[:, 68, : 12 * 68].astype(F32).reshape(16, 12, 68)
-    vectors = [part[:, row].reshape(1, -1) for row in range(8)]
-    return vectors, part[:, 8:].reshape(1, -1)
-
-
-def layer_forward(source, small, wide, weights, low_chunk, table):
-    page, expand, reduce = weights
-    first_gain, first_shift, query_bias, value_bias, output_bias, reduce_bias, gain, shift = small
-    normed, query, here = project_rows(
-        source, first_gain, first_shift, query_bias, value_bias, table, page
-    )
-    away = swapped(here, LINE, 1)
-    beside = swapped(here, SECTION, 1)
-    corner = swapped(away, SECTION, 1)
-    pairs = (here, beside, away, corner)
-    attended, logs = attend(query, *pairs, low_chunk)
-    attended_low, middle, second, active, slope, result = feed(
-        source, attended, gain, shift, output_bias, reduce_bias, table, page, expand, wide, reduce
-    )
-    saved = (source, normed, query, pairs, attended, logs, attended_low, middle, second, active, slope)
-    return result, saved
+    part = page[:, 68, : 12 * 68].astype(F32).reshape(16, 12, 68).transpose(1, 0, 2)
+    return part[:8].reshape(8, -1), part[8:].transpose(1, 0, 2).reshape(1, -1)
+
+
+def layer_forward(source, small, wide, weights, table, shards=None):
+    saved, gathered = forward(source, small, wide, table, *weights, shards=shards)
+    return saved[13], (source,) + tuple(saved[:13]), gathered
 
 
 def layer_gradient(top, saved, small, weights, low_chunk, table):
-    source, normed, query, pairs, attended, logs, attended_low, middle, second, active, slope = saved
+    source, normed, query = saved[:3]
+    pairs = saved[3:7]
+    attended, logs, attended_low, middle, second, active, slope = saved[7:]
     page, expand, reduce = weights
     width = top.shape[1]
     grad_hidden, sum_wide, grad_middle, branch, grad_attended, late = feed_back(
-        top, slope, middle, small[6], table, page, expand, reduce
+        top, slope, middle, small[6:7], table, page, expand, reduce
     )
     grad_query, near, beside, away, corner = attend_back(
         query, grad_attended, attended, logs, *pairs, low_chunk
@@ -1403,7 +1489,7 @@
     near = near + swapped(beside, SECTION, 1).astype(F32)
     near = (near + swapped(away, LINE, 1).astype(F32)).astype(LOW)
     mixture, result, early = project_back(
-        grad_query, near, branch, source, grad_middle, small[0], table, page
+        grad_query, near, branch, source, grad_middle, small[:1], table, page
     )
     order = (early[0], early[1], early[2], early[3], late[2], late[3], late[0], late[1])
     packed = jnp.stack([vector.reshape(16, -1) for vector in order], axis=1)
@@ -1458,23 +1544,30 @@
     other = swapped(jnp.where(core == 0, expand_shard, attention_shard), SECTION, 1)
     lower = jnp.where(core == 0, attention_shard, other)
     upper = jnp.where(core == 0, other, expand_shard)
+    reduce_other = swapped(reduce_weight[0], SECTION, 1)
+    lower_reduce = jnp.where(core == 0, reduce_weight[0], reduce_other)
+    upper_reduce = jnp.where(core == 0, reduce_other, reduce_weight[0])
     rows = to_rows(inputs, core, line)
     top = to_rows(cotangent, core, line)
-    lower_pages, reduce_pages, upper_pages = gather_pages((lower, reduce_weight[0], upper))
     table = spread(width)
-    layers = []
-    for layer, pages in enumerate((lower_pages, upper_pages)):
+
+    def prepared(pages):
         small, wide = small_of(pages[0])
         weights = (
             pages[0].reshape(-1, 4 * width),
             pages[1].reshape(-1, 4 * width),
-            reduce_pages[layer].reshape(-1, width),
+            pages[2].reshape(-1, width),
         )
-        layers.append((small, wide, weights))
+        return small, wide, weights
+
+    layers = [prepared(gather_pages((lower, lower_reduce)))]
     small, wide, weights = layers[0]
-    middle_rows, saved_lower = layer_forward(rows, small, wide, weights, low_chunk, table)
+    middle_rows, saved_lower, upper_pages = layer_forward(
+        rows, small, wide, weights, table, (upper, upper_reduce)
+    )
+    layers.append(prepared(upper_pages))
     small, wide, weights = layers[1]
-    final_rows, saved_upper = layer_forward(middle_rows, small, wide, weights, low_chunk, table)
+    final_rows, saved_upper, _ = layer_forward(middle_rows, small, wide, weights, table)
     layer_outputs = from_rows(middle_rows, final_rows, core, line)
     upper_grad, upper_attention, upper_expand, upper_reduce = layer_gradient(
         top, saved_upper, small, weights, low_chunk, table

time: 1100 us -> 1050 us (0.955)
  waiting for transfers between devices: 83 us -> 24.5 us
  Pallas kernels: 815 us -> 852 us
  local copies, waits for them, and re-layouts: 98.2 us -> 82.6 us
  starting transfers between devices: 26 us -> 12.2 us
    ppermute x20 -> x15, waiting for transfers between devices: 83 us -> 24.5 us  [swapped(): lax.ppermute(value, axis, [(source, source ^ bits) for source in range(co...]
    pallas_call x7 -> x3, Pallas kernels: 379 us -> 414 us  [the longest x2 262 us: forward(): pl.pallas_call(partial(forward_kernel, extra), out_shape=tuple(outs), in_...]
    ppermute x20 -> x15, starting transfers between devices: 26 us -> 12.2 us  [swapped(): lax.ppermute(value, axis, [(source, source ^ bits) for source in range(co...]
    unnamed x196 -> x134, local copies, waits for them, and re-layouts: 30 us -> 26.3 us
  transfers between devices with their start and end apart: 20 -> 15, of which waited for: 6 -> 3; matrix products, arithmetic and copies ran while one was open for 11% -> 10% of each run, Pallas kernels for 35% -> 37%
where the time goes in v3:
time: 1050 us; the launch traced here: 1040 us
  Pallas kernels  852 us (81%)
  local copies, waits for them, and re-layouts  82.6 us (8%)
  other arithmetic  36.7 us (3%)
  matrix products  26.9 us (3%)
  waiting for transfers between devices  24.5 us (2%)
  starting transfers between devices  12.2 us (1%)
    pallas_call x1, Pallas kernels, scatter(): pl.pallas_call(partial(scatter_kernel, slots), out_shape=tuple(out), in_s...  302 us
    pallas_call x2, Pallas kernels, forward(): pl.pallas_call(partial(forward_kernel, extra), out_shape=tuple(outs), in_...  262 us
    pallas_call x1, Pallas kernels, gather_pages(): pl.pallas_call(gather_kernel, out_shape=tuple(gather_shapes(shards)), in_...  153 us
    pallas_call x2, Pallas kernels, feed_back(): pl.pallas_call(partial(feed_back_kernel, steps, width), grid=(steps,), in...  53.9 us
    pallas_call x2, Pallas kernels, attend_back(): pl.pallas_call(attend_back_kernel, grid=(pairs,), in_specs=[flat, flat, f...  33.1 us
    convert_element_type x2, local copies, waits for them, and re-layouts, layer_gradient(): page_reduce = mm_tn(active, top).astype(LOW).reshape(16, -1, width)  28 us
    dot_general x4, matrix products, mm_tn(): lax.dot_general(left, right, (((0,), (0,)), ((), ())), preferred_element_...  26.9 us
    unnamed x134, local copies, waits for them, and re-layouts  26.3 us
  transfers between devices with their start and end apart: 15, of which 3 were waited for; matrix products, arithmetic and copies ran while one was open for 10% of the time, Pallas kernels for 37%

profile of v3, /device:TPU:0, one launch (start us, length us, event | category | flops | bytes accessed | tf_op | source)
XLA Modules:
  0.0 1037.0 jit_solution(2973038561861904803)
XLA Ops:
  2.9 5.0 collective-permute-start
  10.8 2.9 fusion.1.refs_3_.table
  17.2 4.5 collective-permute-done.5
  27.4 152.5 %gather_pages.1 = (bf16[16,72,4352]{2,1,0:T(8,128)(2,1)}, bf16[16,72,4352]{2,1,0:T(8,128)(2,1)}, bf16[16,272,1088]{2,1,0:T(8,128)(2,1)}) custom-call(bf16[72,4352]{1,0:T(8,128)(2,1)} %get-tuple-element.235.refs_0_, bf16[272,1088]{1,0:T(8,128)(2,1)} %get-tuple-element.229.refs_1_), custom_call_target="tpu_custom_call" | custom-call | tf_op jit(solution)/shard_map/gather_pages/pallas_call | solution.py:1219
  182.7 188.5 %forward_gather.1 = (bf16[256,1152]{1,0:T(8,128)(2,1)}, bf16[256,1152]{1,0:T(8,128)(2,1)}, bf16[2,256,1152]{2,1,0:T(8,128)(2,1)}, bf16[2,256,1152]{2,1,0:T(8,128...) custom-call(bf16[256,1088]{1,0:T(8,128)(2,1)} %pad_maximum_fusion.5., ...), custom_call_target="tpu_custom_call" | custom-call | tf_op jit(solution)/shard_map/forward_gather/pallas_call | solution.py:1445
  374.1 73.2 %forward.1 = (bf16[256,1152]{1,0:T(8,128)(2,1)}, bf16[256,1152]{1,0:T(8,128)(2,1)}, bf16[2,256,1152]{2,1,0:T(8,128)(2,1)}, bf16[2,256,1152]{2,1,0:T(8,128)(2,1)}...) custom-call(bf16[256,1088]{1,0:T(8,128)(2,1)} %get-tuple-element.83., ...), custom_call_target="tpu_custom_call" | custom-call | tf_op jit(solution)/shard_map/forward/pallas_call | solution.py:1445
  448.6 26.9 %feed_back.2 = (bf16[256,4352]{1,0:T(8,128)(2,1)}, f32[1,4352]{1,0:T(1,128)S(1)}, f32[256,1088]{1,0:T(8,128)S(1)}, bf16[256,1088]{1,0:T(8,128)(2,1)S(1)}, bf16[2...) custom-call(bf16[256,1088]{1,0:T(8,128)(2,1)S(1)} %pad_maximum_fusion.6.top, bf16[256,4352]{1,0:T(8,128)(2,1)} %get-tuple-element.90.slope, ...), custom_call_target="tpu_custom_call" | custom-call | tf_op jit(solution)/shard_map/feed_back/pallas_call | solution.py:933
  477.5 16.8 %attend_back.2 = (bf16[256,1152]{1,0:T(8,128)(2,1)S(1)}, f32[2,256,1152]{2,1,0:T(8,128)}, bf16[2,256,1152]{2,1,0:T(8,128)(2,1)S(1)}, bf16[2,256,1152]{2,1,0:T(8,128)(2,1)S(1)}, bf16[2,256,1152]{2,1,0:T(8,128)(2,1)}) custom-call(bf16[256,1152]{1,0:T(8,128)(2,1)S(1)} %copy-done.19, bf16[256,1152]{1,0:T(8,128)(2,1)S(1)} %get-tuple-element.92.grad, ...), custom_call_target="tpu_custom_call" | custom-call | tf_op jit(solution)/shard_map/attend_back/pallas_call | solution.py:869
  502.5 7.9 convolution_convert_fusion.1
  510.4 2.7 add_convert_fusion.3
  513.3 5.6 convolution_convert_fusion
  524.4 17.8 %collective-permute-done.8 = bf16[2,256,1152]{2,1,0:T(8,128)(2,1)} collective-permute-done((bf16[2,256,1152]{2,1,0:T(8,128)(2,1)}, bf16[2,256,1152]{2,1,0:T(8,128)(2,1)}, u32[]{:S(2)}, u32[]{:S(2)}) %collective-permute-start.8) | collective-permute-done | bytes 1179680 | tf_op jit(solution)/shard_map/ppermute | solution.py:446
  542.2 2.8 add_convert_fusion.2.pair
  545.0 12.5 %project_back.2 = (bf16[256,4352]{1,0:T(8,128)(2,1)}, bf16[256,1088]{1,0:T(8,128)(2,1)S(1)}, f32[8,1088]{1,0:T(8,128)S(1)}) custom-call(bf16[256,1152]{1,0:T(8,128)(2,1)S(1)} %copy-done.17, bf16[2,256,1152]{2,1,0:T(8,128)(2,1)S(1)} %add_convert_fusion.2.pair, bf16[256,1088]{1,0:T(8,128)(2,1)S(1)} %copy-done.15, bf16[256,1088]{1,0:T(8,128)(2,1)S(1)} %copy-done, ...), custom_call_target="tpu_custom_call" | custom-call | tf_op jit(solution)/shard_map/project_back/pallas_call | solution.py:994
  557.6 27.0 %feed_back.3 = (bf16[256,4352]{1,0:T(8,128)(2,1)}, f32[1,4352]{1,0:T(1,128)S(1)}, f32[256,1088]{1,0:T(8,128)S(1)}, bf16[256,1088]{1,0:T(8,128)(2,1)S(1)}, bf16[2...) custom-call(bf16[256,1088]{1,0:T(8,128)(2,1)S(1)} %get-tuple-element.106.top, bf16[256,4352]{1,0:T(8,128)(2,1)} %get-tuple-element.107.slope, ...), custom_call_target="tpu_custom_call" | custom-call | tf_op jit(solution)/shard_map/feed_back/pallas_call | solution.py:933
  585.6 16.3 %attend_back.3 = (bf16[256,1152]{1,0:T(8,128)(2,1)S(1)}, f32[2,256,1152]{2,1,0:T(8,128)}, bf16[2,256,1152]{2,1,0:T(8,128)(2,1)S(1)}, bf16[2,256,1152]{2,1,0:T(8,128)(2,1)S(1)}, bf16[2,256,1152]{2,1,0:T(8,128)(2,1)}) custom-call(bf16[256,1152]{1,0:T(8,128)(2,1)S(1)} %copy-done.18, bf16[256,1152]{1,0:T(8,128)(2,1)S(1)} %get-tuple-element.109.grad, ...), custom_call_target="tpu_custom_call" | custom-call | tf_op jit(solution)/shard_map/attend_back/pallas_call | solution.py:869
  604.4 13.9 %copy.133 = bf16[4352,1088]{1,0:T(8,128)(2,1)} copy(bf16[4352,1088]{0,1:T(8,128)(2,1)} %convolution_convert_fusion.1) | data formatting | bytes 18939904 | tf_op jit(solution)/shard_map/convert_element_type | solution.py:1501
  620.7 7.8 convolution_convert_fusion.2
  632.8 14.1 %copy.132 = bf16[4352,1088]{1,0:T(8,128)(2,1)} copy(bf16[4352,1088]{0,1:T(8,128)(2,1)} %convolution_convert_fusion.2) | data formatting | bytes 18939904 | tf_op jit(solution)/shard_map/convert_element_type | solution.py:1501
  649.2 11.7 %attention_page.3.refs_4_ = bf16[16,72,4352]{2,1,0:T(8,128)(2,1)} custom-call(bf16[256,1152]{1,0:T(8,128)(2,1)S(1)} %copy-done.22, bf16[256,1152]{1,0:T(8,128)(2,1)S(1)} %copy-done.23, bf16[256,4352]{1,0:T(8,128)(2,1)S(1)} %copy-done.3, bf16[16,1,4352]{2,1,0:T(2,128)(2,1)S(1)} %pad.18.small), custom_call_target="tpu_custom_call" | custom-call | tf_op jit(solution)/shard_map/attention_page/pallas_call | solution.py:1046
  661.0 5.6 convolution_convert_fusion.3
  668.9 12.4 %project_back.3 = (bf16[256,4352]{1,0:T(8,128)(2,1)}, bf16[256,1088]{1,0:T(8,128)(2,1)S(1)}, f32[8,1088]{1,0:T(8,128)S(1)}) custom-call(bf16[256,1152]{1,0:T(8,128)(2,1)S(1)} %copy-done.13, bf16[2,256,1152]{2,1,0:T(8,128)(2,1)S(1)} %add_convert_fusion.pair, bf16[256,1088]{1,0:T(8,128)(2,1)S(1)} %get-tuple-element.121.branch, ...), custom_call_target="tpu_custom_call" | custom-call | tf_op jit(solution)/shard_map/project_back/pallas_call | solution.py:994
  691.1 11.7 %attention_page.2.refs_0_ = bf16[16,72,4352]{2,1,0:T(8,128)(2,1)} custom-call(bf16[256,1152]{1,0:T(8,128)(2,1)S(1)} %copy-done.20, bf16[256,1152]{1,0:T(8,128)(2,1)S(1)} %copy-done.21, bf16[256,4352]{1,0:T(8,128)(2,1)S(1)} %copy-done.4, bf16[16,1,4352]{2,1,0:T(2,128)(2,1)S(1)} %copy-done.11), custom_call_target="tpu_custom_call" | custom-call | tf_op jit(solution)/shard_map/attention_page/pallas_call | solution.py:1046
  702.8 302.5 %scatter_gradients.1 = (f32[72,4352]{1,0:T(8,128)S(1)}, f32[272,1088]{1,0:T(8,128)S(1)}, f32[72,4352]{1,0:T(8,128)S(1)}, bf16[16,72,4352]{2,1,0:T(8,128)(2,1)}, ...) custom-call(bf16[16,72,4352]{2,1,0:T(8,128)(2,1)} %attention_page.2., ...), custom_call_target="tpu_custom_call" | custom-call | tf_op jit(solution)/shard_map/scatter_gradients/pallas_call | solution.py:736
  (264 shorter events, 92.2 us)
Async XLA Ops:
  2.9 13.3 %collective-permute-start = (bf16[128,1088]{1,0:T(8,128)(2,1)}, bf16[128,1088]{1,0:T(8,128)(2,1)}, u32[]{:S(2)}, u32[]{:S(2)}) collective-permute-start(bf16[128,1088]{1,0:T(8,128)(2,1)} %bitcast.1), channel_id=1, source_target_pairs={{0,3},{1,2},{2,1},{3,0},{4,7},{5,6},{6,5},{7,4},{8,11},{9,10},{10,... | collective-permute-start | bytes 835592 | tf_op jit(solution)/shard_map/ppermute | solution.py:446
  8.9 12.8 %collective-permute-start.5 = (bf16[128,1088]{1,0:T(8,128)(2,1)}, bf16[128,1088]{1,0:T(8,128)(2,1)}, u32[]{:S(2)}, u32[]{:S(2)}) collective-permute-start(bf16[128,1088]{1,0:T(8,128)(2,1)} %bitcast.34), channel_id=1, source_target_pairs={{0,3},{1,2},{2,1},{3,0},{4,7},{5,6},{6,5},{7,4},{8,11},{9,10},{10,... | collective-permute-start | bytes 835592 | tf_op jit(solution)/shard_map/ppermute | solution.py:446
  10.2 15.9 %collective-permute-start.1 = (bf16[72,4352]{1,0:T(8,128)(2,1)}, bf16[72,4352]{1,0:T(8,128)(2,1)S(1)}, u32[]{:S(2)}, u32[]{:S(2)}) collective-permute-start(bf16[72,4352]{1,0:T(8,128)(2,1)} %broadcast_select_fusion.7), channel_id=1, source_target_pairs={{0,16},{16,0},{1,17},{17,1},{2,18},{18,2},{3,19},{19,3},{4,20},{20... | collective-permute-start | bytes 1880072 | tf_op jit(solution)/shard_map/ppermute | solution.py:446
  10.2 13.6 %collective-permute-start.2 = (bf16[272,1088]{1,0:T(8,128)(2,1)S(1)}, bf16[272,1088]{1,0:T(8,128)(2,1)}, u32[]{:S(2)}, u32[]{:S(2)}) collective-permute-start(bf16[272,1088]{1,0:T(8,128)(2,1)S(1)} %bitcast.129), channel_id=1, source_target_pairs={{0,16},{16,0},{1,17},{17,1},{2,18},{18,2},{3,19},{19,3},{4,20},{20... | collective-permute-start | bytes 1775624 | tf_op jit(solution)/shard_map/ppermute | solution.py:446
  181.2 190.0 %copy-start.53 = (f32[16,12,68]{2,1,0:T(8,128)}, f32[16,12,68]{2,1,0:T(8,128)S(1)}, u32[]{:S(2)}) copy-start(f32[16,12,68]{2,1,0:T(8,128)S(1)} %reshape.160) | copy-start | bytes 156676
  448.6 29.0 %copy-start.19 = (bf16[256,1152]{1,0:T(8,128)(2,1)S(1)}, bf16[256,1152]{1,0:T(8,128)(2,1)}, u32[]{:S(2)}) copy-start(bf16[256,1152]{1,0:T(8,128)(2,1)} %get-tuple-element.89.query) | copy-start | bytes 1769476
  448.6 29.0 %copy-start.27 = (f32[9,2,256]{2,1,0:T(2,128)S(1)}, f32[9,2,256]{2,1,0:T(2,128)}, u32[]{:S(2)}) copy-start(f32[9,2,256]{2,1,0:T(2,128)} %get-tuple-element.94.logs) | copy-start | bytes 55300
  477.5 19.5 %copy-start = (bf16[256,1088]{1,0:T(8,128)(2,1)S(1)}, bf16[256,1088]{1,0:T(8,128)(2,1)}, u32[]{:S(2)}) copy-start(bf16[256,1088]{1,0:T(8,128)(2,1)} %get-tuple-element.83.refs_0_.x) | copy-start | bytes 1671172
  477.5 19.5 %copy-start.44 = (bf16[256,1088]{1,0:T(8,128)(2,1)S(1)}, bf16[256,1088]{1,0:T(8,128)(2,1)}, u32[]{:S(2)}) copy-start(bf16[256,1088]{1,0:T(8,128)(2,1)} %get-tuple-element.87) | copy-start | bytes 1671172
  496.2 14.2 %collective-permute-start.7 = (bf16[2,256,1152]{2,1,0:T(8,128)(2,1)}, bf16[2,256,1152]{2,1,0:T(8,128)(2,1)}, u32[]{:S(2)}, u32[]{:S(2)}) collective-permute-start(bf16[2,256,1152]{2,1,0:T(8,128)(2,1)} %get-tuple-element.103), channel_id=1, source_target_pairs={{0,16},{16,0},{1,17},{17,1},{2,18},{18,2},{3,19},{19,3},{4,20},{20... | collective-permute-start | bytes 3538952 | tf_op jit(solution)/shard_map/ppermute | solution.py:446
  500.1 20.0 %collective-permute-start.3 = (bf16[2,128,1088]{1,2,0:T(8,128)(2,1)}, bf16[2,128,1088]{1,2,0:T(8,128)(2,1)}, u32[]{:S(2)}, u32[]{:S(2)}) collective-permute-start(bf16[2,128,1088]{1,2,0:T(8,128)(2,1)} %copy.106), channel_id=1, source_target_pairs={{0,3},{1,2},{2,1},{3,0},{4,7},{5,6},{6,5},{7,4},{8,11},{9,10},{10,... | collective-permute-start | bytes 1671176 | tf_op jit(solution)/shard_map/ppermute | solution.py:446
  502.5 21.9 %collective-permute-start.6 = (bf16[2,256,1152]{2,1,0:T(8,128)(2,1)}, bf16[2,256,1152]{2,1,0:T(8,128)(2,1)}, u32[]{:S(2)}, u32[]{:S(2)}) collective-permute-start(bf16[2,256,1152]{2,1,0:T(8,128)(2,1)} %copy-done.31), channel_id=1, source_target_pairs={{0,16},{16,0},{1,17},{17,1},{2,18},{18,2},{3,19},{19,3},{4,20},{20... | collective-permute-start | bytes 3538952 | tf_op jit(solution)/shard_map/ppermute | solution.py:446
  513.1 29.1 %collective-permute-start.8 = (bf16[2,256,1152]{2,1,0:T(8,128)(2,1)}, bf16[2,256,1152]{2,1,0:T(8,128)(2,1)}, u32[]{:S(2)}, u32[]{:S(2)}) collective-permute-start(bf16[2,256,1152]{2,1,0:T(8,128)(2,1)} %add_convert_fusion.3), channel_id=1, source_target_pairs={{0,1},{1,0},{2,3},{3,2},{4,5},{5,4},{6,7},{7,6},{8,9},{9,8},{10,11... | collective-permute-start | bytes 3538952 | tf_op jit(solution)/shard_map/ppermute | solution.py:446
  524.0 94.4 %collective-permute-start.4 = (bf16[2,128,1088]{1,2,0:T(8,128)(2,1)}, bf16[2,128,1088]{1,2,0:T(8,128)(2,1)}, u32[]{:S(2)}, u32[]{:S(2)}) collective-permute-start(bf16[2,128,1088]{1,2,0:T(8,128)(2,1)} %copy.110), channel_id=1, source_target_pairs={{0,16},{16,0},{1,17},{17,1},{2,18},{18,2},{3,19},{19,3},{4,20},{20... | collective-permute-start | bytes 1671176 | tf_op jit(solution)/shard_map/ppermute | solution.py:446
  557.6 28.0 %copy-start.18 = (bf16[256,1152]{1,0:T(8,128)(2,1)S(1)}, bf16[256,1152]{1,0:T(8,128)(2,1)}, u32[]{:S(2)}) copy-start(bf16[256,1152]{1,0:T(8,128)(2,1)} %get-tuple-element.88.query) | copy-start | bytes 1769476
  557.6 28.0 %copy-start.26 = (f32[9,2,256]{2,1,0:T(2,128)S(1)}, f32[9,2,256]{2,1,0:T(2,128)}, u32[]{:S(2)}) copy-start(f32[9,2,256]{2,1,0:T(2,128)} %get-tuple-element.111.logs) | copy-start | bytes 55300
  585.6 17.2 %copy-start.29 = (f32[1,4352]{1,0:T(1,128)S(1)}, f32[1,4352]{1,0:T(1,128)}, u32[]{:S(2)}) copy-start(f32[1,4352]{1,0:T(1,128)} %copy-done.28) | copy-start | bytes 52228
  602.8 25.8 %collective-permute-start.10 = (bf16[2,256,1152]{2,1,0:T(8,128)(2,1)}, bf16[2,256,1152]{2,1,0:T(8,128)(2,1)}, u32[]{:S(2)}, u32[]{:S(2)}) collective-permute-start(bf16[2,256,1152]{2,1,0:T(8,128)(2,1)} %get-tuple-element.120), channel_id=1, source_target_pairs={{0,16},{16,0},{1,17},{17,1},{2,18},{18,2},{3,19},{19,3},{4,20},{20... | collective-permute-start | bytes 3538952 | tf_op jit(solution)/shard_map/ppermute | solution.py:446
  620.7 45.9 %collective-permute-start.9 = (bf16[2,256,1152]{2,1,0:T(8,128)(2,1)}, bf16[2,256,1152]{2,1,0:T(8,128)(2,1)}, u32[]{:S(2)}, u32[]{:S(2)}) collective-permute-start(bf16[2,256,1152]{2,1,0:T(8,128)(2,1)} %copy-done.30), channel_id=1, source_target_pairs={{0,16},{16,0},{1,17},{17,1},{2,18},{18,2},{3,19},{19,3},{4,20},{20... | collective-permute-start | bytes 3538952 | tf_op jit(solution)/shard_map/ppermute | solution.py:446
  631.1 35.5 %collective-permute-start.11 = (bf16[2,256,1152]{2,1,0:T(8,128)(2,1)}, bf16[2,256,1152]{2,1,0:T(8,128)(2,1)}, u32[]{:S(2)}, u32[]{:S(2)}) collective-permute-start(bf16[2,256,1152]{2,1,0:T(8,128)(2,1)} %add_convert_fusion.1), channel_id=1, source_target_pairs={{0,1},{1,0},{2,3},{3,2},{4,5},{5,4},{6,7},{7,6},{8,9},{9,8},{10,11... | collective-permute-start | bytes 3538952 | tf_op jit(solution)/shard_map/ppermute | solution.py:446
  632.8 14.3 %copy-start.3 = (bf16[256,4352]{1,0:T(8,128)(2,1)S(1)}, bf16[256,4352]{1,0:T(8,128)(2,1)}, u32[]{:S(2)}) copy-start(bf16[256,4352]{1,0:T(8,128)(2,1)} %get-tuple-element.136.mixture) | copy-start | bytes 6684676
  686.1 320.6 %collective-permute-start.12 = (bf16[2,128,1088]{1,2,0:T(8,128)(2,1)}, bf16[2,128,1088]{1,2,0:T(8,128)(2,1)}, u32[]{:S(2)}, u32[]{:S(2)}) collective-permute-start(bf16[2,128,1088]{1,2,0:T(8,128)(2,1)} %copy.115), channel_id=1, source_target_pairs={{0,3},{1,2},{2,1},{3,0},{4,7},{5,6},{6,5},{7,4},{8,11},{9,10},{10,... | collective-permute-start | bytes 1671176 | tf_op jit(solution)/shard_map/ppermute | solution.py:446
  1006.7 20.5 %collective-permute-start.14 = (f32[72,4352]{1,0:T(8,128)}, f32[72,4352]{1,0:T(8,128)}, u32[]{:S(2)}, u32[]{:S(2)}) collective-permute-start(f32[72,4352]{1,0:T(8,128)} %broadcast_select_fusion.3), channel_id=1, source_target_pairs={{0,16},{16,0},{1,17},{17,1},{2,18},{18,2},{3,19},{19,3},{4,20},{20... | collective-permute-start | bytes 3760136 | tf_op jit(solution)/shard_map/ppermute | solution.py:446
  1014.6 5.6 collective-permute-start.13
  (55 other events, 213.3 us)

commit v4 on v3

--- a/solution.py
+++ b/solution.py
@@ -531,220 +531,6 @@
 GATHER_NUMBER = {kind: index for index, kind in enumerate(GATHER_KINDS)}
 
 
-KINDS = (
-    [(CORNER, dd) for dd in range(4)]
-    + [(ONCE, k) for k in range(4)]
-    + [(EAST, k) for k in range(4)]
-    + [(NORTH, k) for k in range(4)]
-    + [(LEVEL, k) for k in (1, 2, 3)]
-)
-NUMBER = {kind: i for i, kind in enumerate(KINDS)}
-DEPTH = 8
-
-def scatter_kernel(slots, *refs):
-    n = len(slots)
-    pages = [(refs[2 * t], refs[2 * t + 1]) for t in range(n)]
-    refs = refs[2 * n :]
-    finals, refs = refs[:n], refs[n:]
-    lands, refs = [refs[5 * t : 5 * t + 5] for t in range(n)], refs[5 * n :]
-    shapes = sorted(set(slots))
-    work = {}
-    for i, shape in enumerate(shapes):
-        work[shape] = refs[3 * i : 3 * i + 3]
-    refs = refs[3 * len(shapes) :]
-    send_sem, recv_sem, load_sem, out_sem = refs
-    core, rings, lines, toward = places()
-    greet(toward)
-
-    def remote(t, src, dst, to, kind):
-        i = t * len(KINDS) + NUMBER[kind]
-        return pltpu.make_async_remote_copy(
-            src_ref=src, dst_ref=dst, send_sem=send_sem.at[i], recv_sem=recv_sem.at[i],
-            device_id=toward[to], device_id_type=pl.DeviceIdType.MESH)
-
-    def by_core(make):
-        def start(pair):
-            for index in (0, 1):
-                @pl.when(core == index)
-                def _():
-                    make(pair[index]).start()
-        return start
-
-    pending = []
-
-    def give(t, dd):
-        dst = lands[t][0].at[pl.ds(rings[dd] * 4, 4)]
-        pair = (pages[t][1], pages[t][0])
-        by_core(lambda ref: remote(t, ref.at[pl.ds(rings[dd] * 4, 4)], dst, SIBLING, (CORNER, dd)))(pair)
-        pending.append(remote(t, dst, dst, SIBLING, (CORNER, dd)))
-
-    def arrived(t, ref, to, kind):
-        remote(t, ref, ref, to, kind).wait_recv()
-
-    task = [0]
-    used = {shape: [None] * DEPTH for shape in shapes}
-    count = {shape: 0 for shape in shapes}
-
-    def total_of(t, dd, k, extra):
-        shape = slots[t]
-        loads = work[shape][0]
-        slot = task[0] % 2
-        task[0] += 1
-        index = rings[dd] * 4 + lines[k]
-        buf = lambda j: loads.at[slot, j]
-        sem = lambda j: load_sem.at[slot * 4 + j]
-        by_core(lambda ref: pltpu.make_async_copy(ref.at[index], buf(0), sem(0)))(pages[t])
-        copies = [pltpu.make_async_copy(buf(0), buf(0), sem(0))]
-        sources = [lands[t][0].at[index]] + extra
-        for j, source in enumerate(sources):
-            copy = pltpu.make_async_copy(source, buf(j + 1), sem(j + 1))
-            copy.start()
-            copies.append(copy)
-        for copy in copies:
-            copy.wait()
-        return loads, slot, len(copies)
-
-    def add_up(shape, loads, slot, terms, store):
-        rows, columns = shape
-        if rows == 72:
-            def step(i, _):
-                at = pl.ds(pl.multiple_of(i * 256, 256), 256)
-                value = loads[slot, 0, :, at].astype(jnp.float32)
-                for j in range(1, terms):
-                    value = value + loads[slot, j, :, at].astype(jnp.float32)
-                store((slice(None), at), value)
-                return 0
-            lax.fori_loop(0, columns // 256, step, 0)
-        else:
-            def step(i, _):
-                at = pl.ds(pl.multiple_of(i * 16, 16), 16)
-                value = loads[slot, 0, at, :].astype(jnp.float32)
-                for j in range(1, terms):
-                    value = value + loads[slot, j, at, :].astype(jnp.float32)
-                store((at, slice(None)), value)
-                return 0
-            lax.fori_loop(0, rows // 16, step, 0)
-
-    def sum_and_send(t, dd, k, extra, dst, to, kind):
-        shape = slots[t]
-        loads, slot, terms = total_of(t, dd, k, extra)
-        place = count[shape] % DEPTH
-        count[shape] += 1
-        if used[shape][place] is not None:
-            used[shape][place].wait_send()
-        out = work[shape][1]
-        def store(at, value):
-            out[(place,) + at] = value.astype(jnp.bfloat16)
-        add_up(shape, loads, slot, terms, store)
-        copy = remote(t, out.at[place], dst, to, kind)
-        copy.start()
-        used[shape][place] = copy
-
-    def first(t):
-        one = lands[t][1]
-        arrived(t, lands[t][0].at[pl.ds(rings[3] * 4, 4)], SIBLING, (CORNER, 3))
-        for k in (0, 2, 1, 3):
-            to = EAST if k < 2 else NORTH
-            sum_and_send(t, 3, k, [], one.at[k], to, (ONCE, k))
-
-    def second(t):
-        one, land_x, land_y = lands[t][1:4]
-        arrived(t, lands[t][0].at[pl.ds(rings[1] * 4, 4)], SIBLING, (CORNER, 1))
-        arrived(t, lands[t][0].at[pl.ds(rings[2] * 4, 4)], SIBLING, (CORNER, 2))
-        order = ((1, 0), (2, 3), (1, 1), (2, 2), (1, 3), (2, 0), (1, 2), (2, 1))
-        for dd, k in order:
-            to, land = (EAST, land_x) if dd == 1 else (NORTH, land_y)
-            extra = []
-            if (dd == 1) == (k >= 2):
-                arrived(t, one.at[k], NORTH if k >= 2 else EAST, (ONCE, k))
-                extra = [one.at[k]]
-            sum_and_send(t, dd, k, extra, land.at[k], to, (to, k))
-
-    held = {}
-
-    def third(t):
-        land_x, land_y, land_z = lands[t][2:5]
-        arrived(t, lands[t][0].at[pl.ds(rings[0] * 4, 4)], SIBLING, (CORNER, 0))
-        for k in (3, 2, 1, 0):
-            arrived(t, land_x.at[k], EAST, (EAST, k))
-            arrived(t, land_y.at[k], NORTH, (NORTH, k))
-            extra = [land_x.at[k], land_y.at[k]]
-            if k:
-                sum_and_send(t, 0, k, extra, land_z.at[k], (LEVEL, k), (LEVEL, k))
-            else:
-                shape = slots[t]
-                loads, slot, terms = total_of(t, 0, 0, extra)
-                total = work[shape][2]
-                def store(at, value):
-                    total[at] = value
-                add_up(shape, loads, slot, terms, store)
-
-    def last(t):
-        shape = slots[t]
-        land_z = lands[t][4]
-        loads, _, total = work[shape]
-        slot = task[0] % 2
-        task[0] += 1
-        copies = []
-        for k in (1, 2, 3):
-            arrived(t, land_z.at[k], (LEVEL, k), (LEVEL, k))
-            copy = pltpu.make_async_copy(land_z.at[k], loads.at[slot, k - 1], load_sem.at[slot * 4 + k - 1])
-            copy.start()
-            copies.append(copy)
-        for copy in copies:
-            copy.wait()
-        def store(at, value):
-            total[at] = total[at] + value
-        add_up(shape, loads, slot, 3, store)
-        copy = pltpu.make_async_copy(total, finals[t], out_sem)
-        copy.start()
-        copy.wait()
-
-    for dd in (3, 1, 2, 0):
-        give(0, dd)
-    for t in range(n + 1):
-        if t < n:
-            first(t)
-            if t + 1 < n:
-                for dd in (3, 1, 2, 0):
-                    give(t + 1, dd)
-        if t > 0:
-            third(t - 1)
-        if t < n:
-            second(t)
-        if t > 0:
-            last(t - 1)
-    for copy in pending:
-        copy.wait_send()
-    for shape in shapes:
-        for copy in used[shape]:
-            if copy is not None:
-                copy.wait_send()
-
-def scatter(pairs, name="scatter_gradients", collective=1):
-    slots = [tuple(a.shape[1:]) for a, _ in pairs]
-    n = len(slots)
-    shapes = sorted(set(slots))
-    out = [jax.ShapeDtypeStruct(s, jnp.float32) for s in slots]
-    for s in slots:
-        out += [jax.ShapeDtypeStruct((m,) + s, jnp.bfloat16) for m in (16, 4, 4, 4, 4)]
-    scratch = []
-    for s in shapes:
-        scratch += [pltpu.VMEM((2, 4) + s, jnp.bfloat16), pltpu.VMEM((DEPTH,) + s, jnp.bfloat16), pltpu.VMEM(s, jnp.float32)]
-    m = n * len(KINDS)
-    scratch += [pltpu.SemaphoreType.DMA((m,)), pltpu.SemaphoreType.DMA((m,)), pltpu.SemaphoreType.DMA((8,)), pltpu.SemaphoreType.DMA(())]
-    res = pl.pallas_call(
-        partial(scatter_kernel, slots),
-        out_shape=tuple(out),
-        in_specs=[pl.BlockSpec(memory_space=pl.ANY)] * (2 * n),
-        out_specs=tuple(pl.BlockSpec(memory_space=pl.ANY) for _ in out),
-        scratch_shapes=scratch,
-        compiler_params=pltpu.CompilerParams(collective_id=collective, has_side_effects=True, vmem_limit_bytes=48 << 20),
-        name=name,
-    )(*[x for pair in pairs for x in pair])
-    return res[:n]
-
-
 def mm(left, right):
     return jnp.dot(left, right, preferred_element_type=F32)
 
@@ -778,11 +564,6 @@
     return mm_nt(high, table) + mm_nt(rest, table)
 
 
-def whole(shape):
-    zeros = (0,) * len(shape)
-    return pl.BlockSpec(shape, lambda *_: zeros)
-
-
 def head_pair(rows):
     lane = lax.broadcasted_iota(jnp.int32, rows.shape, 1)
     zero = jnp.zeros_like(rows)
@@ -795,265 +576,6 @@
     n = turned.shape[1] // 2
     own = jnp.concatenate([turned[:HDIM, :n], turned[HDIM:, n:]], axis=0)
     return own.T
-
-
-def attend_back_kernel(query, grad, attended, logs, here, beside, away, corner, first_ref,
-                       query_out, here_out, beside_out, away_out, corner_out):
-    first = first_ref[0] == 0
-    half = query.shape[0] // 2
-
-    def rows_of(place):
-        at = slice(place * half, (place + 1) * half)
-        rows, grads = head_pair(query[at]), head_pair(grad[at])
-        product = (grad[at].astype(F32) * attended[at]).T
-        delta = jnp.concatenate(
-            [jnp.sum(product[:HDIM], axis=0, keepdims=True), jnp.sum(product[HDIM:], axis=0, keepdims=True)],
-            axis=1,
-        )
-        return rows, grads, logs[0, place : place + 1], delta
-
-    low, high = rows_of(0), rows_of(1)
-    last_rows = tuple(jnp.where(first, b, a) for a, b in zip(low, high))
-
-    def block(kind, near, part):
-        at = pl.ds(part * half, half)
-        one, two = (here, beside) if near == 0 else (away, corner)
-        return jnp.concatenate([one[kind, at], two[kind, at]], axis=0)
-
-    def back(rows, keys, values):
-        queries, grads, log, delta = rows
-        weights = jnp.exp(mm_nt(keys, queries) - log)
-        pulled = (weights * (mm_nt(values, grads) - delta)).astype(LOW)
-        return (
-            mm_tn(keys, pulled),
-            mm(pulled, queries),
-            mm(weights.astype(LOW), grads),
-        )
-
-    def put(near, part, grad_keys, grad_values):
-        one, two = (here_out, beside_out) if near == 0 else (away_out, corner_out)
-        at = pl.ds(part * half, half)
-        for kind, value in ((0, grad_keys), (1, grad_values)):
-            one[kind, at] = value[:half].astype(one.dtype)
-            two[kind, at] = value[half:].astype(two.dtype)
-
-    keys, values = block(0, 0, 0), block(1, 0, 0)
-    low_query, keys_a, values_a = back(low, keys, values)
-    high_query, keys_b, values_b = back(high, keys, values)
-    put(0, 0, keys_a + keys_b, values_a + values_b)
-    more, keys_a, values_a = back(high, block(0, 0, 1), block(1, 0, 1))
-    high_query = high_query + more
-    put(0, 1, keys_a, values_a)
-    more, keys_a, values_a = back(high, block(0, 1, 0), block(1, 1, 0))
-    high_query = high_query + more
-    keys = jnp.where(first, block(0, 1, 1), block(0, 1, 0))
-    values = jnp.where(first, block(1, 1, 1), block(1, 1, 0))
-    more, keys_b, values_b = back(last_rows, keys, values)
-    zero = jnp.zeros_like(keys_b)
-    put(1, 0, keys_a + jnp.where(first, zero, keys_b), values_a + jnp.where(first, zero, values_b))
-    put(1, 1, jnp.where(first, keys_b, zero), jnp.where(first, values_b, zero))
-    empty = jnp.zeros_like(more)
-    low_query = low_query + jnp.where(first, empty, more)
-    high_query = high_query + jnp.where(first, more, empty)
-    scale_factor = HDIM ** (-0.5)
-    query_out[:half] = (from_pair(low_query) * scale_factor).astype(LOW)
-    query_out[half:] = (from_pair(high_query) * scale_factor).astype(LOW)
-
-
-def attend_back(query, grad, attended, logs, here, beside, away, corner, low_chunk):
-    rows = query.shape[0]
-    pairs = WIDE // 128
-    flat = pl.BlockSpec((rows, 128), lambda p: (0, p))
-    both = pl.BlockSpec((2, rows, 128), lambda p: (0, 0, p))
-    shape = (2, rows, WIDE)
-    return pl.pallas_call(
-        attend_back_kernel,
-        grid=(pairs,),
-        in_specs=[flat, flat, flat, pl.BlockSpec((1, 2, rows), lambda p: (p, 0, 0))] + [both] * 4
-        + [pl.BlockSpec(memory_space=pltpu.SMEM)],
-        out_specs=(flat, both, both, both, both),
-        out_shape=(jax.ShapeDtypeStruct((rows, WIDE), LOW), jax.ShapeDtypeStruct(shape, F32))
-        + tuple(jax.ShapeDtypeStruct(shape, LOW) for _ in range(3)),
-        compiler_params=pltpu.CompilerParams(vmem_limit_bytes=48 << 20),
-        name="attend_back",
-    )(query, grad, attended, logs, here, beside, away, corner, low_chunk.reshape(1))
-
-
-def feed_back_kernel(steps, width, top, slope, middle, gain, table, page, expand, reduce,
-                     hidden_out, bias_out, middle_out, branch_out, attended_out, sums_out,
-                     second, output, sem):
-    step = pl.program_id(0)
-    lead = 4 * width - WIDE
-    extra = 3 * width - lead
-    rows = top.shape[0]
-
-    @pl.when(step == 0)
-    def _():
-        pltpu.make_async_copy(page.at[:, pl.ds(lead, WIDE)], output, sem).start()
-        second[...] = jnp.zeros_like(second)
-
-    hidden = (mm_nt(top[...], reduce[...]) * slope[...].astype(F32)).astype(LOW)
-    hidden_out[...] = hidden
-    bias_out[...] = jnp.sum(hidden.astype(F32), axis=0, keepdims=True)
-    second[...] += mm_nt(hidden, expand[...])
-
-    @pl.when(step == steps - 1)
-    def _():
-        pltpu.make_async_copy(page.at[:, pl.ds(lead, WIDE)], output, sem).wait()
-        upstream = top[...].astype(F32)
-        grad_second = close_up(second[...], table[...])
-        unit, inverse = normal_parts(middle[...])
-        grad_middle = upstream + normal_back(grad_second * gain[...], unit, inverse)
-        middle_out[...] = grad_middle
-        branch = grad_middle.astype(LOW)
-        branch_out[...] = branch
-        full = jnp.concatenate([jnp.zeros((rows, extra), LOW), branch], axis=1)
-        pulled = mm_nt(full, output[...]).astype(LOW)
-        attended_out[:, :width] = mm_nt(pulled, table[...]).astype(LOW)
-        attended_out[:, width:] = jnp.zeros((rows, WIDE - width), LOW)
-
-        def row(value):
-            return jnp.sum(value, axis=0, keepdims=True)
-
-        sums_out[0:1] = row(grad_second * unit)
-        sums_out[1:2] = row(grad_second)
-        sums_out[2:3] = row(branch.astype(F32))
-        sums_out[3:4] = row(upstream)
-        sums_out[4:8] = jnp.zeros((4, width), F32)
-
-
-def feed_back(top, slope, middle, gain, table, page, expand, reduce):
-    rows, width = top.shape
-    inner = expand.shape[1]
-    tile = 256
-    steps = inner // tile
-    flat = whole((rows, width))
-    wide = whole((rows, WIDE))
-    column = pl.BlockSpec((rows, tile), lambda i: (0, i))
-    return pl.pallas_call(
-        partial(feed_back_kernel, steps, width),
-        grid=(steps,),
-        in_specs=[flat, column, flat, whole((1, width)), whole(table.shape),
-                  pl.BlockSpec(memory_space=pl.ANY),
-                  pl.BlockSpec((WIDE, tile), lambda i: (0, i)),
-                  pl.BlockSpec((tile, width), lambda i: (i, 0))],
-        out_specs=(column, pl.BlockSpec((1, tile), lambda i: (0, i)), flat, flat, wide, whole((8, width))),
-        out_shape=(
-            jax.ShapeDtypeStruct((rows, inner), LOW),
-            jax.ShapeDtypeStruct((1, inner), F32),
-            jax.ShapeDtypeStruct((rows, width), F32),
-            jax.ShapeDtypeStruct((rows, width), LOW),
-            jax.ShapeDtypeStruct((rows, WIDE), LOW),
-            jax.ShapeDtypeStruct((8, width), F32),
-        ),
-        scratch_shapes=[pltpu.VMEM((rows, WIDE), F32), pltpu.VMEM((WIDE, WIDE), LOW), pltpu.SemaphoreType.DMA(())],
-        compiler_params=pltpu.CompilerParams(vmem_limit_bytes=48 << 20),
-        name="feed_back",
-    )(top, slope, middle, gain, table, page, expand, reduce)
-
-
-def project_back_kernel(steps, width, query, pair, branch, x, middle, gain, table, page,
-                        mixture_out, result_out, sums_out, mixture, normed):
-    step = pl.program_id(0)
-    tile = page.shape[1]
-    rows = x.shape[0]
-
-    @pl.when(step == 0)
-    def _():
-        mixture[:, :width] = query[:, :width].astype(F32)
-        mixture[:, width : 2 * width] = pair[0, :, :width].astype(F32)
-        mixture[:, 2 * width : 3 * width] = pair[1, :, :width].astype(F32)
-        mixture[:, 3 * width :] = jnp.zeros((rows, width), F32)
-        normed[...] = jnp.zeros_like(normed)
-
-    part = mixture[:, pl.ds(pl.multiple_of(step * tile, tile), tile)].astype(LOW)
-    normed[...] += mm_nt(part, page[...])
-
-    @pl.when(step == steps - 1)
-    def _():
-        grad_normed = close_up(normed[...], table[...])
-        unit, inverse = normal_parts(x[...].astype(F32))
-        result_out[...] = (middle[...] + normal_back(grad_normed * gain[...], unit, inverse)).astype(LOW)
-
-        def row(value):
-            return jnp.sum(value, axis=0, keepdims=True)
-
-        sums_out[0:1] = row(grad_normed * unit)
-        sums_out[1:2] = row(grad_normed)
-        sums_out[2:3] = row(query[:, :width].astype(F32))
-        sums_out[3:4] = row(pair[1, :, :width].astype(F32))
-        sums_out[4:8] = jnp.zeros((4, width), F32)
-        mixture[:, 3 * width :] = branch[...].astype(F32)
-        mixture_out[...] = mixture[...].astype(LOW)
-
-
-def project_back(query, pair, branch, x, middle, gain, table, page):
-    rows, width = x.shape
-    tile, steps = 640, 6
-    flat = whole((rows, width))
-    return pl.pallas_call(
-        partial(project_back_kernel, steps, width),
-        grid=(steps,),
-        in_specs=[whole((rows, WIDE)), whole((2, rows, WIDE)), flat, flat, flat, whole((1, width)),
-                  whole(table.shape), pl.BlockSpec((WIDE, tile), lambda i: (0, i))],
-        out_specs=(whole((rows, 4 * width)), flat, whole((8, width))),
-        out_shape=(
-            jax.ShapeDtypeStruct((rows, 4 * width), LOW),
-            jax.ShapeDtypeStruct((rows, width), LOW),
-            jax.ShapeDtypeStruct((8, width), F32),
-        ),
-        scratch_shapes=[pltpu.VMEM((rows, 4 * width), F32), pltpu.VMEM((rows, WIDE), F32)],
-        compiler_params=pltpu.CompilerParams(vmem_limit_bytes=48 << 20),
-        name="project_back",
-    )(query, pair, branch, x, middle, gain, table, page)
-
-
-def page_kernel(width, normed, attended, mixture, small, out, left_one, left_two):
-    step = pl.program_id(0)
-    tile = mixture.shape[1]
-    edge = 3 * width
-
-    @pl.when(step == 0)
-    def _():
-        left_one[...] = normed[...].T
-        left_two[...] = attended[...].T
-
-    def put(value):
-        value = value.reshape(16, 72, tile)
-        row = lax.broadcasted_iota(jnp.int32, value.shape, 1)
-        out[...] = jnp.where(row == 68, small[...], value).astype(LOW)
-
-    @pl.when((step + 1) * tile <= edge)
-    def _():
-        put(mm(left_one[...], mixture[...]))
-
-    @pl.when(step * tile >= edge)
-    def _():
-        put(mm(left_two[...], mixture[...]))
-
-    @pl.when(((step + 1) * tile > edge) & (step * tile < edge))
-    def _():
-        column = step * tile + lax.broadcasted_iota(jnp.int32, mixture.shape, 1)
-        value = mixture[...]
-        zero = jnp.zeros_like(value)
-        put(mm(left_one[...], jnp.where(column < edge, value, zero))
-            + mm(left_two[...], jnp.where(column < edge, zero, value)))
-
-
-def attention_page(normed, attended, mixture, small):
-    rows, total = mixture.shape
-    tile = 256
-    return pl.pallas_call(
-        partial(page_kernel, total // 4),
-        grid=(total // tile,),
-        in_specs=[whole((rows, WIDE)), whole((rows, WIDE)), pl.BlockSpec((rows, tile), lambda i: (0, i)),
-                  pl.BlockSpec((16, 1, tile), lambda i: (0, 0, i))],
-        out_specs=pl.BlockSpec((16, 72, tile), lambda i: (0, 0, i)),
-        out_shape=jax.ShapeDtypeStruct((16, 72, total), LOW),
-        scratch_shapes=[pltpu.VMEM((WIDE, rows), LOW), pltpu.VMEM((WIDE, rows), LOW)],
-        compiler_params=pltpu.CompilerParams(vmem_limit_bytes=48 << 20),
-        name="attention_page",
-    )(normed, attended, mixture, small)
 
 
 LEAD_ROWS = 144
@@ -1456,6 +978,574 @@
     return res[:count], res[count:]
 
 
+COLUMNS, ROWS, TINY = range(3)
+SIZES = {COLUMNS: (72, 2176), ROWS: (144, 1088), TINY: (8, 128)}
+DEPTH = 6
+SCATTER_KINDS = (
+    [(SIBLING, dd) for dd in range(4)]
+    + [(ONCE, k) for k in range(4)]
+    + [(EAST, k) for k in range(4)]
+    + [(NORTH, k) for k in range(4)]
+    + [(LEVEL, k) for k in (1, 2, 3)]
+    + [(CORNER, 0)]
+)
+SCATTER_NUMBER = {kind: index for index, kind in enumerate(SCATTER_KINDS)}
+
+
+def kind_type(kind):
+    return F32 if kind == TINY else LOW
+
+
+def landing_shapes(kind):
+    return [jax.ShapeDtypeStruct((many,) + SIZES[kind], kind_type(kind)) for many in (16, 4, 4, 4, 4)]
+
+
+def final_shape(kind):
+    return jax.ShapeDtypeStruct({COLUMNS: (72, 4352), ROWS: (272, 1088), TINY: (16, 128)}[kind], F32)
+
+
+def work_shapes(kinds):
+    shapes = []
+    for kind in sorted(set(kinds)):
+        size, held = SIZES[kind], kind_type(kind)
+        shapes += [pltpu.VMEM((2, 4) + size, held), pltpu.VMEM((DEPTH,) + size, held), pltpu.VMEM(size, F32)]
+    count = len(kinds) * len(SCATTER_KINDS)
+    return shapes + [
+        pltpu.SemaphoreType.DMA((count,)), pltpu.SemaphoreType.DMA((count,)),
+        pltpu.SemaphoreType.DMA((8,)), pltpu.SemaphoreType.DMA(()),
+    ]
+
+
+class Scatter:
+    def __init__(self, kinds, pages, lands, finals, owners, refs, place_of):
+        self.kinds, self.pages, self.lands, self.finals, self.owners = kinds, pages, lands, finals, owners
+        self.core, self.rings, self.lines, self.toward = place_of
+        self.work = {}
+        for index, kind in enumerate(sorted(set(kinds))):
+            self.work[kind] = refs[3 * index : 3 * index + 3]
+        self.send_sem, self.recv_sem, self.load_sem, self.out_sem = refs[3 * len(self.work) :]
+        self.turn = 0
+        self.used = {kind: [None] * DEPTH for kind in self.work}
+        self.count = {kind: 0 for kind in self.work}
+        self.given, self.final_sent = [], []
+
+    def remote(self, t, source, target, to, kind):
+        index = t * len(SCATTER_KINDS) + SCATTER_NUMBER[kind]
+        return remote_copy(source, target, self.send_sem.at[index], self.recv_sem.at[index], self.toward[to])
+
+    def part(self, t, core, index, many=None):
+        page, at = self.pages[t], index if many is None else pl.ds(index, many)
+        if self.kinds[t] == COLUMNS:
+            return page.at[at, :, pl.ds(pl.multiple_of(core * 2176, 128), 2176)]
+        if self.kinds[t] == ROWS:
+            return page.at[pl.ds(pl.multiple_of(index * 272 + core * 128, 16), 144)]
+        return page.at[at, pl.ds(pl.multiple_of(core * 8, 8), 8)]
+
+    def landed(self, t, dd):
+        return self.lands[t][0].at[pl.ds(self.rings[dd] * 4, 4)]
+
+    def give(self, t, dd):
+        base = self.rings[dd] * 4
+        if self.kinds[t] == ROWS:
+            for k in range(4):
+                self.remote(t, self.part(t, 1 - self.core, base + k), self.lands[t][0].at[base + k], SIBLING, (SIBLING, dd)).start()
+        else:
+            self.remote(t, self.part(t, 1 - self.core, base, 4), self.landed(t, dd), SIBLING, (SIBLING, dd)).start()
+        self.given.append(self.remote(t, self.landed(t, dd), self.landed(t, dd), SIBLING, (SIBLING, dd)))
+
+    def arrived(self, t, ref, to, kind):
+        self.remote(t, ref, ref, to, kind).wait_recv()
+
+    def load(self, t, sources):
+        loads = self.work[self.kinds[t]][0]
+        slot = self.turn % 2
+        self.turn += 1
+        copies = []
+        for j, source in enumerate(sources):
+            copies.append(pltpu.make_async_copy(source, loads.at[slot, j], self.load_sem.at[slot * 4 + j]))
+        for copy in copies:
+            copy.start()
+        for copy in copies:
+            copy.wait()
+        return loads, slot, len(copies)
+
+    def add_up(self, t, loaded, store):
+        loads, slot, terms = loaded
+        rows, columns = SIZES[self.kinds[t]]
+        wide = self.kinds[t] != ROWS
+        piece = min(256, columns) if wide else 16
+
+        def step(i, _):
+            at = pl.ds(pl.multiple_of(i * piece, piece), piece)
+            where = (slice(None), at) if wide else (at, slice(None))
+            value = loads[(slot, 0) + where].astype(F32)
+            for j in range(1, terms):
+                value = value + loads[(slot, j) + where].astype(F32)
+            store(where, value)
+            return 0
+
+        steps = (columns if wide else rows) // piece
+        lax.fori_loop(0, steps, step, 0)
+        if wide and steps * piece < columns:
+            where = (slice(None), pl.ds(steps * piece, columns - steps * piece))
+            value = loads[(slot, 0) + where].astype(F32)
+            for j in range(1, terms):
+                value = value + loads[(slot, j) + where].astype(F32)
+            store(where, value)
+
+    def sources(self, t, dd, k, extra):
+        index = self.rings[dd] * 4 + self.lines[k]
+        return [self.part(t, self.core, index), self.lands[t][0].at[index]] + extra
+
+    def sum_and_send(self, t, dd, k, extra, target, to, kind):
+        form = self.kinds[t]
+        loaded = self.load(t, self.sources(t, dd, k, extra))
+        place = self.count[form] % DEPTH
+        self.count[form] += 1
+        if self.used[form][place] is not None:
+            self.used[form][place].wait_send()
+        out = self.work[form][1]
+
+        def store(where, value):
+            out[(place,) + where] = value.astype(out.dtype)
+
+        self.add_up(t, loaded, store)
+        copy = self.remote(t, out.at[place], target, to, kind)
+        copy.start()
+        self.used[form][place] = copy
+
+    def first(self, t, k):
+        if k == 0:
+            self.arrived(t, self.landed(t, 3), SIBLING, (SIBLING, 3))
+        self.sum_and_send(t, 3, k, [], self.lands[t][1].at[k], EAST if k < 2 else NORTH, (ONCE, k))
+
+    def second(self, t, dd, k):
+        if (dd, k) in ((1, 0), (2, 3)):
+            self.arrived(t, self.landed(t, dd), SIBLING, (SIBLING, dd))
+        to, land = (EAST, self.lands[t][2]) if dd == 1 else (NORTH, self.lands[t][3])
+        extra = []
+        if (dd == 1) == (k >= 2):
+            one = self.lands[t][1].at[k]
+            self.arrived(t, one, NORTH if k >= 2 else EAST, (ONCE, k))
+            extra = [one]
+        self.sum_and_send(t, dd, k, extra, land.at[k], to, (to, k))
+
+    def third(self, t, k):
+        if k == 3:
+            self.arrived(t, self.landed(t, 0), SIBLING, (SIBLING, 0))
+        extra = []
+        for to, land in ((EAST, self.lands[t][2]), (NORTH, self.lands[t][3])):
+            self.arrived(t, land.at[k], to, (to, k))
+            extra.append(land.at[k])
+        if k:
+            self.sum_and_send(t, 0, k, extra, self.lands[t][4].at[k], (LEVEL, k), (LEVEL, k))
+        else:
+            loaded = self.load(t, self.sources(t, 0, 0, extra))
+            total = self.work[self.kinds[t]][2]
+
+            def store(where, value):
+                total[where] = value
+
+            self.add_up(t, loaded, store)
+
+    def final_part(self, t, core):
+        if self.kinds[t] == COLUMNS:
+            return (slice(None), slice(None)), (slice(None), pl.ds(2176 * core, 2176))
+        if self.kinds[t] == ROWS:
+            return (pl.ds(16 * core, 144 - 16 * core),), (pl.ds(144 * core, 144 - 16 * core),)
+        return (slice(None),), (pl.ds(8 * core, 8),)
+
+    def last(self, t):
+        land = self.lands[t][4]
+        for k in (1, 2, 3):
+            self.arrived(t, land.at[k], (LEVEL, k), (LEVEL, k))
+        loaded = self.load(t, [land.at[k] for k in (1, 2, 3)])
+        total = self.work[self.kinds[t]][2]
+
+        def store(where, value):
+            total[where] = total[where] + value
+
+        self.add_up(t, loaded, store)
+        owner = self.owners[t]
+
+        def act(core):
+            inner, outer = self.final_part(t, core)
+            source, target = total.at[inner], self.finals[t].at[outer]
+            if core == owner:
+                copy = pltpu.make_async_copy(source, target, self.out_sem)
+                copy.start()
+                copy.wait()
+                theirs = self.finals[t].at[self.final_part(t, 1 - core)[1]]
+                self.remote(t, theirs, theirs, SIBLING, (CORNER, 0)).wait_recv()
+            else:
+                copy = self.remote(t, source, target, SIBLING, (CORNER, 0))
+                copy.start()
+                copy.wait_send()
+
+        per_core(self.core, act)
+
+    def steps(self, t):
+        def of(function, *given):
+            return lambda: function(*given)
+
+        return (
+            [of(self.give, t, dd) for dd in (3, 1, 2, 0)],
+            [of(self.first, t, k) for k in (0, 2, 1, 3)],
+            [of(self.second, t, dd, k) for dd, k in ((1, 0), (2, 3), (1, 1), (2, 2), (1, 3), (2, 0), (1, 2), (2, 1))],
+            [of(self.third, t, k) for k in (3, 2, 1, 0)],
+            [of(self.last, t)],
+        )
+
+    def drain(self):
+        for copy in self.given:
+            copy.wait_send()
+        for held in self.used.values():
+            for copy in held:
+                if copy is not None:
+                    copy.wait_send()
+
+
+def backward_kernel(carried, *refs):
+    (top, x, vectors, table, normed_in, query, here, beside, away, corner, attended, logs, attended_low, middle,
+     second, active, slope) = refs[:17]
+    page_hbm, expand_hbm, reduce_hbm = refs[17:20]
+    refs = refs[20:]
+    if carried:
+        carried_page, refs = refs[0], refs[1:]
+    result_out, page_reduce, page_expand, page_attention, page_small = refs[:5]
+    refs = refs[5:]
+    kinds = (COLUMNS, ROWS, COLUMNS, COLUMNS, TINY) if carried else (ROWS, COLUMNS, TINY)
+    owners = (1, 0, 0, 0, 0) if carried else (1, 1, 1)
+    pages = (carried_page, page_reduce, page_expand, page_attention, page_small) if carried else (page_reduce, page_expand, page_small)
+    n = len(kinds)
+    finals, refs = refs[:n], refs[n:]
+    lands, refs = [refs[5 * t : 5 * t + 5] for t in range(n)], refs[5 * n :]
+    (reduce_ring, expand_ring, output, second_sum, left_one, left_two, stage_wide, stage_tall, wide_sum, query_sum,
+     here_sum, beside_give, away_give, corner_give, beside_got, away_got, corner_got, pair, mixture, grad_middle,
+     grad_attended, sums, small, reduce_sem, expand_sem, output_sem, wide_sem, tall_sem, pair_send, pair_recv) = refs[:30]
+    place_of = places()
+    core, rings, lines, toward = place_of
+    scatter = Scatter(kinds, pages, lands, finals, owners, refs[30:], place_of)
+    rows, width = top.shape
+    half = rows // 2
+    first = low_place(lines[0]) == 0
+    tiles = expand_hbm.shape[1] // 256
+    lead = 4 * width - WIDE
+    edge = 3 * width
+
+    def tile_at(i):
+        return pl.ds(pl.multiple_of(i * 256, 256), 256)
+
+    def reduce_copy(i):
+        slot = lax.rem(i, 3)
+        return pltpu.make_async_copy(reduce_hbm.at[tile_at(i)], reduce_ring.at[slot], reduce_sem.at[slot])
+
+    def expand_copy(i, source):
+        slot = lax.rem(i, 3)
+        return pltpu.make_async_copy(source.at[:, tile_at(i)], expand_ring.at[slot], expand_sem.at[slot])
+
+    def wide_copy(i, target):
+        slot = lax.rem(i, 2)
+        return pltpu.make_async_copy(stage_wide.at[slot], target.at[:, :, tile_at(i)], wide_sem.at[slot])
+
+    def tall_copy(i):
+        slot = lax.rem(i, 2)
+        return pltpu.make_async_copy(stage_tall.at[slot], page_reduce.at[tile_at(i)], tall_sem.at[slot])
+
+    for i in range(3):
+        reduce_copy(i).start()
+        expand_copy(i, expand_hbm).start()
+    output_copy = pltpu.make_async_copy(page_hbm.at[:, pl.ds(lead, WIDE)], output, output_sem)
+    output_copy.start()
+    greet(toward)
+    todo = []
+
+    def progress(count):
+        for _ in range(count):
+            if todo:
+                todo.pop(0)()
+
+    if carried:
+        steps = [scatter.steps(t) for t in range(n)]
+        todo += steps[0][0] + steps[0][1] + steps[0][2]
+    progress(4)
+    left_one[...] = second[...].T
+    second_sum[...] = jnp.zeros_like(second_sum)
+
+    def feed_tile(i, _):
+        at = tile_at(i)
+        slot, side = lax.rem(i, 3), lax.rem(i, 2)
+        reduce_copy(i).wait()
+        hidden = (mm_nt(top[...], reduce_ring[slot]) * slope[:, at].astype(F32)).astype(LOW)
+        wide_sum[0:1, at] = jnp.sum(hidden.astype(F32), axis=0, keepdims=True)
+        expand_copy(i, expand_hbm).wait()
+        second_sum[...] += mm_nt(hidden, expand_ring[slot])
+
+        @pl.when(i + 3 < tiles)
+        def _():
+            reduce_copy(i + 3).start()
+            expand_copy(i + 3, expand_hbm).start()
+
+        @pl.when(i >= 2)
+        def _():
+            wide_copy(i - 2, page_expand).wait()
+            tall_copy(i - 2).wait()
+
+        stage_wide[side] = mm(left_one[...], hidden).reshape(16, 72, 256).astype(LOW)
+        stage_tall[side] = mm_tn(active[:, at], top[...]).astype(LOW)
+        wide_copy(i, page_expand).start()
+        tall_copy(i).start()
+        return 0
+
+    for begin_at in range(0, tiles, 3):
+        lax.fori_loop(begin_at, min(begin_at + 3, tiles), feed_tile, 0)
+        progress(3)
+    for i in (tiles - 2, tiles - 1):
+        wide_copy(i, page_expand).wait()
+        tall_copy(i).wait()
+    if carried:
+        todo += steps[1][0] + steps[2][0] + steps[1][1] + steps[0][3] + steps[1][2] + steps[2][1] + steps[0][4]
+        todo += steps[1][3] + steps[2][2] + steps[1][4] + steps[2][3] + steps[2][4]
+    else:
+        steps = [scatter.steps(t) for t in range(n)]
+        todo += steps[0][0] + steps[1][0] + steps[0][1] + steps[0][2] + steps[1][1] + steps[0][3] + steps[1][2]
+        todo += steps[0][4] + steps[1][3] + steps[1][4]
+    progress(8)
+    for i in range(3):
+        expand_copy(i, page_hbm).start()
+
+    def row(value):
+        return jnp.sum(value, axis=0, keepdims=True)
+
+    upstream = top[...].astype(F32)
+    grad_second = close_up(second_sum[...], table[...])
+    unit, inverse = normal_parts(middle[...])
+    sums[6:7] = row(grad_second * unit)
+    sums[7:8] = row(grad_second)
+    sums[5:6] = row(upstream)
+    value = upstream + normal_back(grad_second * vectors[6:7], unit, inverse)
+    grad_middle[...] = value
+    branch = value.astype(LOW)
+    sums[4:5] = row(branch.astype(F32))
+    progress(2)
+    mixture[:, edge:] = branch.astype(F32)
+    output_copy.wait()
+    full = jnp.concatenate([jnp.zeros((rows, edge - lead), LOW), branch], axis=1)
+    pulled = mm_nt(full, output[...]).astype(LOW)
+    grad_attended[:, :width] = mm_nt(pulled, table[...]).astype(LOW)
+    grad_attended[:, width:] = jnp.zeros((rows, WIDE - width), LOW)
+    progress(2)
+
+    def rows_of(place, at, p):
+        part = slice(place * half, (place + 1) * half)
+        product = (grad_attended[part, at].astype(F32) * attended[part, at]).T
+        delta = jnp.concatenate([row(product[:HDIM]), row(product[HDIM:])], axis=1)
+        return head_pair(query[part, at]), head_pair(grad_attended[part, at]), logs[p, place : place + 1], delta
+
+    def block(kind, near, part, at):
+        rows_at = pl.ds(part * half, half)
+        one, two = (here, beside) if near == 0 else (away, corner)
+        return jnp.concatenate([one[kind, rows_at, at], two[kind, rows_at, at]], axis=0)
+
+    def back(own, keys, values):
+        queries, grads, log, delta = own
+        weights = jnp.exp(mm_nt(keys, queries) - log)
+        lowered = (weights * (mm_nt(values, grads) - delta)).astype(LOW)
+        return mm_tn(keys, lowered), mm(lowered, queries), mm(weights.astype(LOW), grads)
+
+    def put(one, two, part, at, grads):
+        rows_at = pl.ds(part * half, half)
+        for kind, value in enumerate(grads):
+            one[kind, rows_at, at] = value[:half].astype(one.dtype)
+            two[kind, rows_at, at] = value[half:].astype(two.dtype)
+
+    def far_pair(p, _):
+        at = pl.ds(pl.multiple_of(p * 128, 128), 128)
+        low, high = rows_of(0, at, p), rows_of(1, at, p)
+        last_rows = tuple(jnp.where(first, b, a) for a, b in zip(low, high))
+        keys, values = block(0, 1, 0, at), block(1, 1, 0, at)
+        high_query, keys_a, values_a = back(high, keys, values)
+        last_keys = jnp.where(first, block(0, 1, 1, at), keys)
+        last_values = jnp.where(first, block(1, 1, 1, at), values)
+        more, keys_b, values_b = back(last_rows, last_keys, last_values)
+        zero, empty = jnp.zeros_like(keys_b), jnp.zeros_like(more)
+        put(away_give, corner_give, 0, at,
+            (keys_a + jnp.where(first, zero, keys_b), values_a + jnp.where(first, zero, values_b)))
+        put(away_give, corner_give, 1, at, (jnp.where(first, keys_b, zero), jnp.where(first, values_b, zero)))
+        query_sum[:half, at] = from_pair(jnp.where(first, empty, more))
+        query_sum[half:, at] = from_pair(high_query + jnp.where(first, more, empty))
+        return 0
+
+    for begin_at in (0, 3, 6):
+        lax.fori_loop(begin_at, begin_at + 3, far_pair, 0)
+        progress(2)
+
+    def pair_copy(source, target, to, number):
+        return remote_copy(source, target, pair_send.at[number], pair_recv.at[number], toward[to])
+
+    to_corner = pair_copy(corner_give, corner_got, SIBLING, 0)
+    to_away = pair_copy(away_give, away_got, (LEVEL, 1), 1)
+    to_beside = pair_copy(beside_give, beside_got, SIBLING, 2)
+    to_corner.start()
+
+    def near_pair(p, _):
+        at = pl.ds(pl.multiple_of(p * 128, 128), 128)
+        low, high = rows_of(0, at, p), rows_of(1, at, p)
+        keys, values = block(0, 0, 0, at), block(1, 0, 0, at)
+        low_query, keys_a, values_a = back(low, keys, values)
+        high_query, keys_b, values_b = back(high, keys, values)
+        put(here_sum, beside_give, 0, at, (keys_a + keys_b, values_a + values_b))
+        more, keys_a, values_a = back(high, block(0, 0, 1, at), block(1, 0, 1, at))
+        put(here_sum, beside_give, 1, at, (keys_a, values_a))
+        query_sum[:half, at] += from_pair(low_query)
+        query_sum[half:, at] += from_pair(high_query + more)
+        return 0
+
+    lax.fori_loop(0, 3, near_pair, 0)
+    to_corner.wait_recv()
+    for kind in (0, 1):
+        away_give[kind] = (away_give[kind].astype(F32) + corner_got[kind].astype(F32)).astype(LOW)
+    to_away.start()
+    progress(2)
+    for begin_at in (3, 6):
+        lax.fori_loop(begin_at, begin_at + 3, near_pair, 0)
+        progress(2)
+    to_beside.start()
+    mixture[:, :width] = (query_sum[:, :width] * HDIM ** (-0.5)).astype(LOW).astype(F32)
+    sums[2:3] = row(mixture[:, :width])
+    left_one[...] = normed_in[...].T
+    left_two[...] = attended_low[...].T
+    second_sum[...] = jnp.zeros_like(second_sum)
+    progress(4)
+    to_beside.wait_recv()
+    to_away.wait_recv()
+    for kind in (0, 1):
+        value = here_sum[kind] + beside_got[kind].astype(F32) + away_got[kind].astype(F32)
+        mixture[:, (1 + kind) * width : (2 + kind) * width] = value[:, :width].astype(LOW).astype(F32)
+    sums[3:4] = row(mixture[:, 2 * width : edge])
+
+    def project_tile(i, _):
+        at = tile_at(i)
+        slot = lax.rem(i, 3)
+        column = i * 256 + lax.broadcasted_iota(jnp.int32, (rows, 256), 1)
+        part = jnp.where(column < edge, mixture[:, at], 0.0).astype(LOW)
+        expand_copy(i, page_hbm).wait()
+        second_sum[...] += mm_nt(part, expand_ring[slot])
+
+        @pl.when(i + 3 < 13)
+        def _():
+            expand_copy(i + 3, page_hbm).start()
+
+        return 0
+
+    for begin_at, end in ((0, 4), (4, 8), (8, 13)):
+        lax.fori_loop(begin_at, end, project_tile, 0)
+        progress(2)
+    grad_normed = close_up(second_sum[...], table[...])
+    unit, inverse = normal_parts(x[...].astype(F32))
+    sums[0:1] = row(grad_normed * unit)
+    sums[1:2] = row(grad_normed)
+    result_out[...] = (grad_middle[...] + normal_back(grad_normed * vectors[0:1], unit, inverse)).astype(LOW)
+    progress(2)
+
+    def page_tile(number, i):
+        side = lax.rem(i, 2)
+        at = tile_at(i)
+
+        @pl.when(i >= 2)
+        def _():
+            wide_copy(i - 2, page_attention).wait()
+
+        part = mixture[:, at]
+        if number == 1:
+            value = mm(left_one[...], part.astype(LOW))
+        elif number == 2:
+            value = mm(left_two[...], part.astype(LOW))
+        else:
+            column = i * 256 + lax.broadcasted_iota(jnp.int32, (rows, 256), 1)
+            value = mm(left_one[...], jnp.where(column < edge, part, 0.0).astype(LOW))
+            value = value + mm(left_two[...], jnp.where(column < edge, 0.0, part).astype(LOW))
+        stage_wide[side] = value.reshape(16, 72, 256).astype(LOW)
+        wide_copy(i, page_attention).start()
+
+    def page_loop(number, begin_at, end):
+        def step(i, _):
+            page_tile(number, i)
+            return 0
+
+        lax.fori_loop(begin_at, end, step, 0)
+
+    whole_tiles = edge // 256
+    for begin_at in range(0, whole_tiles, 4):
+        page_loop(1, begin_at, begin_at + 4)
+        progress(2)
+    page_loop(3, whole_tiles, whole_tiles + 1)
+    page_loop(2, whole_tiles + 1, tiles)
+    small[...] = jnp.zeros_like(small)
+    for shard in range(16):
+        small[shard, 0:8, 0:68] = sums[:, shard * 68 : (shard + 1) * 68]
+        for part in range(4):
+            begin_at = shard * 272 + part * 68
+            small[shard, 8 + part : 9 + part, 0:68] = wide_sum[0:1, begin_at : begin_at + 68]
+    small_copy = pltpu.make_async_copy(small, page_small, output_sem)
+    small_copy.start()
+    for i in (tiles - 2, tiles - 1):
+        wide_copy(i, page_attention).wait()
+    small_copy.wait()
+    tiny = steps[n - 1]
+    if carried:
+        own = steps[3]
+        todo = own[0] + tiny[0] + todo + own[1] + own[2] + tiny[1] + tiny[2] + own[3] + tiny[3] + tiny[4] + own[4]
+    else:
+        todo = tiny[0] + todo + tiny[1] + tiny[2] + tiny[3] + tiny[4]
+    for task in todo:
+        task()
+    scatter.drain()
+    for copy in (to_corner, to_away, to_beside):
+        copy.wait_send()
+
+
+def backward(top, saved, vectors, table, page, expand, reduce, carried_page=None):
+    source, normed, query = saved[:3]
+    rows, width = top.shape
+    inner = expand.shape[1]
+    anywhere = pl.BlockSpec(memory_space=pl.ANY)
+    inside = pl.BlockSpec(memory_space=pltpu.VMEM)
+    carried = carried_page is not None
+    kinds = (COLUMNS, ROWS, COLUMNS, COLUMNS, TINY) if carried else (ROWS, COLUMNS, TINY)
+    outs = [
+        jax.ShapeDtypeStruct((rows, width), LOW), jax.ShapeDtypeStruct(reduce.shape, LOW),
+        jax.ShapeDtypeStruct((16, 72, inner), LOW), jax.ShapeDtypeStruct((16, 72, inner), LOW),
+        jax.ShapeDtypeStruct((16, 16, 128), F32),
+    ]
+    outs += [final_shape(kind) for kind in kinds]
+    for kind in kinds:
+        outs += landing_shapes(kind)
+    pair = pltpu.VMEM((2, rows, WIDE), LOW)
+    tall = pltpu.VMEM((WIDE, rows), LOW)
+    dma = pltpu.SemaphoreType.DMA
+    scratch = [
+        pltpu.VMEM((3, 256, width), LOW), pltpu.VMEM((3, WIDE, 256), LOW), pltpu.VMEM((WIDE, WIDE), LOW),
+        pltpu.VMEM((rows, WIDE), F32), tall, tall, pltpu.VMEM((2, 16, 72, 256), LOW), pltpu.VMEM((2, 256, width), LOW),
+        pltpu.VMEM((8, inner), F32), pltpu.VMEM((rows, WIDE), F32), pltpu.VMEM((2, rows, WIDE), F32),
+        pair, pair, pair, pair, pair, pair, pltpu.VMEM((8, 128), F32), pltpu.VMEM((rows, inner), F32),
+        pltpu.VMEM((rows, width), F32), pltpu.VMEM((rows, WIDE), LOW), pltpu.VMEM((8, width), F32),
+        pltpu.VMEM((16, 16, 128), F32), dma((3,)), dma((3,)), dma(()), dma((2,)), dma((2,)), dma((3,)), dma((3,)),
+    ] + work_shapes(kinds)
+    res = pl.pallas_call(
+        partial(backward_kernel, carried),
+        out_shape=tuple(outs),
+        in_specs=[inside] * 17 + [anywhere] * (4 if carried else 3),
+        out_specs=(inside,) + (anywhere,) * (len(outs) - 1),
+        scratch_shapes=scratch,
+        compiler_params=pltpu.CompilerParams(
+            collective_id=4 if carried else 5, has_side_effects=True, vmem_limit_bytes=62 << 20
+        ),
+        name="backward_sum" if carried else "backward",
+    )(top, source, vectors, table, *saved[1:], page, expand, reduce, *((carried_page,) if carried else ()))
+    return res[0], res[3], res[5 : 5 + len(kinds)]
+
+
 def spread(width):
     row = lax.broadcasted_iota(jnp.int32, (width, 16 * 72), 0)
     column = lax.broadcasted_iota(jnp.int32, (width, 16 * 72), 1)
@@ -1471,35 +1561,6 @@
 def layer_forward(source, small, wide, weights, table, shards=None):
     saved, gathered = forward(source, small, wide, table, *weights, shards=shards)
     return saved[13], (source,) + tuple(saved[:13]), gathered
-
-
-def layer_gradient(top, saved, small, weights, low_chunk, table):
-    source, normed, query = saved[:3]
-    pairs = saved[3:7]
-    attended, logs, attended_low, middle, second, active, slope = saved[7:]
-    page, expand, reduce = weights
-    width = top.shape[1]
-    grad_hidden, sum_wide, grad_middle, branch, grad_attended, late = feed_back(
-        top, slope, middle, small[6:7], table, page, expand, reduce
-    )
-    grad_query, near, beside, away, corner = attend_back(
-        query, grad_attended, attended, logs, *pairs, low_chunk
-    )
-    away = (away.astype(F32) + swapped(corner, SECTION, 1).astype(F32)).astype(LOW)
-    near = near + swapped(beside, SECTION, 1).astype(F32)
-    near = (near + swapped(away, LINE, 1).astype(F32)).astype(LOW)
-    mixture, result, early = project_back(
-        grad_query, near, branch, source, grad_middle, small[:1], table, page
-    )
-    order = (early[0], early[1], early[2], early[3], late[2], late[3], late[0], late[1])
-    packed = jnp.stack([vector.reshape(16, -1) for vector in order], axis=1)
-    packed = jnp.concatenate([packed, sum_wide.reshape(16, 4, -1)], axis=1)
-    packed = packed.reshape(16, 1, -1).astype(LOW)
-    packed = jnp.pad(packed, ((0, 0), (0, 0), (0, 4 * width - packed.shape[2])))
-    page_attention = attention_page(normed, attended_low, mixture, packed)
-    page_expand = mm_tn(second, grad_hidden).astype(LOW).reshape(16, 72, -1)
-    page_reduce = mm_tn(active, top).astype(LOW).reshape(16, -1, width)
-    return result, page_attention, page_expand, page_reduce
 
 
 def four_by_four(
@@ -1569,26 +1630,17 @@
     small, wide, weights = layers[1]
     final_rows, saved_upper, _ = layer_forward(middle_rows, small, wide, weights, table)
     layer_outputs = from_rows(middle_rows, final_rows, core, line)
-    upper_grad, upper_attention, upper_expand, upper_reduce = layer_gradient(
-        top, saved_upper, small, weights, low_chunk, table
-    )
+    upper_grad, upper_attention, upper_sums = backward(top, saved_upper, small, table, *weights)
     small, wide, weights = layers[0]
-    lower_grad, lower_attention, lower_expand, lower_reduce = layer_gradient(
-        upper_grad, saved_lower, small, weights, low_chunk, table
+    lower_grad, _, lower_sums = backward(
+        upper_grad, saved_lower, small, table, *weights, carried_page=upper_attention
     )
     input_grads = from_rows(lower_grad, upper_grad, core, line)
-    lower_sum, reduce_sum, upper_sum = scatter(
-        [
-            (lower_attention, lower_expand),
-            (lower_reduce, upper_reduce),
-            (upper_attention, upper_expand),
-        ]
-    )
-    kept = jnp.where(core == 0, lower_sum, upper_sum)
-    other = swapped(jnp.where(core == 0, upper_sum, lower_sum), SECTION, 1)
-    attention_sum = jnp.where(core == 0, kept, other)
-    expand_sum = jnp.where(core == 0, other, kept)
-    vectors = attention_sum[68, : 12 * 68].reshape(12, 68)
+    own = core == 0
+    attention_sum = jnp.where(own, lower_sums[3], lower_sums[0])
+    expand_sum = jnp.where(own, lower_sums[2], upper_sums[1])
+    reduce_sum = jnp.where(own, lower_sums[1], upper_sums[0])
+    vectors = jnp.where(own, lower_sums[4], upper_sums[2])[:12, :68]
     return (
         layer_outputs,
         input_grads,

time: 1050 us -> 978 us (0.931)
  the two profiles are of different devices: /device:TPU:0 before, /device:TPU:9 now
where the time goes in v4:
time: 978 us; the launch traced here: 965 us
  Pallas kernels  853 us (87%)
  waiting for transfers between devices  57.5 us (6%)
  local copies, waits for them, and re-layouts  25 us (3%)
  other arithmetic  20.7 us (2%)
    pallas_call x2, Pallas kernels, backward(): pl.pallas_call(partial(backward_kernel, carried), out_shape=tuple(outs),...  448 us
    pallas_call x2, Pallas kernels, forward(): pl.pallas_call(partial(forward_kernel, extra), out_shape=tuple(outs), in_...  245 us
    pallas_call x1, Pallas kernels, gather_pages(): pl.pallas_call(gather_kernel, out_shape=tuple(gather_shapes(shards)), in_...  160 us
    ppermute x8, waiting for transfers between devices, swapped(): lax.ppermute(value, axis, [(source, source ^ bits) for source in range(co...  57.5 us
  transfers between devices with their start and end apart: 8, of which 4 were waited for; matrix products, arithmetic and copies ran while one was open for 3% of the time, Pallas kernels for 0%

profile of v4, /device:TPU:9, one launch (start us, length us, event | category | flops | bytes accessed | tf_op | source)
XLA Modules:
  0.0 965.1 jit_solution(3431771130197255929)
XLA Ops:
  7.7 2.9 fusion.1.refs_3_
  11.0 12.9 %collective-permute-done = bf16[128,1088]{1,0:T(8,128)(2,1)} collective-permute-done((bf16[128,1088]{1,0:T(8,128)(2,1)}, bf16[128,1088]{1,0:T(8,128)(2,1)}, u32[]{:S(2)}, u32[]{:S(2)}) %collective-permute-start) | collective-permute-done | bytes 278560 | tf_op jit(solution)/shard_map/ppermute | solution.py:446
  24.9 5.3 collective-permute-done.5
  33.0 2.3 broadcast_select_fusion
  35.3 1.4 broadcast_select_fusion.3
  36.6 159.6 %gather_pages.1 = (bf16[16,72,4352]{2,1,0:T(8,128)(2,1)}, bf16[16,72,4352]{2,1,0:T(8,128)(2,1)}, bf16[16,272,1088]{2,1,0:T(8,128)(2,1)}) custom-call(bf16[72,4352]{1,0:T(8,128)(2,1)} %get-tuple-element.165.refs_0_, bf16[272,1088]{1,0:T(8,128)(2,1)} %get-tuple-element.159.refs_1_), custom_call_target="tpu_custom_call" | custom-call | tf_op jit(solution)/shard_map/gather_pages/pallas_call | solution.py:741
  199.0 170.8 %forward_gather.1 = (bf16[256,1152]{1,0:T(8,128)(2,1)}, bf16[256,1152]{1,0:T(8,128)(2,1)}, bf16[2,256,1152]{2,1,0:T(8,128)(2,1)}, bf16[2,256,1152]{2,1,0:T(8,128...) custom-call(bf16[256,1088]{1,0:T(8,128)(2,1)} %pad_maximum_fusion.5., ...), custom_call_target="tpu_custom_call" | custom-call | tf_op jit(solution)/shard_map/forward_gather/pallas_call | solution.py:967
  372.6 74.3 %forward.1 = (bf16[256,1152]{1,0:T(8,128)(2,1)}, bf16[256,1152]{1,0:T(8,128)(2,1)}, bf16[2,256,1152]{2,1,0:T(8,128)(2,1)}, bf16[2,256,1152]{2,1,0:T(8,128)(2,1)}...) custom-call(bf16[256,1088]{1,0:T(8,128)(2,1)} %get-tuple-element.63., ...), custom_call_target="tpu_custom_call" | custom-call | tf_op jit(solution)/shard_map/forward/pallas_call | solution.py:967
  446.9 178.2 %backward.1 = (bf16[256,1088]{1,0:T(8,128)(2,1)}, bf16[4352,1088]{1,0:T(8,128)(2,1)}, bf16[16,72,4352]{2,1,0:T(8,128)(2,1)}, bf16[16,72,4352]{2,1,0:T(8,128)(2,1...) custom-call(bf16[256,1088]{1,0:T(8,128)(2,1)} %pad_maximum_fusion.6., ...), custom_call_target="tpu_custom_call" | custom-call | tf_op jit(solution)/shard_map/backward/pallas_call | solution.py:1535
  625.1 269.8 %backward_sum.1 = (bf16[256,1088]{1,0:T(8,128)(2,1)}, bf16[4352,1088]{1,0:T(8,128)(2,1)}, bf16[16,72,4352]{2,1,0:T(8,128)(2,1)}, bf16[16,72,4352]{2,1,0:T(8,128)...) custom-call(bf16[256,1088]{1,0:T(8,128)(2,1)} %get-tuple-element.81., ...), custom_call_target="tpu_custom_call" | custom-call | tf_op jit(solution)/shard_map/backward_sum/pallas_call | solution.py:1535
  894.9 1.4 broadcast_select_fusion.2
  898.2 2.2 copy.89
  900.5 1.8 copy.87
  907.3 2.5 select_bitcast_fusion
  909.7 32.5 %collective-permute-done.6 = bf16[2,128,1088]{1,2,0:T(8,128)(2,1)} collective-permute-done((bf16[2,128,1088]{1,2,0:T(8,128)(2,1)S(1)}, bf16[2,128,1088]{1,2,0:T(8,128)(2,1)}, u32[]{:S(2)}, u32[]{:S(2)}) %collective-permute-start.6) | collective-permute-done | bytes 557088 | tf_op jit(solution)/shard_map/ppermute | solution.py:446
  942.2 1.3 copy.78
  945.0 2.3 collective-permute-start.7
  947.3 6.8 collective-permute-done.3
  955.5 1.5 select_bitcast_fusion.5
  957.4 1.4 collective-permute-start.4
  958.8 1.3 copy.83
  960.5 1.4 copy.86
  961.9 1.3 copy.73
  963.5 1.4 copy.85
  (110 shorter events, 27.0 us)
Async XLA Ops:
  0.7 3.5 copy-start.13
  0.7 3.6 copy-start.20
  0.7 3.6 copy-start.21
  0.7 3.6 copy-start.14
  0.7 3.6 copy-start.15
  0.7 3.6 copy-start.16
  0.7 3.6 copy-start.17
  0.7 3.6 copy-start.18
  0.7 3.6 copy-start.19
  0.7 3.7 copy-start.2
  0.8 3.7 copy-start.5
  0.8 3.7 copy-start.8
  2.0 4.5 copy-start.9
  2.9 21.0 %collective-permute-start = (bf16[128,1088]{1,0:T(8,128)(2,1)}, bf16[128,1088]{1,0:T(8,128)(2,1)}, u32[]{:S(2)}, u32[]{:S(2)}) collective-permute-start(bf16[128,1088]{1,0:T(8,128)(2,1)} %bitcast.1), channel_id=1, source_target_pairs={{0,3},{1,2},{2,1},{3,0},{4,7},{5,6},{6,5},{7,4},{8,11},{9,10},{10,... | collective-permute-start | bytes 835592 | tf_op jit(solution)/shard_map/ppermute | solution.py:446
  4.4 2.1 copy-start.10
  5.5 29.8 %collective-permute-start.1 = (bf16[72,4352]{1,0:T(8,128)(2,1)}, bf16[72,4352]{1,0:T(8,128)(2,1)S(1)}, u32[]{:S(2)}, u32[]{:S(2)}) collective-permute-start(bf16[72,4352]{1,0:T(8,128)(2,1)} %broadcast_select_fusion.5), channel_id=1, source_target_pairs={{0,16},{16,0},{1,17},{17,1},{2,18},{18,2},{3,19},{19,3},{4,20},{20... | collective-permute-start | bytes 1880072 | tf_op jit(solution)/shard_map/ppermute | solution.py:446
  6.4 26.6 %collective-permute-start.2 = (bf16[272,1088]{1,0:T(8,128)(2,1)S(1)}, bf16[272,1088]{1,0:T(8,128)(2,1)}, u32[]{:S(2)}, u32[]{:S(2)}) collective-permute-start(bf16[272,1088]{1,0:T(8,128)(2,1)S(1)} %bitcast.110), channel_id=1, source_target_pairs={{0,16},{16,0},{1,17},{17,1},{2,18},{18,2},{3,19},{19,3},{4,20},{20... | collective-permute-start | bytes 1775624 | tf_op jit(solution)/shard_map/ppermute | solution.py:446
  7.4 22.8 %collective-permute-start.5 = (bf16[128,1088]{1,0:T(8,128)(2,1)}, bf16[128,1088]{1,0:T(8,128)(2,1)}, u32[]{:S(2)}, u32[]{:S(2)}) collective-permute-start(bf16[128,1088]{1,0:T(8,128)(2,1)} %bitcast.115), channel_id=1, source_target_pairs={{0,3},{1,2},{2,1},{3,0},{4,7},{5,6},{6,5},{7,4},{8,11},{9,10},{10,... | collective-permute-start | bytes 835592 | tf_op jit(solution)/shard_map/ppermute | solution.py:446
  900.4 3.5 copy-start.1
  900.4 3.5 copy-start.4
  904.5 37.7 %collective-permute-start.6 = (bf16[2,128,1088]{1,2,0:T(8,128)(2,1)S(1)}, bf16[2,128,1088]{1,2,0:T(8,128)(2,1)}, u32[]{:S(2)}, u32[]{:S(2)}) collective-permute-start(bf16[2,128,1088]{1,2,0:T(8,128)(2,1)S(1)} %copy.77), channel_id=1, source_target_pairs={{0,3},{1,2},{2,1},{3,0},{4,7},{5,6},{6,5},{7,4},{8,11},{9,10},{10,... | collective-permute-start | bytes 1671176 | tf_op jit(solution)/shard_map/ppermute | solution.py:446
  906.6 47.6 %collective-permute-start.3 = (bf16[2,128,1088]{1,2,0:T(8,128)(2,1)}, bf16[2,128,1088]{1,2,0:T(8,128)(2,1)}, u32[]{:S(2)}, u32[]{:S(2)}) collective-permute-start(bf16[2,128,1088]{1,2,0:T(8,128)(2,1)} %copy.68), channel_id=1, source_target_pairs={{0,3},{1,2},{2,1},{3,0},{4,7},{5,6},{6,5},{7,4},{8,11},{9,10},{10,... | collective-permute-start | bytes 1671176 | tf_op jit(solution)/shard_map/ppermute | solution.py:446
  945.0 13.8 %collective-permute-start.7 = (bf16[2,128,1088]{1,2,0:T(8,128)(2,1)}, bf16[2,128,1088]{1,2,0:T(8,128)(2,1)}, u32[]{:S(2)}, u32[]{:S(2)}) collective-permute-start(bf16[2,128,1088]{1,2,0:T(8,128)(2,1)} %copy.82), channel_id=1, source_target_pairs={{0,16},{16,0},{1,17},{17,1},{2,18},{18,2},{3,19},{19,3},{4,20},{20... | collective-permute-start | bytes 1671176 | tf_op jit(solution)/shard_map/ppermute | solution.py:446
  957.4 4.5 collective-permute-start.4
  (6 other events, 7.1 us)

commit v5 on v4

--- a/solution.py
+++ b/solution.py
@@ -14,7 +14,7 @@
 F32, LOW = jnp.float32, jnp.bfloat16
 SECTION, RING, LINE = "section", "dp", "seq"
 OWNERS = (RING, LINE)
-EAST, NORTH, LEVEL, SIBLING, CORNER, ONCE = range(6)
+EAST, NORTH, LEVEL, SIBLING, CORNER, ONCE, UP, DOWN = range(8)
 
 
 epsilon = 1e-05
@@ -441,43 +441,6 @@
     return (layer_outputs, input_grads) + tuple((portion[None] for portion in shares))
 
 
-def swapped(value, axis, bits):
-    count = lax.axis_size(axis)
-    return lax.ppermute(value, axis, [(source, source ^ bits) for source in range(count)])
-
-
-def to_rows(array, core, line):
-    half = array.shape[1] // 2
-    which = line // 2
-
-    def part(index):
-        return lax.dynamic_slice(
-            array, (index, core * half, 0), (1, half, array.shape[2])
-        )[0]
-
-    mine, arrived = part(which), swapped(part(1 - which), LINE, 3)
-    low_side = which == 0
-    return jnp.concatenate(
-        [jnp.where(low_side, mine, arrived), jnp.where(low_side, arrived, mine)], axis=0
-    )
-
-
-def from_rows(lower, upper, core, line):
-    half = lower.shape[0] // 2
-    low_side = line // 2 == 0
-    both = jnp.stack([lower, upper])
-    mine = jnp.where(low_side, both[:, :half], both[:, half:])
-    arrived = swapped(jnp.where(low_side, both[:, half:], both[:, :half]), LINE, 3)
-    pair = jnp.stack(
-        [jnp.where(low_side, mine, arrived), jnp.where(low_side, arrived, mine)], axis=1
-    )
-    kept = jnp.where(core == 0, pair[0], pair[1])
-    other = swapped(jnp.where(core == 0, pair[1], pair[0]), SECTION, 1)
-    return jnp.concatenate(
-        [jnp.where(core == 0, kept, other), jnp.where(core == 0, other, kept)], axis=1
-    )[None]
-
-
 def flip(place, bits):
     return {1: place + 1 - 2 * (place % 2), 2: (place + 2) % 4, 3: 3 - place}[bits]
 
@@ -492,6 +455,9 @@
         (LEVEL, 1): {LINE: lines[1]},
         (LEVEL, 2): {LINE: lines[2]},
         (LEVEL, 3): {LINE: lines[3]},
+        (CORNER, 3): {SECTION: 1 - core, LINE: lines[3]},
+        (LEVEL, UP): {LINE: (line + 1) % 4},
+        (LEVEL, DOWN): {LINE: (line + 3) % 4},
         SIBLING: {SECTION: 1 - core},
     }
     return core, rings, lines, toward
@@ -499,9 +465,10 @@
 
 def greet(toward):
     barrier = pltpu.get_barrier_semaphore()
-    for to in toward.values():
+    partners = [to for name, to in toward.items() if name not in ((LEVEL, UP), (LEVEL, DOWN))]
+    for to in partners:
         pl.semaphore_signal(barrier, inc=1, device_id=to, device_id_type=pl.DeviceIdType.MESH)
-    pl.semaphore_wait(barrier, len(toward))
+    pl.semaphore_wait(barrier, len(partners))
 
 
 def remote_copy(source, target, send_sem, recv_sem, to):
@@ -523,12 +490,9 @@
             act(index)
 
 
-GATHER_KINDS = (
-    [(LEVEL, k) for k in (1, 2, 3)]
-    + [(name, k) for name in (EAST, NORTH, CORNER) for k in range(4)]
-    + [(SIBLING, k) for k in range(4)]
-)
-GATHER_NUMBER = {kind: index for index, kind in enumerate(GATHER_KINDS)}
+GATHER_KINDS = (UP, DOWN, EAST, NORTH, CORNER, SIBLING)
+GATHER_NUMBER = {kind: 4 * index for index, kind in enumerate(GATHER_KINDS)}
+GATHER_SPAN = 4 * len(GATHER_KINDS)
 
 
 def mm(left, right):
@@ -579,190 +543,281 @@
 
 
 LEAD_ROWS = 144
-
-
-def gather_tasks(shards, outs, halved, send_sem, recv_sem, copy_sem, place_of):
+HALF = 2176
+
+
+def gather_tasks(slots, send_sem, recv_sem, copy_sem, land_sem, place_of):
     core, rings, lines, toward = place_of
-    slots = len(shards)
-    sent = []
-
-    def rows_of(t, page):
-        if not halved[t]:
-            return None
-        total = shards[t].shape[0]
-        return pl.ds(0, LEAD_ROWS) if page == 0 else pl.ds(LEAD_ROWS, total - LEAD_ROWS)
-
-    def out_of(t, page):
-        return outs[t][0] if halved[t] else outs[t][page]
-
-    def place(t, page, dd, k):
-        index, rows = rings[dd] * 4 + lines[k], rows_of(t, page)
-        return out_of(t, page).at[index] if rows is None else out_of(t, page).at[index, rows]
-
-    def own(t, page):
-        rows = rows_of(t, page)
-        return shards[t] if rows is None else shards[t].at[rows]
-
-    def group(t, page, dd):
-        at, rows = pl.ds(rings[dd] * 4, 4), rows_of(t, page)
-        return out_of(t, page).at[at] if rows is None else out_of(t, page).at[at, rows]
-
-    def copy_of(t, source, target, to, kind):
-        index = t * len(GATHER_KINDS) + GATHER_NUMBER[kind]
+    line = lines[0]
+    drains = []
+
+    def cut(t, part):
+        if slots[t][1]:
+            return (slice(None), pl.ds(HALF * part if isinstance(part, int) else pl.multiple_of(part * HALF, 128), HALF))
+        rows = slots[t][2].shape[0]
+        return (pl.ds(0, LEAD_ROWS) if part == 0 else pl.ds(LEAD_ROWS, rows - LEAD_ROWS),)
+
+    def landed(t, part):
+        _, by_columns, shard, _, land = slots[t]
+        return land if by_columns else land.at[pl.ds(0, LEAD_ROWS if part == 0 else shard.shape[0] - LEAD_ROWS)]
+
+    def run(t, act):
+        if slots[t][1]:
+            act(core)
+        else:
+            per_core(core, act)
+
+    def place(t, part, dd, j):
+        return slots[t][3].at[(rings[dd] * 4 + j,) + cut(t, part)]
+
+    def group(t, part, dd):
+        return slots[t][3].at[(pl.ds(rings[dd] * 4, 4),) + cut(t, part)]
+
+    def copy_of(t, source, target, to, kind, j):
+        index = t * GATHER_SPAN + GATHER_NUMBER[kind] + j
         return remote_copy(source, target, send_sem.at[index], recv_sem.at[index], toward[to])
 
-    def send(t, dd, k, to, kind, mine=False):
-        def act(page):
-            target = place(t, page, dd, k)
-            copy_of(t, own(t, page) if mine else target, target, to, kind).start()
+    def guarded(valid, act):
+        if valid is None:
+            act()
+        else:
+            pl.when(valid)(act)
+
+    def send(t, dd, j, to, kind, valid=None, mine=False):
+        def start(part):
+            target = place(t, part, dd, j)
+            copy_of(t, target, target, to, kind, j).start()
+
+        def start_mine(index):
+            shard = slots[t][2].at[cut(t, index)] if index == slots[t][0] else landed(t, index)
+            copy_of(t, shard, place(t, index, dd, j), to, kind, j).start()
+
+        def finish(part):
+            target = place(t, part, dd, j)
+            copy_of(t, target, target, to, kind, j).wait_send()
+
+        if mine:
+            guarded(valid, lambda: per_core(core, start_mine))
+        else:
+            guarded(valid, lambda: run(t, start))
+        drains.append(lambda: guarded(valid, lambda: run(t, finish)))
+
+    def arrive(t, dd, j, to, kind, valid=None):
+        def act(part):
+            target = place(t, part, dd, j)
+            copy_of(t, target, target, to, kind, j).wait_recv()
+
+        guarded(valid, lambda: run(t, act))
+
+    def both(one, two):
+        return two if one is None else one & two
+
+    def onward(t, j, valid, up, down, mine=False):
+        if up:
+            send(t, 0, j, (LEVEL, UP), UP, both(valid, line < 3), mine)
+        if down:
+            send(t, 0, j, (LEVEL, DOWN), DOWN, both(valid, line > 0), mine)
+        send(t, 0, j, EAST, EAST, valid, mine)
+        send(t, 0, j, NORTH, NORTH, valid, mine)
+
+    def prelude():
+        def give(index):
+            for t, (owner, _, shard, _, land) in enumerate(slots):
+                if index == owner:
+                    source = shard.at[cut(t, 1 - index)]
+                    remote_copy(source, landed(t, 1 - index), land_sem.at[t], land_sem.at[len(slots) + t], toward[SIBLING]).start()
+
+        per_core(core, give)
+
+    def taken(t):
+        owner, shard = slots[t][0], slots[t][2]
+
+        def act(index):
+            target = landed(t, 1 - owner)
+            copy = remote_copy(target, target, land_sem.at[t], land_sem.at[len(slots) + t], toward[SIBLING])
+            if index == owner:
+                copy.wait_send()
+            else:
+                copy.wait_recv()
 
         per_core(core, act)
-        sent.append((t, lambda page: copy_of(t, place(t, page, dd, k), place(t, page, dd, k), to, kind)))
-
-    def arrive(t, dd, k, to, kind):
-        def act(page):
-            target = place(t, page, dd, k)
-            copy_of(t, target, target, to, kind).wait_recv()
-
-        per_core(core, act)
+
+    def local(t, index):
+        source = slots[t][2].at[cut(t, index)] if index == slots[t][0] else landed(t, index)
+        return pltpu.make_async_copy(source, place(t, index, 0, line), copy_sem.at[t])
+
+    def begin(t):
+        taken(t)
+        onward(t, line, None, True, True, mine=True)
+        per_core(core, lambda index: local(t, index).start())
+
+    def own_ready(t):
+        per_core(core, lambda index: local(t, index).wait())
+
+    def from_line(t, offset):
+        j = line + offset
+        valid = j >= 0 if offset < 0 else j <= 3
+        kind = UP if offset < 0 else DOWN
+        arrive(t, 0, j, (LEVEL, DOWN if offset < 0 else UP), kind, valid)
+        onward(t, j, valid, offset < 0, offset > 0)
+
+    def from_side(t, offset):
+        j = line + offset
+        valid = None if offset == 0 else (j >= 0 if offset < 0 else j <= 3)
+        even, odd = both(valid, j % 2 == 0), both(valid, j % 2 == 1)
+        arrive(t, 1, j, EAST, EAST, valid)
+        send(t, 1, j, NORTH, CORNER, even)
+        arrive(t, 2, j, NORTH, NORTH, valid)
+        send(t, 2, j, EAST, CORNER, odd)
+
+    def from_corner(t, j):
+        arrive(t, 3, j, NORTH if j % 2 == 0 else EAST, CORNER)
 
     def sibling(t, dd):
-        def copy(page):
-            return copy_of(t, group(t, page, dd), group(t, page, dd), SIBLING, (SIBLING, dd))
-
-        per_core(core, lambda page: copy(page).start())
-        sent.append((t, copy))
-
-    def begin_line(t):
-        for k in (1, 2, 3):
-            send(t, 0, 0, (LEVEL, k), (LEVEL, k), mine=True)
-
-    def local(t, page):
-        return pltpu.make_async_copy(own(t, page), place(t, page, 0, 0), copy_sem.at[t])
-
-    def begin_ring(t):
-        send(t, 0, 0, EAST, (EAST, 0), mine=True)
-        send(t, 0, 0, NORTH, (NORTH, 0), mine=True)
-        per_core(core, lambda page: local(t, page).start())
-
-    def own_ready(t):
-        per_core(core, lambda page: local(t, page).wait())
-
-    def from_line(t, k):
-        arrive(t, 0, k, (LEVEL, k), (LEVEL, k))
-        send(t, 0, k, EAST, (EAST, k))
-        send(t, 0, k, NORTH, (NORTH, k))
-
-    def from_east(t, k):
-        arrive(t, 1, k, EAST, (EAST, k))
-        if k < 2:
-            send(t, 1, k, NORTH, (CORNER, k))
-
-    def from_north(t, k):
-        arrive(t, 2, k, NORTH, (NORTH, k))
-        if k >= 2:
-            send(t, 2, k, EAST, (CORNER, k))
-
-    def from_corner(t, k):
-        arrive(t, 3, k, NORTH if k < 2 else EAST, (CORNER, k))
-
-    def last(t, dd):
-        def act(page):
-            target = group(t, 1 - page, dd)
-            copy_of(t, target, target, SIBLING, (SIBLING, dd)).wait_recv()
-
-        per_core(core, act)
+        def copy(part):
+            return copy_of(t, group(t, part, dd), group(t, part, dd), SIBLING, SIBLING, dd)
+
+        run(t, lambda part: copy(part).start())
+        drains.append(lambda: run(t, lambda part: copy(part).wait_send()))
+
+    def last(t):
+        def act(part):
+            for dd in range(4):
+                target = group(t, 1 - part, dd)
+                copy_of(t, target, target, SIBLING, SIBLING, dd).wait_recv()
+
+        run(t, act)
 
     tasks = []
 
     def then(function, *given):
-        tasks.append(lambda: function(*given))
-
-    then(begin_line, 0)
-    then(begin_ring, 0)
-    for t in range(slots):
-        then(from_east, t, 0)
-        then(from_north, t, 0)
+        tasks.append((given[0] if given else 0, lambda: function(*given)))
+
+    count = len(slots)
+    heads, tails = [], []
+    for t in range(count):
+        then(from_line, t, -1)
         then(from_line, t, 1)
-        then(from_line, t, 2)
-        then(from_line, t, 3)
+        then(from_side, t, 0)
+        for far in (2, 3):
+            then(from_line, t, -far)
+            then(from_line, t, far)
+            then(from_side, t, 1 - far)
+            then(from_side, t, far - 1)
         then(own_ready, t)
         then(sibling, t, 0)
-        if t + 1 < slots:
-            then(begin_line, t + 1)
-        then(from_east, t, 1)
-        then(from_north, t, 1)
-        if t + 1 < slots:
-            then(begin_ring, t + 1)
-        for k in (2, 3):
-            then(from_east, t, k)
-            then(from_north, t, k)
+        then(from_side, t, -3)
+        then(from_side, t, 3)
         then(sibling, t, 1)
         then(sibling, t, 2)
-        for k in range(4):
-            then(from_corner, t, k)
+        heads.append(list(tasks))
+        tasks.clear()
+        for j in range(4):
+            then(from_corner, t, j)
         then(sibling, t, 3)
-    for t in range(slots):
-        for dd in range(4):
-            then(last, t, dd)
+        then(last, t)
+        tails.append(list(tasks))
+        tasks.clear()
+    then(prelude)
+    then(begin, 0)
+    if count > 1:
+        then(begin, 1)
+    for t in range(count):
+        tasks += heads[t][:7]
+        if t > 0:
+            tasks += tails[t - 1]
+        if t + 2 < count:
+            then(begin, t + 2)
+        tasks += heads[t][7:]
+    tasks += tails[count - 1]
 
     def drain():
-        for _, copy in sent:
-            per_core(core, lambda page: copy(page).wait_send())
-
-    tasks.append(drain)
-    return tasks
-
-
-HALVED = (False, True)
-
-
-def gather_kernel(*refs):
-    shards, refs = refs[:2], refs[2:]
-    outs, refs = [refs[0:2], refs[2:3]], refs[3:]
+        for act in drains:
+            act()
+
+    return tasks, drain
+
+
+def gather_outs(shards):
+    shapes = []
+    for _, by_columns, shard in shards:
+        rows, columns = shard.shape
+        land = (rows, HALF) if by_columns else (LEAD_ROWS, columns)
+        shapes += [jax.ShapeDtypeStruct((16, rows, columns), LOW), jax.ShapeDtypeStruct(land, LOW)]
+    return shapes
+
+
+def gather_slots(forms, shards, outs):
+    return [form + (shards[t], outs[2 * t], outs[2 * t + 1]) for t, form in enumerate(forms)]
+
+
+def gather_semaphores(count):
+    dma = pltpu.SemaphoreType.DMA
+    return [dma((count * GATHER_SPAN,)), dma((count * GATHER_SPAN,)), dma((count,)), dma((2 * count,))]
+
+
+def row_copies(place_of, source, target, send_sem, recv_sem, local_sem):
+    core, _, lines, toward = place_of
+    half = target.shape[0] // 2
+    which = lines[0] // 2
+    from_here = pl.ds(pl.multiple_of(core * half, half), half)
+    to_there = pl.ds(pl.multiple_of(which * half, half), half)
+    return (
+        pltpu.make_async_copy(source.at[which, from_here], target.at[to_there], local_sem),
+        remote_copy(source.at[1 - which, from_here], target.at[to_there], send_sem, recv_sem, toward[(LEVEL, 3)]),
+    )
+
+
+def gather_kernel(shard, *refs):
+    source, outs, moved, refs = refs[0], refs[1:3], refs[3], refs[4:]
+    sems, row_sems = refs[:4], refs[4:]
     place_of = places()
     greet(place_of[3])
-    for task in gather_tasks(shards, outs, HALVED, *refs, place_of):
+    tasks, drain = gather_tasks(gather_slots(((0, True),), (shard,), outs), *sems, place_of)
+    for _, task in tasks[:11]:
         task()
-
-
-def gather_shapes(shards):
-    pages, reduce = ((16,) + shard.shape for shard in shards)
-    return [jax.ShapeDtypeStruct(shape, LOW) for shape in (pages, pages, reduce)]
-
-
-def gather_semaphores():
-    count = 2 * len(GATHER_KINDS)
-    return [pltpu.SemaphoreType.DMA((count,)), pltpu.SemaphoreType.DMA((count,)), pltpu.SemaphoreType.DMA((2,))]
-
-
-def gather_pages(shards):
+    copies = row_copies(place_of, source, moved, *row_sems)
+    for copy in copies:
+        copy.start()
+    for _, task in tasks[11:]:
+        task()
+    drain()
+    for copy in copies:
+        copy.wait()
+
+
+def gather_page(shard, source):
     anywhere = pl.BlockSpec(memory_space=pl.ANY)
-    return pl.pallas_call(
+    outs = gather_outs(((0, True, shard),)) + [jax.ShapeDtypeStruct(source.shape[1:], LOW)]
+    dma = pltpu.SemaphoreType.DMA
+    res = pl.pallas_call(
         gather_kernel,
-        out_shape=tuple(gather_shapes(shards)),
+        out_shape=tuple(outs),
         in_specs=[anywhere] * 2,
-        out_specs=(anywhere,) * 3,
-        scratch_shapes=gather_semaphores(),
+        out_specs=(anywhere,) * len(outs),
+        scratch_shapes=gather_semaphores(1) + [dma(())] * 3,
         compiler_params=pltpu.CompilerParams(collective_id=0, has_side_effects=True),
-        name="gather_pages",
-    )(*shards)
+        name="gather_page",
+    )(shard, source)
+    return res[0], res[2]
 
 
 def low_place(line):
     return jnp.where(line < 2, line, 3 - line)
 
 
-def forward_kernel(extra, *refs):
-    x, vectors, wide, table, page_hbm, expand_hbm, reduce_hbm = refs[:7]
-    refs = refs[7:]
-    if extra:
-        shards, refs = refs[:2], refs[2:]
+def forward_kernel(forms, *refs):
+    count = len(forms)
+    moving = count == 2
+    x, vectors, wide, table, page_hbm = refs[:5]
+    shards, refs = refs[5 : 5 + count], refs[5 + count :]
+    if moving:
+        row_source, refs = refs[0], refs[1:]
     (normed_out, query_out, here, beside, away, corner, attended_out, log_out, attended_low, middle_out,
      second_out, active_out, slope_out, result_out) = refs[:14]
-    refs = refs[14:]
-    if extra:
-        outs, refs = [refs[0:2], refs[2:3]], refs[3:]
+    outs, refs = refs[14 : 14 + 2 * count], refs[14 + 2 * count :]
+    if moving:
+        row_target, row_sems, refs = refs[0], refs[-3:], refs[1:-3]
     page, expand, reduce, mixture, result, mixed, stats, page_sem, expand_sem, reduce_sem, pair_send, pair_recv = refs[:12]
     place_of = places()
     core, rings, lines, toward = place_of
@@ -776,31 +831,33 @@
 
     def expand_copy(i):
         at = pl.ds(pl.multiple_of(i * 256, 256), 256)
-        return pltpu.make_async_copy(expand_hbm.at[:, at], expand.at[:, at], expand_sem.at[i])
+        return pltpu.make_async_copy(outs[0].at[:, :, at], expand.at[:, :, at], expand_sem.at[i])
 
     def reduce_copy(i):
-        at = pl.ds(pl.multiple_of(i * 256, 256), 256)
-        return pltpu.make_async_copy(reduce_hbm.at[at], reduce.at[at], reduce_sem.at[i])
+        rows_at = pl.ds(pl.multiple_of(i * 272, 16), 272)
+        return pltpu.make_async_copy(outs[2].at[i], reduce.at[rows_at], reduce_sem.at[i])
 
     tiles = page.shape[1] // 256
 
-    def begin(make):
+    def begin(make, steps):
         def step(i, _):
             make(i).start()
             return 0
 
-        lax.fori_loop(0, tiles, step, 0)
-
-    begin(page_copy)
-    begin(expand_copy)
-    begin(reduce_copy)
+        lax.fori_loop(0, steps, step, 0)
+
+    begin(page_copy, tiles)
     greet(toward)
-    todo = list(gather_tasks(shards, outs, HALVED, *refs[12:15], place_of)) if extra else []
-
-    def progress(count):
-        for _ in range(count):
+    todo, drain = gather_tasks(gather_slots(forms, shards, outs), *refs[12:], place_of)
+
+    def progress(many):
+        for _ in range(many):
             if todo:
-                todo.pop(0)()
+                todo.pop(0)[1]()
+
+    def complete(t):
+        while any(slot <= t for slot, _ in todo):
+            progress(1)
 
     progress(2)
     unit, _ = normal_parts(x[...].astype(F32))
@@ -813,7 +870,9 @@
         mixture[:, at] = mm(normed_out[...], page[:, at])
         return 0
 
-    lax.fori_loop(0, 13, column, 0)
+    for begin_at, end in ((0, 4), (4, 8), (8, 13)):
+        lax.fori_loop(begin_at, end, column, 0)
+        progress(2)
     blank = jnp.zeros((rows, WIDE - width), LOW)
     here[0, :, :width] = mixture[:, width : 2 * width].astype(LOW)
     here[0, :, width:] = blank
@@ -831,7 +890,7 @@
     query = ((mixture[:, :width] + vectors[2:3]).astype(LOW).astype(F32) * HDIM ** (-0.5)).astype(LOW)
     query_out[:, :width] = query
     query_out[:, width:] = blank
-    progress(2)
+    progress(1)
     to_beside.wait_recv()
 
     def block(kind, near, part, at):
@@ -870,10 +929,11 @@
 
     for begin_at in (0, 3, 6):
         lax.fori_loop(begin_at, begin_at + 3, local_pair, 0)
-        progress(1)
+        progress(2)
+    progress(8)
     to_away.wait_recv()
     to_corner.start()
-    progress(1)
+    progress(2)
     to_corner.wait_recv()
 
     def far_pair(p, _):
@@ -898,7 +958,7 @@
 
     for begin_at in (0, 3, 6):
         lax.fori_loop(begin_at, begin_at + 3, far_pair, 0)
-        progress(1)
+        progress(2)
 
     def late(i, _):
         page_copy(i).wait()
@@ -910,35 +970,59 @@
     blended = mm(attended_low[...], page[:, lead:])
     middle = x[...].astype(F32) + (blended[:, 3 * width - lead :] + vectors[4:5])
     middle_out[...] = middle
+    progress(2)
     unit, _ = normal_parts(middle)
     second = (unit * vectors[6:7] + vectors[7:8]).astype(LOW)
     second_out[...] = mm(second, table[...]).astype(LOW)
     result[...] = middle + vectors[5:6]
 
+    complete(0)
+    begin(expand_copy, tiles)
+    if moving:
+        for copy in row_copies(place_of, row_source, row_target, *row_sems):
+            copy.start()
+
     def inner(i, _):
         at = pl.ds(pl.multiple_of(i * 256, 256), 256)
         expand_copy(i).wait()
-        hidden = mm(second_out[...], expand[:, at]) + wide[:, at]
+        weights = expand[:, :, at].astype(F32).reshape(WIDE, 256).astype(LOW)
+        hidden = mm(second_out[...], weights) + wide[:, at]
         below = 0.5 + 0.5 * lax.erf(hidden * 0.7071067811865476)
-        active = (hidden * below).astype(LOW)
-        active_out[:, at] = active
+        active_out[:, at] = (hidden * below).astype(LOW)
         slope_out[:, at] = (below + hidden * (0.3989422804014327 * jnp.exp(-0.5 * hidden * hidden))).astype(LOW)
+        return 0
+
+    for begin_at in range(0, tiles, 2):
+        lax.fori_loop(begin_at, min(begin_at + 2, tiles), inner, 0)
+        progress(3)
+    complete(1)
+    begin(reduce_copy, 16)
+
+    def landed(i, _):
         reduce_copy(i).wait()
-        result[...] += mm(active, reduce[at])
         return 0
 
-    for begin_at in range(0, tiles, 4):
-        lax.fori_loop(begin_at, min(begin_at + 4, tiles), inner, 0)
-        progress(2)
+    lax.fori_loop(0, 16, landed, 0)
+
+    def outer(i, _):
+        at = pl.ds(pl.multiple_of(i * 256, 256), 256)
+        result[...] += mm(active_out[:, at], reduce[at])
+        return 0
+
+    lax.fori_loop(0, tiles, outer, 0)
     result_out[...] = result[...].astype(LOW)
     progress(len(todo))
+    drain()
+    if moving:
+        for copy in row_copies(place_of, row_source, row_target, *row_sems):
+            copy.wait()
     for copy in (to_away, to_beside, to_corner):
         copy.wait_send()
 
 
-def forward(x, vectors, wide, table, page, expand, reduce, shards=None):
+def forward(x, vectors, wide, table, page, shards, moved=()):
     rows, width = x.shape
-    inner = expand.shape[1]
+    inner = page.shape[1]
     pairs = WIDE // 128
     anywhere = pl.BlockSpec(memory_space=pl.ANY)
     inside = pl.BlockSpec(memory_space=pltpu.VMEM)
@@ -952,35 +1036,37 @@
         shape(pairs, 2, rows, kind=F32), shape(rows, WIDE), shape(rows, width, kind=F32),
         shape(rows, WIDE), shape(rows, inner), shape(rows, inner), shape(rows, width),
     ]
-    extra = shards is not None
     count = len(outs)
+    dma = pltpu.SemaphoreType.DMA
     scratch = [
-        pltpu.VMEM(page.shape, LOW), pltpu.VMEM(expand.shape, LOW), pltpu.VMEM(reduce.shape, LOW),
+        pltpu.VMEM(page.shape, LOW), pltpu.VMEM((16, 72, inner), LOW), pltpu.VMEM((inner, width), LOW),
         pltpu.VMEM((rows, 13 * 256), F32), pltpu.VMEM((rows, width), F32),
         pltpu.VMEM((pairs, 2, 128, rows), F32), pltpu.VMEM((pairs, 4, rows), F32),
-        pltpu.SemaphoreType.DMA((inner // 256,)), pltpu.SemaphoreType.DMA((inner // 256,)),
-        pltpu.SemaphoreType.DMA((inner // 256,)), pltpu.SemaphoreType.DMA((3,)), pltpu.SemaphoreType.DMA((3,)),
-    ]
-    if extra:
-        outs += gather_shapes(shards)
-        scratch += gather_semaphores()
+        dma((inner // 256,)), dma((inner // 256,)), dma((16,)), dma((3,)), dma((3,)),
+    ] + gather_semaphores(len(shards))
+    outs += gather_outs(shards)
+    gathered = len(outs)
+    outs += [jax.ShapeDtypeStruct(source.shape[1:], LOW) for source in moved]
+    scratch += [dma(())] * (3 * len(moved))
+    forms = tuple(shard[:2] for shard in shards)
     res = pl.pallas_call(
-        partial(forward_kernel, extra),
+        partial(forward_kernel, forms),
         out_shape=tuple(outs),
-        in_specs=[inside] * 4 + [anywhere] * 3 + ([anywhere] * 2 if extra else []),
+        in_specs=[inside] * 4 + [anywhere] * (1 + len(shards) + len(moved)),
         out_specs=(inside,) * count + (anywhere,) * (len(outs) - count),
         scratch_shapes=scratch,
         compiler_params=pltpu.CompilerParams(
-            collective_id=2 if extra else 3, has_side_effects=True, vmem_limit_bytes=60 << 20
+            collective_id=len(shards), has_side_effects=True, vmem_limit_bytes=60 << 20
         ),
-        name="forward_gather" if extra else "forward",
-    )(x, vectors, wide, table, page, expand, reduce, *(shards if extra else ()))
-    return res[:count], res[count:]
-
-
-COLUMNS, ROWS, TINY = range(3)
-SIZES = {COLUMNS: (72, 2176), ROWS: (144, 1088), TINY: (8, 128)}
+        name="forward",
+    )(x, vectors, wide, table, page, *(shard[2] for shard in shards), *moved)
+    return res[:count], res[count:gathered:2], res[gathered:]
+
+
+COLUMNS, ROWS = range(2)
+SIZES = {COLUMNS: (72, 2176), ROWS: (144, 1088)}
 DEPTH = 6
+EASTWARD = (3, 0)
 SCATTER_KINDS = (
     [(SIBLING, dd) for dd in range(4)]
     + [(ONCE, k) for k in range(4)]
@@ -992,23 +1078,19 @@
 SCATTER_NUMBER = {kind: index for index, kind in enumerate(SCATTER_KINDS)}
 
 
-def kind_type(kind):
-    return F32 if kind == TINY else LOW
-
-
 def landing_shapes(kind):
-    return [jax.ShapeDtypeStruct((many,) + SIZES[kind], kind_type(kind)) for many in (16, 4, 4, 4, 4)]
+    return [jax.ShapeDtypeStruct((many,) + SIZES[kind], LOW) for many in (16, 4, 4, 4, 4)]
 
 
 def final_shape(kind):
-    return jax.ShapeDtypeStruct({COLUMNS: (72, 4352), ROWS: (272, 1088), TINY: (16, 128)}[kind], F32)
+    return jax.ShapeDtypeStruct({COLUMNS: (72, 4352), ROWS: (272, 1088)}[kind], F32)
 
 
 def work_shapes(kinds):
     shapes = []
     for kind in sorted(set(kinds)):
-        size, held = SIZES[kind], kind_type(kind)
-        shapes += [pltpu.VMEM((2, 4) + size, held), pltpu.VMEM((DEPTH,) + size, held), pltpu.VMEM(size, F32)]
+        size = SIZES[kind]
+        shapes += [pltpu.VMEM((2, 4) + size, LOW), pltpu.VMEM((DEPTH,) + size, LOW), pltpu.VMEM(size, F32)]
     count = len(kinds) * len(SCATTER_KINDS)
     return shapes + [
         pltpu.SemaphoreType.DMA((count,)), pltpu.SemaphoreType.DMA((count,)),
@@ -1037,9 +1119,7 @@
         page, at = self.pages[t], index if many is None else pl.ds(index, many)
         if self.kinds[t] == COLUMNS:
             return page.at[at, :, pl.ds(pl.multiple_of(core * 2176, 128), 2176)]
-        if self.kinds[t] == ROWS:
-            return page.at[pl.ds(pl.multiple_of(index * 272 + core * 128, 16), 144)]
-        return page.at[at, pl.ds(pl.multiple_of(core * 8, 8), 8)]
+        return page.at[pl.ds(pl.multiple_of(index * 272 + core * 128, 16), 144)]
 
     def landed(self, t, dd):
         return self.lands[t][0].at[pl.ds(self.rings[dd] * 4, 4)]
@@ -1065,12 +1145,13 @@
             copies.append(pltpu.make_async_copy(source, loads.at[slot, j], self.load_sem.at[slot * 4 + j]))
         for copy in copies:
             copy.start()
+        return loads, slot, copies
+
+    def add_up(self, t, loaded, store):
+        loads, slot, copies = loaded
+        terms = len(copies)
         for copy in copies:
             copy.wait()
-        return loads, slot, len(copies)
-
-    def add_up(self, t, loaded, store):
-        loads, slot, terms = loaded
         rows, columns = SIZES[self.kinds[t]]
         wide = self.kinds[t] != ROWS
         piece = min(256, columns) if wide else 16
@@ -1100,35 +1181,40 @@
     def sum_and_send(self, t, dd, k, extra, target, to, kind):
         form = self.kinds[t]
         loaded = self.load(t, self.sources(t, dd, k, extra))
-        place = self.count[form] % DEPTH
-        self.count[form] += 1
-        if self.used[form][place] is not None:
-            self.used[form][place].wait_send()
-        out = self.work[form][1]
-
-        def store(where, value):
-            out[(place,) + where] = value.astype(out.dtype)
-
-        self.add_up(t, loaded, store)
-        copy = self.remote(t, out.at[place], target, to, kind)
-        copy.start()
-        self.used[form][place] = copy
+
+        def finish():
+            place = self.count[form] % DEPTH
+            self.count[form] += 1
+            if self.used[form][place] is not None:
+                self.used[form][place].wait_send()
+            out = self.work[form][1]
+
+            def store(where, value):
+                out[(place,) + where] = value.astype(out.dtype)
+
+            self.add_up(t, loaded, store)
+            copy = self.remote(t, out.at[place], target, to, kind)
+            copy.start()
+            self.used[form][place] = copy
+
+        return finish
 
     def first(self, t, k):
-        if k == 0:
+        if k == 3:
             self.arrived(t, self.landed(t, 3), SIBLING, (SIBLING, 3))
-        self.sum_and_send(t, 3, k, [], self.lands[t][1].at[k], EAST if k < 2 else NORTH, (ONCE, k))
+        to = EAST if k in EASTWARD else NORTH
+        return self.sum_and_send(t, 3, k, [], self.lands[t][1].at[k], to, (ONCE, k))
 
     def second(self, t, dd, k):
-        if (dd, k) in ((1, 0), (2, 3)):
+        if (dd, k) in ((1, 3), (2, 2)):
             self.arrived(t, self.landed(t, dd), SIBLING, (SIBLING, dd))
         to, land = (EAST, self.lands[t][2]) if dd == 1 else (NORTH, self.lands[t][3])
         extra = []
-        if (dd == 1) == (k >= 2):
+        if (dd == 1) != (k in EASTWARD):
             one = self.lands[t][1].at[k]
-            self.arrived(t, one, NORTH if k >= 2 else EAST, (ONCE, k))
+            self.arrived(t, one, EAST if k in EASTWARD else NORTH, (ONCE, k))
             extra = [one]
-        self.sum_and_send(t, dd, k, extra, land.at[k], to, (to, k))
+        return self.sum_and_send(t, dd, k, extra, land.at[k], to, (to, k))
 
     def third(self, t, k):
         if k == 3:
@@ -1138,22 +1224,19 @@
             self.arrived(t, land.at[k], to, (to, k))
             extra.append(land.at[k])
         if k:
-            self.sum_and_send(t, 0, k, extra, self.lands[t][4].at[k], (LEVEL, k), (LEVEL, k))
-        else:
-            loaded = self.load(t, self.sources(t, 0, 0, extra))
-            total = self.work[self.kinds[t]][2]
-
-            def store(where, value):
-                total[where] = value
-
-            self.add_up(t, loaded, store)
+            return self.sum_and_send(t, 0, k, extra, self.lands[t][4].at[k], (LEVEL, k), (LEVEL, k))
+        loaded = self.load(t, self.sources(t, 0, 0, extra))
+        total = self.work[self.kinds[t]][2]
+
+        def store(where, value):
+            total[where] = value
+
+        return lambda: self.add_up(t, loaded, store)
 
     def final_part(self, t, core):
         if self.kinds[t] == COLUMNS:
             return (slice(None), slice(None)), (slice(None), pl.ds(2176 * core, 2176))
-        if self.kinds[t] == ROWS:
-            return (pl.ds(16 * core, 144 - 16 * core),), (pl.ds(144 * core, 144 - 16 * core),)
-        return (slice(None),), (pl.ds(8 * core, 8),)
+        return (pl.ds(16 * core, 144 - 16 * core),), (pl.ds(144 * core, 144 - 16 * core),)
 
     def last(self, t):
         land = self.lands[t][4]
@@ -1161,12 +1244,10 @@
             self.arrived(t, land.at[k], (LEVEL, k), (LEVEL, k))
         loaded = self.load(t, [land.at[k] for k in (1, 2, 3)])
         total = self.work[self.kinds[t]][2]
+        owner = self.owners[t]
 
         def store(where, value):
             total[where] = total[where] + value
-
-        self.add_up(t, loaded, store)
-        owner = self.owners[t]
 
         def act(core):
             inner, outer = self.final_part(t, core)
@@ -1182,18 +1263,26 @@
                 copy.start()
                 copy.wait_send()
 
-        per_core(self.core, act)
+        def finish():
+            self.add_up(t, loaded, store)
+            per_core(self.core, act)
+
+        return finish
+
+    def give_all(self, t):
+        for dd in (3, 1, 2, 0):
+            self.give(t, dd)
 
     def steps(self, t):
-        def of(function, *given):
-            return lambda: function(*given)
-
+        def of(waits, function, *given):
+            return waits, lambda: function(*given)
+
+        ways = ((1, 3), (2, 2), (1, 0), (2, 1), (1, 2), (2, 3), (1, 1), (2, 0))
         return (
-            [of(self.give, t, dd) for dd in (3, 1, 2, 0)],
-            [of(self.first, t, k) for k in (0, 2, 1, 3)],
-            [of(self.second, t, dd, k) for dd, k in ((1, 0), (2, 3), (1, 1), (2, 2), (1, 3), (2, 0), (1, 2), (2, 1))],
-            [of(self.third, t, k) for k in (3, 2, 1, 0)],
-            [of(self.last, t)],
+            [of(k == 3, self.first, t, k) for k in (3, 2, 0, 1)],
+            [of((dd == 1) != (k in EASTWARD), self.second, t, dd, k) for dd, k in ways],
+            [of(True, self.third, t, k) for k in (3, 2, 1, 0)],
+            [of(True, self.last, t)],
         )
 
     def drain(self):
@@ -1205,27 +1294,94 @@
                     copy.wait_send()
 
 
+def in_turn(earlier, later, done=()):
+    return later[0] + earlier[2][:2] + later[1][:4] + earlier[2][2:] + list(done) + later[1][4:]
+
+
+def tiny_shapes():
+    return [
+        pltpu.VMEM((16, 16, 128), F32), pltpu.VMEM((16, 16, 128), F32), pltpu.VMEM((2, 4, 16, 128), F32),
+        pltpu.VMEM((4, 16, 128), F32), pltpu.VMEM((3, 16, 128), F32),
+        pltpu.SemaphoreType.DMA((7,)), pltpu.SemaphoreType.DMA((7,)),
+    ]
+
+
+def tiny_steps(both, final, refs, place_of):
+    total, land, land_east, land_north, land_line, send_sem, recv_sem = refs
+    core, rings, lines, toward = place_of
+    blocks = [pl.ds(rings[dd] * 4, 4) for dd in range(4)]
+
+    def copy(number, source, target, to):
+        return remote_copy(source, target, send_sem.at[number], recv_sem.at[number], toward[to])
+
+    over = copy(0, both.at[1 - core], land, SIBLING)
+    east = [copy(1 + i, total.at[blocks[dd]], land_east.at[i], EAST) for i, dd in enumerate((1, 3))]
+    north = copy(3, total.at[blocks[2]], land_north, NORTH)
+    line = [copy(3 + k, total.at[rings[0] * 4 + lines[k]], land_line.at[k - 1], (LEVEL, k)) for k in (1, 2, 3)]
+
+    def zero():
+        over.start()
+        return lambda: None
+
+    def one():
+        over.wait_recv()
+        total[...] = both[core] + land[...]
+        for each in east:
+            each.start()
+        return lambda: None
+
+    def two():
+        for i, each in enumerate(east):
+            each.wait_recv()
+            total[blocks[2 * i]] = total[blocks[2 * i]] + land_east[i]
+        north.start()
+        return lambda: None
+
+    def three():
+        north.wait_recv()
+        total[blocks[0]] = total[blocks[0]] + land_north[...]
+        for each in line:
+            each.start()
+        return lambda: None
+
+    def four():
+        value = total[rings[0] * 4 + lines[0]]
+        for i, each in enumerate(line):
+            each.wait_recv()
+            value = value + land_line[i]
+        final[...] = value
+        for each in [over, north] + east + line:
+            each.wait_send()
+        return lambda: None
+
+    return [(True, step) for step in (zero, one, two, three, four)]
+
+
 def backward_kernel(carried, *refs):
     (top, x, vectors, table, normed_in, query, here, beside, away, corner, attended, logs, attended_low, middle,
      second, active, slope) = refs[:17]
     page_hbm, expand_hbm, reduce_hbm = refs[17:20]
     refs = refs[20:]
+    passed, refs = refs[0], refs[1:]
     if carried:
-        carried_page, refs = refs[0], refs[1:]
-    result_out, page_reduce, page_expand, page_attention, page_small = refs[:5]
-    refs = refs[5:]
-    kinds = (COLUMNS, ROWS, COLUMNS, COLUMNS, TINY) if carried else (ROWS, COLUMNS, TINY)
-    owners = (1, 0, 0, 0, 0) if carried else (1, 1, 1)
-    pages = (carried_page, page_reduce, page_expand, page_attention, page_small) if carried else (page_reduce, page_expand, page_small)
+        passed_small, refs = refs[0], refs[1:]
+    result_out, small_out, page_reduce, page_expand, page_attention, shipped = refs[:6]
+    refs = refs[6:]
+    kinds = (COLUMNS, ROWS, COLUMNS, COLUMNS) if carried else (ROWS, COLUMNS)
+    owners = (1, 0, 0, 0) if carried else (1, 1)
+    pages = (page_reduce, page_expand)
+    if carried:
+        pages = (passed, page_reduce, page_expand, page_attention)
     n = len(kinds)
     finals, refs = refs[:n], refs[n:]
     lands, refs = [refs[5 * t : 5 * t + 5] for t in range(n)], refs[5 * n :]
     (reduce_ring, expand_ring, output, second_sum, left_one, left_two, stage_wide, stage_tall, wide_sum, query_sum,
-     here_sum, beside_give, away_give, corner_give, beside_got, away_got, corner_got, pair, mixture, grad_middle,
-     grad_attended, sums, small, reduce_sem, expand_sem, output_sem, wide_sem, tall_sem, pair_send, pair_recv) = refs[:30]
+     here_sum, beside_give, away_give, corner_give, beside_got, away_got, corner_got, hidden_all, mixture, grad_middle,
+     grad_attended, sums, both, reduce_sem, expand_sem, output_sem, wide_sem, tall_sem, pair_send, pair_recv, ship_send, ship_recv, ship_sem) = refs[:33]
     place_of = places()
     core, rings, lines, toward = place_of
-    scatter = Scatter(kinds, pages, lands, finals, owners, refs[30:], place_of)
+    tiny_refs, refs = refs[33:40], refs[40:]
+    scatter = Scatter(kinds, pages, lands, finals, owners, refs, place_of)
     rows, width = top.shape
     half = rows // 2
     first = low_place(lines[0]) == 0
@@ -1258,26 +1414,112 @@
     output_copy = pltpu.make_async_copy(page_hbm.at[:, pl.ds(lead, WIDE)], output, output_sem)
     output_copy.start()
     greet(toward)
-    todo = []
+    todo, open_ends = [], []
 
     def progress(count):
         for _ in range(count):
             if todo:
-                todo.pop(0)()
-
+                waits, begin = todo.pop(0)
+                if waits and open_ends:
+                    open_ends.pop()()
+                ended = begin()
+                if open_ends:
+                    open_ends.pop()()
+                open_ends.append(ended)
+
+    which = lines[0] // 2
+    mine = pl.ds(pl.multiple_of(core * half, half), half)
+    other = pl.ds(pl.multiple_of((1 - core) * half, half), half)
+    near_rows = pl.ds(pl.multiple_of(which * half, half), half)
+    far_rows = pl.ds(pl.multiple_of((1 - which) * half, half), half)
+
+    def ship_copies(rows_ref):
+        target = shipped.at[which, mine]
+        near, away = rows_ref.at[near_rows], rows_ref.at[far_rows]
+        ways = ((near, SIBLING), (away, (LEVEL, 3)), (away, (CORNER, 3)))
+        remote = [
+            remote_copy(source, target, ship_send.at[index], ship_recv.at[index], toward[to])
+            for index, (source, to) in enumerate(ways)
+        ]
+        return pltpu.make_async_copy(near, target, ship_sem), remote
+
+    def ship(layer, rows_ref):
+        local, remote = ship_copies(rows_ref)
+
+        def act(index):
+            for copy in (local, remote[1]) if index == layer else (remote[0], remote[2]):
+                copy.start()
+
+        per_core(core, act)
+
+    def shipped_all():
+        local, remote = ship_copies(top)
+        local.wait()
+        for index, (sequence, part) in enumerate(((which, other), (1 - which, mine), (1 - which, other))):
+            remote[index].wait_send()
+            ref = shipped.at[sequence, part]
+            remote_copy(ref, ref, ship_send.at[index], ship_recv.at[index], toward[SIBLING]).wait_recv()
+
+    steps = [scatter.steps(t) for t in range(n)]
     if carried:
-        steps = [scatter.steps(t) for t in range(n)]
-        todo += steps[0][0] + steps[0][1] + steps[0][2]
-    progress(4)
+        scatter.give_all(0)
+        todo += steps[0][0] + steps[0][1]
+        ship(1, top)
+    else:
+        ship(0, x)
+        ship(1, passed)
+    second_sum[...] = jnp.zeros_like(second_sum)
+
+    def tall_tile(i, _):
+        side = lax.rem(i, 2)
+
+        @pl.when(i >= 2)
+        def _():
+            tall_copy(i - 2).wait()
+
+        stage_tall[side] = mm_tn(active[:, tile_at(i)], top[...]).astype(LOW)
+        tall_copy(i).start()
+        return 0
+
+    def tall_page(t):
+        for begin_at in range(0, tiles, 6):
+            lax.fori_loop(begin_at, min(begin_at + 6, tiles), tall_tile, 0)
+            progress(1)
+        for i in (tiles - 2, tiles - 1):
+            tall_copy(i).wait()
+        scatter.give_all(t)
+
+    def wide_tile(i, _):
+        side = lax.rem(i, 2)
+
+        @pl.when(i >= 2)
+        def _():
+            wide_copy(i - 2, page_expand).wait()
+
+        stage_wide[side] = mm(left_one[...], hidden_all[:, tile_at(i)]).reshape(16, 72, 256).astype(LOW)
+        wide_copy(i, page_expand).start()
+        return 0
+
+    def wide_page(t):
+        for begin_at in range(0, tiles, 5):
+            lax.fori_loop(begin_at, min(begin_at + 5, tiles), wide_tile, 0)
+            progress(1)
+        for i in (tiles - 2, tiles - 1):
+            wide_copy(i, page_expand).wait()
+        scatter.give_all(t)
+
+    if not carried:
+        tall_page(0)
+        todo += steps[0][0] + steps[0][1]
     left_one[...] = second[...].T
-    second_sum[...] = jnp.zeros_like(second_sum)
 
     def feed_tile(i, _):
         at = tile_at(i)
-        slot, side = lax.rem(i, 3), lax.rem(i, 2)
+        slot = lax.rem(i, 3)
         reduce_copy(i).wait()
         hidden = (mm_nt(top[...], reduce_ring[slot]) * slope[:, at].astype(F32)).astype(LOW)
         wide_sum[0:1, at] = jnp.sum(hidden.astype(F32), axis=0, keepdims=True)
+        hidden_all[:, at] = hidden
         expand_copy(i, expand_hbm).wait()
         second_sum[...] += mm_nt(hidden, expand_ring[slot])
 
@@ -1286,31 +1528,11 @@
             reduce_copy(i + 3).start()
             expand_copy(i + 3, expand_hbm).start()
 
-        @pl.when(i >= 2)
-        def _():
-            wide_copy(i - 2, page_expand).wait()
-            tall_copy(i - 2).wait()
-
-        stage_wide[side] = mm(left_one[...], hidden).reshape(16, 72, 256).astype(LOW)
-        stage_tall[side] = mm_tn(active[:, at], top[...]).astype(LOW)
-        wide_copy(i, page_expand).start()
-        tall_copy(i).start()
         return 0
 
     for begin_at in range(0, tiles, 3):
         lax.fori_loop(begin_at, min(begin_at + 3, tiles), feed_tile, 0)
-        progress(3)
-    for i in (tiles - 2, tiles - 1):
-        wide_copy(i, page_expand).wait()
-        tall_copy(i).wait()
-    if carried:
-        todo += steps[1][0] + steps[2][0] + steps[1][1] + steps[0][3] + steps[1][2] + steps[2][1] + steps[0][4]
-        todo += steps[1][3] + steps[2][2] + steps[1][4] + steps[2][3] + steps[2][4]
-    else:
-        steps = [scatter.steps(t) for t in range(n)]
-        todo += steps[0][0] + steps[1][0] + steps[0][1] + steps[0][2] + steps[1][1] + steps[0][3] + steps[1][2]
-        todo += steps[0][4] + steps[1][3] + steps[1][4]
-    progress(8)
+        progress(1)
     for i in range(3):
         expand_copy(i, page_hbm).start()
 
@@ -1327,14 +1549,14 @@
     grad_middle[...] = value
     branch = value.astype(LOW)
     sums[4:5] = row(branch.astype(F32))
-    progress(2)
-    mixture[:, edge:] = branch.astype(F32)
+    progress(1)
+    mixture[:, edge:] = branch
     output_copy.wait()
     full = jnp.concatenate([jnp.zeros((rows, edge - lead), LOW), branch], axis=1)
     pulled = mm_nt(full, output[...]).astype(LOW)
     grad_attended[:, :width] = mm_nt(pulled, table[...]).astype(LOW)
     grad_attended[:, width:] = jnp.zeros((rows, WIDE - width), LOW)
-    progress(2)
+    progress(1)
 
     def rows_of(place, at, p):
         part = slice(place * half, (place + 1) * half)
@@ -1378,7 +1600,7 @@
 
     for begin_at in (0, 3, 6):
         lax.fori_loop(begin_at, begin_at + 3, far_pair, 0)
-        progress(2)
+        progress(1)
 
     def pair_copy(source, target, to, number):
         return remote_copy(source, target, pair_send.at[number], pair_recv.at[number], toward[to])
@@ -1401,18 +1623,27 @@
         query_sum[half:, at] += from_pair(high_query + more)
         return 0
 
-    lax.fori_loop(0, 3, near_pair, 0)
+    lax.fori_loop(0, 2, near_pair, 0)
     to_corner.wait_recv()
     for kind in (0, 1):
         away_give[kind] = (away_give[kind].astype(F32) + corner_got[kind].astype(F32)).astype(LOW)
     to_away.start()
-    progress(2)
-    for begin_at in (3, 6):
-        lax.fori_loop(begin_at, begin_at + 3, near_pair, 0)
-        progress(2)
+    progress(1)
+    for begin_at, end in ((2, 5), (5, 9)):
+        lax.fori_loop(begin_at, end, near_pair, 0)
+        progress(1)
     to_beside.start()
-    mixture[:, :width] = (query_sum[:, :width] * HDIM ** (-0.5)).astype(LOW).astype(F32)
-    sums[2:3] = row(mixture[:, :width])
+    if carried:
+        tall_page(1)
+        todo += in_turn(steps[0], steps[1])
+        wide_page(2)
+        todo += in_turn(steps[1], steps[2], steps[0][3])
+    else:
+        wide_page(1)
+        todo += in_turn(steps[0], steps[1])
+    low = (query_sum[:, :width] * HDIM ** (-0.5)).astype(LOW)
+    mixture[:, :width] = low
+    sums[2:3] = row(low.astype(F32))
     left_one[...] = normed_in[...].T
     left_two[...] = attended_low[...].T
     second_sum[...] = jnp.zeros_like(second_sum)
@@ -1421,14 +1652,16 @@
     to_away.wait_recv()
     for kind in (0, 1):
         value = here_sum[kind] + beside_got[kind].astype(F32) + away_got[kind].astype(F32)
-        mixture[:, (1 + kind) * width : (2 + kind) * width] = value[:, :width].astype(LOW).astype(F32)
-    sums[3:4] = row(mixture[:, 2 * width : edge])
+        low = value[:, :width].astype(LOW)
+        mixture[:, (1 + kind) * width : (2 + kind) * width] = low
+    sums[3:4] = row(low.astype(F32))
 
     def project_tile(i, _):
         at = tile_at(i)
         slot = lax.rem(i, 3)
         column = i * 256 + lax.broadcasted_iota(jnp.int32, (rows, 256), 1)
-        part = jnp.where(column < edge, mixture[:, at], 0.0).astype(LOW)
+        part = mixture[:, at]
+        part = jnp.where(column < edge, part, jnp.zeros_like(part))
         expand_copy(i, page_hbm).wait()
         second_sum[...] += mm_nt(part, expand_ring[slot])
 
@@ -1440,12 +1673,14 @@
 
     for begin_at, end in ((0, 4), (4, 8), (8, 13)):
         lax.fori_loop(begin_at, end, project_tile, 0)
-        progress(2)
+        progress(1)
     grad_normed = close_up(second_sum[...], table[...])
     unit, inverse = normal_parts(x[...].astype(F32))
     sums[0:1] = row(grad_normed * unit)
     sums[1:2] = row(grad_normed)
     result_out[...] = (grad_middle[...] + normal_back(grad_normed * vectors[0:1], unit, inverse)).astype(LOW)
+    if carried:
+        ship(0, result_out)
     progress(2)
 
     def page_tile(number, i):
@@ -1458,13 +1693,14 @@
 
         part = mixture[:, at]
         if number == 1:
-            value = mm(left_one[...], part.astype(LOW))
+            value = mm(left_one[...], part)
         elif number == 2:
-            value = mm(left_two[...], part.astype(LOW))
+            value = mm(left_two[...], part)
         else:
             column = i * 256 + lax.broadcasted_iota(jnp.int32, (rows, 256), 1)
-            value = mm(left_one[...], jnp.where(column < edge, part, 0.0).astype(LOW))
-            value = value + mm(left_two[...], jnp.where(column < edge, 0.0, part).astype(LOW))
+            zero = jnp.zeros_like(part)
+            value = mm(left_one[...], jnp.where(column < edge, part, zero))
+            value = value + mm(left_two[...], jnp.where(column < edge, zero, part))
         stage_wide[side] = value.reshape(16, 72, 256).astype(LOW)
         wide_copy(i, page_attention).start()
 
@@ -1478,45 +1714,48 @@
     whole_tiles = edge // 256
     for begin_at in range(0, whole_tiles, 4):
         page_loop(1, begin_at, begin_at + 4)
-        progress(2)
+        progress(1)
     page_loop(3, whole_tiles, whole_tiles + 1)
     page_loop(2, whole_tiles + 1, tiles)
-    small[...] = jnp.zeros_like(small)
+    for i in (tiles - 2, tiles - 1):
+        wide_copy(i, page_attention).wait()
+    if carried:
+        scatter.give_all(3)
+    small = both.at[0] if carried else small_out
+    small[...] = jnp.zeros(small.shape, F32)
     for shard in range(16):
         small[shard, 0:8, 0:68] = sums[:, shard * 68 : (shard + 1) * 68]
         for part in range(4):
             begin_at = shard * 272 + part * 68
             small[shard, 8 + part : 9 + part, 0:68] = wide_sum[0:1, begin_at : begin_at + 68]
-    small_copy = pltpu.make_async_copy(small, page_small, output_sem)
-    small_copy.start()
-    for i in (tiles - 2, tiles - 1):
-        wide_copy(i, page_attention).wait()
-    small_copy.wait()
-    tiny = steps[n - 1]
     if carried:
-        own = steps[3]
-        todo = own[0] + tiny[0] + todo + own[1] + own[2] + tiny[1] + tiny[2] + own[3] + tiny[3] + tiny[4] + own[4]
+        both[1] = passed_small[...]
+        tiny, own = tiny_steps(both, small_out, tiny_refs, place_of), steps[3]
+        todo += in_turn(steps[2], own, steps[1][3])
+        todo = tiny[:1] + todo[:3] + tiny[1:2] + todo[3:6] + tiny[2:3] + todo[6:9] + tiny[3:4] + todo[9:12] + tiny[4:] + todo[12:]
+        todo = todo + own[2][:3] + steps[2][3] + own[2][3:] + own[3]
     else:
-        todo = tiny[0] + todo + tiny[1] + tiny[2] + tiny[3] + tiny[4]
-    for task in todo:
-        task()
+        todo += steps[1][2] + steps[0][3] + steps[1][3]
+    progress(len(todo))
+    open_ends.pop()()
     scatter.drain()
+    shipped_all()
     for copy in (to_corner, to_away, to_beside):
         copy.wait_send()
 
 
-def backward(top, saved, vectors, table, page, expand, reduce, carried_page=None):
+def backward(top, saved, vectors, table, page, expand, reduce, *passed):
     source, normed, query = saved[:3]
     rows, width = top.shape
     inner = expand.shape[1]
     anywhere = pl.BlockSpec(memory_space=pl.ANY)
     inside = pl.BlockSpec(memory_space=pltpu.VMEM)
-    carried = carried_page is not None
-    kinds = (COLUMNS, ROWS, COLUMNS, COLUMNS, TINY) if carried else (ROWS, COLUMNS, TINY)
+    carried = len(passed) == 2
+    kinds = (COLUMNS, ROWS, COLUMNS, COLUMNS) if carried else (ROWS, COLUMNS)
     outs = [
-        jax.ShapeDtypeStruct((rows, width), LOW), jax.ShapeDtypeStruct(reduce.shape, LOW),
-        jax.ShapeDtypeStruct((16, 72, inner), LOW), jax.ShapeDtypeStruct((16, 72, inner), LOW),
-        jax.ShapeDtypeStruct((16, 16, 128), F32),
+        jax.ShapeDtypeStruct((rows, width), LOW), jax.ShapeDtypeStruct((16, 128) if carried else (16, 16, 128), F32),
+        jax.ShapeDtypeStruct(reduce.shape, LOW), jax.ShapeDtypeStruct((16, 72, inner), LOW),
+        jax.ShapeDtypeStruct((16, 72, inner), LOW), jax.ShapeDtypeStruct((2, rows, width), LOW),
     ]
     outs += [final_shape(kind) for kind in kinds]
     for kind in kinds:
@@ -1528,22 +1767,23 @@
         pltpu.VMEM((3, 256, width), LOW), pltpu.VMEM((3, WIDE, 256), LOW), pltpu.VMEM((WIDE, WIDE), LOW),
         pltpu.VMEM((rows, WIDE), F32), tall, tall, pltpu.VMEM((2, 16, 72, 256), LOW), pltpu.VMEM((2, 256, width), LOW),
         pltpu.VMEM((8, inner), F32), pltpu.VMEM((rows, WIDE), F32), pltpu.VMEM((2, rows, WIDE), F32),
-        pair, pair, pair, pair, pair, pair, pltpu.VMEM((8, 128), F32), pltpu.VMEM((rows, inner), F32),
+        pair, pair, pair, pair, pair, pair, pltpu.VMEM((rows, inner), LOW), pltpu.VMEM((rows, inner), LOW),
         pltpu.VMEM((rows, width), F32), pltpu.VMEM((rows, WIDE), LOW), pltpu.VMEM((8, width), F32),
-        pltpu.VMEM((16, 16, 128), F32), dma((3,)), dma((3,)), dma(()), dma((2,)), dma((2,)), dma((3,)), dma((3,)),
-    ] + work_shapes(kinds)
+        pltpu.VMEM((2, 16, 16, 128), F32), dma((3,)), dma((3,)), dma(()), dma((2,)), dma((2,)), dma((3,)), dma((3,)),
+        dma((3,)), dma((3,)), dma(()),
+    ] + tiny_shapes() + work_shapes(kinds)
     res = pl.pallas_call(
         partial(backward_kernel, carried),
         out_shape=tuple(outs),
-        in_specs=[inside] * 17 + [anywhere] * (4 if carried else 3),
-        out_specs=(inside,) + (anywhere,) * (len(outs) - 1),
+        in_specs=[inside] * 17 + [anywhere] * 4 + [inside] * (len(passed) - 1),
+        out_specs=(inside,) * 2 + (anywhere,) * (len(outs) - 2),
         scratch_shapes=scratch,
         compiler_params=pltpu.CompilerParams(
             collective_id=4 if carried else 5, has_side_effects=True, vmem_limit_bytes=62 << 20
         ),
         name="backward_sum" if carried else "backward",
-    )(top, source, vectors, table, *saved[1:], page, expand, reduce, *((carried_page,) if carried else ()))
-    return res[0], res[3], res[5 : 5 + len(kinds)]
+    )(top, source, vectors, table, *saved[1:], page, expand, reduce, *passed)
+    return res[0], (res[4], res[1]), res[5][None], res[6 : 6 + len(kinds)]
 
 
 def spread(width):
@@ -1556,11 +1796,6 @@
 def small_of(page):
     part = page[:, 68, : 12 * 68].astype(F32).reshape(16, 12, 68).transpose(1, 0, 2)
     return part[:8].reshape(8, -1), part[8:].transpose(1, 0, 2).reshape(1, -1)
-
-
-def layer_forward(source, small, wide, weights, table, shards=None):
-    saved, gathered = forward(source, small, wide, table, *weights, shards=shards)
-    return saved[13], (source,) + tuple(saved[:13]), gathered
 
 
 def four_by_four(
@@ -1581,8 +1816,6 @@
     reduce_bias,
 ):
     core = lax.axis_index(SECTION)
-    line = lax.axis_index(LINE)
-    low_chunk = jnp.where(line < 2, line, 3 - line)
     width = HEADS * HDIM
     packed = jnp.concatenate(
         [
@@ -1602,45 +1835,36 @@
         [jnp.concatenate([joint_weight[0], output_weight[0]], axis=1), packed], axis=0
     )
     expand_shard = jnp.pad(expand_weight[0], ((0, 4), (0, 0)))
-    other = swapped(jnp.where(core == 0, expand_shard, attention_shard), SECTION, 1)
-    lower = jnp.where(core == 0, attention_shard, other)
-    upper = jnp.where(core == 0, other, expand_shard)
-    reduce_other = swapped(reduce_weight[0], SECTION, 1)
-    lower_reduce = jnp.where(core == 0, reduce_weight[0], reduce_other)
-    upper_reduce = jnp.where(core == 0, reduce_other, reduce_weight[0])
-    rows = to_rows(inputs, core, line)
-    top = to_rows(cotangent, core, line)
+    reduce_shard = reduce_weight[0]
     table = spread(width)
 
-    def prepared(pages):
-        small, wide = small_of(pages[0])
-        weights = (
-            pages[0].reshape(-1, 4 * width),
-            pages[1].reshape(-1, 4 * width),
-            pages[2].reshape(-1, width),
-        )
-        return small, wide, weights
-
-    layers = [prepared(gather_pages((lower, lower_reduce)))]
-    small, wide, weights = layers[0]
-    middle_rows, saved_lower, upper_pages = layer_forward(
-        rows, small, wide, weights, table, (upper, upper_reduce)
-    )
-    layers.append(prepared(upper_pages))
-    small, wide, weights = layers[1]
-    final_rows, saved_upper, _ = layer_forward(middle_rows, small, wide, weights, table)
-    layer_outputs = from_rows(middle_rows, final_rows, core, line)
-    upper_grad, upper_attention, upper_sums = backward(top, saved_upper, small, table, *weights)
-    small, wide, weights = layers[0]
-    lower_grad, _, lower_sums = backward(
-        upper_grad, saved_lower, small, table, *weights, carried_page=upper_attention
-    )
-    input_grads = from_rows(lower_grad, upper_grad, core, line)
+    def flat(page):
+        return page.reshape(-1, page.shape[2])
+
+    lower_page, rows = gather_page(attention_shard, inputs)
+    small, wide = small_of(lower_page)
+    shards = ((0, True, expand_shard), (0, False, reduce_shard), (1, True, attention_shard))
+    saved, (lower_expand, lower_reduce, upper_page), _ = forward(rows, small, wide, table, flat(lower_page), shards)
+    weights = (flat(lower_page), flat(lower_expand), flat(lower_reduce))
+    saved_lower, middle_rows = (rows,) + tuple(saved[:13]), saved[13]
+    upper_small, upper_wide = small_of(upper_page)
+    shards = ((1, True, expand_shard), (1, False, reduce_shard))
+    saved, (upper_expand, upper_reduce), (top,) = forward(
+        middle_rows, upper_small, upper_wide, table, flat(upper_page), shards, (cotangent,)
+    )
+    upper_weights = (flat(upper_page), flat(upper_expand), flat(upper_reduce))
+    saved_upper, final_rows = (middle_rows,) + tuple(saved[:13]), saved[13]
+    upper_grad, upper_pages, layer_outputs, upper_sums = backward(
+        top, saved_upper, upper_small, table, *upper_weights, final_rows
+    )
+    _, (_, vectors), input_grads, lower_sums = backward(
+        upper_grad, saved_lower, small, table, *weights, *upper_pages
+    )
     own = core == 0
     attention_sum = jnp.where(own, lower_sums[3], lower_sums[0])
     expand_sum = jnp.where(own, lower_sums[2], upper_sums[1])
     reduce_sum = jnp.where(own, lower_sums[1], upper_sums[0])
-    vectors = jnp.where(own, lower_sums[4], upper_sums[2])[:12, :68]
+    vectors = vectors[:12, :68]
     return (
         layer_outputs,
         input_grads,

time: 978 us -> 748 us (0.76)
  the two profiles are of different devices: /device:TPU:9 before, /device:TPU:0 now
where the time goes in v5:
time: 748 us; the launch traced here: 742 us
  Pallas kernels  715 us (96%)
  local copies, waits for them, and re-layouts  16.4 us (2%)
  other arithmetic  9.17 us (1%)
    pallas_call x2, Pallas kernels, backward(): pl.pallas_call(partial(backward_kernel, carried), out_shape=tuple(outs),...  383 us
    pallas_call x2, Pallas kernels, forward(): pl.pallas_call(partial(forward_kernel, forms), out_shape=tuple(outs), in_...  275 us
    pallas_call x1, Pallas kernels, gather_page(): pl.pallas_call(gather_kernel, out_shape=tuple(outs), in_specs=[anywhere]...  57 us

profile of v5, /device:TPU:0, one launch (start us, length us, event | category | flops | bytes accessed | tf_op | source)
XLA Modules:
  0.0 741.7 jit_solution(11979924801003088753)
XLA Ops:
  0.9 2.9 fusion.1.refs_3_
  4.0 0.9 fusion.4.shard.refs_7_
  5.0 1.4 copy.41.refs_0_
  6.4 57.0 %gather_page.1 = (bf16[16,72,4352]{2,1,0:T(8,128)(2,1)}, bf16[72,2176]{1,0:T(8,128)(2,1)}, bf16[256,1088]{1,0:T(8,128)(2,1)}) custom-call(bf16[72,4352]{1,0:T(8,128)(2,1)} %fusion.4.shard.refs_7_, bf16[2,256,1088]{2,1,0:T(8,128)(2,1)} %copy.41.refs_0_), custom_call_target="tpu_custom_call" | custom-call | tf_op jit(solution)/shard_map/gather_page/pallas_call | solution.py:793
  63.5 1.1 convert_reduce_fusion.1
  64.8 0.7 reshape.73.refs_1_.refs_2_
  65.5 0.7 reshape.74.refs_2_
  66.2 0.9 pad.9.refs_5_
  67.1 153.1 %forward.2 = (bf16[256,1152]{1,0:T(8,128)(2,1)}, bf16[256,1152]{1,0:T(8,128)(2,1)}, bf16[2,256,1152]{2,1,0:T(8,128)(2,1)}, bf16[2,256,1152]{2,1,0:T(8,128)(2,1)}...) custom-call(bf16[256,1088]{1,0:T(8,128)(2,1)} %get-tuple-element.63., ...), custom_call_target="tpu_custom_call" | custom-call | tf_op jit(solution)/shard_map/forward/pallas_call | solution.py:1052
  220.2 1.1 convert_reduce_fusion
  221.5 0.7 reshape.76.refs_1_.refs_2_
  222.2 0.7 reshape.77.refs_2_
  222.9 1.4 copy.44.refs_7_
  224.3 121.9 %forward.3 = (bf16[256,1152]{1,0:T(8,128)(2,1)}, bf16[256,1152]{1,0:T(8,128)(2,1)}, bf16[2,256,1152]{2,1,0:T(8,128)(2,1)}, bf16[2,256,1152]{2,1,0:T(8,128)(2,1)}...) custom-call(bf16[256,1088]{1,0:T(8,128)(2,1)} %get-tuple-element.65., ...), custom_call_target="tpu_custom_call" | custom-call | tf_op jit(solution)/shard_map/forward/pallas_call | solution.py:1052
  346.2 150.1 %backward.1 = (bf16[256,1088]{1,0:T(8,128)(2,1)}, f32[16,16,128]{2,1,0:T(8,128)}, bf16[4352,1088]{1,0:T(8,128)(2,1)}, bf16[16,72,4352]{2,1,0:T(8,128)(2,1)}, bf1...) custom-call(bf16[256,1088]{1,0:T(8,128)(2,1)} %get-tuple-element.67., ...), custom_call_target="tpu_custom_call" | custom-call | tf_op jit(solution)/shard_map/backward/pallas_call | solution.py:1775
  496.3 232.8 %backward_sum.1 = (bf16[256,1088]{1,0:T(8,128)(2,1)}, f32[16,128]{1,0:T(8,128)}, bf16[4352,1088]{1,0:T(8,128)(2,1)}, bf16[16,72,4352]{2,1,0:T(8,128)(2,1)}, bf16...) custom-call(bf16[256,1088]{1,0:T(8,128)(2,1)} %get-tuple-element.85., ...), custom_call_target="tpu_custom_call" | custom-call | tf_op jit(solution)/shard_map/backward_sum/pallas_call | solution.py:1775
  729.2 2.6 select_bitcast_fusion
  732.0 2.2 copy.49
  734.5 1.9 copy.47
  736.5 1.0 copy.48
  737.6 1.4 copy.46
  738.9 0.5 fusion.17
  739.5 0.6 reshape.83
  740.1 1.4 copy.45
  (66 shorter events, 1.2 us)
Async XLA Ops:
  0.7 3.1 copy-start.13
  0.7 3.1 copy-start.14
  0.8 3.1 copy-start.15
  0.8 3.1 copy-start.16
  0.8 3.1 copy-start.17
  0.8 3.1 copy-start.18
  0.8 3.0 copy-start.19
  0.8 3.0 copy-start.20
  0.8 3.0 copy-start.21
  0.8 3.2 copy-start.10
  0.9 3.1 copy-start.11
  3.8 1.2 copy-start.7
  6.4 59.8 %copy-start.9 = (bf16[1,68,4352]{2,1,0:T(8,128)(2,1)S(1)}, bf16[1,68,4352]{2,1,0:T(8,128)(2,1)}, u32[]{:S(2)}) copy-start(bf16[1,68,4352]{2,1,0:T(8,128)(2,1)} %param.26) | copy-start | bytes 1775620
  67.1 155.8 %copy-start.8 = (bf16[2,256,1088]{1,2,0:T(8,128)(2,1)S(1)}, bf16[2,256,1088]{1,2,0:T(8,128)(2,1)}, u32[]{:S(2)}) copy-start(bf16[2,256,1088]{1,2,0:T(8,128)(2,1)} %param.16) | copy-start | bytes 3342340
  496.3 232.9 %copy-start.1 = (f32[272,1088]{1,0:T(8,128)S(1)}, f32[272,1088]{1,0:T(8,128)}, u32[]{:S(2)}) copy-start(f32[272,1088]{1,0:T(8,128)} %get-tuple-element.110) | copy-start | bytes 3551236
  729.1 2.6 copy-start
  729.2 2.6 copy-start.4
  731.8 2.4 copy-start.3
  732.0 2.2 copy-start.2
  734.5 3.1 copy-start.6
  737.5 1.4 copy-start.12
  737.5 2.6 copy-start.5

commit v6 on v5

--- a/solution.py
+++ b/solution.py
@@ -2,6 +2,7 @@
 
 import jax
 import jax.numpy as jnp
+import numpy as np
 from jax import lax
 from jax.experimental import pallas as pl
 from jax.experimental.pallas import tpu as pltpu
@@ -813,11 +814,13 @@
     shards, refs = refs[5 : 5 + count], refs[5 + count :]
     if moving:
         row_source, refs = refs[0], refs[1:]
-    (normed_out, query_out, here, beside, away, corner, attended_out, log_out, attended_low, middle_out,
-     second_out, active_out, slope_out, result_out) = refs[:14]
-    outs, refs = refs[14 : 14 + 2 * count], refs[14 + 2 * count :]
+    stored, refs = refs[:14], refs[14:]
+    outs, refs = refs[: 2 * count], refs[2 * count :]
     if moving:
         row_target, row_sems, refs = refs[0], refs[-3:], refs[1:-3]
+    held, store_sem, refs = refs[:14], refs[14], refs[15:]
+    (normed_out, query_out, here, beside, away, corner, attended_out, log_out, attended_low, middle_out,
+     second_out, active_out, slope_out, result_out) = held
     page, expand, reduce, mixture, result, mixed, stats, page_sem, expand_sem, reduce_sem, pair_send, pair_recv = refs[:12]
     place_of = places()
     core, rings, lines, toward = place_of
@@ -825,6 +828,13 @@
     half = rows // 2
     first = low_place(lines[0]) == 0
 
+    def store_copy(i):
+        return pltpu.make_async_copy(held[i], stored[i], store_sem.at[i])
+
+    def store(*numbers):
+        for i in numbers:
+            store_copy(i).start()
+
     def page_copy(i):
         at = pl.ds(pl.multiple_of(i * 256, 256), 256)
         return pltpu.make_async_copy(page_hbm.at[:, at], page.at[:, at], page_sem.at[i])
@@ -863,6 +873,7 @@
     unit, _ = normal_parts(x[...].astype(F32))
     normed = (unit * vectors[0:1] + vectors[1:2]).astype(LOW)
     normed_out[...] = mm(normed, table[...]).astype(LOW)
+    store(0)
 
     def column(i, _):
         page_copy(i).wait()
@@ -890,8 +901,10 @@
     query = ((mixture[:, :width] + vectors[2:3]).astype(LOW).astype(F32) * HDIM ** (-0.5)).astype(LOW)
     query_out[:, :width] = query
     query_out[:, width:] = blank
+    store(1, 2)
     progress(1)
     to_beside.wait_recv()
+    store(3)
 
     def block(kind, near, part, at):
         rows_at = pl.ds(part * half, half)
@@ -933,8 +946,10 @@
     progress(8)
     to_away.wait_recv()
     to_corner.start()
+    store(4)
     progress(2)
     to_corner.wait_recv()
+    store(5)
 
     def far_pair(p, _):
         at = pl.ds(pl.multiple_of(p * 128, 128), 128)
@@ -966,14 +981,18 @@
 
     lax.fori_loop(13, tiles, late, 0)
     lead = 4 * width - WIDE
+    store(6, 7)
     attended_low[...] = mm(attended_out[:, :width].astype(LOW), table[...]).astype(LOW)
+    store(8)
     blended = mm(attended_low[...], page[:, lead:])
     middle = x[...].astype(F32) + (blended[:, 3 * width - lead :] + vectors[4:5])
     middle_out[...] = middle
+    store(9)
     progress(2)
     unit, _ = normal_parts(middle)
     second = (unit * vectors[6:7] + vectors[7:8]).astype(LOW)
     second_out[...] = mm(second, table[...]).astype(LOW)
+    store(10)
     result[...] = middle + vectors[5:6]
 
     complete(0)
@@ -995,6 +1014,7 @@
     for begin_at in range(0, tiles, 2):
         lax.fori_loop(begin_at, min(begin_at + 2, tiles), inner, 0)
         progress(3)
+    store(11, 12)
     complete(1)
     begin(reduce_copy, 16)
 
@@ -1011,8 +1031,11 @@
 
     lax.fori_loop(0, tiles, outer, 0)
     result_out[...] = result[...].astype(LOW)
+    store(13)
     progress(len(todo))
     drain()
+    for i in range(14):
+        store_copy(i).wait()
     if moving:
         for copy in row_copies(place_of, row_source, row_target, *row_sems):
             copy.wait()
@@ -1038,8 +1061,8 @@
     ]
     count = len(outs)
     dma = pltpu.SemaphoreType.DMA
-    scratch = [
-        pltpu.VMEM(page.shape, LOW), pltpu.VMEM((16, 72, inner), LOW), pltpu.VMEM((inner, width), LOW),
+    scratch = [pltpu.VMEM(out.shape, out.dtype) for out in outs] + [
+        dma((count,)), pltpu.VMEM(page.shape, LOW), pltpu.VMEM((16, 72, inner), LOW), pltpu.VMEM((inner, width), LOW),
         pltpu.VMEM((rows, 13 * 256), F32), pltpu.VMEM((rows, width), F32),
         pltpu.VMEM((pairs, 2, 128, rows), F32), pltpu.VMEM((pairs, 4, rows), F32),
         dma((inner // 256,)), dma((inner // 256,)), dma((16,)), dma((3,)), dma((3,)),
@@ -1053,7 +1076,7 @@
         partial(forward_kernel, forms),
         out_shape=tuple(outs),
         in_specs=[inside] * 4 + [anywhere] * (1 + len(shards) + len(moved)),
-        out_specs=(inside,) * count + (anywhere,) * (len(outs) - count),
+        out_specs=(anywhere,) * len(outs),
         scratch_shapes=scratch,
         compiler_params=pltpu.CompilerParams(
             collective_id=len(shards), has_side_effects=True, vmem_limit_bytes=60 << 20
@@ -1295,7 +1318,7 @@
 
 
 def in_turn(earlier, later, done=()):
-    return later[0] + earlier[2][:2] + later[1][:4] + earlier[2][2:] + list(done) + later[1][4:]
+    return later[0] + earlier[2][:2] + later[1][:4] + list(done) + earlier[2][2:] + later[1][4:]
 
 
 def tiny_shapes():
@@ -1357,63 +1380,36 @@
     return [(True, step) for step in (zero, one, two, three, four)]
 
 
-def backward_kernel(carried, *refs):
-    (top, x, vectors, table, normed_in, query, here, beside, away, corner, attended, logs, attended_low, middle,
-     second, active, slope) = refs[:17]
-    page_hbm, expand_hbm, reduce_hbm = refs[17:20]
-    refs = refs[20:]
-    passed, refs = refs[0], refs[1:]
-    if carried:
-        passed_small, refs = refs[0], refs[1:]
-    result_out, small_out, page_reduce, page_expand, page_attention, shipped = refs[:6]
-    refs = refs[6:]
-    kinds = (COLUMNS, ROWS, COLUMNS, COLUMNS) if carried else (ROWS, COLUMNS)
-    owners = (1, 0, 0, 0) if carried else (1, 1)
-    pages = (page_reduce, page_expand)
-    if carried:
-        pages = (passed, page_reduce, page_expand, page_attention)
+def backward_kernel(*refs):
+    vectors_of, table, refs = refs[:2], refs[2], refs[3:]
+    stored_of, refs = ((None,) + refs[:14], refs[14:29]), refs[29:]
+    weights_of, outer_rows, refs = (refs[:3], refs[3:6]), refs[6], refs[7:]
+    small_out, refs = refs[0], refs[1:]
+    pages_of, refs = (refs[:3], refs[3:6]), refs[6:]
+    shipped_of, refs = refs[:2], refs[2:]
+    reduce_final, expand_final, attention_final, refs = refs[0], refs[1], refs[2], refs[3:]
+    kinds = (ROWS, COLUMNS, COLUMNS) * 2
+    owners = (1, 1, 1, 0, 0, 0)
     n = len(kinds)
-    finals, refs = refs[:n], refs[n:]
     lands, refs = [refs[5 * t : 5 * t + 5] for t in range(n)], refs[5 * n :]
     (reduce_ring, expand_ring, output, second_sum, left_one, left_two, stage_wide, stage_tall, wide_sum, query_sum,
-     here_sum, beside_give, away_give, corner_give, beside_got, away_got, corner_got, hidden_all, mixture, grad_middle,
-     grad_attended, sums, both, reduce_sem, expand_sem, output_sem, wide_sem, tall_sem, pair_send, pair_recv, ship_send, ship_recv, ship_sem) = refs[:33]
+     here_sum, beside_give, away_give, corner_give, beside_got, away_got_one, away_got_two, corner_got, hidden_all, mixture,
+     grad_middle, grad_attended, sums, both, result_one, result_two, reduce_sem, expand_sem, output_sem, wide_sem, tall_sem,
+     pair_send, pair_recv, ship_send, ship_recv, ship_sem) = refs[:36]
+    refs = refs[36:]
+    tiny_refs, held, load_sem, refs = refs[:7], refs[7:22], refs[22], refs[23:]
+    (top, x, normed_in, query, here, beside, away, corner, attended, logs, attended_low, middle, second, active,
+     slope) = held
     place_of = places()
     core, rings, lines, toward = place_of
-    tiny_refs, refs = refs[33:40], refs[40:]
-    scatter = Scatter(kinds, pages, lands, finals, owners, refs, place_of)
+    scatter = Scatter(kinds, pages_of[1] + pages_of[0], lands, (reduce_final, expand_final, attention_final) * 2, owners, refs, place_of)
+    steps = [scatter.steps(t) for t in range(n)]
     rows, width = top.shape
     half = rows // 2
     first = low_place(lines[0]) == 0
-    tiles = expand_hbm.shape[1] // 256
+    tiles = weights_of[0][1].shape[1] // 256
     lead = 4 * width - WIDE
     edge = 3 * width
-
-    def tile_at(i):
-        return pl.ds(pl.multiple_of(i * 256, 256), 256)
-
-    def reduce_copy(i):
-        slot = lax.rem(i, 3)
-        return pltpu.make_async_copy(reduce_hbm.at[tile_at(i)], reduce_ring.at[slot], reduce_sem.at[slot])
-
-    def expand_copy(i, source):
-        slot = lax.rem(i, 3)
-        return pltpu.make_async_copy(source.at[:, tile_at(i)], expand_ring.at[slot], expand_sem.at[slot])
-
-    def wide_copy(i, target):
-        slot = lax.rem(i, 2)
-        return pltpu.make_async_copy(stage_wide.at[slot], target.at[:, :, tile_at(i)], wide_sem.at[slot])
-
-    def tall_copy(i):
-        slot = lax.rem(i, 2)
-        return pltpu.make_async_copy(stage_tall.at[slot], page_reduce.at[tile_at(i)], tall_sem.at[slot])
-
-    for i in range(3):
-        reduce_copy(i).start()
-        expand_copy(i, expand_hbm).start()
-    output_copy = pltpu.make_async_copy(page_hbm.at[:, pl.ds(lead, WIDE)], output, output_sem)
-    output_copy.start()
-    greet(toward)
     todo, open_ends = [], []
 
     def progress(count):
@@ -1427,24 +1423,27 @@
                     open_ends.pop()()
                 open_ends.append(ended)
 
+    def row(value):
+        return jnp.sum(value, axis=0, keepdims=True)
+
     which = lines[0] // 2
     mine = pl.ds(pl.multiple_of(core * half, half), half)
     other = pl.ds(pl.multiple_of((1 - core) * half, half), half)
     near_rows = pl.ds(pl.multiple_of(which * half, half), half)
     far_rows = pl.ds(pl.multiple_of((1 - which) * half, half), half)
 
-    def ship_copies(rows_ref):
-        target = shipped.at[which, mine]
-        near, away = rows_ref.at[near_rows], rows_ref.at[far_rows]
-        ways = ((near, SIBLING), (away, (LEVEL, 3)), (away, (CORNER, 3)))
+    def ship_copies(number, rows_ref):
+        target = shipped_of[number].at[which, mine]
+        near, distant = rows_ref.at[near_rows], rows_ref.at[far_rows]
+        ways = ((near, SIBLING), (distant, (LEVEL, 3)), (distant, (CORNER, 3)))
         remote = [
-            remote_copy(source, target, ship_send.at[index], ship_recv.at[index], toward[to])
+            remote_copy(source, target, ship_send.at[3 * number + index], ship_recv.at[3 * number + index], toward[to])
             for index, (source, to) in enumerate(ways)
         ]
-        return pltpu.make_async_copy(near, target, ship_sem), remote
-
-    def ship(layer, rows_ref):
-        local, remote = ship_copies(rows_ref)
+        return pltpu.make_async_copy(near, target, ship_sem.at[number]), remote
+
+    def ship(number, layer, rows_ref):
+        local, remote = ship_copies(number, rows_ref)
 
         def act(index):
             for copy in (local, remote[1]) if index == layer else (remote[0], remote[2]):
@@ -1452,350 +1451,406 @@
 
         per_core(core, act)
 
-    def shipped_all():
-        local, remote = ship_copies(top)
+    def shipped_all(number):
+        local, remote = ship_copies(number, result_one)
         local.wait()
         for index, (sequence, part) in enumerate(((which, other), (1 - which, mine), (1 - which, other))):
             remote[index].wait_send()
-            ref = shipped.at[sequence, part]
-            remote_copy(ref, ref, ship_send.at[index], ship_recv.at[index], toward[SIBLING]).wait_recv()
-
-    steps = [scatter.steps(t) for t in range(n)]
-    if carried:
-        scatter.give_all(0)
-        todo += steps[0][0] + steps[0][1]
-        ship(1, top)
-    else:
-        ship(0, x)
-        ship(1, passed)
-    second_sum[...] = jnp.zeros_like(second_sum)
-
-    def tall_tile(i, _):
-        side = lax.rem(i, 2)
-
-        @pl.when(i >= 2)
-        def _():
-            tall_copy(i - 2).wait()
-
-        stage_tall[side] = mm_tn(active[:, tile_at(i)], top[...]).astype(LOW)
-        tall_copy(i).start()
-        return 0
-
-    def tall_page(t):
-        for begin_at in range(0, tiles, 6):
-            lax.fori_loop(begin_at, min(begin_at + 6, tiles), tall_tile, 0)
+            ref = shipped_of[number].at[sequence, part]
+            place = 3 * number + index
+            remote_copy(ref, ref, ship_send.at[place], ship_recv.at[place], toward[SIBLING]).wait_recv()
+
+    def load_copy(layer, i):
+        return pltpu.make_async_copy(stored_of[layer][i], held[i], load_sem.at[i])
+
+    def load(layer, *numbers):
+        for i in numbers:
+            load_copy(layer, i).start()
+
+    def pair_copy(layer, source, target, to, number):
+        index = 3 * layer + number
+        return remote_copy(source, target, pair_send.at[index], pair_recv.at[index], toward[to])
+
+    def pair_copies(layer):
+        away_got = away_got_one if layer == 1 else away_got_two
+        return (
+            pair_copy(layer, corner_give, corner_got, SIBLING, 0),
+            pair_copy(layer, away_give, away_got, (LEVEL, 1), 1),
+            pair_copy(layer, beside_give, beside_got, SIBLING, 2),
+        )
+
+    def layer_pass(layer):
+        page_hbm, expand_hbm, reduce_hbm = weights_of[layer]
+        page_reduce, page_expand, page_attention = pages_of[layer]
+        vectors = vectors_of[layer]
+        away_got = away_got_one if layer == 1 else away_got_two
+
+        def tile_at(i):
+            return pl.ds(pl.multiple_of(i * 256, 256), 256)
+
+        def reduce_copy(i):
+            slot = lax.rem(i, 3)
+            return pltpu.make_async_copy(reduce_hbm.at[tile_at(i)], reduce_ring.at[slot], reduce_sem.at[slot])
+
+        def expand_copy(i, source):
+            slot = lax.rem(i, 3)
+            return pltpu.make_async_copy(source.at[:, tile_at(i)], expand_ring.at[slot], expand_sem.at[slot])
+
+        def wide_copy(i, target):
+            slot = lax.rem(i, 2)
+            return pltpu.make_async_copy(stage_wide.at[slot], target.at[:, :, tile_at(i)], wide_sem.at[slot])
+
+        def tall_copy(i):
+            slot = lax.rem(i, 2)
+            return pltpu.make_async_copy(stage_tall.at[slot], page_reduce.at[tile_at(i)], tall_sem.at[slot])
+
+        def loaded(*numbers):
+            for i in numbers:
+                load_copy(layer, i).wait()
+
+        for i in range(3):
+            reduce_copy(i).start()
+            expand_copy(i, expand_hbm).start()
+        output_copy = pltpu.make_async_copy(page_hbm.at[:, pl.ds(lead, WIDE)], output, output_sem)
+        output_copy.start()
+        if layer == 1:
+            load(1, 11, 3, 8, 9, 4, 5, 6, 7, 10, 2, 1)
+            greet(toward)
+            ship(0, 0, stored_of[1][1])
+            ship(0, 1, outer_rows)
+        else:
+            top[...] = result_one[...]
+            for copy in pair_copies(1):
+                copy.wait_send()
+        second_sum[...] = jnp.zeros_like(second_sum)
+
+        def tall_tile(i, _):
+            side = lax.rem(i, 2)
+
+            @pl.when(i >= 2)
+            def _():
+                tall_copy(i - 2).wait()
+
+            stage_tall[side] = mm_tn(active[:, tile_at(i)], top[...]).astype(LOW)
+            tall_copy(i).start()
+            return 0
+
+        def tall_page(t):
+            for begin_at in range(0, tiles, 6):
+                lax.fori_loop(begin_at, min(begin_at + 6, tiles), tall_tile, 0)
+                progress(1)
+            for i in (tiles - 2, tiles - 1):
+                tall_copy(i).wait()
+            scatter.give_all(t)
+
+        def wide_tile(i, _):
+            side = lax.rem(i, 2)
+
+            @pl.when(i >= 2)
+            def _():
+                wide_copy(i - 2, page_expand).wait()
+
+            stage_wide[side] = mm(left_one[...], hidden_all[:, tile_at(i)]).reshape(16, 72, 256).astype(LOW)
+            wide_copy(i, page_expand).start()
+            return 0
+
+        def wide_page(t):
+            for begin_at in range(0, tiles, 5):
+                lax.fori_loop(begin_at, min(begin_at + 5, tiles), wide_tile, 0)
+                progress(1)
+            for i in (tiles - 2, tiles - 1):
+                wide_copy(i, page_expand).wait()
+            scatter.give_all(t)
+
+        if layer == 1:
+            loaded(0, 13)
+            tall_page(0)
+            todo.extend(steps[0][0] + steps[0][1])
+        loaded(14, 12)
+        left_one[...] = second[...].T
+
+        def feed_tile(i, _):
+            at = tile_at(i)
+            slot = lax.rem(i, 3)
+            reduce_copy(i).wait()
+            hidden = (mm_nt(top[...], reduce_ring[slot]) * slope[:, at].astype(F32)).astype(LOW)
+            wide_sum[0:1, at] = jnp.sum(hidden.astype(F32), axis=0, keepdims=True)
+            hidden_all[:, at] = hidden
+            expand_copy(i, expand_hbm).wait()
+            second_sum[...] += mm_nt(hidden, expand_ring[slot])
+
+            @pl.when(i + 3 < tiles)
+            def _():
+                reduce_copy(i + 3).start()
+                expand_copy(i + 3, expand_hbm).start()
+
+            return 0
+
+        for begin_at in range(0, tiles, 2):
+            lax.fori_loop(begin_at, min(begin_at + 2, tiles), feed_tile, 0)
             progress(1)
+        for i in range(3):
+            expand_copy(i, page_hbm).start()
+
+        loaded(11)
+        upstream = top[...].astype(F32)
+        grad_second = close_up(second_sum[...], table[...])
+        unit, inverse = normal_parts(middle[...])
+        sums[6:7] = row(grad_second * unit)
+        sums[7:8] = row(grad_second)
+        sums[5:6] = row(upstream)
+        value = upstream + normal_back(grad_second * vectors[6:7], unit, inverse)
+        grad_middle[...] = value
+        branch = value.astype(LOW)
+        sums[4:5] = row(branch.astype(F32))
+        progress(1)
+        mixture[:, edge:] = branch
+        output_copy.wait()
+        full = jnp.concatenate([jnp.zeros((rows, edge - lead), LOW), branch], axis=1)
+        pulled = mm_nt(full, output[...]).astype(LOW)
+        grad_attended[:, :width] = mm_nt(pulled, table[...]).astype(LOW)
+        grad_attended[:, width:] = jnp.zeros((rows, WIDE - width), LOW)
+        progress(1)
+
+        loaded(3, 8, 9, 4, 5, 6, 7)
+
+        def rows_of(place, at, p):
+            part = slice(place * half, (place + 1) * half)
+            product = (grad_attended[part, at].astype(F32) * attended[part, at]).T
+            delta = jnp.concatenate([row(product[:HDIM]), row(product[HDIM:])], axis=1)
+            return head_pair(query[part, at]), head_pair(grad_attended[part, at]), logs[p, place : place + 1], delta
+
+        def block(kind, near, part, at):
+            rows_at = pl.ds(part * half, half)
+            one, two = (here, beside) if near == 0 else (away, corner)
+            return jnp.concatenate([one[kind, rows_at, at], two[kind, rows_at, at]], axis=0)
+
+        def back(own, keys, values):
+            queries, grads, log, delta = own
+            weights = jnp.exp(mm_nt(keys, queries) - log)
+            lowered = (weights * (mm_nt(values, grads) - delta)).astype(LOW)
+            return mm_tn(keys, lowered), mm(lowered, queries), mm(weights.astype(LOW), grads)
+
+        def put(one, two, part, at, grads):
+            rows_at = pl.ds(part * half, half)
+            for kind, value in enumerate(grads):
+                one[kind, rows_at, at] = value[:half].astype(one.dtype)
+                two[kind, rows_at, at] = value[half:].astype(two.dtype)
+
+        def far_pair(p, _):
+            at = pl.ds(pl.multiple_of(p * 128, 128), 128)
+            low, high = rows_of(0, at, p), rows_of(1, at, p)
+            last_rows = tuple(jnp.where(first, b, a) for a, b in zip(low, high))
+            keys, values = block(0, 1, 0, at), block(1, 1, 0, at)
+            high_query, keys_a, values_a = back(high, keys, values)
+            last_keys = jnp.where(first, block(0, 1, 1, at), keys)
+            last_values = jnp.where(first, block(1, 1, 1, at), values)
+            more, keys_b, values_b = back(last_rows, last_keys, last_values)
+            zero, empty = jnp.zeros_like(keys_b), jnp.zeros_like(more)
+            put(away_give, corner_give, 0, at,
+                (keys_a + jnp.where(first, zero, keys_b), values_a + jnp.where(first, zero, values_b)))
+            put(away_give, corner_give, 1, at, (jnp.where(first, keys_b, zero), jnp.where(first, values_b, zero)))
+            query_sum[:half, at] = from_pair(jnp.where(first, empty, more))
+            query_sum[half:, at] = from_pair(high_query + jnp.where(first, more, empty))
+            return 0
+
+        for begin_at in (0, 3, 6):
+            lax.fori_loop(begin_at, begin_at + 3, far_pair, 0)
+            progress(1)
+
+        to_corner, to_away, to_beside = pair_copies(layer)
+        to_corner.start()
+
+        def near_pair(p, _):
+            at = pl.ds(pl.multiple_of(p * 128, 128), 128)
+            low, high = rows_of(0, at, p), rows_of(1, at, p)
+            keys, values = block(0, 0, 0, at), block(1, 0, 0, at)
+            low_query, keys_a, values_a = back(low, keys, values)
+            high_query, keys_b, values_b = back(high, keys, values)
+            put(here_sum, beside_give, 0, at, (keys_a + keys_b, values_a + values_b))
+            more, keys_a, values_a = back(high, block(0, 0, 1, at), block(1, 0, 1, at))
+            put(here_sum, beside_give, 1, at, (keys_a, values_a))
+            query_sum[:half, at] += from_pair(low_query)
+            query_sum[half:, at] += from_pair(high_query + more)
+            return 0
+
+        lax.fori_loop(0, 2, near_pair, 0)
+        to_corner.wait_recv()
+        for kind in (0, 1):
+            away_give[kind] = (away_give[kind].astype(F32) + corner_got[kind].astype(F32)).astype(LOW)
+        to_away.start()
+        progress(1)
+        for begin_at, end in ((2, 5), (5, 9)):
+            lax.fori_loop(begin_at, end, near_pair, 0)
+            progress(1)
+        to_beside.start()
+        if layer == 1:
+            wide_page(1)
+            todo.extend(in_turn(steps[0], steps[1]))
+        else:
+            loaded(13)
+            tall_page(3)
+            todo.extend(in_turn(steps[2], steps[3], steps[1][3]))
+            wide_page(4)
+            todo.extend(in_turn(steps[3], steps[4], steps[2][3]))
+        low = (query_sum[:, :width] * HDIM ** (-0.5)).astype(LOW)
+        mixture[:, :width] = low
+        sums[2:3] = row(low.astype(F32))
+        loaded(10, 2, 1)
+        left_one[...] = normed_in[...].T
+        left_two[...] = attended_low[...].T
+        second_sum[...] = jnp.zeros_like(second_sum)
+        progress(4)
+        to_beside.wait_recv()
+        to_away.wait_recv()
+        for kind in (0, 1):
+            value = here_sum[kind] + beside_got[kind].astype(F32) + away_got[kind].astype(F32)
+            low = value[:, :width].astype(LOW)
+            mixture[:, (1 + kind) * width : (2 + kind) * width] = low
+        sums[3:4] = row(low.astype(F32))
+
+        def project_tile(i, _):
+            at = tile_at(i)
+            slot = lax.rem(i, 3)
+            column = i * 256 + lax.broadcasted_iota(jnp.int32, (rows, 256), 1)
+            part = mixture[:, at]
+            part = jnp.where(column < edge, part, jnp.zeros_like(part))
+            expand_copy(i, page_hbm).wait()
+            second_sum[...] += mm_nt(part, expand_ring[slot])
+
+            @pl.when(i + 3 < 13)
+            def _():
+                expand_copy(i + 3, page_hbm).start()
+
+            return 0
+
+        for begin_at, end in ((0, 4), (4, 8), (8, 13)):
+            lax.fori_loop(begin_at, end, project_tile, 0)
+            progress(1)
+        grad_normed = close_up(second_sum[...], table[...])
+        unit, inverse = normal_parts(x[...].astype(F32))
+        sums[0:1] = row(grad_normed * unit)
+        sums[1:2] = row(grad_normed)
+        result = result_one if layer == 1 else result_two
+        result[...] = (grad_middle[...] + normal_back(grad_normed * vectors[0:1], unit, inverse)).astype(LOW)
+        if layer == 1:
+            load(0, 14, 12, 11, 3, 8, 9, 4, 5, 6, 7, 13, 10, 2, 1)
+        ship(1, layer, result)
+        progress(2)
+
+        def page_tile(number, i):
+            side = lax.rem(i, 2)
+            at = tile_at(i)
+
+            @pl.when(i >= 2)
+            def _():
+                wide_copy(i - 2, page_attention).wait()
+
+            part = mixture[:, at]
+            if number == 1:
+                value = mm(left_one[...], part)
+            elif number == 2:
+                value = mm(left_two[...], part)
+            else:
+                column = i * 256 + lax.broadcasted_iota(jnp.int32, (rows, 256), 1)
+                zero = jnp.zeros_like(part)
+                value = mm(left_one[...], jnp.where(column < edge, part, zero))
+                value = value + mm(left_two[...], jnp.where(column < edge, zero, part))
+            stage_wide[side] = value.reshape(16, 72, 256).astype(LOW)
+            wide_copy(i, page_attention).start()
+
+        def page_loop(number, begin_at, end):
+            def step(i, _):
+                page_tile(number, i)
+                return 0
+
+            lax.fori_loop(begin_at, end, step, 0)
+
+        whole_tiles = edge // 256
+        for begin_at in range(0, whole_tiles, 4):
+            page_loop(1, begin_at, begin_at + 4)
+            progress(1)
+        page_loop(3, whole_tiles, whole_tiles + 1)
+        page_loop(2, whole_tiles + 1, tiles)
         for i in (tiles - 2, tiles - 1):
-            tall_copy(i).wait()
-        scatter.give_all(t)
-
-    def wide_tile(i, _):
-        side = lax.rem(i, 2)
-
-        @pl.when(i >= 2)
-        def _():
-            wide_copy(i - 2, page_expand).wait()
-
-        stage_wide[side] = mm(left_one[...], hidden_all[:, tile_at(i)]).reshape(16, 72, 256).astype(LOW)
-        wide_copy(i, page_expand).start()
-        return 0
-
-    def wide_page(t):
-        for begin_at in range(0, tiles, 5):
-            lax.fori_loop(begin_at, min(begin_at + 5, tiles), wide_tile, 0)
-            progress(1)
-        for i in (tiles - 2, tiles - 1):
-            wide_copy(i, page_expand).wait()
-        scatter.give_all(t)
-
-    if not carried:
-        tall_page(0)
-        todo += steps[0][0] + steps[0][1]
-    left_one[...] = second[...].T
-
-    def feed_tile(i, _):
-        at = tile_at(i)
-        slot = lax.rem(i, 3)
-        reduce_copy(i).wait()
-        hidden = (mm_nt(top[...], reduce_ring[slot]) * slope[:, at].astype(F32)).astype(LOW)
-        wide_sum[0:1, at] = jnp.sum(hidden.astype(F32), axis=0, keepdims=True)
-        hidden_all[:, at] = hidden
-        expand_copy(i, expand_hbm).wait()
-        second_sum[...] += mm_nt(hidden, expand_ring[slot])
-
-        @pl.when(i + 3 < tiles)
-        def _():
-            reduce_copy(i + 3).start()
-            expand_copy(i + 3, expand_hbm).start()
-
-        return 0
-
-    for begin_at in range(0, tiles, 3):
-        lax.fori_loop(begin_at, min(begin_at + 3, tiles), feed_tile, 0)
-        progress(1)
-    for i in range(3):
-        expand_copy(i, page_hbm).start()
-
-    def row(value):
-        return jnp.sum(value, axis=0, keepdims=True)
-
-    upstream = top[...].astype(F32)
-    grad_second = close_up(second_sum[...], table[...])
-    unit, inverse = normal_parts(middle[...])
-    sums[6:7] = row(grad_second * unit)
-    sums[7:8] = row(grad_second)
-    sums[5:6] = row(upstream)
-    value = upstream + normal_back(grad_second * vectors[6:7], unit, inverse)
-    grad_middle[...] = value
-    branch = value.astype(LOW)
-    sums[4:5] = row(branch.astype(F32))
-    progress(1)
-    mixture[:, edge:] = branch
-    output_copy.wait()
-    full = jnp.concatenate([jnp.zeros((rows, edge - lead), LOW), branch], axis=1)
-    pulled = mm_nt(full, output[...]).astype(LOW)
-    grad_attended[:, :width] = mm_nt(pulled, table[...]).astype(LOW)
-    grad_attended[:, width:] = jnp.zeros((rows, WIDE - width), LOW)
-    progress(1)
-
-    def rows_of(place, at, p):
-        part = slice(place * half, (place + 1) * half)
-        product = (grad_attended[part, at].astype(F32) * attended[part, at]).T
-        delta = jnp.concatenate([row(product[:HDIM]), row(product[HDIM:])], axis=1)
-        return head_pair(query[part, at]), head_pair(grad_attended[part, at]), logs[p, place : place + 1], delta
-
-    def block(kind, near, part, at):
-        rows_at = pl.ds(part * half, half)
-        one, two = (here, beside) if near == 0 else (away, corner)
-        return jnp.concatenate([one[kind, rows_at, at], two[kind, rows_at, at]], axis=0)
-
-    def back(own, keys, values):
-        queries, grads, log, delta = own
-        weights = jnp.exp(mm_nt(keys, queries) - log)
-        lowered = (weights * (mm_nt(values, grads) - delta)).astype(LOW)
-        return mm_tn(keys, lowered), mm(lowered, queries), mm(weights.astype(LOW), grads)
-
-    def put(one, two, part, at, grads):
-        rows_at = pl.ds(part * half, half)
-        for kind, value in enumerate(grads):
-            one[kind, rows_at, at] = value[:half].astype(one.dtype)
-            two[kind, rows_at, at] = value[half:].astype(two.dtype)
-
-    def far_pair(p, _):
-        at = pl.ds(pl.multiple_of(p * 128, 128), 128)
-        low, high = rows_of(0, at, p), rows_of(1, at, p)
-        last_rows = tuple(jnp.where(first, b, a) for a, b in zip(low, high))
-        keys, values = block(0, 1, 0, at), block(1, 1, 0, at)
-        high_query, keys_a, values_a = back(high, keys, values)
-        last_keys = jnp.where(first, block(0, 1, 1, at), keys)
-        last_values = jnp.where(first, block(1, 1, 1, at), values)
-        more, keys_b, values_b = back(last_rows, last_keys, last_values)
-        zero, empty = jnp.zeros_like(keys_b), jnp.zeros_like(more)
-        put(away_give, corner_give, 0, at,
-            (keys_a + jnp.where(first, zero, keys_b), values_a + jnp.where(first, zero, values_b)))
-        put(away_give, corner_give, 1, at, (jnp.where(first, keys_b, zero), jnp.where(first, values_b, zero)))
-        query_sum[:half, at] = from_pair(jnp.where(first, empty, more))
-        query_sum[half:, at] = from_pair(high_query + jnp.where(first, more, empty))
-        return 0
-
-    for begin_at in (0, 3, 6):
-        lax.fori_loop(begin_at, begin_at + 3, far_pair, 0)
-        progress(1)
-
-    def pair_copy(source, target, to, number):
-        return remote_copy(source, target, pair_send.at[number], pair_recv.at[number], toward[to])
-
-    to_corner = pair_copy(corner_give, corner_got, SIBLING, 0)
-    to_away = pair_copy(away_give, away_got, (LEVEL, 1), 1)
-    to_beside = pair_copy(beside_give, beside_got, SIBLING, 2)
-    to_corner.start()
-
-    def near_pair(p, _):
-        at = pl.ds(pl.multiple_of(p * 128, 128), 128)
-        low, high = rows_of(0, at, p), rows_of(1, at, p)
-        keys, values = block(0, 0, 0, at), block(1, 0, 0, at)
-        low_query, keys_a, values_a = back(low, keys, values)
-        high_query, keys_b, values_b = back(high, keys, values)
-        put(here_sum, beside_give, 0, at, (keys_a + keys_b, values_a + values_b))
-        more, keys_a, values_a = back(high, block(0, 0, 1, at), block(1, 0, 1, at))
-        put(here_sum, beside_give, 1, at, (keys_a, values_a))
-        query_sum[:half, at] += from_pair(low_query)
-        query_sum[half:, at] += from_pair(high_query + more)
-        return 0
-
-    lax.fori_loop(0, 2, near_pair, 0)
-    to_corner.wait_recv()
-    for kind in (0, 1):
-        away_give[kind] = (away_give[kind].astype(F32) + corner_got[kind].astype(F32)).astype(LOW)
-    to_away.start()
-    progress(1)
-    for begin_at, end in ((2, 5), (5, 9)):
-        lax.fori_loop(begin_at, end, near_pair, 0)
-        progress(1)
-    to_beside.start()
-    if carried:
-        tall_page(1)
-        todo += in_turn(steps[0], steps[1])
-        wide_page(2)
-        todo += in_turn(steps[1], steps[2], steps[0][3])
-    else:
-        wide_page(1)
-        todo += in_turn(steps[0], steps[1])
-    low = (query_sum[:, :width] * HDIM ** (-0.5)).astype(LOW)
-    mixture[:, :width] = low
-    sums[2:3] = row(low.astype(F32))
-    left_one[...] = normed_in[...].T
-    left_two[...] = attended_low[...].T
-    second_sum[...] = jnp.zeros_like(second_sum)
-    progress(4)
-    to_beside.wait_recv()
-    to_away.wait_recv()
-    for kind in (0, 1):
-        value = here_sum[kind] + beside_got[kind].astype(F32) + away_got[kind].astype(F32)
-        low = value[:, :width].astype(LOW)
-        mixture[:, (1 + kind) * width : (2 + kind) * width] = low
-    sums[3:4] = row(low.astype(F32))
-
-    def project_tile(i, _):
-        at = tile_at(i)
-        slot = lax.rem(i, 3)
-        column = i * 256 + lax.broadcasted_iota(jnp.int32, (rows, 256), 1)
-        part = mixture[:, at]
-        part = jnp.where(column < edge, part, jnp.zeros_like(part))
-        expand_copy(i, page_hbm).wait()
-        second_sum[...] += mm_nt(part, expand_ring[slot])
-
-        @pl.when(i + 3 < 13)
-        def _():
-            expand_copy(i + 3, page_hbm).start()
-
-        return 0
-
-    for begin_at, end in ((0, 4), (4, 8), (8, 13)):
-        lax.fori_loop(begin_at, end, project_tile, 0)
-        progress(1)
-    grad_normed = close_up(second_sum[...], table[...])
-    unit, inverse = normal_parts(x[...].astype(F32))
-    sums[0:1] = row(grad_normed * unit)
-    sums[1:2] = row(grad_normed)
-    result_out[...] = (grad_middle[...] + normal_back(grad_normed * vectors[0:1], unit, inverse)).astype(LOW)
-    if carried:
-        ship(0, result_out)
-    progress(2)
-
-    def page_tile(number, i):
-        side = lax.rem(i, 2)
-        at = tile_at(i)
-
-        @pl.when(i >= 2)
-        def _():
-            wide_copy(i - 2, page_attention).wait()
-
-        part = mixture[:, at]
-        if number == 1:
-            value = mm(left_one[...], part)
-        elif number == 2:
-            value = mm(left_two[...], part)
-        else:
-            column = i * 256 + lax.broadcasted_iota(jnp.int32, (rows, 256), 1)
-            zero = jnp.zeros_like(part)
-            value = mm(left_one[...], jnp.where(column < edge, part, zero))
-            value = value + mm(left_two[...], jnp.where(column < edge, zero, part))
-        stage_wide[side] = value.reshape(16, 72, 256).astype(LOW)
-        wide_copy(i, page_attention).start()
-
-    def page_loop(number, begin_at, end):
-        def step(i, _):
-            page_tile(number, i)
-            return 0
-
-        lax.fori_loop(begin_at, end, step, 0)
-
-    whole_tiles = edge // 256
-    for begin_at in range(0, whole_tiles, 4):
-        page_loop(1, begin_at, begin_at + 4)
-        progress(1)
-    page_loop(3, whole_tiles, whole_tiles + 1)
-    page_loop(2, whole_tiles + 1, tiles)
-    for i in (tiles - 2, tiles - 1):
-        wide_copy(i, page_attention).wait()
-    if carried:
-        scatter.give_all(3)
-    small = both.at[0] if carried else small_out
-    small[...] = jnp.zeros(small.shape, F32)
-    for shard in range(16):
-        small[shard, 0:8, 0:68] = sums[:, shard * 68 : (shard + 1) * 68]
-        for part in range(4):
-            begin_at = shard * 272 + part * 68
-            small[shard, 8 + part : 9 + part, 0:68] = wide_sum[0:1, begin_at : begin_at + 68]
-    if carried:
-        both[1] = passed_small[...]
-        tiny, own = tiny_steps(both, small_out, tiny_refs, place_of), steps[3]
-        todo += in_turn(steps[2], own, steps[1][3])
-        todo = tiny[:1] + todo[:3] + tiny[1:2] + todo[3:6] + tiny[2:3] + todo[6:9] + tiny[3:4] + todo[9:12] + tiny[4:] + todo[12:]
-        todo = todo + own[2][:3] + steps[2][3] + own[2][3:] + own[3]
-    else:
-        todo += steps[1][2] + steps[0][3] + steps[1][3]
+            wide_copy(i, page_attention).wait()
+        scatter.give_all(2 if layer == 1 else 5)
+        if layer == 1:
+            todo.extend(in_turn(steps[1], steps[2], steps[0][3]))
+        small = both.at[layer]
+        small[...] = jnp.zeros(small.shape, F32)
+        for shard in range(16):
+            small[shard, 0:8, 0:68] = sums[:, shard * 68 : (shard + 1) * 68]
+            for part in range(4):
+                begin_at = shard * 272 + part * 68
+                small[shard, 8 + part : 9 + part, 0:68] = wide_sum[0:1, begin_at : begin_at + 68]
+
+    load(1, 0, 13, 14, 12)
+    layer_pass(1)
+    layer_pass(0)
+    tiny = tiny_steps(both, small_out, tiny_refs, place_of)
+    todo += in_turn(steps[4], steps[5], steps[3][3])
+    for place, step in enumerate(tiny):
+        todo.insert(min(4 * place, len(todo)), step)
+    todo += steps[5][2][:3] + steps[4][3] + steps[5][2][3:] + steps[5][3]
     progress(len(todo))
     open_ends.pop()()
     scatter.drain()
-    shipped_all()
-    for copy in (to_corner, to_away, to_beside):
+    shipped_all(0)
+    shipped_all(1)
+    for copy in pair_copies(0):
         copy.wait_send()
 
 
-def backward(top, saved, vectors, table, page, expand, reduce, *passed):
-    source, normed, query = saved[:3]
+def backward(top, saved, vectors, table, weights, outer_rows):
     rows, width = top.shape
-    inner = expand.shape[1]
+    inner = weights[0][1].shape[1]
     anywhere = pl.BlockSpec(memory_space=pl.ANY)
     inside = pl.BlockSpec(memory_space=pltpu.VMEM)
-    carried = len(passed) == 2
-    kinds = (COLUMNS, ROWS, COLUMNS, COLUMNS) if carried else (ROWS, COLUMNS)
-    outs = [
-        jax.ShapeDtypeStruct((rows, width), LOW), jax.ShapeDtypeStruct((16, 128) if carried else (16, 16, 128), F32),
-        jax.ShapeDtypeStruct(reduce.shape, LOW), jax.ShapeDtypeStruct((16, 72, inner), LOW),
-        jax.ShapeDtypeStruct((16, 72, inner), LOW), jax.ShapeDtypeStruct((2, rows, width), LOW),
-    ]
-    outs += [final_shape(kind) for kind in kinds]
+    kinds = (ROWS, COLUMNS, COLUMNS) * 2
+    page = jax.ShapeDtypeStruct((16, 72, inner), LOW)
+    outs = [jax.ShapeDtypeStruct((16, 128), F32)]
+    outs += [jax.ShapeDtypeStruct((inner, width), LOW), page, page] * 2
+    outs += [jax.ShapeDtypeStruct((2, rows, width), LOW)] * 2
+    outs += [final_shape(kind) for kind in kinds[:3]]
     for kind in kinds:
         outs += landing_shapes(kind)
     pair = pltpu.VMEM((2, rows, WIDE), LOW)
     tall = pltpu.VMEM((WIDE, rows), LOW)
+    flat = pltpu.VMEM((rows, width), LOW)
     dma = pltpu.SemaphoreType.DMA
     scratch = [
         pltpu.VMEM((3, 256, width), LOW), pltpu.VMEM((3, WIDE, 256), LOW), pltpu.VMEM((WIDE, WIDE), LOW),
         pltpu.VMEM((rows, WIDE), F32), tall, tall, pltpu.VMEM((2, 16, 72, 256), LOW), pltpu.VMEM((2, 256, width), LOW),
         pltpu.VMEM((8, inner), F32), pltpu.VMEM((rows, WIDE), F32), pltpu.VMEM((2, rows, WIDE), F32),
-        pair, pair, pair, pair, pair, pair, pltpu.VMEM((rows, inner), LOW), pltpu.VMEM((rows, inner), LOW),
+        pair, pair, pair, pair, pair, pair, pair, pltpu.VMEM((rows, inner), LOW), pltpu.VMEM((rows, inner), LOW),
         pltpu.VMEM((rows, width), F32), pltpu.VMEM((rows, WIDE), LOW), pltpu.VMEM((8, width), F32),
-        pltpu.VMEM((2, 16, 16, 128), F32), dma((3,)), dma((3,)), dma(()), dma((2,)), dma((2,)), dma((3,)), dma((3,)),
-        dma((3,)), dma((3,)), dma(()),
-    ] + tiny_shapes() + work_shapes(kinds)
+        pltpu.VMEM((2, 16, 16, 128), F32), flat, flat, dma((3,)), dma((3,)), dma(()), dma((2,)), dma((2,)),
+        dma((6,)), dma((6,)), dma((6,)), dma((6,)), dma((2,)),
+    ] + tiny_shapes() + [pltpu.VMEM(value.shape, value.dtype) for value in (top,) + saved[1]] + [dma((15,))] + work_shapes(kinds)
     res = pl.pallas_call(
-        partial(backward_kernel, carried),
+        backward_kernel,
         out_shape=tuple(outs),
-        in_specs=[inside] * 17 + [anywhere] * 4 + [inside] * (len(passed) - 1),
-        out_specs=(inside,) * 2 + (anywhere,) * (len(outs) - 2),
+        in_specs=[inside] * 3 + [anywhere] * (29 + 7),
+        out_specs=(inside,) + (anywhere,) * (len(outs) - 1),
         scratch_shapes=scratch,
-        compiler_params=pltpu.CompilerParams(
-            collective_id=4 if carried else 5, has_side_effects=True, vmem_limit_bytes=62 << 20
-        ),
-        name="backward_sum" if carried else "backward",
-    )(top, source, vectors, table, *saved[1:], page, expand, reduce, *passed)
-    return res[0], (res[4], res[1]), res[5][None], res[6 : 6 + len(kinds)]
+        compiler_params=pltpu.CompilerParams(collective_id=4, has_side_effects=True, vmem_limit_bytes=63 << 20),
+        name="backward",
+    )(*vectors, table, *saved[0], top, *saved[1], *weights[0], *weights[1], outer_rows)
+    return res[0], res[7][None], res[8][None], res[9:12]
 
 
 def spread(width):
-    row = lax.broadcasted_iota(jnp.int32, (width, 16 * 72), 0)
-    column = lax.broadcasted_iota(jnp.int32, (width, 16 * 72), 1)
-    same = (row // 68 == column // 72) & (row % 68 == column % 72)
-    return same.astype(LOW)
+    feature = np.arange(width)
+    table = np.zeros((width, 16 * 72), np.float32)
+    table[feature, feature // 68 * 72 + feature % 68] = 1
+    return jnp.asarray(table, LOW)
 
 
 def small_of(page):
-    part = page[:, 68, : 12 * 68].astype(F32).reshape(16, 12, 68).transpose(1, 0, 2)
-    return part[:8].reshape(8, -1), part[8:].transpose(1, 0, 2).reshape(1, -1)
+    row = page[:, 68].astype(F32)
+    vectors = row[:, : 8 * 128].reshape(16, 8, 128)[:, :, :68].transpose(1, 0, 2)
+    return vectors.reshape(8, -1), row[:, 8 * 128 : 8 * 128 + 4 * 68].reshape(1, -1)
 
 
 def four_by_four(
@@ -1817,20 +1872,21 @@
 ):
     core = lax.axis_index(SECTION)
     width = HEADS * HDIM
-    packed = jnp.concatenate(
-        [
-            first_gain[0],
-            first_shift[0],
-            query_bias[0],
-            value_bias[0],
-            output_bias[0],
-            reduce_bias[0],
-            second_gain[0],
-            second_shift[0],
-            expand_bias[0],
-        ]
-    )
-    packed = jnp.pad(packed[None], ((0, 3), (0, 4 * width - packed.shape[0])))
+    vectors = (
+        first_gain,
+        first_shift,
+        query_bias,
+        value_bias,
+        output_bias,
+        reduce_bias,
+        second_gain,
+        second_shift,
+        expand_bias,
+    )
+    packed = sum(
+        jnp.pad(vector, ((0, 3), (128 * place, 4 * width - 128 * place - vector.shape[1])))
+        for place, vector in enumerate(vectors)
+    )
     attention_shard = jnp.concatenate(
         [jnp.concatenate([joint_weight[0], output_weight[0]], axis=1), packed], axis=0
     )
@@ -1854,16 +1910,9 @@
     )
     upper_weights = (flat(upper_page), flat(upper_expand), flat(upper_reduce))
     saved_upper, final_rows = (middle_rows,) + tuple(saved[:13]), saved[13]
-    upper_grad, upper_pages, layer_outputs, upper_sums = backward(
-        top, saved_upper, upper_small, table, *upper_weights, final_rows
-    )
-    _, (_, vectors), input_grads, lower_sums = backward(
-        upper_grad, saved_lower, small, table, *weights, *upper_pages
-    )
-    own = core == 0
-    attention_sum = jnp.where(own, lower_sums[3], lower_sums[0])
-    expand_sum = jnp.where(own, lower_sums[2], upper_sums[1])
-    reduce_sum = jnp.where(own, lower_sums[1], upper_sums[0])
+    vectors, layer_outputs, input_grads, (reduce_sum, expand_sum, attention_sum) = backward(
+        top, (saved_lower, saved_upper), (small, upper_small), table, (weights, upper_weights), final_rows
+    )
     vectors = vectors[:12, :68]
     return (
         layer_outputs,

time: 748 us -> 704 us (0.941)
  Pallas kernels: 715 us -> 673 us
    pallas_call x2 -> x1, Pallas kernels: 383 us -> 347 us  [backward(): pl.pallas_call(backward_kernel, out_shape=tuple(outs), in_specs=[inside]...]
where the time goes in v6:
time: 704 us; the launch traced here: 698 us
  Pallas kernels  673 us (96%)
  local copies, waits for them, and re-layouts  18.1 us (3%)
    pallas_call x1, Pallas kernels, backward(): pl.pallas_call(backward_kernel, out_shape=tuple(outs), in_specs=[inside]...  347 us
    pallas_call x2, Pallas kernels, forward(): pl.pallas_call(partial(forward_kernel, forms), out_shape=tuple(outs), in_...  269 us
    pallas_call x1, Pallas kernels, gather_page(): pl.pallas_call(gather_kernel, out_shape=tuple(outs), in_specs=[anywhere]...  57 us

profile of v6, /device:TPU:0, one launch (start us, length us, event | category | flops | bytes accessed | tf_op | source)
XLA Modules:
  0.0 698.3 jit_solution(17223380559742599043)
XLA Ops:
  0.7 0.9 pad_add_fusion
  1.5 2.1 fusion.shard.refs_7_
  3.7 0.9 pad.49.refs_5_
  4.5 1.4 copy.31.refs_0_
  6.0 1.4 copy.34.refs_7_
  7.4 57.0 %gather_page.1 = (bf16[16,72,4352]{2,1,0:T(8,128)(2,1)}, bf16[72,2176]{1,0:T(8,128)(2,1)}, bf16[256,1088]{1,0:T(8,128)(2,1)}) custom-call(bf16[72,4352]{1,0:T(8,128)(2,1)} %fusion.shard.refs_7_, bf16[2,256,1088]{2,1,0:T(8,128)(2,1)} %copy.31.refs_0_), custom_call_target="tpu_custom_call" | custom-call | tf_op jit(solution)/shard_map/gather_page/pallas_call | solution.py:794
  64.4 1.5 slice_convert_fusion.1
  65.9 0.7 reshape.77.refs_2_
  66.7 0.7 reshape.76.refs_1_.refs_0_
  67.4 150.2 %forward.2 = (bf16[256,1152]{1,0:T(8,128)(2,1)}, bf16[256,1152]{1,0:T(8,128)(2,1)}, bf16[2,256,1152]{2,1,0:T(8,128)(2,1)}, bf16[2,256,1152]{2,1,0:T(8,128)(2,1)}...) custom-call(bf16[256,1088]{1,0:T(8,128)(2,1)} %get-tuple-element.58., ...), custom_call_target="tpu_custom_call" | custom-call | tf_op jit(solution)/shard_map/forward/pallas_call | solution.py:1075
  217.5 1.5 slice_convert_fusion
  219.1 0.7 reshape.81.refs_2_
  219.8 0.7 reshape.80.refs_1_
  220.5 119.1 %forward.3 = (bf16[256,1152]{1,0:T(8,128)(2,1)}, bf16[256,1152]{1,0:T(8,128)(2,1)}, bf16[2,256,1152]{2,1,0:T(8,128)(2,1)}, bf16[2,256,1152]{2,1,0:T(8,128)(2,1)}...) custom-call(bf16[256,1088]{1,0:T(8,128)(2,1)} %get-tuple-element.73., ...), custom_call_target="tpu_custom_call" | custom-call | tf_op jit(solution)/shard_map/forward/pallas_call | solution.py:1075
  339.7 346.9 %backward.1 = (f32[16,128]{1,0:T(8,128)}, bf16[4352,1088]{1,0:T(8,128)(2,1)}, bf16[16,72,4352]{2,1,0:T(8,128)(2,1)}, bf16[16,72,4352]{2,1,0:T(8,128)(2,1)}, bf16...) custom-call(f32[8,1088]{1,0:T(8,128)} %reshape.76.refs_1_.refs_0_, ...), custom_call_target="tpu_custom_call" | custom-call | tf_op jit(solution)/shard_map/backward/pallas_call | solution.py:1831
  686.6 2.4 copy.35
  689.0 1.4 copy.36
  690.4 0.5 fusion.1
  691.0 0.6 reshape.87
  691.6 0.1 slice_bitcast_fusion.2
  691.9 1.9 copy.37
  693.7 1.0 copy.38
  694.8 2.2 copy.39
  697.1 1.0 copy.55
  (29 shorter events, 0.3 us)
Async XLA Ops:
  0.6 3.0 copy-start.6
  1.5 3.0 copy-start.4
  4.5 1.4 copy-start.5
  686.6 2.4 copy-start.3
  689.0 1.4 copy-start.7
  689.0 2.6 copy-start
  691.8 2.9 copy-start.2
  694.8 2.2 copy-start.1

commit v7 on v6

--- a/solution.py
+++ b/solution.py
@@ -807,47 +807,27 @@
     return jnp.where(line < 2, line, 3 - line)
 
 
-def forward_kernel(forms, *refs):
-    count = len(forms)
-    moving = count == 2
-    x, vectors, wide, table, page_hbm = refs[:5]
-    shards, refs = refs[5 : 5 + count], refs[5 + count :]
-    if moving:
-        row_source, refs = refs[0], refs[1:]
-    stored, refs = refs[:14], refs[14:]
-    outs, refs = refs[: 2 * count], refs[2 * count :]
-    if moving:
-        row_target, row_sems, refs = refs[0], refs[-3:], refs[1:-3]
-    held, store_sem, refs = refs[:14], refs[14], refs[15:]
-    (normed_out, query_out, here, beside, away, corner, attended_out, log_out, attended_low, middle_out,
-     second_out, active_out, slope_out, result_out) = held
-    page, expand, reduce, mixture, result, mixed, stats, page_sem, expand_sem, reduce_sem, pair_send, pair_recv = refs[:12]
+def forward_kernel(*refs):
+    x_in, vectors_in, wide_in, table, page_hbm, row_source = refs[:6]
+    shards, refs = refs[6:11], refs[11:]
+    stored_of, refs = (refs[:14], refs[14:28]), refs[28:]
+    outs, row_target, vectors_out, refs = refs[:10], refs[10], refs[11], refs[12:]
+    held_of, refs = (refs[:14], refs[:3] + refs[14:17] + refs[6:14]), refs[17:]
+    (store_sem, big, reduce, mixture, result, mixed, stats, wide_own, page_sem, expand_sem, reduce_sem, pair_send,
+     pair_recv) = refs[:13]
+    gather_sems, row_sems = refs[13:17], refs[17:]
     place_of = places()
     core, rings, lines, toward = place_of
-    rows, width = x.shape
+    rows, width = x_in.shape
     half = rows // 2
     first = low_place(lines[0]) == 0
-
-    def store_copy(i):
-        return pltpu.make_async_copy(held[i], stored[i], store_sem.at[i])
-
-    def store(*numbers):
-        for i in numbers:
-            store_copy(i).start()
-
-    def page_copy(i):
-        at = pl.ds(pl.multiple_of(i * 256, 256), 256)
-        return pltpu.make_async_copy(page_hbm.at[:, at], page.at[:, at], page_sem.at[i])
-
-    def expand_copy(i):
-        at = pl.ds(pl.multiple_of(i * 256, 256), 256)
-        return pltpu.make_async_copy(outs[0].at[:, :, at], expand.at[:, :, at], expand_sem.at[i])
-
-    def reduce_copy(i):
-        rows_at = pl.ds(pl.multiple_of(i * 272, 16), 272)
-        return pltpu.make_async_copy(outs[2].at[i], reduce.at[rows_at], reduce_sem.at[i])
-
-    tiles = page.shape[1] // 256
+    tiles = big.shape[2] // 256
+
+    def tile_at(i):
+        return pl.ds(pl.multiple_of(i * 256, 256), 256)
+
+    def tile_of(at):
+        return big[:, :, at].astype(F32).reshape(WIDE, 256).astype(LOW)
 
     def begin(make, steps):
         def step(i, _):
@@ -856,9 +836,18 @@
 
         lax.fori_loop(0, steps, step, 0)
 
-    begin(page_copy, tiles)
-    greet(toward)
-    todo, drain = gather_tasks(gather_slots(forms, shards, outs), *refs[12:], place_of)
+    def pair_copies(layer):
+        here, beside, away, corner = held_of[layer][2:6]
+        ways = ((here, away, (LEVEL, 1)), (here, beside, SIBLING), (away, corner, SIBLING))
+        return [
+            remote_copy(source, target, pair_send.at[3 * layer + number], pair_recv.at[3 * layer + number], toward[to])
+            for number, (source, target, to) in enumerate(ways)
+        ]
+
+    def store_copy(layer, i):
+        return pltpu.make_async_copy(held_of[layer][i], stored_of[layer][i], store_sem.at[i])
+
+    todo, drain = gather_tasks(gather_slots(FORMS, shards, outs), *gather_sems, place_of)
 
     def progress(many):
         for _ in range(many):
@@ -868,48 +857,6 @@
     def complete(t):
         while any(slot <= t for slot, _ in todo):
             progress(1)
-
-    progress(2)
-    unit, _ = normal_parts(x[...].astype(F32))
-    normed = (unit * vectors[0:1] + vectors[1:2]).astype(LOW)
-    normed_out[...] = mm(normed, table[...]).astype(LOW)
-    store(0)
-
-    def column(i, _):
-        page_copy(i).wait()
-        at = pl.ds(pl.multiple_of(i * 256, 256), 256)
-        mixture[:, at] = mm(normed_out[...], page[:, at])
-        return 0
-
-    for begin_at, end in ((0, 4), (4, 8), (8, 13)):
-        lax.fori_loop(begin_at, end, column, 0)
-        progress(2)
-    blank = jnp.zeros((rows, WIDE - width), LOW)
-    here[0, :, :width] = mixture[:, width : 2 * width].astype(LOW)
-    here[0, :, width:] = blank
-    here[1, :, :width] = (mixture[:, 2 * width : 3 * width] + vectors[3:4]).astype(LOW)
-    here[1, :, width:] = blank
-
-    def pair_copy(source, target, to, number):
-        return remote_copy(source, target, pair_send.at[number], pair_recv.at[number], toward[to])
-
-    to_away = pair_copy(here, away, (LEVEL, 1), 0)
-    to_beside = pair_copy(here, beside, SIBLING, 1)
-    to_corner = pair_copy(away, corner, SIBLING, 2)
-    to_away.start()
-    to_beside.start()
-    query = ((mixture[:, :width] + vectors[2:3]).astype(LOW).astype(F32) * HDIM ** (-0.5)).astype(LOW)
-    query_out[:, :width] = query
-    query_out[:, width:] = blank
-    store(1, 2)
-    progress(1)
-    to_beside.wait_recv()
-    store(3)
-
-    def block(kind, near, part, at):
-        rows_at = pl.ds(part * half, half)
-        one, two = (here, beside) if near == 0 else (away, corner)
-        return jnp.concatenate([one[kind, rows_at, at], two[kind, rows_at, at]], axis=0)
 
     def one_unit(queries, keys, values):
         scores = mm_nt(keys, queries)
@@ -928,124 +875,216 @@
             out = out + share * part
         return peak, total, out
 
-    def local_pair(p, _):
-        at = pl.ds(pl.multiple_of(p * 128, 128), 128)
-        low, high = head_pair(query_out[:half, at]), head_pair(query_out[half:, at])
-        keys, values = block(0, 0, 0, at), block(1, 0, 0, at)
-        bottom = one_unit(low, keys, values)
-        top = merge([one_unit(high, keys, values), one_unit(high, block(0, 0, 1, at), block(1, 0, 1, at))])
-        for place, (level, sums, out) in enumerate((bottom, top)):
-            stats[p, 2 * place : 2 * place + 1] = level
-            stats[p, 2 * place + 1 : 2 * place + 2] = sums
-            mixed[p, place] = out
-        return 0
-
-    for begin_at in (0, 3, 6):
-        lax.fori_loop(begin_at, begin_at + 3, local_pair, 0)
+    def layer_pass(layer):
+        (normed_out, query_out, here, beside, away, corner, attended_out, log_out, attended_low, middle_out,
+         second_out, active_out, slope_out, result_out) = held_of[layer]
+        x = x_in if layer == 0 else result_out
+        vectors, wide = (vectors_in, wide_in) if layer == 0 else (vectors_out, wide_own)
+        page_source, expand_source, reduce_source = (page_hbm, outs[0], outs[2]) if layer == 0 else (outs[4], outs[6], outs[8])
+
+        def store(*numbers):
+            for i in numbers:
+                store_copy(layer, i).start()
+
+        def page_copy(i):
+            return pltpu.make_async_copy(page_source.at[:, :, tile_at(i)], big.at[:, :, tile_at(i)], page_sem.at[i])
+
+        def expand_copy(i):
+            return pltpu.make_async_copy(expand_source.at[:, :, tile_at(i)], big.at[:, :, tile_at(i)], expand_sem.at[i])
+
+        def reduce_copy(i):
+            rows_at = pl.ds(pl.multiple_of(i * 272, 16), 272)
+            return pltpu.make_async_copy(reduce_source.at[i], reduce.at[rows_at], reduce_sem.at[i])
+
+        if layer == 0:
+            begin(page_copy, tiles)
+            greet(toward)
+            progress(3)
+        else:
+            complete(2)
+            begin(page_copy, tiles)
+            for i in range(14):
+                store_copy(0, i).wait()
+            for copy in pair_copies(0):
+                copy.wait_send()
+
+            def arrived(i, _):
+                page_copy(i).wait()
+                return 0
+
+            lax.fori_loop(0, tiles, arrived, 0)
+            for shard in range(16):
+                line = big[shard, 64:72, 0:1408].astype(F32)[4:5]
+                for place in range(8):
+                    vectors[place : place + 1, shard * 68 : (shard + 1) * 68] = line[:, place * 128 : place * 128 + 68]
+                wide[0:1, shard * 272 : (shard + 1) * 272] = line[:, 1024:1296]
+        unit, _ = normal_parts(x[...].astype(F32))
+        normed = (unit * vectors[0:1] + vectors[1:2]).astype(LOW)
+        normed_out[...] = mm(normed, table[...]).astype(LOW)
+        store(0)
+
+        def column(i, _):
+            if layer == 0:
+                page_copy(i).wait()
+            at = tile_at(i)
+            mixture[:, at] = mm(normed_out[...], tile_of(at))
+            return 0
+
+        for begin_at, end in ((0, 4), (4, 8), (8, 13)):
+            lax.fori_loop(begin_at, end, column, 0)
+            progress(2)
+        blank = jnp.zeros((rows, WIDE - width), LOW)
+        here[0, :, :width] = mixture[:, width : 2 * width].astype(LOW)
+        here[0, :, width:] = blank
+        here[1, :, :width] = (mixture[:, 2 * width : 3 * width] + vectors[3:4]).astype(LOW)
+        here[1, :, width:] = blank
+
+        to_away, to_beside, to_corner = pair_copies(layer)
+        to_away.start()
+        to_beside.start()
+        query = ((mixture[:, :width] + vectors[2:3]).astype(LOW).astype(F32) * HDIM ** (-0.5)).astype(LOW)
+        query_out[:, :width] = query
+        query_out[:, width:] = blank
+        store(1, 2)
+        progress(1)
+        to_beside.wait_recv()
+        store(3)
+
+        def block(kind, near, part, at):
+            rows_at = pl.ds(part * half, half)
+            one, two = (here, beside) if near == 0 else (away, corner)
+            return jnp.concatenate([one[kind, rows_at, at], two[kind, rows_at, at]], axis=0)
+
+        def local_pair(p, _):
+            at = pl.ds(pl.multiple_of(p * 128, 128), 128)
+            low, high = head_pair(query_out[:half, at]), head_pair(query_out[half:, at])
+            keys, values = block(0, 0, 0, at), block(1, 0, 0, at)
+            bottom = one_unit(low, keys, values)
+            top = merge([one_unit(high, keys, values), one_unit(high, block(0, 0, 1, at), block(1, 0, 1, at))])
+            for place, (level, sums, out) in enumerate((bottom, top)):
+                stats[p, 2 * place : 2 * place + 1] = level
+                stats[p, 2 * place + 1 : 2 * place + 2] = sums
+                mixed[p, place] = out
+            return 0
+
+        for begin_at in (0, 3, 6):
+            lax.fori_loop(begin_at, begin_at + 3, local_pair, 0)
+            progress(2)
+        progress(8)
+        to_away.wait_recv()
+        to_corner.start()
+        store(4)
         progress(2)
-    progress(8)
-    to_away.wait_recv()
-    to_corner.start()
-    store(4)
-    progress(2)
-    to_corner.wait_recv()
-    store(5)
-
-    def far_pair(p, _):
-        at = pl.ds(pl.multiple_of(p * 128, 128), 128)
-        low, high = head_pair(query_out[:half, at]), head_pair(query_out[half:, at])
-        keys, values = block(0, 1, 0, at), block(1, 1, 0, at)
-        last_keys = jnp.where(first, block(0, 1, 1, at), keys)
-        last_values = jnp.where(first, block(1, 1, 1, at), values)
-        near = one_unit(high, keys, values)
-        last = one_unit(jnp.where(first, high, low), last_keys, last_values)
-        low_last = (jnp.where(first, far_below, last[0]),) + last[1:]
-        high_last = (jnp.where(first, last[0], far_below),) + last[1:]
-
-        def before(place):
-            return (stats[p, 2 * place : 2 * place + 1], stats[p, 2 * place + 1 : 2 * place + 2], mixed[p, place])
-
-        for place, units in enumerate(([before(0), low_last], [before(1), near, high_last])):
-            peak, total, out = merge(units)
-            attended_out[place * half : (place + 1) * half, at] = from_pair(out / total)
-            log_out[p, place : place + 1] = peak + jnp.log(total)
-        return 0
-
-    for begin_at in (0, 3, 6):
-        lax.fori_loop(begin_at, begin_at + 3, far_pair, 0)
+        to_corner.wait_recv()
+        store(5)
+
+        def far_pair(p, _):
+            at = pl.ds(pl.multiple_of(p * 128, 128), 128)
+            low, high = head_pair(query_out[:half, at]), head_pair(query_out[half:, at])
+            keys, values = block(0, 1, 0, at), block(1, 1, 0, at)
+            last_keys = jnp.where(first, block(0, 1, 1, at), keys)
+            last_values = jnp.where(first, block(1, 1, 1, at), values)
+            near = one_unit(high, keys, values)
+            last = one_unit(jnp.where(first, high, low), last_keys, last_values)
+            low_last = (jnp.where(first, far_below, last[0]),) + last[1:]
+            high_last = (jnp.where(first, last[0], far_below),) + last[1:]
+
+            def before(place):
+                return (stats[p, 2 * place : 2 * place + 1], stats[p, 2 * place + 1 : 2 * place + 2], mixed[p, place])
+
+            for place, units in enumerate(([before(0), low_last], [before(1), near, high_last])):
+                peak, total, out = merge(units)
+                attended_out[place * half : (place + 1) * half, at] = from_pair(out / total)
+                log_out[p, place : place + 1] = peak + jnp.log(total)
+            return 0
+
+        for begin_at in (0, 3, 6):
+            lax.fori_loop(begin_at, begin_at + 3, far_pair, 0)
+            progress(2)
+
+        def late(i, _):
+            page_copy(i).wait()
+            return 0
+
+        if layer == 0:
+            lax.fori_loop(13, tiles, late, 0)
+        lead = 4 * width - WIDE
+        store(6, 7)
+        attended_low[...] = mm(attended_out[:, :width].astype(LOW), table[...]).astype(LOW)
+        store(8)
+
+        def blend(i, _):
+            at = pl.ds(pl.multiple_of(lead + i * 128, 128), 128)
+            weights = big[:, :, at].astype(F32).reshape(WIDE, 128).astype(LOW)
+            mixture[:, pl.ds(pl.multiple_of(i * 128, 128), 128)] = mm(attended_low[...], weights)
+            return 0
+
+        lax.fori_loop(0, WIDE // 128, blend, 0)
+        middle = x[...].astype(F32) + (mixture[:, 3 * width - lead : WIDE] + vectors[4:5])
+        middle_out[...] = middle
+        store(9)
         progress(2)
-
-    def late(i, _):
-        page_copy(i).wait()
-        return 0
-
-    lax.fori_loop(13, tiles, late, 0)
-    lead = 4 * width - WIDE
-    store(6, 7)
-    attended_low[...] = mm(attended_out[:, :width].astype(LOW), table[...]).astype(LOW)
-    store(8)
-    blended = mm(attended_low[...], page[:, lead:])
-    middle = x[...].astype(F32) + (blended[:, 3 * width - lead :] + vectors[4:5])
-    middle_out[...] = middle
-    store(9)
-    progress(2)
-    unit, _ = normal_parts(middle)
-    second = (unit * vectors[6:7] + vectors[7:8]).astype(LOW)
-    second_out[...] = mm(second, table[...]).astype(LOW)
-    store(10)
-    result[...] = middle + vectors[5:6]
-
-    complete(0)
-    begin(expand_copy, tiles)
-    if moving:
-        for copy in row_copies(place_of, row_source, row_target, *row_sems):
-            copy.start()
-
-    def inner(i, _):
-        at = pl.ds(pl.multiple_of(i * 256, 256), 256)
-        expand_copy(i).wait()
-        weights = expand[:, :, at].astype(F32).reshape(WIDE, 256).astype(LOW)
-        hidden = mm(second_out[...], weights) + wide[:, at]
-        below = 0.5 + 0.5 * lax.erf(hidden * 0.7071067811865476)
-        active_out[:, at] = (hidden * below).astype(LOW)
-        slope_out[:, at] = (below + hidden * (0.3989422804014327 * jnp.exp(-0.5 * hidden * hidden))).astype(LOW)
-        return 0
-
-    for begin_at in range(0, tiles, 2):
-        lax.fori_loop(begin_at, min(begin_at + 2, tiles), inner, 0)
-        progress(3)
-    store(11, 12)
-    complete(1)
-    begin(reduce_copy, 16)
-
-    def landed(i, _):
-        reduce_copy(i).wait()
-        return 0
-
-    lax.fori_loop(0, 16, landed, 0)
-
-    def outer(i, _):
-        at = pl.ds(pl.multiple_of(i * 256, 256), 256)
-        result[...] += mm(active_out[:, at], reduce[at])
-        return 0
-
-    lax.fori_loop(0, tiles, outer, 0)
-    result_out[...] = result[...].astype(LOW)
-    store(13)
+        unit, _ = normal_parts(middle)
+        second = (unit * vectors[6:7] + vectors[7:8]).astype(LOW)
+        second_out[...] = mm(second, table[...]).astype(LOW)
+        store(10)
+        result[...] = middle + vectors[5:6]
+
+        complete(3 * layer)
+        begin(expand_copy, tiles)
+        if layer == 1:
+            for copy in row_copies(place_of, row_source, row_target, *row_sems):
+                copy.start()
+
+        def inner(i, _):
+            at = tile_at(i)
+            expand_copy(i).wait()
+            hidden = mm(second_out[...], tile_of(at)) + wide[0:1, at]
+            below = 0.5 + 0.5 * lax.erf(hidden * 0.7071067811865476)
+            active_out[:, at] = (hidden * below).astype(LOW)
+            slope_out[:, at] = (below + hidden * (0.3989422804014327 * jnp.exp(-0.5 * hidden * hidden))).astype(LOW)
+            return 0
+
+        for begin_at in range(0, tiles, 2):
+            lax.fori_loop(begin_at, min(begin_at + 2, tiles), inner, 0)
+            progress(3)
+        store(11, 12)
+        complete(1 + 3 * layer)
+        begin(reduce_copy, 16)
+
+        def landed(i, _):
+            reduce_copy(i).wait()
+            return 0
+
+        lax.fori_loop(0, 16, landed, 0)
+
+        def outer(i, _):
+            at = pl.ds(pl.multiple_of(i * 256, 256), 256)
+            result[...] += mm(active_out[:, at], reduce[at])
+            return 0
+
+        lax.fori_loop(0, tiles, outer, 0)
+        result_out[...] = result[...].astype(LOW)
+        store(13)
+
+    layer_pass(0)
+    layer_pass(1)
     progress(len(todo))
     drain()
     for i in range(14):
-        store_copy(i).wait()
-    if moving:
-        for copy in row_copies(place_of, row_source, row_target, *row_sems):
-            copy.wait()
-    for copy in (to_away, to_beside, to_corner):
+        store_copy(1, i).wait()
+    for copy in row_copies(place_of, row_source, row_target, *row_sems):
+        copy.wait()
+    for copy in pair_copies(1):
         copy.wait_send()
 
 
-def forward(x, vectors, wide, table, page, shards, moved=()):
+FORMS = ((0, True), (0, False), (1, True), (1, True), (1, False))
+
+
+def forward(x, vectors, wide, table, page, row_source, shards):
     rows, width = x.shape
-    inner = page.shape[1]
+    inner = page.shape[2]
     pairs = WIDE // 128
     anywhere = pl.BlockSpec(memory_space=pl.ANY)
     inside = pl.BlockSpec(memory_space=pltpu.VMEM)
@@ -1054,41 +1093,35 @@
         return jax.ShapeDtypeStruct(dims, kind)
 
     pair = shape(2, rows, WIDE)
-    outs = [
+    kept = [
         shape(rows, WIDE), shape(rows, WIDE), pair, pair, pair, pair, shape(rows, WIDE, kind=F32),
         shape(pairs, 2, rows, kind=F32), shape(rows, WIDE), shape(rows, width, kind=F32),
         shape(rows, WIDE), shape(rows, inner), shape(rows, inner), shape(rows, width),
     ]
-    count = len(outs)
+    outs = kept * 2 + gather_outs(tuple(form + (shard,) for form, shard in zip(FORMS, shards)))
+    outs += [shape(rows, width), shape(8, width, kind=F32)]
     dma = pltpu.SemaphoreType.DMA
-    scratch = [pltpu.VMEM(out.shape, out.dtype) for out in outs] + [
-        dma((count,)), pltpu.VMEM(page.shape, LOW), pltpu.VMEM((16, 72, inner), LOW), pltpu.VMEM((inner, width), LOW),
+    scratch = [pltpu.VMEM(out.shape, out.dtype) for out in kept + [pair] * 3] + [
+        dma((14,)), pltpu.VMEM((16, 72, inner), LOW), pltpu.VMEM((inner, width), LOW),
         pltpu.VMEM((rows, 13 * 256), F32), pltpu.VMEM((rows, width), F32),
-        pltpu.VMEM((pairs, 2, 128, rows), F32), pltpu.VMEM((pairs, 4, rows), F32),
-        dma((inner // 256,)), dma((inner // 256,)), dma((16,)), dma((3,)), dma((3,)),
-    ] + gather_semaphores(len(shards))
-    outs += gather_outs(shards)
-    gathered = len(outs)
-    outs += [jax.ShapeDtypeStruct(source.shape[1:], LOW) for source in moved]
-    scratch += [dma(())] * (3 * len(moved))
-    forms = tuple(shard[:2] for shard in shards)
+        pltpu.VMEM((pairs, 2, 128, rows), F32), pltpu.VMEM((pairs, 4, rows), F32), pltpu.VMEM((8, inner), F32),
+        dma((inner // 256,)), dma((inner // 256,)), dma((16,)), dma((6,)), dma((6,)),
+    ] + gather_semaphores(len(shards)) + [dma(())] * 3
     res = pl.pallas_call(
-        partial(forward_kernel, forms),
+        forward_kernel,
         out_shape=tuple(outs),
-        in_specs=[inside] * 4 + [anywhere] * (1 + len(shards) + len(moved)),
-        out_specs=(anywhere,) * len(outs),
+        in_specs=[inside] * 4 + [anywhere] * (2 + len(shards)),
+        out_specs=(anywhere,) * (len(outs) - 1) + (inside,),
         scratch_shapes=scratch,
-        compiler_params=pltpu.CompilerParams(
-            collective_id=len(shards), has_side_effects=True, vmem_limit_bytes=60 << 20
-        ),
+        compiler_params=pltpu.CompilerParams(collective_id=3, has_side_effects=True, vmem_limit_bytes=62 << 20),
         name="forward",
-    )(x, vectors, wide, table, page, *(shard[2] for shard in shards), *moved)
-    return res[:count], res[count:gathered:2], res[gathered:]
+    )(x, vectors, wide, table, page, row_source, *shards)
+    return res[:14], res[14:28], res[28:38:2], res[38], res[39]
 
 
 COLUMNS, ROWS = range(2)
 SIZES = {COLUMNS: (72, 2176), ROWS: (144, 1088)}
-DEPTH = 6
+DEPTH = 8
 EASTWARD = (3, 0)
 SCATTER_KINDS = (
     [(SIBLING, dd) for dd in range(4)]
@@ -1586,8 +1619,8 @@
 
             return 0
 
-        for begin_at in range(0, tiles, 2):
-            lax.fori_loop(begin_at, min(begin_at + 2, tiles), feed_tile, 0)
+        for begin_at in range(0, tiles, 3):
+            lax.fori_loop(begin_at, min(begin_at + 3, tiles), feed_tile, 0)
             progress(1)
         for i in range(3):
             expand_copy(i, page_hbm).start()
@@ -1899,17 +1932,15 @@
 
     lower_page, rows = gather_page(attention_shard, inputs)
     small, wide = small_of(lower_page)
-    shards = ((0, True, expand_shard), (0, False, reduce_shard), (1, True, attention_shard))
-    saved, (lower_expand, lower_reduce, upper_page), _ = forward(rows, small, wide, table, flat(lower_page), shards)
+    shards = (expand_shard, reduce_shard, attention_shard, expand_shard, reduce_shard)
+    saved, saved_upper, gathered, top, upper_small = forward(
+        rows, small, wide, table, lower_page, cotangent, shards
+    )
+    lower_expand, lower_reduce, upper_page, upper_expand, upper_reduce = gathered
     weights = (flat(lower_page), flat(lower_expand), flat(lower_reduce))
-    saved_lower, middle_rows = (rows,) + tuple(saved[:13]), saved[13]
-    upper_small, upper_wide = small_of(upper_page)
-    shards = ((1, True, expand_shard), (1, False, reduce_shard))
-    saved, (upper_expand, upper_reduce), (top,) = forward(
-        middle_rows, upper_small, upper_wide, table, flat(upper_page), shards, (cotangent,)
-    )
     upper_weights = (flat(upper_page), flat(upper_expand), flat(upper_reduce))
-    saved_upper, final_rows = (middle_rows,) + tuple(saved[:13]), saved[13]
+    middle_rows, final_rows = saved[13], saved_upper[13]
+    saved_lower, saved_upper = (rows,) + tuple(saved[:13]), (middle_rows,) + tuple(saved_upper[:13])
     vectors, layer_outputs, input_grads, (reduce_sum, expand_sum, attention_sum) = backward(
         top, (saved_lower, saved_upper), (small, upper_small), table, (weights, upper_weights), final_rows
     )

time: 704 us -> 687 us (0.976)
  Pallas kernels: 673 us -> 655 us
    pallas_call x2 -> x1, Pallas kernels: 269 us -> 259 us  [forward(): pl.pallas_call(forward_kernel, out_shape=tuple(outs), in_specs=[inside] *...]
    pallas_call x1, Pallas kernels: 347 us -> 339 us  [backward(): pl.pallas_call(backward_kernel, out_shape=tuple(outs), in_specs=[inside]...]
where the time goes in v7:
time: 687 us; the launch traced here: 677 us
  Pallas kernels  655 us (95%)
  local copies, waits for them, and re-layouts  16.6 us (2%)
    pallas_call x1, Pallas kernels, backward(): pl.pallas_call(backward_kernel, out_shape=tuple(outs), in_specs=[inside]...  339 us
    pallas_call x1, Pallas kernels, forward(): pl.pallas_call(forward_kernel, out_shape=tuple(outs), in_specs=[inside] *...  259 us
    pallas_call x1, Pallas kernels, gather_page(): pl.pallas_call(gather_kernel, out_shape=tuple(outs), in_specs=[anywhere]...  57 us

profile of v7, /device:TPU:0, one launch (start us, length us, event | category | flops | bytes accessed | tf_op | source)
XLA Modules:
  0.0 677.3 jit_solution(17965844747758704643)
XLA Ops:
  0.7 0.9 pad_add_fusion
  1.5 0.0 copy-start.4
  1.5 2.1 fusion.shard.refs_8_
  3.7 0.9 pad.49.refs_6_.refs_9_
  4.5 0.0 copy-done.4
  4.5 1.4 copy.31.refs_0_
  6.0 1.4 copy.33.refs_5_
  7.4 57.0 %gather_page.1 = (bf16[16,72,4352]{2,1,0:T(8,128)(2,1)}, bf16[72,2176]{1,0:T(8,128)(2,1)}, bf16[256,1088]{1,0:T(8,128)(2,1)}) custom-call(bf16[72,4352]{1,0:T(8,128)(2,1)} %fusion.shard.refs_8_, bf16[2,256,1088]{2,1,0:T(8,128)(2,1)} %copy.31.refs_0_), custom_call_target="tpu_custom_call" | custom-call | tf_op jit(solution)/shard_map/gather_page/pallas_call | solution.py:794
  64.4 1.5 slice_convert_fusion
  65.9 0.7 reshape.64.refs_2_
  66.7 0.7 reshape.63.refs_1_.refs_0_
  67.4 259.1 %forward.1 = (bf16[256,1152]{1,0:T(8,128)(2,1)}, bf16[256,1152]{1,0:T(8,128)(2,1)}, bf16[2,256,1152]{2,1,0:T(8,128)(2,1)}, bf16[2,256,1152]{2,1,0:T(8,128)(2,1)}...) custom-call(bf16[256,1088]{1,0:T(8,128)(2,1)} %get-tuple-element.59., ...), custom_call_target="tpu_custom_call" | custom-call | tf_op jit(solution)/shard_map/forward/pallas_call | solution.py:1110
  326.4 338.9 %backward.1 = (f32[16,128]{1,0:T(8,128)}, bf16[4352,1088]{1,0:T(8,128)(2,1)}, bf16[16,72,4352]{2,1,0:T(8,128)(2,1)}, bf16[16,72,4352]{2,1,0:T(8,128)(2,1)}, bf16...) custom-call(f32[8,1088]{1,0:T(8,128)} %reshape.63.refs_1_.refs_0_, ...), custom_call_target="tpu_custom_call" | custom-call | tf_op jit(solution)/shard_map/backward/pallas_call | solution.py:1864
  665.4 2.4 copy.34
  667.8 1.4 copy.35
  669.2 0.5 fusion.1
  669.8 0.6 reshape.71
  670.4 0.1 slice_bitcast_fusion.2
  670.6 0.1 slice_bitcast_fusion.1
  670.6 1.9 copy.36
  672.5 1.0 copy.37
  673.5 0.1 slice_bitcast_fusion
  673.6 2.2 copy.38
  675.9 1.0 copy.47
  (20 shorter events, 0.1 us)
Async XLA Ops:
  0.6 3.0 copy-start.6
  1.5 3.0 copy-start.4
  4.5 1.4 copy-start.5
  665.4 2.4 copy-start.3
  667.8 1.4 copy-start.7
  667.8 2.6 copy-start
  670.6 2.9 copy-start.2
  673.6 2.2 copy-start.1

commit v8 on v7

--- a/solution.py
+++ b/solution.py
@@ -721,12 +721,12 @@
         tasks.clear()
     then(prelude)
     then(begin, 0)
-    if count > 1:
-        then(begin, 1)
     for t in range(count):
         tasks += heads[t][:7]
         if t > 0:
             tasks += tails[t - 1]
+        if t == 0:
+            then(begin, 1)
         if t + 2 < count:
             then(begin, t + 2)
         tasks += heads[t][7:]
@@ -769,53 +769,18 @@
     )
 
 
-def gather_kernel(shard, *refs):
-    source, outs, moved, refs = refs[0], refs[1:3], refs[3], refs[4:]
-    sems, row_sems = refs[:4], refs[4:]
-    place_of = places()
-    greet(place_of[3])
-    tasks, drain = gather_tasks(gather_slots(((0, True),), (shard,), outs), *sems, place_of)
-    for _, task in tasks[:11]:
-        task()
-    copies = row_copies(place_of, source, moved, *row_sems)
-    for copy in copies:
-        copy.start()
-    for _, task in tasks[11:]:
-        task()
-    drain()
-    for copy in copies:
-        copy.wait()
-
-
-def gather_page(shard, source):
-    anywhere = pl.BlockSpec(memory_space=pl.ANY)
-    outs = gather_outs(((0, True, shard),)) + [jax.ShapeDtypeStruct(source.shape[1:], LOW)]
-    dma = pltpu.SemaphoreType.DMA
-    res = pl.pallas_call(
-        gather_kernel,
-        out_shape=tuple(outs),
-        in_specs=[anywhere] * 2,
-        out_specs=(anywhere,) * len(outs),
-        scratch_shapes=gather_semaphores(1) + [dma(())] * 3,
-        compiler_params=pltpu.CompilerParams(collective_id=0, has_side_effects=True),
-        name="gather_page",
-    )(shard, source)
-    return res[0], res[2]
-
-
 def low_place(line):
     return jnp.where(line < 2, line, 3 - line)
 
 
 def forward_kernel(*refs):
-    x_in, vectors_in, wide_in, table, page_hbm, row_source = refs[:6]
-    shards, refs = refs[6:11], refs[11:]
+    table, row_sources, shards, refs = refs[0], refs[1:3], refs[3:9], refs[9:]
     stored_of, refs = (refs[:14], refs[14:28]), refs[28:]
-    outs, row_target, vectors_out, refs = refs[:10], refs[10], refs[11], refs[12:]
+    outs, row_targets, vectors_of, refs = refs[:12], refs[12:14], refs[14:16], refs[16:]
     held_of, refs = (refs[:14], refs[:3] + refs[14:17] + refs[6:14]), refs[17:]
-    (store_sem, big, reduce, mixture, result, mixed, stats, wide_own, page_sem, expand_sem, reduce_sem, pair_send,
-     pair_recv) = refs[:13]
-    gather_sems, row_sems = refs[13:17], refs[17:]
+    (store_sem, big, reduce, mixture, result, mixed, stats, wide, x_in, page_sem, expand_sem, reduce_sem, pair_send,
+     pair_recv, x_sem) = refs[:15]
+    gather_sems, row_sems = refs[15:19], refs[19:]
     place_of = places()
     core, rings, lines, toward = place_of
     rows, width = x_in.shape
@@ -843,6 +808,9 @@
             remote_copy(source, target, pair_send.at[3 * layer + number], pair_recv.at[3 * layer + number], toward[to])
             for number, (source, target, to) in enumerate(ways)
         ]
+
+    def rows_of(layer):
+        return row_copies(place_of, row_sources[layer], row_targets[layer], *row_sems[3 * layer : 3 * layer + 3])
 
     def store_copy(layer, i):
         return pltpu.make_async_copy(held_of[layer][i], stored_of[layer][i], store_sem.at[i])
@@ -879,8 +847,8 @@
         (normed_out, query_out, here, beside, away, corner, attended_out, log_out, attended_low, middle_out,
          second_out, active_out, slope_out, result_out) = held_of[layer]
         x = x_in if layer == 0 else result_out
-        vectors, wide = (vectors_in, wide_in) if layer == 0 else (vectors_out, wide_own)
-        page_source, expand_source, reduce_source = (page_hbm, outs[0], outs[2]) if layer == 0 else (outs[4], outs[6], outs[8])
+        vectors = vectors_of[layer]
+        page_source, expand_source, reduce_source = outs[6 * layer : 6 * layer + 6 : 2]
 
         def store(*numbers):
             for i in numbers:
@@ -897,35 +865,40 @@
             return pltpu.make_async_copy(reduce_source.at[i], reduce.at[rows_at], reduce_sem.at[i])
 
         if layer == 0:
-            begin(page_copy, tiles)
             greet(toward)
-            progress(3)
+            progress(12)
+            for copy in rows_of(0):
+                copy.start()
+        complete(3 * layer)
+        begin(page_copy, tiles)
+        if layer == 0:
+            for copy in rows_of(0):
+                copy.wait()
+            x_copy = pltpu.make_async_copy(row_targets[0], x_in, x_sem)
+            x_copy.start()
+            x_copy.wait()
         else:
-            complete(2)
-            begin(page_copy, tiles)
             for i in range(14):
                 store_copy(0, i).wait()
             for copy in pair_copies(0):
                 copy.wait_send()
 
-            def arrived(i, _):
-                page_copy(i).wait()
-                return 0
-
-            lax.fori_loop(0, tiles, arrived, 0)
-            for shard in range(16):
-                line = big[shard, 64:72, 0:1408].astype(F32)[4:5]
-                for place in range(8):
-                    vectors[place : place + 1, shard * 68 : (shard + 1) * 68] = line[:, place * 128 : place * 128 + 68]
-                wide[0:1, shard * 272 : (shard + 1) * 272] = line[:, 1024:1296]
+        def arrived(i, _):
+            page_copy(i).wait()
+            return 0
+
+        lax.fori_loop(0, tiles, arrived, 0)
+        for shard in range(16):
+            line = big[shard, 64:72, 0:1408].astype(F32)[4:5]
+            for place in range(8):
+                vectors[place : place + 1, shard * 68 : (shard + 1) * 68] = line[:, place * 128 : place * 128 + 68]
+            wide[0:1, shard * 272 : (shard + 1) * 272] = line[:, 1024:1296]
         unit, _ = normal_parts(x[...].astype(F32))
         normed = (unit * vectors[0:1] + vectors[1:2]).astype(LOW)
         normed_out[...] = mm(normed, table[...]).astype(LOW)
         store(0)
 
         def column(i, _):
-            if layer == 0:
-                page_copy(i).wait()
             at = tile_at(i)
             mixture[:, at] = mm(normed_out[...], tile_of(at))
             return 0
@@ -1002,12 +975,6 @@
             lax.fori_loop(begin_at, begin_at + 3, far_pair, 0)
             progress(2)
 
-        def late(i, _):
-            page_copy(i).wait()
-            return 0
-
-        if layer == 0:
-            lax.fori_loop(13, tiles, late, 0)
         lead = 4 * width - WIDE
         store(6, 7)
         attended_low[...] = mm(attended_out[:, :width].astype(LOW), table[...]).astype(LOW)
@@ -1030,10 +997,10 @@
         store(10)
         result[...] = middle + vectors[5:6]
 
-        complete(3 * layer)
+        complete(1 + 3 * layer)
         begin(expand_copy, tiles)
         if layer == 1:
-            for copy in row_copies(place_of, row_source, row_target, *row_sems):
+            for copy in rows_of(1):
                 copy.start()
 
         def inner(i, _):
@@ -1047,9 +1014,9 @@
 
         for begin_at in range(0, tiles, 2):
             lax.fori_loop(begin_at, min(begin_at + 2, tiles), inner, 0)
-            progress(3)
+            progress(2)
         store(11, 12)
-        complete(1 + 3 * layer)
+        complete(2 + 3 * layer)
         begin(reduce_copy, 16)
 
         def landed(i, _):
@@ -1073,18 +1040,18 @@
     drain()
     for i in range(14):
         store_copy(1, i).wait()
-    for copy in row_copies(place_of, row_source, row_target, *row_sems):
+    for copy in rows_of(1):
         copy.wait()
     for copy in pair_copies(1):
         copy.wait_send()
 
 
-FORMS = ((0, True), (0, False), (1, True), (1, True), (1, False))
-
-
-def forward(x, vectors, wide, table, page, row_source, shards):
-    rows, width = x.shape
-    inner = page.shape[2]
+FORMS = ((0, True), (0, True), (0, False), (1, True), (1, True), (1, False))
+
+
+def forward(table, row_sources, shards):
+    rows, width = row_sources[0].shape[1:]
+    inner = shards[0].shape[1]
     pairs = WIDE // 128
     anywhere = pl.BlockSpec(memory_space=pl.ANY)
     inside = pl.BlockSpec(memory_space=pltpu.VMEM)
@@ -1099,24 +1066,24 @@
         shape(rows, WIDE), shape(rows, inner), shape(rows, inner), shape(rows, width),
     ]
     outs = kept * 2 + gather_outs(tuple(form + (shard,) for form, shard in zip(FORMS, shards)))
-    outs += [shape(rows, width), shape(8, width, kind=F32)]
+    outs += [shape(rows, width)] * 2 + [shape(8, width, kind=F32)] * 2
     dma = pltpu.SemaphoreType.DMA
     scratch = [pltpu.VMEM(out.shape, out.dtype) for out in kept + [pair] * 3] + [
         dma((14,)), pltpu.VMEM((16, 72, inner), LOW), pltpu.VMEM((inner, width), LOW),
         pltpu.VMEM((rows, 13 * 256), F32), pltpu.VMEM((rows, width), F32),
         pltpu.VMEM((pairs, 2, 128, rows), F32), pltpu.VMEM((pairs, 4, rows), F32), pltpu.VMEM((8, inner), F32),
-        dma((inner // 256,)), dma((inner // 256,)), dma((16,)), dma((6,)), dma((6,)),
-    ] + gather_semaphores(len(shards)) + [dma(())] * 3
+        pltpu.VMEM((rows, width), LOW), dma((inner // 256,)), dma((inner // 256,)), dma((16,)), dma((6,)), dma((6,)), dma(()),
+    ] + gather_semaphores(len(shards)) + [dma(())] * 6
     res = pl.pallas_call(
         forward_kernel,
         out_shape=tuple(outs),
-        in_specs=[inside] * 4 + [anywhere] * (2 + len(shards)),
-        out_specs=(anywhere,) * (len(outs) - 1) + (inside,),
+        in_specs=[inside] + [anywhere] * (2 + len(shards)),
+        out_specs=(anywhere,) * (len(outs) - 2) + (inside,) * 2,
         scratch_shapes=scratch,
         compiler_params=pltpu.CompilerParams(collective_id=3, has_side_effects=True, vmem_limit_bytes=62 << 20),
         name="forward",
-    )(x, vectors, wide, table, page, row_source, *shards)
-    return res[:14], res[14:28], res[28:38:2], res[38], res[39]
+    )(table, *row_sources, *shards)
+    return res[:14], res[14:28], res[28:40:2], res[40:42], res[42:]
 
 
 COLUMNS, ROWS = range(2)
@@ -1733,7 +1700,7 @@
         left_one[...] = normed_in[...].T
         left_two[...] = attended_low[...].T
         second_sum[...] = jnp.zeros_like(second_sum)
-        progress(4)
+        progress(8)
         to_beside.wait_recv()
         to_away.wait_recv()
         for kind in (0, 1):
@@ -1759,7 +1726,7 @@
 
         for begin_at, end in ((0, 4), (4, 8), (8, 13)):
             lax.fori_loop(begin_at, end, project_tile, 0)
-            progress(1)
+            progress(2)
         grad_normed = close_up(second_sum[...], table[...])
         unit, inverse = normal_parts(x[...].astype(F32))
         sums[0:1] = row(grad_normed * unit)
@@ -1802,7 +1769,7 @@
         whole_tiles = edge // 256
         for begin_at in range(0, whole_tiles, 4):
             page_loop(1, begin_at, begin_at + 4)
-            progress(1)
+            progress(3)
         page_loop(3, whole_tiles, whole_tiles + 1)
         page_loop(2, whole_tiles + 1, tiles)
         for i in (tiles - 2, tiles - 1):
@@ -1880,12 +1847,6 @@
     return jnp.asarray(table, LOW)
 
 
-def small_of(page):
-    row = page[:, 68].astype(F32)
-    vectors = row[:, : 8 * 128].reshape(16, 8, 128)[:, :, :68].transpose(1, 0, 2)
-    return vectors.reshape(8, -1), row[:, 8 * 128 : 8 * 128 + 4 * 68].reshape(1, -1)
-
-
 def four_by_four(
     inputs,
     cotangent,
@@ -1930,19 +1891,15 @@
     def flat(page):
         return page.reshape(-1, page.shape[2])
 
-    lower_page, rows = gather_page(attention_shard, inputs)
-    small, wide = small_of(lower_page)
-    shards = (expand_shard, reduce_shard, attention_shard, expand_shard, reduce_shard)
-    saved, saved_upper, gathered, top, upper_small = forward(
-        rows, small, wide, table, lower_page, cotangent, shards
-    )
-    lower_expand, lower_reduce, upper_page, upper_expand, upper_reduce = gathered
+    shards = (attention_shard, expand_shard, reduce_shard) * 2
+    saved, saved_upper, gathered, (rows, top), smalls = forward(table, (inputs, cotangent), shards)
+    lower_page, lower_expand, lower_reduce, upper_page, upper_expand, upper_reduce = gathered
     weights = (flat(lower_page), flat(lower_expand), flat(lower_reduce))
     upper_weights = (flat(upper_page), flat(upper_expand), flat(upper_reduce))
     middle_rows, final_rows = saved[13], saved_upper[13]
     saved_lower, saved_upper = (rows,) + tuple(saved[:13]), (middle_rows,) + tuple(saved_upper[:13])
     vectors, layer_outputs, input_grads, (reduce_sum, expand_sum, attention_sum) = backward(
-        top, (saved_lower, saved_upper), (small, upper_small), table, (weights, upper_weights), final_rows
+        top, (saved_lower, saved_upper), smalls, table, (weights, upper_weights), final_rows
     )
     vectors = vectors[:12, :68]
     return (

time: 687 us -> 657 us (0.956)
  Pallas kernels: 655 us -> 631 us
    pallas_call x2 -> x1, Pallas kernels: 316 us -> 304 us  [forward(): pl.pallas_call(forward_kernel, out_shape=tuple(outs), in_specs=[inside] +...]
    pallas_call x1, Pallas kernels: 339 us -> 327 us  [backward(): pl.pallas_call(backward_kernel, out_shape=tuple(outs), in_specs=[inside]...]
where the time goes in v8:
time: 657 us; the launch traced here: 650 us
  Pallas kernels  631 us (96%)
  local copies, waits for them, and re-layouts  15.1 us (2%)
    pallas_call x1, Pallas kernels, backward(): pl.pallas_call(backward_kernel, out_shape=tuple(outs), in_specs=[inside]...  327 us
    pallas_call x1, Pallas kernels, forward(): pl.pallas_call(forward_kernel, out_shape=tuple(outs), in_specs=[inside] +...  304 us

profile of v8, /device:TPU:0, one launch (start us, length us, event | category | flops | bytes accessed | tf_op | source)
XLA Modules:
  0.0 650.1 jit_solution(3948482565322636789)
XLA Ops:
  0.6 0.0 copy-start.6
  0.7 0.9 pad_add_fusion
  1.5 0.0 copy-start.4
  1.5 2.1 fusion.refs_3_.refs_6_
  3.7 0.0 copy-done.6
  3.7 0.9 pad.49.refs_4_.refs_7_
  4.5 0.0 copy-done.4
  4.5 1.4 copy.31.refs_1_
  6.0 1.4 copy.32.refs_2_
  7.4 303.8 %forward.1 = (bf16[256,1152]{1,0:T(8,128)(2,1)}, bf16[256,1152]{1,0:T(8,128)(2,1)}, bf16[2,256,1152]{2,1,0:T(8,128)(2,1)}, bf16[2,256,1152]{2,1,0:T(8,128)(2,1)}...) custom-call(bf16[1088,1152]{1,0:T(8,128)(2,1)} %constant.5.clone.ref, ...), custom_call_target="tpu_custom_call" | custom-call | tf_op jit(solution)/shard_map/forward/pallas_call | solution.py:1077
  311.2 327.0 %backward.1 = (f32[16,128]{1,0:T(8,128)}, bf16[4352,1088]{1,0:T(8,128)(2,1)}, bf16[16,72,4352]{2,1,0:T(8,128)(2,1)}, bf16[16,72,4352]{2,1,0:T(8,128)(2,1)}, bf16...) custom-call(f32[8,1088]{1,0:T(8,128)} %get-tuple-element.59.refs_0_,, ...), custom_call_target="tpu_custom_call" | custom-call | tf_op jit(solution)/shard_map/backward/pallas_call | solution.py:1831
  638.2 2.4 copy.33
  640.6 0.0 copy-done.3
  640.6 1.4 copy.34
  642.0 0.5 fusion.1
  642.6 0.6 reshape.57
  643.2 0.1 slice_bitcast_fusion.2
  643.4 0.1 slice_bitcast_fusion.1
  643.4 1.9 copy.35
  645.3 1.0 copy.36
  646.3 0.1 slice_bitcast_fusion
  646.4 0.0 copy-start.1
  646.4 2.2 copy.37
  648.7 1.0 copy.39
  (11 shorter events, 0.0 us)
Async XLA Ops:
  0.6 3.0 copy-start.6
  1.5 3.0 copy-start.4
  4.5 1.4 copy-start.5
  638.2 2.4 copy-start.3
  640.6 1.4 copy-start.7
  640.6 2.6 copy-start
  643.4 2.9 copy-start.2
  646.4 2.2 copy-start.1
